TPU v7x, 32 devices: a whole 2x2x4 slice. The times are simulated.
32 devices in a mesh: rows: 4 (over y, x), blk: 8 (over z, core).
Axes of the slice: x: 2, y: 2, z: 4, core: 2. Of those that a mesh axis runs over, the one named last changes fastest.
Arguments:
- tokens: bfloat16 [4, 1024, 2048], P('rows', 'blk'), may hold values from -6 to 6
- cotangent: bfloat16 [4, 1024, 2048], P('rows', 'blk'), may hold values from -6 to 6
- lengths: int32 [4], P('rows'), may hold values from 512 to 1024, as said below
- block_map: int32 [4, 16], P('rows'), may hold values from 0 to 15, as said below
- gain_attend: float32 [2048], replicated, may hold values from 0.5 to 1.5
- gain_expand: float32 [2048], replicated, may hold values from 0.5 to 1.5
- attend_in: float32 [2048, 6144], P(('rows', 'blk')), may hold values from -0.125 to 0.125
- attend_out: float32 [2048, 2048], P(None, ('rows', 'blk')), may hold values from -2 to 2
- expand_in: float32 [2048, 16384], P(('rows', 'blk')), may hold values from -0.125 to 0.125
- reduce_out: float32 [8192, 2048], P(None, ('rows', 'blk')), may hold values from -0.0625 to 0.0625
- attend_in_first: float32 [2048, 6144], P(('rows', 'blk')), may hold values from -72 to 72
- attend_out_first: float32 [2048, 2048], P(None, ('rows', 'blk')), may hold values from -0.6 to 0.6
- expand_in_first: float32 [2048, 16384], P(('rows', 'blk')), may hold values from -0.6 to 0.6
- reduce_out_first: float32 [8192, 2048], P(None, ('rows', 'blk')), may hold values from -0.6 to 0.6
- attend_in_second: float32 [2048, 6144], P(('rows', 'blk')), may hold values from 12.288 to 1228.8
- attend_out_second: float32 [2048, 2048], P(None, ('rows', 'blk')), may hold values from 0.24576 to 24.576
- expand_in_second: float32 [2048, 16384], P(('rows', 'blk')), may hold values from 0.001 to 1
- reduce_out_second: float32 [8192, 2048], P(None, ('rows', 'blk')), may hold values from 0.01 to 100
Outputs:
- layer_out: bfloat16 [4, 1024, 2048], P('rows', 'blk')
- grad_input: float32 [4, 1024, 2048], P('rows', 'blk')
- grad_gain_attend: float32 [2048], replicated
- grad_gain_expand: float32 [2048], replicated
- attend_in_next: float32 [2048, 6144], P(('rows', 'blk'))
- attend_in_first_next: float32 [2048, 6144], P(('rows', 'blk'))
- attend_in_second_next: float32 [2048, 6144], P(('rows', 'blk'))
- attend_out_first_next: float32 [2048, 2048], P(None, ('rows', 'blk'))
- attend_out_second_next: float32 [2048, 2048], P(None, ('rows', 'blk'))
- expand_in_next: float32 [2048, 16384], P(('rows', 'blk'))
- expand_in_first_next: float32 [2048, 16384], P(('rows', 'blk'))
- expand_in_second_next: float32 [2048, 16384], P(('rows', 'blk'))
- reduce_out_next: float32 [8192, 2048], P(None, ('rows', 'blk'))
- reduce_out_first_next: float32 [8192, 2048], P(None, ('rows', 'blk'))
- reduce_out_second_next: float32 [8192, 2048], P(None, ('rows', 'blk'))
Inputs may be any that keep to these rules, and one draw needn't show every extreme that they name: `lengths`: one row of every draw has length exactly 1024. `block_map`: in each row, the blocks stored at indices 2 j and 2 j + 1 are b and 15 - b for some b < 8; every block of the row is stored once.
All inputs are finite; a program needn't handle non-finite values.
Results may differ from a plain program's by a relative error of at most 0.033.
Values may be sent and summed in bfloat16 or wider, within the bound.
A program may use at most 896 MiB of HBM per device.

v0:
```python
import math

import jax
import jax.numpy as jnp
from jax import lax
from jax.sharding import PartitionSpec as P

HEADS = 32
HEAD_DIM = 64


theta_base = 130000.0
norm_eps = 1e-05
neg_large = -1e30
beta_one = 0.9
beta_two = 0.95
learn_rate = 0.01
decay_rate = 0.1
adam_eps = 1e-08
step_count = 10


def from_behind(x, axis, by):
    size = lax.axis_size(axis)
    return lax.ppermute(x, axis, [(i, (i + by) % size) for i in range(size)])


def rope_tables(positions, head_size):
    halfway = head_size // 2
    frequency = jnp.exp(
        -jnp.arange(halfway, dtype=jnp.float32) * (2.0 / head_size) * math.log(theta_base)
    )
    angles = positions.astype(jnp.float32)[:, None] * frequency[None, :]
    return (jnp.cos(angles)[:, None, :], jnp.sin(angles)[:, None, :])


def rotate(values, cosine, sine_table):
    halfway = values.shape[-1] // 2
    front_half = values[..., :halfway]
    back_half = values[..., halfway:]
    return jnp.concatenate(
        [
            front_half * cosine - back_half * sine_table,
            back_half * cosine + front_half * sine_table,
        ],
        axis=-1,
    )


def rotate_back(values, cosine, sine_table):
    halfway = values.shape[-1] // 2
    front_half = values[..., :halfway]
    back_half = values[..., halfway:]
    return jnp.concatenate(
        [
            front_half * cosine + back_half * sine_table,
            back_half * cosine - front_half * sine_table,
        ],
        axis=-1,
    )


def norm_forward(values, gain_vector):
    inverse = lax.rsqrt(jnp.mean(values * values, axis=-1, keepdims=True) + norm_eps)
    unit_values = values * inverse
    return (unit_values, inverse, (unit_values * gain_vector).astype(jnp.bfloat16))


def norm_backward(grad_normed, unit_values, inverse, gain_vector):
    grad_unit = grad_normed * gain_vector
    grad_values = inverse * (
        grad_unit - unit_values * jnp.mean(grad_unit * unit_values, axis=-1, keepdims=True)
    )
    return (grad_values, jnp.sum(grad_normed * unit_values, axis=0))


def contract_last(left, right):
    return lax.dot_general(
        left, right, (((1,), (1,)), ((), ())), preferred_element_type=jnp.float32
    )


def gather_weights(masters):
    attend_in, attend_out, expand_in, reduce_out = masters
    return (
        lax.all_gather(attend_in.astype(jnp.bfloat16), ("rows", "blk"), axis=0, tiled=True),
        lax.all_gather(expand_in.astype(jnp.bfloat16), ("rows", "blk"), axis=0, tiled=True),
        lax.all_gather(attend_out.T.astype(jnp.bfloat16), ("rows", "blk"), axis=0, tiled=True),
        lax.all_gather(reduce_out.T.astype(jnp.bfloat16), ("rows", "blk"), axis=0, tiled=True),
    )


def cycle_turns(keys_low, values_low, state, visit):
    cycle_size = lax.axis_size("blk")

    def turn(turn_index, carried):
        key_now, value_now, inner = carried
        inner = visit(turn_index, key_now, value_now, inner)
        key_now, value_now = from_behind((key_now, value_now), "blk", 1)
        return (key_now, value_now, inner)

    return lax.fori_loop(0, cycle_size, turn, (keys_low, values_low, state))[2]


def cycle_attend(queries, keys_low, values_low, query_pos, key_pos_all, length):
    head_count, seq_len, head_size = queries.shape
    factor = 1.0 / math.sqrt(head_size)
    cycle_size = lax.axis_size("blk")
    position_here = lax.axis_index("blk")
    initial = (
        jnp.full((head_count, seq_len), neg_large, jnp.float32),
        jnp.zeros((head_count, seq_len), jnp.float32),
        jnp.zeros((head_count, seq_len, head_size), jnp.float32),
    )

    def visit(turn_index, key_now, value_now, running):
        top_score, denominator, accumulated = running
        source = (position_here - turn_index) % cycle_size
        key_place = lax.dynamic_slice_in_dim(key_pos_all, source * seq_len, seq_len, 0)
        key_block = key_now.reshape(seq_len, head_count, head_size)
        value_block = value_now.reshape(seq_len, head_count, head_size)
        scores = (
            jnp.einsum("hqe,khe->hqk", queries, key_block, preferred_element_type=jnp.float32)
            * factor
        )
        allowed = (key_place[None, None, :] <= query_pos[None, :, None]) & (
            key_place[None, None, :] < length
        )
        scores = jnp.where(allowed, scores, neg_large)
        new_top = jnp.maximum(top_score, jnp.max(scores, axis=-1))
        shrink = jnp.exp(top_score - new_top)
        weights = jnp.exp(scores - new_top[..., None])
        denominator = denominator * shrink + jnp.sum(weights, axis=-1)
        accumulated = accumulated * shrink[..., None] + jnp.einsum(
            "hqk,khe->hqe",
            weights.astype(jnp.bfloat16),
            value_block,
            preferred_element_type=jnp.float32,
        )
        return (new_top, denominator, accumulated)

    top_score, denominator, accumulated = cycle_turns(keys_low, values_low, initial, visit)
    live_rows = (query_pos < length)[None, :, None]
    outputs = jnp.where(live_rows, accumulated / denominator[..., None], 0.0)
    return (outputs, top_score + jnp.log(denominator))


def cycle_attend_back(
    queries, keys_low, values_low, grad_heads, row_delta, log_total, query_pos, key_pos_all, length
):
    head_count, seq_len, head_size = queries.shape
    factor = 1.0 / math.sqrt(head_size)
    cycle_size = lax.axis_size("blk")
    position_here = lax.axis_index("blk")
    zero_keys = jnp.zeros(keys_low.shape, jnp.float32)
    initial = (zero_keys, zero_keys, jnp.zeros(queries.shape, jnp.float32))

    def visit(turn_index, key_now, value_now, running):
        grad_keys, grad_values, grad_queries = running
        source = (position_here - turn_index) % cycle_size
        key_place = lax.dynamic_slice_in_dim(key_pos_all, source * seq_len, seq_len, 0)
        key_block = key_now.reshape(seq_len, head_count, head_size)
        value_block = value_now.reshape(seq_len, head_count, head_size)
        scores = (
            jnp.einsum("hqe,khe->hqk", queries, key_block, preferred_element_type=jnp.float32)
            * factor
        )
        allowed = (key_place[None, None, :] <= query_pos[None, :, None]) & (
            key_place[None, None, :] < length
        )
        probabilities = jnp.where(allowed, jnp.exp(scores - log_total[..., None]), 0.0)
        grad_values = grad_values + jnp.einsum(
            "hqk,hqe->khe",
            probabilities.astype(jnp.bfloat16),
            grad_heads,
            preferred_element_type=jnp.float32,
        ).reshape(seq_len, -1)
        grad_probs = jnp.einsum(
            "hqe,khe->hqk", grad_heads, value_block, preferred_element_type=jnp.float32
        )
        grad_scores = (probabilities * (grad_probs - row_delta[..., None])).astype(jnp.bfloat16)
        grad_queries = grad_queries + jnp.einsum(
            "hqk,khe->hqe", grad_scores, key_block, preferred_element_type=jnp.float32
        )
        grad_keys = grad_keys + jnp.einsum(
            "hqk,hqe->khe", grad_scores, queries, preferred_element_type=jnp.float32
        ).reshape(seq_len, -1)
        grad_keys, grad_values = (
            from_behind(grad_keys.astype(jnp.bfloat16), "blk", 1).astype(grad_keys.dtype),
            from_behind(grad_values.astype(jnp.bfloat16), "blk", 1).astype(grad_values.dtype),
        )
        return (grad_keys, grad_values, grad_queries)

    finished = cycle_turns(keys_low, values_low, initial, visit)
    return (finished[2] * factor, finished[0] * factor, finished[1])


def whole_forward(
    tokens_wide, gain_attend, gain_expand, full_weights, query_pos, key_pos_all, length
):
    mixing_full, gating_full, attend_side, reduce_side = full_weights
    seq_len, model_width = tokens_wide.shape
    unit_one, inverse_one, normed_one = norm_forward(tokens_wide, gain_attend)
    mixed_qkv = jnp.dot(normed_one, mixing_full, preferred_element_type=jnp.float32).reshape(
        seq_len, 3, HEADS, HEAD_DIM
    )
    cosine, sine_table = rope_tables(query_pos, HEAD_DIM)
    query_rows = rotate(mixed_qkv[:, 0], cosine, sine_table).astype(jnp.bfloat16)
    keys_low = (
        rotate(mixed_qkv[:, 1], cosine, sine_table)
        .astype(jnp.bfloat16)
        .reshape(seq_len, model_width)
    )
    values_low = mixed_qkv[:, 2].astype(jnp.bfloat16).reshape(seq_len, model_width)
    queries = jnp.transpose(query_rows, (1, 0, 2))
    attended, log_total = cycle_attend(
        queries, keys_low, values_low, query_pos, key_pos_all, length
    )
    attended_low = (
        jnp.transpose(attended, (1, 0, 2)).reshape(seq_len, model_width).astype(jnp.bfloat16)
    )
    residual = tokens_wide + contract_last(attended_low, attend_side)
    unit_two, inverse_two, normed_two = norm_forward(residual, gain_expand)
    gate_up = jnp.dot(normed_two, gating_full, preferred_element_type=jnp.float32)
    units = gate_up.shape[1] // 2
    gate_part = gate_up[:, :units]
    up_part = gate_up[:, units:]
    hidden_low = (gate_part * jax.nn.sigmoid(gate_part) * up_part).astype(jnp.bfloat16)
    return (
        unit_one,
        inverse_one,
        normed_one,
        queries,
        keys_low,
        values_low,
        attended,
        log_total,
        attended_low,
        residual,
        unit_two,
        inverse_two,
        normed_two,
        gate_part,
        up_part,
        hidden_low,
    )


def whole_layer(tokens_wide, grad_low, gains, masters, query_pos, key_pos_all, length):
    gain_attend, gain_expand = gains
    seq_len, model_width = tokens_wide.shape
    full_weights = gather_weights(masters)
    mixing_full, gating_full, attend_side, reduce_side = full_weights
    saved = whole_forward(
        tokens_wide, gain_attend, gain_expand, full_weights, query_pos, key_pos_all, length
    )
    result = saved[9] + contract_last(saved[15], reduce_side)
    (
        unit_one,
        inverse_one,
        normed_one,
        queries,
        keys_low,
        values_low,
        attended,
        log_total,
        attended_low,
        residual,
        unit_two,
        inverse_two,
        normed_two,
        gate_part,
        up_part,
        hidden_low,
    ) = saved
    grad_output = grad_low.astype(jnp.float32)
    grad_hidden = jnp.dot(grad_low, reduce_side, preferred_element_type=jnp.float32)
    gate_sigmoid = jax.nn.sigmoid(gate_part)
    grad_gate = grad_hidden * up_part * (gate_sigmoid * (1.0 + gate_part * (1.0 - gate_sigmoid)))
    grad_up = grad_hidden * (gate_part * gate_sigmoid)
    grad_expand_low = jnp.concatenate([grad_gate, grad_up], axis=1).astype(jnp.bfloat16)
    grad_normed_two = contract_last(grad_expand_low, gating_full)
    grad_middle, grad_gain_two = norm_backward(grad_normed_two, unit_two, inverse_two, gain_expand)
    grad_resid = grad_output + grad_middle
    grad_branch = grad_resid.astype(jnp.bfloat16)
    grad_attended = jnp.dot(grad_branch, attend_side, preferred_element_type=jnp.float32)
    live_rows = (query_pos < length)[None, :, None]
    grad_heads = jnp.where(
        live_rows,
        jnp.transpose(grad_attended.reshape(seq_len, HEADS, HEAD_DIM), (1, 0, 2)).astype(
            jnp.bfloat16
        ),
        jnp.zeros((), jnp.bfloat16),
    )
    row_delta = jnp.sum(grad_heads.astype(jnp.float32) * attended, axis=-1)
    grad_queries, grad_keys, grad_values = cycle_attend_back(
        queries,
        keys_low,
        values_low,
        grad_heads,
        row_delta,
        log_total,
        query_pos,
        key_pos_all,
        length,
    )
    cosine, sine_table = rope_tables(query_pos, HEAD_DIM)
    query_rows = jnp.transpose(grad_queries.astype(jnp.bfloat16).astype(jnp.float32), (1, 0, 2))
    key_rows = grad_keys.astype(jnp.bfloat16).astype(jnp.float32).reshape(seq_len, HEADS, HEAD_DIM)
    value_rows = grad_values.reshape(seq_len, HEADS, HEAD_DIM)
    grad_mixed = (
        jnp.stack(
            [
                rotate_back(query_rows, cosine, sine_table),
                rotate_back(key_rows, cosine, sine_table),
                value_rows,
            ],
            axis=1,
        )
        .reshape(seq_len, 3 * model_width)
        .astype(jnp.bfloat16)
    )
    grad_normed_one = contract_last(grad_mixed, mixing_full)
    grad_first, grad_gain_one = norm_backward(grad_normed_one, unit_one, inverse_one, gain_attend)
    grad_input = grad_resid + grad_first
    contract_rows = (((0,), (0,)), ((), ()))
    first = lax.dot_general(
        normed_one, grad_mixed, contract_rows, preferred_element_type=jnp.float32
    )
    second = lax.dot_general(
        normed_two, grad_expand_low, contract_rows, preferred_element_type=jnp.float32
    )
    third = lax.dot_general(
        grad_branch, attended_low, contract_rows, preferred_element_type=jnp.float32
    )
    fourth = lax.dot_general(
        grad_low, hidden_low, contract_rows, preferred_element_type=jnp.float32
    )
    summed = lax.psum_scatter(
        jnp.concatenate([first, second, third, fourth], axis=1),
        ("rows", "blk"),
        scatter_dimension=0,
        tiled=True,
    )
    width_qkv = mixing_full.shape[1]
    width_gu = gating_full.shape[1]
    grad_attend_in = summed[:, :width_qkv]
    grad_expand = summed[:, width_qkv : width_qkv + width_gu]
    grad_attend_out = summed[:, width_qkv + width_gu : width_qkv + width_gu + model_width].T
    grad_reduce = summed[:, width_qkv + width_gu + model_width :].T
    return (
        result,
        grad_input,
        grad_gain_one,
        grad_gain_two,
        grad_attend_in,
        grad_attend_out,
        grad_expand,
        grad_reduce,
    )


def adam_step(master, moment_one, moment_two, gradient):
    moment_one = beta_one * moment_one + (1.0 - beta_one) * gradient
    moment_two = beta_two * moment_two + (1.0 - beta_two) * gradient * gradient
    update = (
        moment_one
        / (1.0 - beta_one**step_count)
        / (jnp.sqrt(moment_two / (1.0 - beta_two**step_count)) + adam_eps)
    )
    return (master - learn_rate * (update + decay_rate * master), moment_one, moment_two)


def moment_step(moment_one, moment_two, gradient):
    moment_one = beta_one * moment_one + (1.0 - beta_one) * gradient
    moment_two = beta_two * moment_two + (1.0 - beta_two) * gradient * gradient
    return (moment_one, moment_two)


def shards(
    tokens,
    cotangent,
    lengths,
    block_map,
    gain_attend,
    gain_expand,
    attend_in,
    attend_out,
    expand_in,
    reduce_out,
    attend_in_first,
    attend_out_first,
    expand_in_first,
    reduce_out_first,
    attend_in_second,
    attend_out_second,
    expand_in_second,
    reduce_out_second,
):
    seq_len = tokens.shape[1]
    block_rows = seq_len // 2
    length = lengths[0]
    offsets = jnp.arange(block_rows, dtype=jnp.int32)
    key_pos_all = (block_map[0][:, None] * block_rows + offsets[None, :]).reshape(-1)
    query_pos = lax.dynamic_slice_in_dim(key_pos_all, lax.axis_index("blk") * seq_len, seq_len, 0)
    tokens_wide = tokens[0].astype(jnp.float32)
    gains = (gain_attend, gain_expand)
    masters = (attend_in, attend_out, expand_in, reduce_out)
    outcome = whole_layer(tokens_wide, cotangent[0], gains, masters, query_pos, key_pos_all, length)
    (
        result,
        grad_input,
        grad_gain_one,
        grad_gain_two,
        grad_attend_in,
        grad_attend_out,
        grad_expand,
        grad_reduce,
    ) = outcome
    gain_grads = lax.psum((grad_gain_one, grad_gain_two), ("rows", "blk"))
    set_one = adam_step(attend_in, attend_in_first, attend_in_second, grad_attend_in)
    set_two = moment_step(attend_out_first, attend_out_second, grad_attend_out)
    set_three = adam_step(expand_in, expand_in_first, expand_in_second, grad_expand)
    set_four = adam_step(reduce_out, reduce_out_first, reduce_out_second, grad_reduce)
    return (
        result.astype(jnp.bfloat16).reshape(tokens.shape),
        grad_input.reshape(tokens.shape),
        gain_grads[0],
        gain_grads[1],
        set_one[0],
        set_one[1],
        set_one[2],
        set_two[0],
        set_two[1],
        set_three[0],
        set_three[1],
        set_three[2],
        set_four[0],
        set_four[1],
        set_four[2],
    )


def solution(mesh):
    placed = (
        P("rows", "blk", None),
        P("rows", "blk", None),
        P("rows"),
        P("rows", None),
        P(),
        P(),
        P(("rows", "blk"), None),
        P(None, ("rows", "blk")),
        P(("rows", "blk"), None),
        P(None, ("rows", "blk")),
        P(("rows", "blk"), None),
        P(None, ("rows", "blk")),
        P(("rows", "blk"), None),
        P(None, ("rows", "blk")),
        P(("rows", "blk"), None),
        P(None, ("rows", "blk")),
        P(("rows", "blk"), None),
        P(None, ("rows", "blk")),
    )
    return jax.shard_map(
        shards,
        mesh=mesh,
        in_specs=placed,
        out_specs=(
            P("rows", "blk", None),
            P("rows", "blk", None),
            P(),
            P(),
            P(("rows", "blk"), None),
            P(("rows", "blk"), None),
            P(("rows", "blk"), None),
            P(None, ("rows", "blk")),
            P(None, ("rows", "blk")),
            P(("rows", "blk"), None),
            P(("rows", "blk"), None),
            P(("rows", "blk"), None),
            P(None, ("rows", "blk")),
            P(None, ("rows", "blk")),
            P(None, ("rows", "blk")),
        ),
        check_vma=False,
    )
```

profile of v0, /device:TPU:0, one launch (start us, length us, event | category | flops | bytes accessed | tf_op | source)
XLA Modules:
  0.0 4310.6 jit_solution(7057668405267007472)
XLA Ops:
  18.5 150.5 %all-gather.5.cloned.1.call-done = bf16[2048,6144]{1,0:T(8,128)(2,1)} async-done(((bf16[64,6144]{1,0:T(8,128)(2,1)}), bf16[2048,6144]{1,0:T(8,128)(2,1)}) %all-gather.5.cloned.1.call-update) | async-done | bytes 25165840 | tf_op jit(solution)/shard_map/all_gather | solution.py:86
  169.0 32.9 copy.39
  202.0 13.5 fusion.38
  221.8 261.5 %while.48 = (s32[]{:T(128)}, bf16[128,2048]{0,1:T(8,128)(2,1)}, bf16[128,2048]{0,1:T(8,128)(2,1)}, f32[32,128]{1,0:T(8,128)S(1)}, f32[32,128]{1,0:T(8,128)S(1)},...) while((s32[]{:T(128)}, bf16[128,2048]{0,1:T(8,128)(2,1)}, ...), condition=%wide.region_4.5_spmd.clone, body=%wide.region_1.4_spmd.clone.sunk | while | flops 140824720 | bytes 16583336 | solution.py:102
  226.9 17.8 collective-permute-done
  244.6 11.6 collective-permute-done.1
  261.0 6.8 collective-permute-done
  267.8 5.8 collective-permute-done.1
  278.4 18.0 collective-permute-done
  296.4 16.9 collective-permute-done.1
  318.0 17.3 collective-permute-done
  335.4 5.6 collective-permute-done.1
  345.9 18.0 collective-permute-done
  363.8 16.8 collective-permute-done.1
  385.4 18.0 collective-permute-done
  403.5 16.8 collective-permute-done.1
  425.1 18.0 collective-permute-done
  443.0 16.9 collective-permute-done.1
  473.0 10.3 collective-permute-done.1
  484.3 6.7 multiply_reduce_fusion.3
  491.0 173.9 %all-gather.9.cloned.1.call-done = bf16[2048,16384]{1,0:T(8,128)(2,1)} async-done(((bf16[64,16384]{1,0:T(8,128)(2,1)}), bf16[2048,16384]{1,0:T(8,128)(2,1)}) %all-gather.9.cloned.1.call-update) | async-done | bytes 67108880 | tf_op jit(solution)/shard_map/all_gather | solution.py:87
  664.9 27.0 fusion.53
  691.9 178.2 %all-gather.11.cloned.1.call-done = bf16[2048,8192]{1,0:T(8,128)(2,1)} async-done(((bf16[64,8192]{1,0:T(8,128)(2,1)}), bf16[2048,8192]{1,0:T(8,128)(2,1)}) %all-gather.11.cloned.1.call-update) | async-done | bytes 33554448 | tf_op jit(solution)/shard_map/all_gather | solution.py:89
  870.1 19.4 multiply_convert_fusion.2
  889.5 45.5 %fusion.17 = f32[2048,16384]{1,0:T(8,128)} fusion(bf16[128,8192]{1,0:T(8,128)(2,1)} %get-tuple-element.778, bf16[128,8192]{1,0:T(8,128)(2,1)} %get-tuple-element.777, f32[128,2048]{1,0:T(8,128)S(1)} %get-tuple-element.799, f32[2048]{0:T(1024)S(1)} %copy-done.20, f32[128]{0:T(128)S(1)} %add_rsqrt_fusion), kind=kOutput, calls=%fused_computation.44 | convolution fusion | flops 8599109632 | bytes 139469312 | tf_op jit(solution)/shard_map/dot_general | solution.py:330
  935.0 30.9 multiply_reduce_fusion
  967.6 8.1 fusion.46
  981.1 277.4 %while.49 = (s32[]{:T(128)}, bf16[128,2048]{0,1:T(8,128)(2,1)}, bf16[128,2048]{0,1:T(8,128)(2,1)}, f32[128,2048]{0,1:T(8,128)}, f32[128,2048]{0,1:T(8,128)}, /*i...) while((s32[]{:T(128)}, bf16[128,2048]{0,1:T(8,128)(2,1)}, ...), condition=%wide.region_9.10_spmd.clone, body=%wide.region_8.9_spmd.clone.sunk | while | flops 341868672 | bytes 44632900 | solution.py:102
  1010.2 5.6 collective-permute-done.3
  1028.1 5.5 collective-permute-done.4
  1044.9 5.6 collective-permute-done.3
  1079.5 5.6 collective-permute-done.3
  1097.4 5.5 collective-permute-done.4
  1114.2 5.6 collective-permute-done.3
  1148.8 5.6 collective-permute-done.3
  1166.7 5.5 collective-permute-done.4
  1183.5 5.6 collective-permute-done.3
  1218.2 5.6 collective-permute-done.3
  1252.8 5.6 collective-permute-done.3
  1262.2 19.6 fusion.43
  1281.8 24.7 convolution_bitcast_fusion
  1306.5 176.9 %pad_maximum_fusion = f32[2048,32768]{1,0:T(8,128)} fusion(f32[2048,8192]{1,0:T(8,128)} %convolution_bitcast_fusion, f32[2048,2048]{1,0:T(8,128)} %fusion.46, f32[2048,16384]{1,0:T(8,128)} %fusion.17, f32[2048,6144]{1,0:T(8,128)} %fusion.43), kind=kLoop, calls=%fused_computation.30 | loop fusion | flops 201326592 | bytes 536870912 | tf_op jit(solution)/shard_map/concatenate | solution.py:340
  1484.4 15.3 fusion.33
  1499.7 39.1 all-reduce
  1541.5 17.1 fusion.20
  1558.7 2722.3 %reduce-scatter.2.cloned.1.call-done = f32[64,32768]{1,0:T(8,128)} async-done(((f32[2048,32768]{1,0:T(8,128)}), f32[64,32768]{1,0:T(8,128)}) %reduce-scatter.2.cloned.1.call-update) | async-done | bytes 8388624 | tf_op jit(solution)/shard_map/reduce_scatter | solution.py:339
  4290.1 6.2 multiply_subtract_fusion.1
  4298.3 5.6 multiply_subtract_fusion
  (412 shorter events, 305.3 us)
Async XLA Ops:
  7.2 161.8 %all-gather.5.cloned.1.call-start = ((), (), s32[]{:S(2)}) async-start(), calls=%async_computation.1 | async-start | bytes 25952256 | tf_op jit(solution)/shard_map/all_gather | solution.py:86
  9.7 474.6 %all-gather.7.cloned.1.call-start = ((), (), s32[]{:S(2)}) async-start(), calls=%async_computation.2 | async-start | bytes 8650752 | tf_op jit(solution)/shard_map/all_gather | solution.py:88
  10.5 654.4 %all-gather.9.cloned.1.call-start = ((), (), s32[]{:S(2)}) async-start(), calls=%async_computation.3 | async-start | bytes 69206016 | tf_op jit(solution)/shard_map/all_gather | solution.py:87
  14.3 855.7 %all-gather.11.cloned.1.call-start = ((), (), s32[]{:S(2)}) async-start(), calls=%async_computation.4 | async-start | bytes 34603008 | tf_op jit(solution)/shard_map/all_gather | solution.py:89
  17.1 4263.9 %reduce-scatter.2.cloned.1.call-start = ((), (), s32[]{:S(2)}) async-start(), calls=%async_computation.5 | async-start | bytes 276824064 | tf_op jit(solution)/shard_map/reduce_scatter | solution.py:339
  222.9 21.8 collective-permute-start
  224.2 32.0 collective-permute-start.1
  258.3 15.3 collective-permute-start.1
  274.6 21.8 collective-permute-start
  275.7 37.6 collective-permute-start.1
  314.3 21.1 collective-permute-start
  315.3 25.7 collective-permute-start.1
  342.1 21.8 collective-permute-start
  343.2 37.5 collective-permute-start.1
  381.7 21.8 collective-permute-start
  382.7 37.5 collective-permute-start.1
  421.3 21.7 collective-permute-start
  422.4 37.5 collective-permute-start.1
  460.9 12.1 collective-permute-start
  465.5 17.8 collective-permute-start.1
  988.2 10.7 collective-permute-start.4
  990.4 14.2 collective-permute-start.5
  990.6 19.6 collective-permute-start.2
  990.6 25.2 collective-permute-start.3
  1022.9 10.7 collective-permute-start.4
  1025.0 14.2 collective-permute-start.5
  1025.0 19.8 collective-permute-start.2
  1025.0 25.4 collective-permute-start.3
  1057.6 10.7 collective-permute-start.4
  1059.7 14.2 collective-permute-start.5
  1059.7 19.8 collective-permute-start.2
  1059.7 25.4 collective-permute-start.3
  1092.2 10.7 collective-permute-start.4
  1094.4 14.2 collective-permute-start.5
  1094.4 19.8 collective-permute-start.2
  1094.4 25.4 collective-permute-start.3
  1129.0 14.2 collective-permute-start.5
  1129.0 19.8 collective-permute-start.2
  1129.0 25.4 collective-permute-start.3
  1163.7 14.2 collective-permute-start.5
  1163.7 19.8 collective-permute-start.2
  1163.7 25.4 collective-permute-start.3
  1198.4 14.2 collective-permute-start.5
  1198.4 19.8 collective-permute-start.2
  1198.4 25.4 collective-permute-start.3
  1233.0 14.2 collective-permute-start.5
  1233.0 19.8 collective-permute-start.2
  1233.0 25.4 collective-permute-start.3
  (56 other events, 7231.1 us)
Sparse Core Ops, SparseCore 0:
  11.6 157.3 all-gather.4
  172.6 81.2 all-gather.6
  257.5 407.3 all-gather.8
  668.3 201.7 all-gather.10
  1483.5 2797.4 reduce-scatter.1
where the time goes:
time: 4320 us; the launch traced here: 4310 us
  waiting for transfers between devices  3590 us (83%)
  matrix products  289 us (7%)
  other arithmetic  280 us (6%)
  local copies, waits for them, and re-layouts  90.8 us (2%)
    reduce_scatter x1, waiting for transfers between devices, whole_layer(): lax.psum_scatter(jnp.concatenate([first, second, third, fourth], axis=1),...  2720 us
    ppermute x48, waiting for transfers between devices, from_behind(): return lax.ppermute(x, axis, [(i, (i + by) % size) for i in range(size)])  362 us
    all_gather x1, waiting for transfers between devices, gather_weights(): lax.all_gather(reduce_out.T.astype(jnp.bfloat16), ('rows', 'blk'), axis=0...  178 us
    concatenate x1, other arithmetic, whole_layer(): jnp.concatenate([first, second, third, fourth], axis=1)  177 us
    all_gather x1, waiting for transfers between devices, gather_weights(): lax.all_gather(expand_in.astype(jnp.bfloat16), ('rows', 'blk'), axis=0, t...  174 us
    all_gather x1, waiting for transfers between devices, gather_weights(): lax.all_gather(attend_in.astype(jnp.bfloat16), ('rows', 'blk'), axis=0, t...  151 us
  transfers between devices with their start and end apart: 53, of which 52 were waited for; matrix products, arithmetic and copies ran while one was open for 5% of the time, Pallas kernels for 0%

commit v1 on v0

v1 whole, which is shorter than its diff:
```python
import functools
import math

import jax
import jax.numpy as jnp
from jax import lax
from jax.experimental import pallas as pl
from jax.experimental.pallas import tpu as pltpu
from jax.sharding import PartitionSpec as P

HEADS = 32
HEAD_DIM = 64
MESH = pl.DeviceIdType.MESH
MIB = 1 << 20

theta_base = 130000.0
norm_eps = 1e-05
neg_large = -1e30
beta_one = 0.9
beta_two = 0.95
learn_rate = 0.01
decay_rate = 0.1
adam_eps = 1e-08
step_count = 10


def line_place():
    b = lax.axis_index("blk")
    return lax.axis_index("rows"), b // 2, b % 2

def greet(neighbours):
    barrier = pltpu.get_barrier_semaphore()
    for cond, dev in neighbours:
        def sig(dev=dev):
            pl.semaphore_signal(barrier, inc=1, device_id=dev, device_id_type=MESH)
        if cond is None: sig()
        else: pl.when(cond)(sig)
    count = 0
    for cond, dev in neighbours:
        count = count + (1 if cond is None else cond.astype(jnp.int32))
    pl.semaphore_wait(barrier, count)

def gather_kernel(chips, x_ref, o_ref, copy_sem, send_up, send_down, send_side, recv):
    r, z, c = line_place()
    t = x_ref.shape[0]
    up, down, side = (r, 2 * (z + 1) + c), (r, 2 * (z - 1) + c), (r, 2 * z + 1 - c)
    has_up, has_down = z < chips - 1, z > 0
    greet([(None, side), (has_up, up), (has_down, down)])
    def piece(j): return o_ref.at[pl.ds(pl.multiple_of(j * t, t), t)]
    def remote(src, j, sem, dev):
        return pltpu.make_async_remote_copy(src_ref=src, dst_ref=piece(j), send_sem=sem.at[j], recv_sem=recv.at[j], device_id=dev, device_id_type=MESH)
    mine = 2 * z + c
    pl.when(has_up)(lambda: remote(x_ref, mine, send_up, up).start())
    pl.when(has_down)(lambda: remote(x_ref, mine, send_down, down).start())
    remote(x_ref, mine, send_side, side).start()
    local = pltpu.make_async_copy(x_ref, piece(mine), copy_sem)
    local.start()
    for k in range(1, chips):
        @pl.when(z - k >= 0)
        def _():
            j = 2 * (z - k) + c
            remote(piece(j), j, send_up, up).wait_recv()
            pl.when(has_up)(lambda: remote(piece(j), j, send_up, up).start())
            remote(piece(j), j, send_side, side).start()
        @pl.when(z + k < chips)
        def _():
            j = 2 * (z + k) + c
            remote(piece(j), j, send_down, down).wait_recv()
            pl.when(has_down)(lambda: remote(piece(j), j, send_down, down).start())
            remote(piece(j), j, send_side, side).start()
    for y in range(chips):
        j = 2 * y + (1 - c)
        remote(piece(j), j, send_side, side).wait_recv()
    for y in range(chips):
        j = 2 * y + c
        pl.when(has_up & (z >= y))(lambda: remote(piece(j), j, send_up, up).wait_send())
        pl.when(has_down & (z <= y))(lambda: remote(piece(j), j, send_down, down).wait_send())
        remote(piece(j), j, send_side, side).wait_send()
    local.wait()

def line_gather(x, cid, mem=pl.ANY):
    nb = lax.axis_size("blk")
    return pl.pallas_call(
        functools.partial(gather_kernel, nb // 2),
        out_shape=jax.ShapeDtypeStruct((nb * x.shape[0],) + x.shape[1:], x.dtype),
        in_specs=[pl.BlockSpec(memory_space=mem)],
        out_specs=pl.BlockSpec(memory_space=mem),
        scratch_shapes=[pltpu.SemaphoreType.DMA] + [pltpu.SemaphoreType.DMA((nb,))] * 4,
        compiler_params=pltpu.CompilerParams(collective_id=cid, has_side_effects=True, vmem_limit_bytes=60*2**20),
        cost_estimate=pl.CostEstimate(flops=0, bytes_accessed=150000000, transcendentals=0),
    )(x)

def scatter_kernel(chips, x_ref, o_ref, side_buf, up_buf, down_buf, out_buf, send_side, recv_side, send_up, recv_up, send_down, recv_down):
    r, z, c = line_place()
    t = o_ref.shape[0]
    up, down, side = (r, 2 * (z + 1) + c), (r, 2 * (z - 1) + c), (r, 2 * z + 1 - c)
    has_up, has_down = z < chips - 1, z > 0
    greet([(None, side), (has_up, up), (has_down, down)])
    def piece(j): return x_ref.at[pl.ds(pl.multiple_of(j * t, t), t)]
    def to_side(y):
        return pltpu.make_async_remote_copy(src_ref=piece(2 * y + 1 - c), dst_ref=side_buf.at[y], send_sem=send_side.at[y], recv_sem=recv_side.at[y], device_id=side, device_id_type=MESH)
    def to_up(y):
        return pltpu.make_async_remote_copy(src_ref=out_buf.at[y], dst_ref=up_buf.at[y], send_sem=send_up.at[y], recv_sem=recv_up.at[y], device_id=up, device_id_type=MESH)
    def to_down(y):
        return pltpu.make_async_remote_copy(src_ref=out_buf.at[y], dst_ref=down_buf.at[y], send_sem=send_down.at[y], recv_sem=recv_down.at[y], device_id=down, device_id_type=MESH)
    order = []
    lo, hi = 0, chips - 1
    while lo <= hi:
        order.append(hi)
        if lo != hi: order.append(lo)
        lo += 1; hi -= 1
    for y in order:
        to_side(y).start()
    f32 = jnp.float32
    def total(y):
        return piece(2 * y + c)[...].astype(f32) + side_buf[y].astype(f32)
    for step in range(chips - 1):
        y = chips - 1 - step
        @pl.when(y > z)
        def _():
            to_side(y).wait_recv()
            @pl.when(has_down)
            def _():
                to_up(y).wait_recv()
                out_buf[y] = (total(y) + up_buf[y].astype(f32)).astype(out_buf.dtype)
            @pl.when(z == 0)
            def _():
                out_buf[y] = total(y).astype(out_buf.dtype)
            to_up(y).start()
        w = step
        @pl.when(w < z)
        def _():
            to_side(w).wait_recv()
            @pl.when(has_up)
            def _():
                to_down(w).wait_recv()
                out_buf[w] = (total(w) + down_buf[w].astype(f32)).astype(out_buf.dtype)
            @pl.when(z == chips - 1)
            def _():
                out_buf[w] = total(w).astype(out_buf.dtype)
            to_down(w).start()
    for y in range(chips):
        @pl.when(z == y)
        def _():
            to_side(y).wait_recv()
            o_ref[...] = total(y)
            @pl.when(has_down)
            def _():
                to_up(y).wait_recv()
                o_ref[...] += up_buf[y].astype(f32)
            @pl.when(has_up)
            def _():
                to_down(y).wait_recv()
                o_ref[...] += down_buf[y].astype(f32)
    for y in range(chips):
        to_side(y).wait_send()
        pl.when(y > z)(lambda: to_up(y).wait_send())
        pl.when(y < z)(lambda: to_down(y).wait_send())

def line_scatter(x, cid):
    nb = lax.axis_size("blk")
    t = x.shape[0] // nb
    w = x.shape[1]
    V = pl.BlockSpec(memory_space=pltpu.VMEM)
    D = pltpu.SemaphoreType.DMA((nb // 2,))
    return pl.pallas_call(
        functools.partial(scatter_kernel, nb // 2),
        out_shape=jax.ShapeDtypeStruct((t, w), jnp.float32),
        in_specs=[V], out_specs=V,
        scratch_shapes=[pltpu.VMEM((nb // 2, t, w), x.dtype)] * 4 + [D] * 6,
        compiler_params=pltpu.CompilerParams(collective_id=cid, has_side_effects=True, vmem_limit_bytes=60*2**20),
        cost_estimate=pl.CostEstimate(flops=0, bytes_accessed=150000000, transcendentals=0),
    )(x)


def rope_tables(positions, head_size):
    halfway = head_size // 2
    frequency = jnp.exp(
        -jnp.arange(halfway, dtype=jnp.float32) * (2.0 / head_size) * math.log(theta_base)
    )
    angles = positions.astype(jnp.float32)[:, None] * frequency[None, :]
    return (jnp.cos(angles)[:, None, :], jnp.sin(angles)[:, None, :])


def rotate(values, cosine, sine_table):
    halfway = values.shape[-1] // 2
    front_half = values[..., :halfway]
    back_half = values[..., halfway:]
    return jnp.concatenate(
        [
            front_half * cosine - back_half * sine_table,
            back_half * cosine + front_half * sine_table,
        ],
        axis=-1,
    )


def rotate_back(values, cosine, sine_table):
    halfway = values.shape[-1] // 2
    front_half = values[..., :halfway]
    back_half = values[..., halfway:]
    return jnp.concatenate(
        [
            front_half * cosine + back_half * sine_table,
            back_half * cosine - front_half * sine_table,
        ],
        axis=-1,
    )


def norm_forward(values, gain_vector):
    inverse = lax.rsqrt(jnp.mean(values * values, axis=-1, keepdims=True) + norm_eps)
    unit_values = values * inverse
    return (unit_values, inverse, (unit_values * gain_vector).astype(jnp.bfloat16))


def norm_backward(grad_normed, unit_values, inverse, gain_vector):
    grad_unit = grad_normed * gain_vector
    grad_values = inverse * (
        grad_unit - unit_values * jnp.mean(grad_unit * unit_values, axis=-1, keepdims=True)
    )
    return (grad_values, jnp.sum(grad_normed * unit_values, axis=0))


def contract_last(left, right):
    return lax.dot_general(
        left, right, (((1,), (1,)), ((), ())), preferred_element_type=jnp.float32
    )


def adam_step(master, moment_one, moment_two, gradient):
    moment_one = beta_one * moment_one + (1.0 - beta_one) * gradient
    moment_two = beta_two * moment_two + (1.0 - beta_two) * gradient * gradient
    update = (
        moment_one
        / (1.0 - beta_one**step_count)
        / (jnp.sqrt(moment_two / (1.0 - beta_two**step_count)) + adam_eps)
    )
    return (master - learn_rate * (update + decay_rate * master), moment_one, moment_two)


def moment_step(moment_one, moment_two, gradient):
    moment_one = beta_one * moment_one + (1.0 - beta_one) * gradient
    moment_two = beta_two * moment_two + (1.0 - beta_two) * gradient * gradient
    return (moment_one, moment_two)


def attend_kernel(q_ref, k_ref, v_ref, q_place, k_place, length_ref, o_ref, p_ref):
    scores = lax.dot_general(
        q_ref[0], k_ref[0], (((1,), (1,)), ((), ())), preferred_element_type=jnp.float32
    ) * (1.0 / math.sqrt(HEAD_DIM))
    place = q_place[...]
    scores = jnp.where(k_place[...] <= place, scores, neg_large)
    top = jnp.max(scores, axis=-1, keepdims=True)
    weights = jnp.exp(scores - top)
    weights = weights * (1.0 / jnp.sum(weights, axis=-1, keepdims=True))
    low = weights.astype(jnp.bfloat16)
    p_ref[0] = low
    out = jnp.dot(low, v_ref[0], preferred_element_type=jnp.float32)
    o_ref[0] = jnp.where(place < length_ref[0], out, 0.0).astype(jnp.bfloat16)


def attend(q, k, v, place, live_place, length):
    heads, seq, size = q.shape
    tile = 256
    whole = pl.BlockSpec((1, seq, size), lambda h, i: (h, 0, 0))
    part = pl.BlockSpec((1, tile, size), lambda h, i: (h, i, 0))
    return pl.pallas_call(
        attend_kernel,
        grid=(heads, seq // tile),
        in_specs=[
            part,
            whole,
            whole,
            pl.BlockSpec((tile, 1), lambda h, i: (i, 0)),
            pl.BlockSpec((1, seq), lambda h, i: (0, 0)),
            pl.BlockSpec(memory_space=pltpu.SMEM),
        ],
        out_specs=[part, pl.BlockSpec((1, tile, seq), lambda h, i: (h, i, 0))],
        out_shape=[
            jax.ShapeDtypeStruct((heads, seq, size), jnp.bfloat16),
            jax.ShapeDtypeStruct((heads, seq, seq), jnp.bfloat16),
        ],
        compiler_params=pltpu.CompilerParams(vmem_limit_bytes=56 * MIB),
        cost_estimate=pl.CostEstimate(
            flops=4 * heads * seq * seq * size, bytes_accessed=2 * heads * seq * seq,
            transcendentals=heads * seq * seq,
        ),
    )(q, k, v, place[:, None], live_place[None, :], length.reshape(1))


def attend_back_kernel(
    q_ref, k_ref, v_ref, o_ref, g_ref, p_ref, dq_ref, dk_ref, dv_ref, dk_acc, dv_acc
):
    step = pl.program_id(1)

    @pl.when(step == 0)
    def _():
        dk_acc[...] = jnp.zeros_like(dk_acc)
        dv_acc[...] = jnp.zeros_like(dv_acc)

    f32 = jnp.float32
    low = p_ref[0]
    grad = g_ref[0]
    over_rows = (((0,), (0,)), ((), ()))
    dv_acc[...] += lax.dot_general(low, grad, over_rows, preferred_element_type=f32)
    delta = jnp.sum(grad.astype(f32) * o_ref[0].astype(f32), axis=-1, keepdims=True)
    grad_p = lax.dot_general(
        grad, v_ref[0], (((1,), (1,)), ((), ())), preferred_element_type=f32
    )
    grad_s = (low.astype(f32) * (grad_p - delta)).astype(jnp.bfloat16)
    factor = 1.0 / math.sqrt(HEAD_DIM)
    dq_ref[0] = jnp.dot(grad_s, k_ref[0], preferred_element_type=f32) * factor
    dk_acc[...] += lax.dot_general(grad_s, q_ref[0], over_rows, preferred_element_type=f32)

    @pl.when(step == pl.num_programs(1) - 1)
    def _():
        dk_ref[0] = dk_acc[...] * factor
        dv_ref[0] = dv_acc[...]


def attend_back(q, k, v, o, g, p):
    heads, seq, size = q.shape
    tile = 256
    whole = pl.BlockSpec((1, seq, size), lambda h, i: (h, 0, 0))
    part = pl.BlockSpec((1, tile, size), lambda h, i: (h, i, 0))
    shape = jax.ShapeDtypeStruct((heads, seq, size), jnp.float32)
    return pl.pallas_call(
        attend_back_kernel,
        grid=(heads, seq // tile),
        in_specs=[
            part, whole, whole, part, part, pl.BlockSpec((1, tile, seq), lambda h, i: (h, i, 0)),
        ],
        out_specs=[part, whole, whole],
        out_shape=[shape] * 3,
        scratch_shapes=[pltpu.VMEM((seq, size), jnp.float32)] * 2,
        compiler_params=pltpu.CompilerParams(vmem_limit_bytes=56 * MIB),
        cost_estimate=pl.CostEstimate(
            flops=10 * heads * seq * seq * size, bytes_accessed=2 * heads * seq * seq,
            transcendentals=0,
        ),
    )(q, k, v, o, g, p)


def spread(weight, parts):
    rows, columns = weight.shape
    nb = lax.axis_size("blk")
    pieces = weight.astype(jnp.bfloat16).reshape(rows, parts, nb, columns // (parts * nb))
    pieces = pieces.transpose(2, 0, 1, 3).reshape(nb * rows, columns // nb)
    mine = lax.all_to_all(pieces, "blk", 0, 0, tiled=True)
    return lax.all_gather(mine, "rows", axis=0, tiled=True)


def collect(gradient, parts):
    nb = lax.axis_size("blk")
    mine = lax.psum_scatter(
        gradient.astype(jnp.bfloat16), "rows", scatter_dimension=0, tiled=True
    )
    pieces = lax.all_to_all(mine, "blk", 0, 0, tiled=True)
    rows, width = pieces.shape[0] // nb, pieces.shape[1]
    pieces = pieces.reshape(nb, rows, parts, width // parts).transpose(1, 2, 0, 3)
    return pieces.reshape(rows, nb * width).astype(jnp.float32)


def over_tokens(left, right):
    return lax.dot_general(
        left, right, (((0,), (0,)), ((), ())), preferred_element_type=jnp.float32
    )


def shards(
    tokens, cotangent, lengths, block_map, gain_attend, gain_expand,
    attend_in, attend_out, expand_in, reduce_out,
    attend_in_first, attend_out_first, expand_in_first, reduce_out_first,
    attend_in_second, attend_out_second, expand_in_second, reduce_out_second,
):
    f32, bf16 = jnp.float32, jnp.bfloat16
    nb = lax.axis_size("blk")
    near = tokens.shape[1]
    seq = near * nb
    heads = HEADS // nb
    block_rows = near // 2
    length = lengths[0]
    offsets = jnp.arange(block_rows, dtype=jnp.int32)
    place = (block_map[0][:, None] * block_rows + offsets[None, :]).reshape(-1)
    live_place = jnp.where(place < length, place, jnp.int32(1 << 30))
    cosine, sine = rope_tables(place, HEAD_DIM)

    x = tokens[0].astype(f32)
    unit_one, inverse_one, h1 = norm_forward(x, gain_attend)
    w_in = spread(attend_in, 3)
    h1_all = line_gather(h1, 0)
    w_out = spread(attend_out.T, 1)
    w_gu = spread(expand_in, 2)
    w_red = spread(reduce_out.T, 1)
    g_all = line_gather(cotangent[0], 0)

    mixed = jnp.dot(h1_all, w_in, preferred_element_type=f32).reshape(seq, 3, heads, HEAD_DIM)
    q = rotate(mixed[:, 0], cosine, sine).astype(bf16).transpose(1, 0, 2)
    k = rotate(mixed[:, 1], cosine, sine).astype(bf16).transpose(1, 0, 2)
    v = mixed[:, 2].astype(bf16).transpose(1, 0, 2)
    o, p = attend(q, k, v, place, live_place, length)
    attended = o.transpose(1, 0, 2).reshape(seq, heads * HEAD_DIM)
    x1 = x + line_scatter(contract_last(attended, w_out).astype(bf16), 1)
    unit_two, inverse_two, h2 = norm_forward(x1, gain_expand)
    h2_all = line_gather(h2, 0)
    gate_up = jnp.dot(h2_all, w_gu, preferred_element_type=f32)
    units = gate_up.shape[1] // 2
    gate, up = gate_up[:, :units], gate_up[:, units:]
    sigmoid = jax.nn.sigmoid(gate)
    silu = gate * sigmoid
    hidden = (silu * up).astype(bf16)
    grad_hidden = jnp.dot(g_all, w_red, preferred_element_type=f32)
    grad_gate = grad_hidden * up * (sigmoid * (1.0 + gate * (1.0 - sigmoid)))
    grad_up = grad_hidden * silu
    grad_gu = jnp.concatenate([grad_gate, grad_up], axis=1).astype(bf16)
    grad_h2 = line_scatter(contract_last(grad_gu, w_gu).astype(bf16), 1)
    y = x1 + line_scatter(contract_last(hidden, w_red).astype(bf16), 1)
    grad_expand = collect(over_tokens(h2_all, grad_gu), 2)
    grad_reduce = collect(over_tokens(g_all, hidden), 1)
    middle, gain_two = norm_backward(grad_h2, unit_two, inverse_two, gain_expand)
    grad_x1 = cotangent[0].astype(f32) + middle
    branch_all = line_gather(grad_x1.astype(bf16), 0)
    grad_o = jnp.dot(branch_all, w_out, preferred_element_type=f32).astype(bf16)
    grad_o = jnp.where((place < length)[:, None], grad_o, jnp.zeros((), bf16))
    grad_o = grad_o.reshape(seq, heads, HEAD_DIM).transpose(1, 0, 2)
    grad_q, grad_k, grad_v = attend_back(q, k, v, o, grad_o, p)
    grad_out = collect(over_tokens(branch_all, attended), 1)

    def by_token(value):
        return value.astype(bf16).astype(f32).transpose(1, 0, 2)

    grad_mixed = jnp.stack(
        [
            rotate_back(by_token(grad_q), cosine, sine),
            rotate_back(by_token(grad_k), cosine, sine),
            by_token(grad_v),
        ],
        axis=1,
    ).reshape(seq, -1).astype(bf16)
    grad_h1 = line_scatter(contract_last(grad_mixed, w_in).astype(bf16), 1)
    grad_in = collect(over_tokens(h1_all, grad_mixed), 3)
    first, gain_one = norm_backward(grad_h1, unit_one, inverse_one, gain_attend)
    grad_input = grad_x1 + first
    gain_one, gain_two = lax.psum((gain_one, gain_two), ("rows", "blk"))
    set_one = adam_step(attend_in, attend_in_first, attend_in_second, grad_in)
    set_two = moment_step(attend_out_first, attend_out_second, grad_out.T)
    set_three = adam_step(expand_in, expand_in_first, expand_in_second, grad_expand)
    set_four = adam_step(reduce_out, reduce_out_first, reduce_out_second, grad_reduce.T)
    return (
        (y.astype(bf16).reshape(tokens.shape), grad_input.reshape(tokens.shape), gain_one, gain_two)
        + set_one + set_two + set_three + set_four
    )


def solution(mesh):
    placed = (
        P("rows", "blk", None),
        P("rows", "blk", None),
        P("rows"),
        P("rows", None),
        P(),
        P(),
        P(("rows", "blk"), None),
        P(None, ("rows", "blk")),
        P(("rows", "blk"), None),
        P(None, ("rows", "blk")),
        P(("rows", "blk"), None),
        P(None, ("rows", "blk")),
        P(("rows", "blk"), None),
        P(None, ("rows", "blk")),
        P(("rows", "blk"), None),
        P(None, ("rows", "blk")),
        P(("rows", "blk"), None),
        P(None, ("rows", "blk")),
    )
    return jax.shard_map(
        shards,
        mesh=mesh,
        in_specs=placed,
        out_specs=(
            P("rows", "blk", None),
            P("rows", "blk", None),
            P(),
            P(),
            P(("rows", "blk"), None),
            P(("rows", "blk"), None),
            P(("rows", "blk"), None),
            P(None, ("rows", "blk")),
            P(None, ("rows", "blk")),
            P(("rows", "blk"), None),
            P(("rows", "blk"), None),
            P(("rows", "blk"), None),
            P(None, ("rows", "blk")),
            P(None, ("rows", "blk")),
            P(None, ("rows", "blk")),
        ),
        check_vma=False,
    )
```

time: 4320 us -> 942 us (0.22)
  waiting for transfers between devices: 3590 us -> 160 us
  Pallas kernels: 0 us -> 432 us
  other arithmetic: 280 us -> 50.5 us
  matrix products: 289 us -> 109 us
    reduce_scatter x1 -> x4, waiting for transfers between devices: 2720 us -> 49.1 us  [collect(): lax.psum_scatter(gradient.astype(jnp.bfloat16), 'rows', scatter_dimension...]
    all_gather x4, waiting for transfers between devices: 503 us -> 0.05 us  [spread(): return lax.all_gather(mine, 'rows', axis=0, tiled=True)]
    pallas_call x0 -> x10, Pallas kernels: none -> 432 us  [the longest x4 229 us: line_scatter(): pl.pallas_call(functools.partial(scatter_kernel, nb // 2), out_shape=jax....]
    ppermute x48 -> x0, waiting for transfers between devices: 362 us -> none  [from_behind(): return lax.ppermute(x, axis, [(i, (i + by) % size) for i in range(size)])]
    concatenate x2 -> x0, other arithmetic: 178 us -> none  [the longest x1 177 us: whole_layer(): jnp.concatenate([first, second, third, fourth], axis=1)]
    dot_general x64 -> x8, matrix products: 219 us -> 75.4 us  [the longest x4 36 us: over_tokens(): lax.dot_general(left, right, (((0,), (0,)), ((), ())), preferred_element_...]
    all_to_all x0 -> x6, waiting for transfers between devices: none -> 110 us  [the longest x3 74.5 us: spread(): mine = lax.all_to_all(pieces, 'blk', 0, 0, tiled=True)]
    convert_element_type x40 -> x7, other arithmetic: 60 us -> 7.4 us  [the longest x4 4.35 us: spread(): weight.astype(jnp.bfloat16)]
  transfers between devices with their start and end apart: 53 -> 14, of which waited for: 52 -> 6; matrix products, arithmetic and copies ran while one was open for 5% -> 16% of each run, Pallas kernels for 0% -> 36%
where the time goes in v1:
time: 942 us; the launch traced here: 933 us
  Pallas kernels  432 us (46%)
  waiting for transfers between devices  160 us (17%)
  matrix products  109 us (12%)
  blocking collectives  79.5 us (8%)
  local copies, waits for them, and re-layouts  60.9 us (6%)
  other arithmetic  50.5 us (5%)
  starting transfers between devices  25.6 us (3%)
  between operations  15.6 us (2%)
    pallas_call x4, Pallas kernels, line_scatter(): pl.pallas_call(functools.partial(scatter_kernel, nb // 2), out_shape=jax....  229 us
    pallas_call x4, Pallas kernels, line_gather(): pl.pallas_call(functools.partial(gather_kernel, nb // 2), out_shape=jax.S...  166 us
    all_to_all x3, waiting for transfers between devices, spread(): mine = lax.all_to_all(pieces, 'blk', 0, 0, tiled=True)  74.5 us
    reduce_scatter x4, waiting for transfers between devices, collect(): lax.psum_scatter(gradient.astype(jnp.bfloat16), 'rows', scatter_dimension...  49.1 us
    psum x1, blocking collectives, shards(): gain_one, gain_two = lax.psum((gain_one, gain_two), ('rows', 'blk'))  39.2 us
    dot_general x4, matrix products, over_tokens(): lax.dot_general(left, right, (((0,), (0,)), ((), ())), preferred_element_...  36 us
    all_to_all x3, waiting for transfers between devices, collect(): pieces = lax.all_to_all(mine, 'blk', 0, 0, tiled=True)  35.6 us
    dot_general x4, matrix products, contract_last(): lax.dot_general(left, right, (((1,), (1,)), ((), ())), preferred_element_...  33.6 us
  transfers between devices with their start and end apart: 14, of which 6 were waited for; matrix products, arithmetic and copies ran while one was open for 16% of the time, Pallas kernels for 36%

profile of v1, /device:TPU:0, one launch (start us, length us, event | category | flops | bytes accessed | tf_op | source)
XLA Modules:
  0.0 932.8 jit_solution(6679820685429515953)
XLA Ops:
  10.3 27.2 %all_to_all.84 = bf16[8,64,768]{2,1,0:T(8,128)(2,1)} all-to-all(bf16[8,64,768]{2,1,0:T(8,128)(2,1)S(1)} %all_to_all.56), channel_id=1, replica_groups=mesh['rows'=4,'blk'=8] {'blk'}, dimensions={0} | all-to-all | bytes 1572864 | tf_op jit(solution)/shard_map/all_to_all | solution.py:350
  38.3 3.4 all-to-all-start.1
  47.9 2.8 all_to_all.62
  52.1 4.3 all-to-all-start.2
  57.3 48.3 %all-to-all-done.2 = bf16[8,64,2048]{2,1,0:T(8,128)(2,1)} async-done(((bf16[8,64,2048]{2,1,0:T(8,128)(2,1)}), bf16[8,64,2048]{2,1,0:T(8,128)(2,1)}, u32[]{:S(2)}, u32[]{:S(2)}) %all-to-all-start.2) | async-done | bytes 2097184 | tf_op jit(solution)/shard_map/all_to_all | solution.py:350
  107.9 3.7 all-to-all-start.3
  112.7 25.5 %all-to-all-done.3 = bf16[8,64,1024]{2,1,0:T(8,128)(2,1)S(1)} async-done(((bf16[8,64,1024]{2,1,0:T(8,128)(2,1)}), bf16[8,64,1024]{2,1,0:T(8,128)(2,1)S(1)}, u32[]{:S(2)}, u32[]{:S(2)}) %all-to-all-start.3) | async-done | bytes 1048608 | tf_op jit(solution)/shard_map/all_to_all | solution.py:350
  141.7 40.8 %shard_map.289 = bf16[1024,2048]{1,0:T(8,128)(2,1)} custom-call(bf16[128,2048]{1,0:T(8,128)(2,1)} %fusion.10.x_ref), custom_call_target="tpu_custom_call" | custom-call | bytes 150000000 | tf_op jit(solution)/shard_map/pallas_call | solution.py:83
  182.5 43.8 %shard_map.294 = bf16[1024,2048]{1,0:T(8,128)(2,1)} custom-call(bf16[128,2048]{1,0:T(8,128)(2,1)} %bitcast.174), custom_call_target="tpu_custom_call" | custom-call | bytes 150000000 | tf_op jit(solution)/shard_map/pallas_call | solution.py:83
  226.9 2.9 multiply_cosine_fusion
  229.9 6.4 fusion.33
  239.4 3.1 fusion.30
  244.3 3.2 copy.108
  247.4 3.8 subtract_convert_fusion.2
  253.7 16.5 %shard_map.290 = (bf16[4,1024,64]{2,1,0:T(8,128)(2,1)}, bf16[4,1024,1024]{2,1,0:T(8,128)(2,1)}) custom-call(bf16[4,1024,64]{2,1,0:T(8,128)(2,1)} %get-tuple-element.67.q_ref, bf16[4,1024,64]{2,1,0:T(8,128)(2,1)} %get-tuple-element.68.k_ref, bf16[4,1024,64]{2,1,0:T(8,128)(2,1)} %bitcast.180, s32[1024,1]{1,0:T(8,128)} %add.184.q_place, ...), custom_call_target="tpu_custom_call" | custom-call | flops 1073741824 | bytes 8388608 | tf_op jit(solution)/shard_map/pallas_call | solution.py:268
  271.8 4.7 convolution_convert_fusion.2.x_ref
  276.5 56.2 %shard_map.291 = f32[128,2048]{1,0:T(8,128)} custom-call(bf16[1024,2048]{1,0:T(8,128)(2,1)} %convolution_convert_fusion.2.x_ref), custom_call_target="tpu_custom_call" | custom-call | bytes 150000000 | tf_op jit(solution)/shard_map/pallas_call | solution.py:166
  335.1 40.6 %shard_map.292 = bf16[1024,2048]{1,0:T(8,128)(2,1)} custom-call(bf16[128,2048]{1,0:T(8,128)(2,1)} %multiply_convert_fusion.3.x_ref), custom_call_target="tpu_custom_call" | custom-call | bytes 150000000 | tf_op jit(solution)/shard_map/pallas_call | solution.py:83
  375.8 14.6 %fusion.34 = f32[1024,2048]{1,0:T(8,128)} fusion(bf16[1024,2048]{1,0:T(8,128)(2,1)} %shard_map.292, bf16[2048,2048]{1,0:T(8,128)(2,1)} %all-gather.9.cloned.1.call-done), kind=kOutput, calls=%fused_computation.95 | convolution fusion | flops 8589934592 | bytes 20971520 | tf_op jit(solution)/shard_map/dot_general | solution.py:407
  390.3 13.8 %multiply_convert_fusion.1 = (bf16[1024,1024]{1,0:T(8,128)(2,1)S(1)}, bf16[1024,1024]{1,0:T(8,128)(2,1)}, bf16[1024,1024]{1,0:T(8,128)(2,1)}) fusion(f32[1024,2048]{1,0:T(8,128)} %fusion.34, bf16[1024,2048]{1,0:T(8,128)(2,1)} %shard_map.294, bf16[2048,1024]{1,0:T(8,128)(2,1)} %all-gather.11.cloned.1.call-done), kind=kOutput, calls=%fused_computation.8 | convolution fusion | flops 4310695936 | bytes 23068672 | tf_op jit(solution)/shard_map/dot_general | solution.py:413
  405.5 11.6 %convolution_convert_fusion.1.x_ref = bf16[1024,2048]{1,0:T(8,128)(2,1)} fusion(bf16[2048,2048]{1,0:T(8,128)(2,1)S(1)} %copy-done.28, bf16[1024,1024]{1,0:T(8,128)(2,1)} %get-tuple-element.43, bf16[1024,1024]{1,0:T(8,128)(2,1)S(1)} %get-tuple-element.42), kind=kOutput, calls=%fused_computation.12 | convolution fusion | flops 8600420352 | bytes 16777216 | tf_op jit(solution)/shard_map/dot_general | solution.py:226
  417.1 56.0 %shard_map.295 = f32[128,2048]{1,0:T(8,128)} custom-call(bf16[1024,2048]{1,0:T(8,128)(2,1)} %convolution_convert_fusion.1.x_ref), custom_call_target="tpu_custom_call" | custom-call | bytes 150000000 | tf_op jit(solution)/shard_map/pallas_call | solution.py:166
  475.9 40.6 %shard_map.296 = bf16[1024,2048]{1,0:T(8,128)(2,1)} custom-call(bf16[128,2048]{1,0:T(8,128)(2,1)} %fusion.25.x_ref), custom_call_target="tpu_custom_call" | custom-call | bytes 150000000 | tf_op jit(solution)/shard_map/pallas_call | solution.py:83
  516.6 4.5 convolution_convert_fusion.6
  521.6 4.6 fusion.9
  528.5 20.5 %shard_map.297 = (f32[4,1024,64]{2,1,0:T(8,128)}, f32[4,1024,64]{2,1,0:T(8,128)}, f32[4,1024,64]{2,1,0:T(8,128)}) custom-call(bf16[4,1024,64]{2,1,0:T(8,128)(2,1)} %get-tuple-element.67.q_ref, bf16[4,1024,64]{2,1,0:T(8,128)(2,1)} %get-tuple-element.68.k_ref, bf16[4,1024,64]{2,1,0:T(8,128)(2,1)} %bitcast.181, bf16[4,1024,64]{2,1,0:T(8,128)(2,1)} %get-tuple-element.20.o_ref, ...), custom_call_target="tpu_custom_call" | custom-call | flops 2684354560 | bytes 8388608 | tf_op jit(solution)/shard_map/pallas_call | solution.py:328
  558.6 4.3 copy.101
  562.9 7.9 convolution_convert_fusion.5
  571.1 9.4 %convert_bitcast_fusion = bf16[2048,1024]{0,1:T(8,128)(2,1)} fusion(bf16[1024,1024]{1,0:T(8,128)(2,1)} %get-tuple-element.44, bf16[1024,2048]{1,0:T(8,128)(2,1)} %shard_map.294), kind=kOutput, calls=%fused_computation.4 | convolution fusion | flops 4297064448 | bytes 10485760 | tf_op jit(solution)/shard_map/dot_general | solution.py:366
  580.6 14.2 %convolution_convert_fusion = bf16[2048,2048]{1,0:T(8,128)(2,1)} fusion(bf16[1024,2048]{1,0:T(8,128)(2,1)} %shard_map.292, bf16[1024,1024]{1,0:T(8,128)(2,1)} %get-tuple-element.43, bf16[1024,1024]{1,0:T(8,128)(2,1)} %copy-done.30), kind=kOutput, calls=%fused_computation | convolution fusion | flops 8602517504 | bytes 16777216 | tf_op jit(solution)/shard_map/dot_general | solution.py:366
  594.8 13.1 %all_to_all.85 = bf16[8,64,256]{2,1,0:T(8,128)(2,1)S(1)} all-to-all(bf16[8,64,256]{2,1,0:T(8,128)(2,1)} %bitcast.200), channel_id=1, replica_groups=mesh['rows'=4,'blk'=8] {'blk'}, dimensions={0} | all-to-all | bytes 524288 | tf_op jit(solution)/shard_map/all_to_all | solution.py:359
  607.9 6.8 reduce-scatter.5.cloned.1.call-done
  614.8 4.9 all-to-all-start.4
  619.6 9.4 %convolution_convert_fusion.4.x_ref = bf16[1024,2048]{1,0:T(8,128)(2,1)} fusion(bf16[1024,1024]{1,0:T(8,128)(2,1)} %get-tuple-element.44, bf16[2048,1024]{1,0:T(8,128)(2,1)} %all-gather.11.cloned.1.call-done), kind=kOutput, calls=%fused_computation.15 | convolution fusion | flops 4297064448 | bytes 10485760 | tf_op jit(solution)/shard_map/dot_general | solution.py:226
  629.0 42.2 %reduce-scatter.11.cloned.1.call-done = bf16[512,1024]{0,1:T(8,128)(2,1)} async-done(((bf16[2048,1024]{0,1:T(8,128)(2,1)}), bf16[512,1024]{0,1:T(8,128)(2,1)}) %reduce-scatter.11.cloned.1.call-update) | async-done | bytes 1048592 | tf_op jit(solution)/shard_map/reduce_scatter | solution.py:356
  673.5 4.6 all-to-all-start.7
  678.1 7.9 convolution_convert_fusion.3.x_ref
  686.0 62.5 %shard_map.293 = f32[128,2048]{1,0:T(8,128)} custom-call(bf16[1024,2048]{1,0:T(8,128)(2,1)} %convolution_convert_fusion.4.x_ref), custom_call_target="tpu_custom_call" | custom-call | bytes 150000000 | tf_op jit(solution)/shard_map/pallas_call | solution.py:166
  748.5 54.3 %shard_map.298 = f32[128,2048]{1,0:T(8,128)} custom-call(bf16[1024,2048]{1,0:T(8,128)(2,1)} %convolution_convert_fusion.3.x_ref), custom_call_target="tpu_custom_call" | custom-call | bytes 150000000 | tf_op jit(solution)/shard_map/pallas_call | solution.py:166
  804.4 39.2 %all-reduce = (f32[2048]{0:T(1024)}, f32[2048]{0:T(1024)}) all-reduce(f32[2048]{0:T(1024)S(1)} %get-tuple-element.27, f32[2048]{0:T(1024)S(1)} %get-tuple-element.25), channel_id=1, replica_groups=mesh['rows'=4,'blk'=8] {'rows','blk'}, use_global_device_ids=true, to_apply=%region_5.6 | all-reduce | flops 4096 | bytes 32768 | tf_op jit(solution)/shard_map/psum | solution.py:445
  843.6 3.1 fusion.15
  854.1 3.8 all-to-all-start.6
  857.9 5.8 multiply_subtract_fusion.2
  867.6 3.7 multiply_subtract_fusion.1
  871.3 35.6 %all-to-all-done.6 = bf16[8,64,2048]{2,1,0:T(8,128)(2,1)S(1)} async-done(((bf16[8,64,2048]{2,1,0:T(8,128)(2,1)}), bf16[8,64,2048]{2,1,0:T(8,128)(2,1)S(1)}, u32[]{:S(2)}, u32[]{:S(2)}) %all-to-all-start.6) | async-done | bytes 2097184 | tf_op jit(solution)/shard_map/all_to_all | solution.py:359
  906.9 5.1 reshape.284
  912.0 4.8 copy.104
  920.2 5.6 multiply_subtract_fusion
  (143 shorter events, 65.8 us)
Async XLA Ops:
  7.2 222.7 %all-gather.5.cloned.1.call-start = ((), (), s32[]{:S(2)}) async-start(), calls=%async_computation.12 | async-start | bytes 3932160 | tf_op jit(solution)/shard_map/all_gather | solution.py:351
  9.3 28.2 %copy-start.22 = (f32[2048,64]{0,1:T(8,128)S(1)}, f32[2048,64]{0,1:T(8,128)}, u32[]{:S(2)}) copy-start(f32[2048,64]{0,1:T(8,128)} %param.25) | copy-start | bytes 1572868
  38.3 13.1 %all-to-all-start.1 = ((bf16[8,64,256]{2,1,0:T(8,128)(2,1)}), bf16[8,64,256]{2,1,0:T(8,128)(2,1)S(1)}, u32[]{:S(2)}, u32[]{:S(2)}) async-start(bf16[8,64,256]{2,1,0:T(8,128)(2,1)} %copy.95), calls=%async_computation.1 | async-start | bytes 524288 | tf_op jit(solution)/shard_map/all_to_all | solution.py:350
  51.4 0.7 copy-start.19
  52.1 53.5 %all-to-all-start.2 = ((bf16[8,64,2048]{2,1,0:T(8,128)(2,1)}), bf16[8,64,2048]{2,1,0:T(8,128)(2,1)}, u32[]{:S(2)}, u32[]{:S(2)}) async-start(bf16[8,64,2048]{2,1,0:T(8,128)(2,1)} %all_to_all.62), calls=%async_computation.2 | async-start | bytes 4194304 | tf_op jit(solution)/shard_map/all_to_all | solution.py:350
  56.5 49.1 %copy-start.3 = (f32[8192,64]{0,1:T(8,128)S(1)}, f32[8192,64]{0,1:T(8,128)}, u32[]{:S(2)}) copy-start(f32[8192,64]{0,1:T(8,128)} %param.27) | copy-start | bytes 6291460
  56.5 215.3 %all-gather.7.cloned.1.call-start = ((), (), s32[]{:S(2)}) async-start(), calls=%async_computation.13 | async-start | bytes 1310720 | tf_op jit(solution)/shard_map/all_gather | solution.py:351
  57.3 318.5 %all-gather.9.cloned.1.call-start = ((), (), s32[]{:S(2)}) async-start(), calls=%async_computation.14 | async-start | bytes 10485760 | tf_op jit(solution)/shard_map/all_gather | solution.py:351
  106.3 6.0 copy-start.2
  106.4 6.2 copy-start.29
  107.9 32.8 %copy-start.24 = (f32[2048]{0:T(1024)S(1)}, f32[2048]{0:T(1024)}, u32[]{:S(2)}) copy-start(f32[2048]{0:T(1024)} %param.22) | copy-start | bytes 24580
  107.9 30.2 %all-to-all-start.3 = ((bf16[8,64,1024]{2,1,0:T(8,128)(2,1)}), bf16[8,64,1024]{2,1,0:T(8,128)(2,1)S(1)}, u32[]{:S(2)}, u32[]{:S(2)}) async-start(bf16[8,64,1024]{2,1,0:T(8,128)(2,1)} %copy.97), calls=%async_computation.3 | async-start | bytes 2097152 | tf_op jit(solution)/shard_map/all_to_all | solution.py:350
  111.6 278.7 %all-gather.11.cloned.1.call-start = ((), (), s32[]{:S(2)}) async-start(), calls=%async_computation.15 | async-start | bytes 5242880 | tf_op jit(solution)/shard_map/all_gather | solution.py:351
  138.1 1.0 copy-start.11
  139.1 455.6 %reduce-scatter.7.cloned.1.call-start = ((), (), s32[]{:S(2)}) async-start(), calls=%async_computation.17 | async-start | bytes 1310720 | tf_op jit(solution)/shard_map/reduce_scatter | solution.py:356
  139.2 43.3 %copy-start.26 = (f32[128]{0:T(128)}, f32[128]{0:T(128)S(1)}, u32[]{:S(2)}) copy-start(f32[128]{0:T(128)S(1)} %add_rsqrt_fusion.1) | copy-start | bytes 1540
  229.9 17.6 %copy-start.6 = (f32[1024,32]{1,0:T(8,128)}, f32[1024,32]{1,0:T(8,128)S(1)}, u32[]{:S(2)}) copy-start(f32[1024,32]{1,0:T(8,128)S(1)} %get-tuple-element.63) | copy-start | bytes 393220
  236.3 1.7 copy-start.14
  271.7 4.8 copy-start.12
  332.7 1.5 copy-start.23
  390.3 15.2 %copy-start.28 = (bf16[2048,2048]{1,0:T(8,128)(2,1)S(1)}, bf16[2048,2048]{1,0:T(8,128)(2,1)}, u32[]{:S(2)}) copy-start(bf16[2048,2048]{1,0:T(8,128)(2,1)} %all-gather.9.cloned.1.call-done) | copy-start | bytes 25165828
  404.2 1.3 copy-start.30
  473.1 1.7 copy-start.1
  473.1 1.7 copy-start.5
  475.9 40.6 %copy-start.13 = (bf16[1024,4,64]{0,2,1:T(8,128)(2,1)S(1)}, bf16[1024,4,64]{0,2,1:T(8,128)(2,1)}, u32[]{:S(2)}) copy-start(bf16[1024,4,64]{0,2,1:T(8,128)(2,1)} %copy-done.12) | copy-start | bytes 1572868
  521.1 93.7 %reduce-scatter.5.cloned.1.call-start = ((), (), s32[]{:S(2)}) async-start(), calls=%async_computation.16 | async-start | bytes 3932160 | tf_op jit(solution)/shard_map/reduce_scatter | solution.py:356
  549.0 2.2 copy-start.18
  551.2 1.0 copy-start.7
  551.2 1.2 copy-start.8
  554.5 1.6 copy-start.17
  570.9 100.4 %reduce-scatter.11.cloned.1.call-start = ((), (), s32[]{:S(2)}) async-start(), calls=%async_computation.19 | async-start | bytes 5242880 | tf_op jit(solution)/shard_map/reduce_scatter | solution.py:356
  580.5 273.6 %reduce-scatter.9.cloned.1.call-start = ((), (), s32[]{:S(2)}) async-start(), calls=%async_computation.18 | async-start | bytes 10485760 | tf_op jit(solution)/shard_map/reduce_scatter | solution.py:356
  614.8 58.8 %all-to-all-start.4 = ((bf16[8,64,768]{2,1,0:T(8,128)(2,1)}), bf16[8,64,768]{2,1,0:T(8,128)(2,1)}, u32[]{:S(2)}, u32[]{:S(2)}) async-start(bf16[8,64,768]{2,1,0:T(8,128)(2,1)} %bitcast.198), calls=%async_computation.5 | async-start | bytes 1572864 | tf_op jit(solution)/shard_map/all_to_all | solution.py:359
  673.5 180.6 %all-to-all-start.7 = ((bf16[8,64,1024]{2,1,0:T(8,128)(2,1)}), bf16[8,64,1024]{2,1,0:T(8,128)(2,1)}, u32[]{:S(2)}, u32[]{:S(2)}) async-start(bf16[8,64,1024]{2,1,0:T(8,128)(2,1)} %bitcast.178), calls=%async_computation.11 | async-start | bytes 2097152 | tf_op jit(solution)/shard_map/all_to_all | solution.py:359
  748.4 54.3 %copy-start.25 = (f32[2048]{0:T(1024)S(1)}, f32[2048]{0:T(1024)}, u32[]{:S(2)}) copy-start(f32[2048]{0:T(1024)} %param.22) | copy-start | bytes 24580
  748.5 54.3 %copy-start.27 = (f32[128]{0:T(128)S(1)}, f32[128]{0:T(128)}, u32[]{:S(2)}) copy-start(f32[128]{0:T(128)} %copy-done.26) | copy-start | bytes 1540
  846.7 1.0 copy-start.20
  846.7 1.2 copy-start.21
  854.1 52.8 %all-to-all-start.6 = ((bf16[8,64,2048]{2,1,0:T(8,128)(2,1)}), bf16[8,64,2048]{2,1,0:T(8,128)(2,1)S(1)}, u32[]{:S(2)}, u32[]{:S(2)}) async-start(bf16[8,64,2048]{2,1,0:T(8,128)(2,1)} %bitcast.192), calls=%async_computation.9 | async-start | bytes 4194304 | tf_op jit(solution)/shard_map/all_to_all | solution.py:359
  863.7 1.9 copy-start.16
  865.3 1.7 copy-start.4
  865.3 2.3 copy-start.15
  912.0 7.2 copy-start.10
  916.8 2.4 copy-start
  916.8 3.5 copy-start.9
Sparse Core Ops, SparseCore 0:
  37.6 42.8 all-gather.4
  82.9 26.6 all-gather.6
  111.5 87.6 all-gather.8
  201.4 52.6 all-gather.10
  521.2 27.4 reduce-scatter.6
  571.0 43.7 reduce-scatter.4
  618.6 52.6 reduce-scatter.10
  674.3 86.3 reduce-scatter.8

commit v2 on v1

v2 whole, which is shorter than its diff:
```python
import functools
import math

import jax
import jax.numpy as jnp
from jax import lax
from jax.experimental import pallas as pl
from jax.experimental.pallas import tpu as pltpu
from jax.sharding import PartitionSpec as P

HEADS = 32
HEAD_DIM = 64
MESH = pl.DeviceIdType.MESH
MIB = 1 << 20

theta_base = 130000.0
norm_eps = 1e-05
neg_large = -1e30
beta_one = 0.9
beta_two = 0.95
learn_rate = 0.01
decay_rate = 0.1
adam_eps = 1e-08
step_count = 10


def line_place():
    b = lax.axis_index("blk")
    return lax.axis_index("rows"), b // 2, b % 2


def greet(chips, swaps):
    r, z, c = line_place()
    barrier = pltpu.get_barrier_semaphore()

    def signal(b):
        pl.semaphore_signal(barrier, inc=1, device_id=(r, b), device_id_type=MESH)

    if swaps:
        b, nb = 2 * z + c, 2 * chips
        for k in range(1, nb):
            signal(lax.rem(b + k, nb))
        pl.semaphore_wait(barrier, nb - 1)
        return
    signal(2 * z + 1 - c)
    pl.when(z < chips - 1)(lambda: signal(2 * (z + 1) + c))
    pl.when(z > 0)(lambda: signal(2 * (z - 1) + c))
    pl.semaphore_wait(barrier, 1 + (z < chips - 1).astype(jnp.int32) + (z > 0).astype(jnp.int32))


def swap_copies(src, dst, local, send, recv):
    r, b = lax.axis_index("rows"), lax.axis_index("blk")
    nb = src.shape[0]
    others = [lax.rem(b + k, nb) for k in range(1, nb)]

    def remote(other, slot):
        return pltpu.make_async_remote_copy(
            src_ref=src.at[other], dst_ref=dst.at[slot], send_sem=send.at[other],
            recv_sem=recv.at[slot], device_id=(r, other), device_id_type=MESH,
        )

    def start():
        for other in others:
            remote(other, b).start()
        pltpu.make_async_copy(src.at[b], dst.at[b], local).start()

    def wait():
        for other in others:
            remote(other, other).wait_recv()
        for other in others:
            remote(other, b).wait_send()
        pltpu.make_async_copy(src.at[b], dst.at[b], local).wait()

    return start, wait


def swap_sems(swaps):
    sems = []
    for pieces in swaps:
        sems += [pltpu.SemaphoreType.DMA] + [pltpu.SemaphoreType.DMA((pieces.shape[0],))] * 2
    return sems


def swap_list(srcs, dsts, sems):
    made = [swap_copies(s, d, *sems[3 * i : 3 * i + 3]) for i, (s, d) in enumerate(zip(srcs, dsts))]
    return [one[0] for one in made], [one[1] for one in made]


def swap_kernel(n, *refs):
    starts, waits = swap_list(refs[:n], refs[n : 2 * n], refs[2 * n :])
    greet(refs[0].shape[0] // 2, True)
    for start in starts:
        start()
    for wait in waits:
        wait()


def like(value):
    return jax.ShapeDtypeStruct(value.shape, value.dtype)


ANY = pl.BlockSpec(memory_space=pl.ANY)
VMEM = pl.BlockSpec(memory_space=pltpu.VMEM)


def params(cid):
    return pltpu.CompilerParams(
        collective_id=cid, has_side_effects=True, vmem_limit_bytes=60 * MIB
    )


def cost(flops):
    return pl.CostEstimate(flops=flops, bytes_accessed=150_000_000, transcendentals=0)


def swap(cid, *pieces):
    n = len(pieces)
    return pl.pallas_call(
        functools.partial(swap_kernel, n),
        out_shape=[like(value) for value in pieces],
        in_specs=[ANY] * n,
        out_specs=[ANY] * n,
        scratch_shapes=swap_sems(pieces),
        compiler_params=params(cid),
        cost_estimate=cost(0),
    )(*pieces)


def gather_kernel(chips, cuts, tile, with_dot, n, *refs):
    refs = list(refs)
    x_ref = refs.pop(0)
    w_ref = refs.pop(0) if with_dot else None
    srcs = [refs.pop(0) for _ in range(n)]
    o_ref = refs.pop(0)
    prod_ref = refs.pop(0) if with_dot else None
    dsts = [refs.pop(0) for _ in range(n)]
    copy_sem, send_up, send_down, send_side, recv = refs[:5]
    starts, waits = swap_list(srcs, dsts, refs[5:])
    r, z, c = line_place()
    t = x_ref.shape[0]
    h = t // cuts
    up, down, side = (r, 2 * (z + 1) + c), (r, 2 * (z - 1) + c), (r, 2 * z + 1 - c)
    has_up, has_down = z < chips - 1, z > 0
    greet(chips, n > 0)

    def piece(j, q):
        return o_ref.at[pl.ds(pl.multiple_of(j * t + q * h, h), h)]

    def remote(src, j, q, sem, dev):
        return pltpu.make_async_remote_copy(
            src_ref=src, dst_ref=piece(j, q), send_sem=sem.at[j, q], recv_sem=recv.at[j, q],
            device_id=dev, device_id_type=MESH,
        )

    def dot(y):
        if not with_dot:
            return
        rows = pl.ds(pl.multiple_of(y * 2 * t, 2 * t), 2 * t)

        def one(i, _):
            cols = pl.ds(pl.multiple_of(i * tile, tile), tile)
            prod_ref[rows, cols] = jnp.dot(
                o_ref[rows, :], w_ref[:, cols], preferred_element_type=jnp.float32
            ).astype(prod_ref.dtype)
            return 0

        lax.fori_loop(0, w_ref.shape[1] // tile, one, 0)

    mine = 2 * z + c
    for q in range(cuts):
        from_here = x_ref.at[pl.ds(q * h, h)]
        pl.when(has_up)(lambda: remote(from_here, mine, q, send_up, up).start())
        pl.when(has_down)(lambda: remote(from_here, mine, q, send_down, down).start())
        remote(from_here, mine, q, send_side, side).start()
    whole = o_ref.at[pl.ds(pl.multiple_of(mine * t, t), t)]
    local = pltpu.make_async_copy(x_ref, whole, copy_sem)
    local.start()
    for start in starts:
        start()

    def from_side(y):
        for q in range(cuts):
            j = 2 * y + 1 - c
            remote(piece(j, q), j, q, send_side, side).wait_recv()

    from_side(z)
    local.wait()
    dot(z)
    for k in range(1, chips):
        for q in range(cuts):
            @pl.when(z - k >= 0)
            def _():
                j = 2 * (z - k) + c
                remote(piece(j, q), j, q, send_up, up).wait_recv()
                pl.when(has_up)(lambda: remote(piece(j, q), j, q, send_up, up).start())
                remote(piece(j, q), j, q, send_side, side).start()

            @pl.when(z + k < chips)
            def _():
                j = 2 * (z + k) + c
                remote(piece(j, q), j, q, send_down, down).wait_recv()
                pl.when(has_down)(lambda: remote(piece(j, q), j, q, send_down, down).start())
                remote(piece(j, q), j, q, send_side, side).start()

        @pl.when(z - k >= 0)
        def _():
            from_side(z - k)
            dot(z - k)

        @pl.when(z + k < chips)
        def _():
            from_side(z + k)
            dot(z + k)

    for y in range(chips):
        j = 2 * y + c
        for q in range(cuts):
            pl.when(has_up & (z >= y))(lambda: remote(piece(j, q), j, q, send_up, up).wait_send())
            pl.when(has_down & (z <= y))(
                lambda: remote(piece(j, q), j, q, send_down, down).wait_send()
            )
            remote(piece(j, q), j, q, send_side, side).wait_send()
    for wait in waits:
        wait()


def line_gather(cid, x, w=None, swaps=(), cuts=2, tile=512):
    nb = lax.axis_size("blk")
    all_rows = nb * x.shape[0]
    with_dot = w is not None
    place = VMEM if with_dot else ANY
    outs = [jax.ShapeDtypeStruct((all_rows, x.shape[1]), x.dtype)]
    flops = 0
    if with_dot:
        outs.append(jax.ShapeDtypeStruct((all_rows, w.shape[1]), jnp.bfloat16))
        flops = 2 * all_rows * w.shape[0] * w.shape[1]
        tile = min(tile, w.shape[1])
    return pl.pallas_call(
        functools.partial(gather_kernel, nb // 2, cuts, tile, with_dot, len(swaps)),
        out_shape=outs + [like(value) for value in swaps],
        in_specs=[place] * (1 + with_dot) + [ANY] * len(swaps),
        out_specs=[place] * (1 + with_dot) + [ANY] * len(swaps),
        scratch_shapes=[pltpu.SemaphoreType.DMA]
        + [pltpu.SemaphoreType.DMA((nb, cuts))] * 4
        + swap_sems(swaps),
        compiler_params=params(cid),
        cost_estimate=cost(flops),
    )(*([x, w] if with_dot else [x]), *swaps)


def need_order(chips):
    table = []
    for z in range(chips):
        need = {
            y: (chips - 1 + z - y) if y > z else (chips - 1 - z + y)
            for y in range(chips) if y != z
        }
        table.append(sorted(need, key=lambda y: need[y]) + [z])
    return table


def pick(table, z, k):
    out = 0
    for at, row in enumerate(table):
        out = out + jnp.where(z == at, row[k], 0)
    return out


def scatter_kernel(chips, cuts, tile, n, *refs):
    refs = list(refs)
    a_ref, w_ref = refs.pop(0), refs.pop(0)
    srcs = [refs.pop(0) for _ in range(n)]
    o_ref = refs.pop(0)
    dsts = [refs.pop(0) for _ in range(n)]
    mine, away, side_buf, up_buf, down_buf, out_buf = refs[:6]
    send_side, recv_side, send_up, recv_up, send_down, recv_down = refs[6:12]
    starts, waits = swap_list(srcs, dsts, refs[12:])
    r, z, c = line_place()
    t, width = o_ref.shape
    low, f32 = away.dtype, jnp.float32
    up, down, side = (r, 2 * (z + 1) + c), (r, 2 * (z - 1) + c), (r, 2 * z + 1 - c)
    has_up, has_down = z < chips - 1, z > 0
    greet(chips, n > 0)
    h = t // cuts

    def remote(src, dst, y, q, send, recv, dev):
        return pltpu.make_async_remote_copy(
            src_ref=src.at[y, pl.ds(q * h, h)], dst_ref=dst.at[y, pl.ds(q * h, h)],
            send_sem=send.at[y, q], recv_sem=recv.at[y, q], device_id=dev, device_id_type=MESH,
        )

    def to_side(y, q):
        return remote(away, side_buf, y, q, send_side, recv_side, side)

    def to_up(y, q):
        return remote(out_buf, up_buf, y, q, send_up, recv_up, up)

    def to_down(y, q):
        return remote(out_buf, down_buf, y, q, send_down, recv_down, down)

    def rows(q):
        return pl.ds(q * h, h)

    def total(y, q):
        to_side(y, q).wait_recv()
        return mine[y, rows(q)].astype(f32) + side_buf[y, rows(q)].astype(f32)

    def make(y):
        a = a_ref[pl.ds(pl.multiple_of(2 * y * t, 2 * t), 2 * t)]

        def one(i, _):
            cols = pl.ds(pl.multiple_of(i * tile, tile), tile)
            got = lax.dot_general(
                a, w_ref[cols], (((1,), (1,)), ((), ())), preferred_element_type=f32
            ).astype(low)

            @pl.when(c == 0)
            def _():
                mine[y, :, cols] = got[:t]
                away[y, :, cols] = got[t:]

            @pl.when(c == 1)
            def _():
                mine[y, :, cols] = got[t:]
                away[y, :, cols] = got[:t]

            return 0

        lax.fori_loop(0, width // tile, one, 0)
        for q in range(cuts):
            to_side(y, q).start()

    table = need_order(chips)
    for s in range(chips):
        make(pick(table, z, s))
        if s == chips - 1:
            break
        y = chips - 1 + z - s
        w = s - (chips - 1) + z
        for q in range(cuts):
            @pl.when(y <= chips - 1)
            def _():
                now = total(y, q)

                @pl.when(has_down)
                def _():
                    to_up(y, q).wait_recv()
                    out_buf[y, rows(q)] = (now + up_buf[y, rows(q)].astype(f32)).astype(low)

                @pl.when(z == 0)
                def _():
                    out_buf[y, rows(q)] = now.astype(low)

                to_up(y, q).start()

            @pl.when(w >= 0)
            def _():
                now = total(w, q)

                @pl.when(has_up)
                def _():
                    to_down(w, q).wait_recv()
                    out_buf[w, rows(q)] = (now + down_buf[w, rows(q)].astype(f32)).astype(low)

                @pl.when(z == chips - 1)
                def _():
                    out_buf[w, rows(q)] = now.astype(low)

                to_down(w, q).start()

        if s == 0:
            for start in starts:
                start()
    for q in range(cuts):
        o_ref[rows(q)] = total(z, q)
    for q in range(cuts):
        @pl.when(has_down)
        def _():
            to_up(z, q).wait_recv()
            o_ref[rows(q)] += up_buf[z, rows(q)].astype(f32)

        @pl.when(has_up)
        def _():
            to_down(z, q).wait_recv()
            o_ref[rows(q)] += down_buf[z, rows(q)].astype(f32)

    for y in range(chips):
        for q in range(cuts):
            to_side(y, q).wait_send()
            pl.when(y > z)(lambda: to_up(y, q).wait_send())
            pl.when(y < z)(lambda: to_down(y, q).wait_send())
    for wait in waits:
        wait()


def dot_scatter(cid, a, w, swaps=(), cuts=2, tile=1024):
    nb = lax.axis_size("blk")
    t, width = a.shape[0] // nb, w.shape[0]
    n = len(swaps)
    sems = pltpu.SemaphoreType.DMA((nb // 2, cuts))
    return pl.pallas_call(
        functools.partial(scatter_kernel, nb // 2, cuts, tile, n),
        out_shape=[jax.ShapeDtypeStruct((t, width), jnp.float32)] + [like(s) for s in swaps],
        in_specs=[VMEM, VMEM] + [ANY] * n,
        out_specs=[VMEM] + [ANY] * n,
        scratch_shapes=[pltpu.VMEM((nb // 2, t, width), jnp.bfloat16)] * 6
        + [sems] * 6
        + swap_sems(swaps),
        compiler_params=params(cid),
        cost_estimate=cost(2 * a.shape[0] * width * w.shape[1]),
    )(a, w, *swaps)


def rope_tables(positions, head_size):
    halfway = head_size // 2
    frequency = jnp.exp(
        -jnp.arange(halfway, dtype=jnp.float32) * (2.0 / head_size) * math.log(theta_base)
    )
    angles = positions.astype(jnp.float32)[:, None] * frequency[None, :]
    return (jnp.cos(angles)[:, None, :], jnp.sin(angles)[:, None, :])


def rotate(values, cosine, sine_table):
    halfway = values.shape[-1] // 2
    front_half = values[..., :halfway]
    back_half = values[..., halfway:]
    return jnp.concatenate(
        [
            front_half * cosine - back_half * sine_table,
            back_half * cosine + front_half * sine_table,
        ],
        axis=-1,
    )


def rotate_back(values, cosine, sine_table):
    halfway = values.shape[-1] // 2
    front_half = values[..., :halfway]
    back_half = values[..., halfway:]
    return jnp.concatenate(
        [
            front_half * cosine + back_half * sine_table,
            back_half * cosine - front_half * sine_table,
        ],
        axis=-1,
    )


def norm_forward(values, gain_vector):
    inverse = lax.rsqrt(jnp.mean(values * values, axis=-1, keepdims=True) + norm_eps)
    unit_values = values * inverse
    return (unit_values, inverse, (unit_values * gain_vector).astype(jnp.bfloat16))


def norm_backward(grad_normed, unit_values, inverse, gain_vector):
    grad_unit = grad_normed * gain_vector
    grad_values = inverse * (
        grad_unit - unit_values * jnp.mean(grad_unit * unit_values, axis=-1, keepdims=True)
    )
    return (grad_values, jnp.sum(grad_normed * unit_values, axis=0))


def contract_last(left, right):
    return lax.dot_general(
        left, right, (((1,), (1,)), ((), ())), preferred_element_type=jnp.float32
    )


def adam_step(master, moment_one, moment_two, gradient):
    moment_one = beta_one * moment_one + (1.0 - beta_one) * gradient
    moment_two = beta_two * moment_two + (1.0 - beta_two) * gradient * gradient
    update = (
        moment_one
        / (1.0 - beta_one**step_count)
        / (jnp.sqrt(moment_two / (1.0 - beta_two**step_count)) + adam_eps)
    )
    return (master - learn_rate * (update + decay_rate * master), moment_one, moment_two)


def moment_step(moment_one, moment_two, gradient):
    moment_one = beta_one * moment_one + (1.0 - beta_one) * gradient
    moment_two = beta_two * moment_two + (1.0 - beta_two) * gradient * gradient
    return (moment_one, moment_two)


def beside_grid(n, starts, waits, chips):
    if not n:
        return lambda: None
    first = (pl.program_id(0) == 0) & (pl.program_id(1) == 0)
    last = (pl.program_id(0) == pl.num_programs(0) - 1) & (
        pl.program_id(1) == pl.num_programs(1) - 1
    )

    @pl.when(first)
    def _():
        greet(chips, True)
        for start in starts:
            start()

    def finish():
        @pl.when(last)
        def _():
            for wait in waits:
                wait()

    return finish


def attend_kernel(chips, n, *refs):
    q_ref, k_ref, v_ref, q_place, k_place, length_ref = refs[:6]
    o_ref, p_ref = refs[6 + n : 8 + n]
    starts, waits = swap_list(refs[6 : 6 + n], refs[8 + n : 8 + 2 * n], refs[8 + 2 * n :])
    finish = beside_grid(n, starts, waits, chips)
    scores = lax.dot_general(
        q_ref[0], k_ref[0], (((1,), (1,)), ((), ())), preferred_element_type=jnp.float32
    ) * (1.0 / math.sqrt(HEAD_DIM))
    place = q_place[...]
    scores = jnp.where(k_place[...] <= place, scores, neg_large)
    top = jnp.max(scores, axis=-1, keepdims=True)
    weights = jnp.exp(scores - top)
    weights = weights * (1.0 / jnp.sum(weights, axis=-1, keepdims=True))
    low = weights.astype(jnp.bfloat16)
    p_ref[0] = low
    out = jnp.dot(low, v_ref[0], preferred_element_type=jnp.float32)
    o_ref[0] = jnp.where(place < length_ref[0], out, 0.0).astype(jnp.bfloat16)
    finish()


def attend(cid, q, k, v, place, live_place, length, swaps=()):
    heads, seq, size = q.shape
    tile = 256
    n = len(swaps)
    whole = pl.BlockSpec((1, seq, size), lambda h, i: (h, 0, 0))
    part = pl.BlockSpec((1, tile, size), lambda h, i: (h, i, 0))
    return pl.pallas_call(
        functools.partial(attend_kernel, lax.axis_size("blk") // 2, n),
        grid=(heads, seq // tile),
        in_specs=[
            part,
            whole,
            whole,
            pl.BlockSpec((tile, 1), lambda h, i: (i, 0)),
            pl.BlockSpec((1, seq), lambda h, i: (0, 0)),
            pl.BlockSpec(memory_space=pltpu.SMEM),
        ]
        + [ANY] * n,
        out_specs=[part, pl.BlockSpec((1, tile, seq), lambda h, i: (h, i, 0))] + [ANY] * n,
        out_shape=[
            jax.ShapeDtypeStruct((heads, seq, size), jnp.bfloat16),
            jax.ShapeDtypeStruct((heads, seq, seq), jnp.bfloat16),
        ]
        + [like(value) for value in swaps],
        scratch_shapes=swap_sems(swaps),
        compiler_params=params(cid),
        cost_estimate=cost(4 * heads * seq * seq * size),
    )(q, k, v, place[:, None], live_place[None, :], length.reshape(1), *swaps)


def attend_back_kernel(chips, n, *refs):
    q_ref, k_ref, v_ref, o_ref, g_ref, p_ref = refs[:6]
    dq_ref, dk_ref, dv_ref = refs[6 + n : 9 + n]
    dk_acc, dv_acc = refs[9 + 2 * n : 11 + 2 * n]
    starts, waits = swap_list(refs[6 : 6 + n], refs[9 + n : 9 + 2 * n], refs[11 + 2 * n :])
    finish = beside_grid(n, starts, waits, chips)
    step = pl.program_id(1)

    @pl.when(step == 0)
    def _():
        dk_acc[...] = jnp.zeros_like(dk_acc)
        dv_acc[...] = jnp.zeros_like(dv_acc)

    f32 = jnp.float32
    low = p_ref[0]
    grad = g_ref[0]
    over_rows = (((0,), (0,)), ((), ()))
    dv_acc[...] += lax.dot_general(low, grad, over_rows, preferred_element_type=f32)
    delta = jnp.sum(grad.astype(f32) * o_ref[0].astype(f32), axis=-1, keepdims=True)
    grad_p = lax.dot_general(
        grad, v_ref[0], (((1,), (1,)), ((), ())), preferred_element_type=f32
    )
    grad_s = (low.astype(f32) * (grad_p - delta)).astype(jnp.bfloat16)
    factor = 1.0 / math.sqrt(HEAD_DIM)
    dq_ref[0] = jnp.dot(grad_s, k_ref[0], preferred_element_type=f32) * factor
    dk_acc[...] += lax.dot_general(grad_s, q_ref[0], over_rows, preferred_element_type=f32)

    @pl.when(step == pl.num_programs(1) - 1)
    def _():
        dk_ref[0] = dk_acc[...] * factor
        dv_ref[0] = dv_acc[...]

    finish()


def attend_back(cid, q, k, v, o, g, p, swaps=()):
    heads, seq, size = q.shape
    tile = 256
    n = len(swaps)
    whole = pl.BlockSpec((1, seq, size), lambda h, i: (h, 0, 0))
    part = pl.BlockSpec((1, tile, size), lambda h, i: (h, i, 0))
    shape = jax.ShapeDtypeStruct((heads, seq, size), jnp.float32)
    return pl.pallas_call(
        functools.partial(attend_back_kernel, lax.axis_size("blk") // 2, n),
        grid=(heads, seq // tile),
        in_specs=[
            part, whole, whole, part, part, pl.BlockSpec((1, tile, seq), lambda h, i: (h, i, 0)),
        ]
        + [ANY] * n,
        out_specs=[part, whole, whole] + [ANY] * n,
        out_shape=[shape] * 3 + [like(value) for value in swaps],
        scratch_shapes=[pltpu.VMEM((seq, size), jnp.float32)] * 2 + swap_sems(swaps),
        compiler_params=params(cid),
        cost_estimate=cost(10 * heads * seq * seq * size),
    )(q, k, v, o, g, p, *swaps)


def arrange_kernel(*refs):
    wide = refs[0].shape[1]
    out = refs[-1]
    for part, ref in enumerate(refs[:-1]):
        out[0, :, part * wide : (part + 1) * wide] = ref[...].astype(out.dtype)


def arrange(weight, parts):
    rows, columns = weight.shape
    nb = lax.axis_size("blk")
    wide = columns // (parts * nb)
    return pl.pallas_call(
        arrange_kernel,
        grid=(nb,),
        in_specs=[
            pl.BlockSpec((rows, wide), lambda j, part=part: (0, part * nb + j))
            for part in range(parts)
        ],
        out_specs=pl.BlockSpec((1, rows, parts * wide), lambda j: (j, 0, 0)),
        out_shape=jax.ShapeDtypeStruct((nb, rows, parts * wide), jnp.bfloat16),
        cost_estimate=pl.CostEstimate(
            flops=0, bytes_accessed=6 * rows * columns, transcendentals=0
        ),
    )(*([weight] * parts))


def over_rows(pieces):
    nb, rows, wide = pieces.shape
    return lax.all_gather(pieces.reshape(nb * rows, wide), "rows", axis=0, tiled=True)


def sum_rows(gradient):
    nb = lax.axis_size("blk")
    mine = lax.psum_scatter(
        gradient.astype(jnp.bfloat16), "rows", scatter_dimension=0, tiled=True
    )
    return mine.reshape(nb, mine.shape[0] // nb, mine.shape[1])


def step_kernel(with_master, grad, *refs):
    gradient = grad[0].astype(jnp.float32)
    if with_master:
        master, one, two, master_next, one_next, two_next = refs
        master_next[...], one_next[...], two_next[...] = adam_step(
            master[...], one[...], two[...], gradient
        )
    else:
        one, two, one_next, two_next = refs
        one_next[...], two_next[...] = moment_step(one[...], two[...], gradient)


def step(pieces, parts, states):
    nb = pieces.shape[0]
    rows, columns = states[0].shape
    wide = columns // (parts * nb)
    at = pl.BlockSpec((rows, wide), lambda j, part: (0, part * nb + j))
    outs = len(states)
    return pl.pallas_call(
        functools.partial(step_kernel, outs == 3),
        grid=(nb, parts),
        in_specs=[pl.BlockSpec((1, rows, wide), lambda j, part: (j, 0, part))] + [at] * outs,
        out_specs=[at] * outs,
        out_shape=[jax.ShapeDtypeStruct((rows, columns), jnp.float32)] * outs,
        cost_estimate=pl.CostEstimate(
            flops=0, bytes_accessed=(8 * outs + 2) * rows * columns, transcendentals=0
        ),
    )(pieces, *states)


def total_kernel(nr, nb, x_ref, o_ref, held, rows_held, send_one, recv_one, send_two, recv_two):
    r, b = lax.axis_index("rows"), lax.axis_index("blk")
    barrier = pltpu.get_barrier_semaphore()
    across = [lax.rem(b + k, nb) for k in range(1, nb)]
    along = [lax.rem(r + k, nr) for k in range(1, nr)]
    for other in across:
        pl.semaphore_signal(barrier, inc=1, device_id=(r, other), device_id_type=MESH)
    for other in along:
        pl.semaphore_signal(barrier, inc=1, device_id=(other, b), device_id_type=MESH)
    pl.semaphore_wait(barrier, nb + nr - 2)
    held[b] = x_ref[...]

    def first(other, slot):
        return pltpu.make_async_remote_copy(
            src_ref=held.at[b], dst_ref=held.at[slot], send_sem=send_one.at[other],
            recv_sem=recv_one.at[slot], device_id=(r, other), device_id_type=MESH,
        )

    def second(other, slot):
        return pltpu.make_async_remote_copy(
            src_ref=rows_held.at[r], dst_ref=rows_held.at[slot], send_sem=send_two.at[other],
            recv_sem=recv_two.at[slot], device_id=(other, b), device_id_type=MESH,
        )

    for other in across:
        first(other, b).start()
    for other in across:
        first(other, other).wait_recv()
    rows_held[r] = jnp.sum(held[...], axis=0)
    for other in along:
        second(other, r).start()
    for other in along:
        second(other, other).wait_recv()
    o_ref[...] = jnp.sum(rows_held[...], axis=0)
    for other in across:
        first(other, b).wait_send()
    for other in along:
        second(other, r).wait_send()


def total_of(x, cid):
    nr, nb = lax.axis_size("rows"), lax.axis_size("blk")
    return pl.pallas_call(
        functools.partial(total_kernel, nr, nb),
        out_shape=jax.ShapeDtypeStruct(x.shape, x.dtype),
        in_specs=[pl.BlockSpec(memory_space=pltpu.VMEM)],
        out_specs=pl.BlockSpec(memory_space=pltpu.VMEM),
        scratch_shapes=[pltpu.VMEM((nb,) + x.shape, x.dtype), pltpu.VMEM((nr,) + x.shape, x.dtype)]
        + [pltpu.SemaphoreType.DMA((nb,))] * 2 + [pltpu.SemaphoreType.DMA((nr,))] * 2,
        compiler_params=pltpu.CompilerParams(collective_id=cid, has_side_effects=True),
    )(x)


def after(value, *others):
    return lax.optimization_barrier((value,) + others)[0]


def over_tokens(left, right):
    return lax.dot_general(
        left, right, (((0,), (0,)), ((), ())), preferred_element_type=jnp.float32
    )


def shards(
    tokens, cotangent, lengths, block_map, gain_attend, gain_expand,
    attend_in, attend_out, expand_in, reduce_out,
    attend_in_first, attend_out_first, expand_in_first, reduce_out_first,
    attend_in_second, attend_out_second, expand_in_second, reduce_out_second,
):
    f32, bf16 = jnp.float32, jnp.bfloat16
    nb = lax.axis_size("blk")
    near = tokens.shape[1]
    seq = near * nb
    heads = HEADS // nb
    block_rows = near // 2
    length = lengths[0]
    offsets = jnp.arange(block_rows, dtype=jnp.int32)
    place = (block_map[0][:, None] * block_rows + offsets[None, :]).reshape(-1)
    live_place = jnp.where(place < length, place, jnp.int32(1 << 30))
    cosine, sine = rope_tables(place, HEAD_DIM)

    x = tokens[0].astype(f32)
    unit_one, inverse_one, h1 = norm_forward(x, gain_attend)
    swap_in, swap_out = swap(2, arrange(attend_in, 3), arrange(attend_out.T, 1))
    w_in = over_rows(swap_in)
    w_out = over_rows(swap_out)
    h1_all, swap_gu = line_gather(3, after(h1, swap_in), swaps=[arrange(expand_in, 2)])
    w_gu = over_rows(swap_gu)

    mixed = jnp.dot(h1_all, w_in, preferred_element_type=f32).reshape(seq, 3, heads, HEAD_DIM)
    q = rotate(mixed[:, 0], cosine, sine).astype(bf16).transpose(1, 0, 2)
    k = rotate(mixed[:, 1], cosine, sine).astype(bf16).transpose(1, 0, 2)
    v = mixed[:, 2].astype(bf16).transpose(1, 0, 2)
    o, p, swap_red = attend(
        4, q, k, v, place, live_place, length, swaps=[arrange(reduce_out.T, 1)]
    )
    w_red = over_rows(swap_red)
    attended = o.transpose(1, 0, 2).reshape(seq, heads * HEAD_DIM)
    x1 = x + dot_scatter(5, attended, w_out)[0]
    unit_two, inverse_two, h2 = norm_forward(x1, gain_expand)
    h2_all, gate_up = line_gather(6, h2, w_gu)
    (g_all,) = line_gather(7, after(cotangent[0], gate_up))
    units = gate_up.shape[1] // 2
    gate, up = gate_up[:, :units].astype(f32), gate_up[:, units:].astype(f32)
    sigmoid = jax.nn.sigmoid(gate)
    silu = gate * sigmoid
    hidden = (silu * up).astype(bf16)
    part_reduce = over_tokens(g_all, hidden).astype(bf16)
    grad_hidden = jnp.dot(g_all, w_red, preferred_element_type=f32)
    grad_gate = grad_hidden * up * (sigmoid * (1.0 + gate * (1.0 - sigmoid)))
    grad_up = grad_hidden * silu
    grad_gu = jnp.concatenate([grad_gate, grad_up], axis=1).astype(bf16)
    part_expand = over_tokens(h2_all, grad_gu).astype(bf16)
    (grad_h2,) = dot_scatter(8, after(grad_gu, part_expand, part_reduce), w_gu)
    rows_reduce = sum_rows(part_reduce)
    rows_expand = sum_rows(part_expand)
    middle, gain_two = norm_backward(grad_h2, unit_two, inverse_two, gain_expand)
    grad_x1 = cotangent[0].astype(f32) + middle
    branch_all, grad_o = line_gather(9, grad_x1.astype(bf16), w_out)
    part_out = over_tokens(branch_all, attended).astype(bf16)
    rows_out = sum_rows(part_out)
    grad_o = jnp.where((place < length)[:, None], grad_o, jnp.zeros((), bf16))
    grad_o = grad_o.reshape(seq, heads, HEAD_DIM).transpose(1, 0, 2)
    grad_q, grad_k, grad_v, own_reduce = attend_back(
        10, q, k, v, o, after(grad_o, part_out), p, swaps=[rows_reduce]
    )

    def by_token(value):
        return value.astype(bf16).astype(f32).transpose(1, 0, 2)

    grad_mixed = jnp.stack(
        [
            rotate_back(by_token(grad_q), cosine, sine),
            rotate_back(by_token(grad_k), cosine, sine),
            by_token(grad_v),
        ],
        axis=1,
    ).reshape(seq, -1).astype(bf16)
    part_in = over_tokens(h1_all, grad_mixed).astype(bf16)
    grad_h1, own_expand = dot_scatter(11, after(grad_mixed, part_in), w_in, swaps=[rows_expand])
    rows_in = sum_rows(part_in)
    y, own_out, own_in = dot_scatter(
        12, after(hidden, grad_h1), w_red, swaps=[rows_out, rows_in]
    )
    y = x1 + y
    first, gain_one = norm_backward(grad_h1, unit_one, inverse_one, gain_attend)
    grad_input = grad_x1 + first
    gains = total_of(jnp.stack([gain_one, gain_two]), 13)
    set_three = step(own_expand, 2, (expand_in, expand_in_first, expand_in_second))
    set_four = step(own_reduce, 1, (reduce_out.T, reduce_out_first.T, reduce_out_second.T))
    set_two = step(own_out, 1, (attend_out_first.T, attend_out_second.T))
    set_one = step(own_in, 3, (attend_in, attend_in_first, attend_in_second))
    return (
        y.astype(bf16).reshape(tokens.shape),
        grad_input.reshape(tokens.shape),
        gains[0],
        gains[1],
        *set_one,
        *[value.T for value in set_two],
        *set_three,
        *[value.T for value in set_four],
    )


def solution(mesh):
    placed = (
        P("rows", "blk", None),
        P("rows", "blk", None),
        P("rows"),
        P("rows", None),
        P(),
        P(),
        P(("rows", "blk"), None),
        P(None, ("rows", "blk")),
        P(("rows", "blk"), None),
        P(None, ("rows", "blk")),
        P(("rows", "blk"), None),
        P(None, ("rows", "blk")),
        P(("rows", "blk"), None),
        P(None, ("rows", "blk")),
        P(("rows", "blk"), None),
        P(None, ("rows", "blk")),
        P(("rows", "blk"), None),
        P(None, ("rows", "blk")),
    )
    return jax.shard_map(
        shards,
        mesh=mesh,
        in_specs=placed,
        out_specs=(
            P("rows", "blk", None),
            P("rows", "blk", None),
            P(),
            P(),
            P(("rows", "blk"), None),
            P(("rows", "blk"), None),
            P(("rows", "blk"), None),
            P(None, ("rows", "blk")),
            P(None, ("rows", "blk")),
            P(("rows", "blk"), None),
            P(("rows", "blk"), None),
            P(("rows", "blk"), None),
            P(None, ("rows", "blk")),
            P(None, ("rows", "blk")),
            P(None, ("rows", "blk")),
        ),
        check_vma=False,
    )
```

time: 942 us -> 755 us (0.80)
  Pallas kernels: 432 us -> 607 us
  waiting for transfers between devices: 160 us -> 0.89 us
  blocking collectives: 79.5 us -> 0 us
  matrix products: 109 us -> 52.8 us
  local copies, waits for them, and re-layouts: 60.9 us -> 30.2 us
  starting transfers between devices: 25.6 us -> 0.97 us
  other arithmetic: 50.5 us -> 34.8 us
    pallas_call x10 -> x20, Pallas kernels: 432 us -> 607 us  [the longest x4 235 us: dot_scatter(): pl.pallas_call(functools.partial(scatter_kernel, nb // 2, cuts, tile, n),...]
    all_to_all x6 -> x0, waiting for transfers between devices: 110 us -> none  [the longest x3 74.5 us: spread(): mine = lax.all_to_all(pieces, 'blk', 0, 0, tiled=True)]
    dot_general x6 -> x0, matrix products: 52.7 us -> none  [the longest x4 33.6 us: contract_last(): lax.dot_general(left, right, (((1,), (1,)), ((), ())), preferred_element_...]
    reduce_scatter x4, waiting for transfers between devices: 49.1 us -> 0.03 us  [sum_rows(): lax.psum_scatter(gradient.astype(jnp.bfloat16), 'rows', scatter_dimension...]
    all_to_all x2 -> x0, blocking collectives: 40.4 us -> none  [the longest x1 27.2 us: spread(): mine = lax.all_to_all(pieces, 'blk', 0, 0, tiled=True)]
    psum x1 -> x0, blocking collectives: 39.2 us -> none  [shards(): gain_one, gain_two = lax.psum((gain_one, gain_two), ('rows', 'blk'))]
    all_to_all x6 -> x0, starting transfers between devices: 24.7 us -> none  [the longest x3 13.3 us: collect(): pieces = lax.all_to_all(mine, 'blk', 0, 0, tiled=True)]
    sub x3 -> x0, other arithmetic: 15.1 us -> none  [adam_step(): master - learn_rate * (update + decay_rate * master)]
  transfers between devices with their start and end apart: 14 -> 8, of which waited for: 6 -> 0; matrix products, arithmetic and copies ran while one was open for 16% -> 12% of each run, Pallas kernels for 36% -> 64%
where the time goes in v2:
time: 755 us; the launch traced here: 742 us
  Pallas kernels  607 us (80%)
  matrix products  52.8 us (7%)
  other arithmetic  34.8 us (5%)
  local copies, waits for them, and re-layouts  30.2 us (4%)
  between operations  15.4 us (2%)
    pallas_call x4, Pallas kernels, dot_scatter(): pl.pallas_call(functools.partial(scatter_kernel, nb // 2, cuts, tile, n),...  235 us
    pallas_call x4, Pallas kernels, line_gather(): pl.pallas_call(functools.partial(gather_kernel, nb // 2, cuts, tile, with...  220 us
    pallas_call x4, Pallas kernels, step(): pl.pallas_call(functools.partial(step_kernel, outs == 3), grid=(nb, parts...  44.1 us
    dot_general x4, matrix products, over_tokens(): lax.dot_general(left, right, (((0,), (0,)), ((), ())), preferred_element_...  32.9 us
    pallas_call x1, Pallas kernels, swap(): pl.pallas_call(functools.partial(swap_kernel, n), out_shape=[like(value)...  27.6 us
    pallas_call x1, Pallas kernels, attend_back(): pl.pallas_call(functools.partial(attend_back_kernel, lax.axis_size('blk')...  23.6 us
    pallas_call x1, Pallas kernels, attend(): pl.pallas_call(functools.partial(attend_kernel, lax.axis_size('blk') // 2...  22.5 us
    pallas_call x4, Pallas kernels, arrange(): pl.pallas_call(arrange_kernel, grid=(nb,), in_specs=[pl.BlockSpec((rows,...  21.4 us
  transfers between devices with their start and end apart: 8, of which 0 were waited for; matrix products, arithmetic and copies ran while one was open for 12% of the time, Pallas kernels for 64%

profile of v2, /device:TPU:0, one launch (start us, length us, event | category | flops | bytes accessed | tf_op | source)
XLA Modules:
  0.0 741.9 jit_solution(9759573534270467321)
XLA Ops:
  7.2 5.2 shard_map.289.refs_0_
  12.4 4.7 shard_map.290.refs_1_
  17.1 27.6 %shard_map.291 = (bf16[8,64,768]{2,1,0:T(8,128)(2,1)}, bf16[8,64,256]{2,1,0:T(8,128)(2,1)}) custom-call(bf16[8,64,768]{2,1,0:T(8,128)(2,1)} %shard_map.289.refs_0_, bf16[8,64,256]{2,1,0:T(8,128)(2,1)} %shard_map.290.refs_1_), custom_call_target="tpu_custom_call" | custom-call | bytes 150000000 | tf_op jit(solution)/shard_map/pallas_call | solution.py:118
  46.8 6.0 shard_map.292.refs_1_
  52.8 82.7 %shard_map.293 = (bf16[1024,2048]{1,0:T(8,128)(2,1)}, bf16[8,64,2048]{2,1,0:T(8,128)(2,1)}) custom-call(bf16[128,2048]{1,0:T(8,128)(2,1)} %fusion.12.refs_0_, bf16[8,64,2048]{2,1,0:T(8,128)(2,1)} %shard_map.292.refs_1_), custom_call_target="tpu_custom_call" | custom-call | bytes 150000000 | tf_op jit(solution)/shard_map/pallas_call | solution.py:238
  137.8 5.5 shard_map.294.refs_6_
  143.8 1.9 multiply_cosine_fusion
  145.8 7.0 fusion.26
  153.6 1.5 fusion.24
  155.1 1.8 copy.62
  156.9 3.2 copy.63
  160.1 2.4 copy.64
  162.4 3.6 subtract_convert_fusion.2
  166.1 2.5 maximum_bitcast_fusion
  168.5 22.5 %shard_map.295 = (bf16[4,1024,64]{2,1,0:T(8,128)(2,1)}, bf16[4,1024,1024]{2,1,0:T(8,128)(2,1)}, bf16[8,64,1024]{2,1,0:T(8,128)(2,1)}) custom-call(bf16[4,1024,64]{2,1,0:T(8,128)(2,1)} %get-tuple-element.120.refs_0_, bf16[4,1024,64]{2,1,0:T(8,128)(2,1)} %get-tuple-element.121.refs_1_, bf16[4,1024,64]{2,1,0:T(8,128)(2,1)} %bitcast.87, ...), custom_call_target="tpu_custom_call" | custom-call | flops 1073741824 | bytes 150000000 | tf_op jit(solution)/shard_map/pallas_call | solution.py:535
  191.1 1.5 copy.53
  193.6 45.5 %shard_map.296 = f32[128,2048]{1,0:T(8,128)} custom-call(bf16[1024,256]{1,0:T(8,128)(2,1)} %copy.54.refs_0_, bf16[2048,256]{1,0:T(8,128)(2,1)} %all-gather.7.cloned.1.call-done.refs_1_), custom_call_target="tpu_custom_call" | custom-call | flops 1073741824 | bytes 150000000 | tf_op jit(solution)/shard_map/pallas_call | solution.py:401
  239.2 1.5 multiply_reduce_fusion.2
  241.6 49.1 %shard_map.297 = (bf16[1024,2048]{1,0:T(8,128)(2,1)}, bf16[1024,2048]{1,0:T(8,128)(2,1)}) custom-call(bf16[128,2048]{1,0:T(8,128)(2,1)} %multiply_convert_fusion.1.refs_0_, bf16[2048,2048]{1,0:T(8,128)(2,1)} %all-gather.9.cloned.1.call-done.refs_1_), custom_call_target="tpu_custom_call" | custom-call | flops 8589934592 | bytes 150000000 | tf_op jit(solution)/shard_map/pallas_call | solution.py:238
  290.7 45.2 %shard_map.298 = bf16[1024,2048]{1,0:T(8,128)(2,1)} custom-call(bf16[128,2048]{1,0:T(8,128)(2,1)} %bitcast.93), custom_call_target="tpu_custom_call" | custom-call | bytes 150000000 | tf_op jit(solution)/shard_map/pallas_call | solution.py:238
  336.0 12.9 %fusion.2 = (bf16[1024,1024]{1,0:T(8,128)(2,1)}, bf16[1024,1024]{1,0:T(8,128)(2,1)}, bf16[1024,1024]{1,0:T(8,128)(2,1)S(1)}) fusion(bf16[1024,2048]{1,0:T(8,128)(2,1)} %get-tuple-element.58, bf16[1024,2048]{1,0:T(8,128)(2,1)} %shard_map.298, bf16[2048,1024]{1,0:T(8,128)(2,1)} %all-gather.11.cloned.1.call-done.refs_1_), kind=kOutput, calls=%fused_computation.8 | convolution fusion | flops 4312793088 | bytes 18874368 | tf_op jit(solution)/shard_map/dot_general | solution.py:793
  350.2 6.2 convolution_convert_fusion.1
  356.5 14.0 %convolution_convert_fusion = bf16[2048,2048]{1,0:T(8,128)(2,1)} fusion(bf16[1024,2048]{1,0:T(8,128)(2,1)} %get-tuple-element.61, bf16[1024,1024]{1,0:T(8,128)(2,1)} %get-tuple-element.96, bf16[1024,1024]{1,0:T(8,128)(2,1)} %get-tuple-element.95), kind=kOutput, calls=%fused_computation | convolution fusion | flops 8602517504 | bytes 16777216 | tf_op jit(solution)/shard_map/dot_general | solution.py:743
  371.2 5.0 pad_maximum_fusion.refs_0_
  376.2 45.2 %shard_map.299 = f32[128,2048]{1,0:T(8,128)} custom-call(bf16[1024,2048]{1,0:T(8,128)(2,1)} %pad_maximum_fusion.refs_0_, bf16[2048,2048]{1,0:T(8,128)(2,1)} %all-gather.9.cloned.1.call-done.refs_1_), custom_call_target="tpu_custom_call" | custom-call | flops 8589934592 | bytes 150000000 | tf_op jit(solution)/shard_map/pallas_call | solution.py:401
  421.4 1.7 multiply_reduce_fusion
  424.3 43.4 %shard_map.300 = (bf16[1024,2048]{1,0:T(8,128)(2,1)}, bf16[1024,256]{1,0:T(8,128)(2,1)}) custom-call(bf16[128,2048]{1,0:T(8,128)(2,1)} %fusion.23.refs_0_, bf16[2048,256]{1,0:T(8,128)(2,1)} %all-gather.7.cloned.1.call-done.refs_1_), custom_call_target="tpu_custom_call" | custom-call | flops 1073741824 | bytes 150000000 | tf_op jit(solution)/shard_map/pallas_call | solution.py:238
  467.7 2.0 broadcast_select_fusion
  469.7 2.0 copy.57
  471.8 2.4 copy.58
  474.2 4.7 convolution_convert_fusion.3
  479.1 23.6 %shard_map.301 = (f32[4,1024,64]{2,1,0:T(8,128)}, f32[4,1024,64]{2,1,0:T(8,128)}, f32[4,1024,64]{2,1,0:T(8,128)}, bf16[8,64,1024]{2,1,0:T(8,128)(2,1)}) custom-call(bf16[4,1024,64]{2,1,0:T(8,128)(2,1)} %get-tuple-element.120.refs_0_, bf16[4,1024,64]{2,1,0:T(8,128)(2,1)} %get-tuple-element.121.refs_1_, bf16[4,1024,64]{2,1,0:T(8,128)(2,1)} %bitcast.88, ...), custom_call_target="tpu_custom_call" | custom-call | flops 2684354560 | bytes 150000000 | tf_op jit(solution)/shard_map/pallas_call | solution.py:601
  502.7 1.9 convert_bitcast_fusion
  506.1 1.4 add_convert_fusion.1
  509.9 2.4 pad_maximum_fusion.1
  512.3 4.3 copy.59
  516.7 8.0 %convolution_convert_fusion.2 = bf16[2048,768]{1,0:T(8,128)(2,1)} fusion(bf16[1024,2048]{1,0:T(8,128)(2,1)} %get-tuple-element.54, bf16[1024,768]{0,1:T(8,128)(2,1)} %bitcast.91), kind=kOutput, calls=%fused_computation.17 | convolution fusion | flops 3222798336 | bytes 8912896 | tf_op jit(solution)/shard_map/dot_general | solution.py:743
  524.7 2.6 copy.60.refs_0_
  527.3 8.4 %shard_map.308 = (f32[64,8192]{1,0:T(8,128)}, f32[64,8192]{1,0:T(8,128)}, f32[64,8192]{1,0:T(8,128)}) custom-call(bf16[8,64,1024]{2,1,0:T(8,128)(2,1)} %get-tuple-element.85.grad, f32[64,8192]{1,0:T(8,128)} %bitcast.90, f32[64,8192]{1,0:T(8,128)} %bitcast.98, f32[64,8192]{1,0:T(8,128)} %bitcast.99), custom_call_target="tpu_custom_call" | custom-call | bytes 13631488 | tf_op jit(solution)/shard_map/pallas_call | solution.py:673
  535.7 82.6 %shard_map.302 = (f32[128,2048]{1,0:T(8,128)}, bf16[8,64,2048]{2,1,0:T(8,128)(2,1)}) custom-call(bf16[1024,768]{1,0:T(8,128)(2,1)} %copy.60.refs_0_, bf16[2048,768]{1,0:T(8,128)(2,1)} %all-gather.5.cloned.1.call-done.refs_1_, bf16[8,64,2048]{2,1,0:T(8,128)(2,1)} %bitcast.115), custom_call_target="tpu_custom_call" | custom-call | flops 3221225472 | bytes 150000000 | tf_op jit(solution)/shard_map/pallas_call | solution.py:401
  618.3 1.6 fusion.18
  620.6 12.5 %shard_map.304 = f32[2,2048]{1,0:T(2,128)} custom-call(f32[2,2048]{1,0:T(2,128)} %pad_maximum_fusion.2.x_ref), custom_call_target="tpu_custom_call" | custom-call | tf_op jit(solution)/shard_map/pallas_call | solution.py:727
  633.1 1.4 fusion.25
  634.5 61.5 %shard_map.303 = (f32[128,2048]{1,0:T(8,128)}, bf16[8,64,256]{2,1,0:T(8,128)(2,1)}, bf16[8,64,768]{2,1,0:T(8,128)(2,1)}) custom-call(bf16[1024,1024]{1,0:T(8,128)(2,1)} %copy-done.15, bf16[2048,1024]{1,0:T(8,128)(2,1)} %all-gather.11.cloned.1.call-done.refs_1_, bf16[8,64,256]{2,1,0:T(8,128)(2,1)} %bitcast.122, bf16[8,64,768]{2,1,0:T(8,128)(2,1)} %bitcast.119), custom_call_target="tpu_custom_call" | custom-call | flops 4294967296 | bytes 150000000 | tf_op jit(solution)/shard_map/pallas_call | solution.py:401
  696.0 3.2 fusion.17
  699.2 16.2 %shard_map.307 = (f32[64,16384]{1,0:T(8,128)}, f32[64,16384]{1,0:T(8,128)}, f32[64,16384]{1,0:T(8,128)}) custom-call(bf16[8,64,2048]{2,1,0:T(8,128)(2,1)} %get-tuple-element.81.grad, f32[64,16384]{1,0:T(8,128)} %refs_0_.7, f32[64,16384]{1,0:T(8,128)} %refs_1_.7, f32[64,16384]{1,0:T(8,128)} %refs_2_.5), custom_call_target="tpu_custom_call" | custom-call | bytes 27262976 | tf_op jit(solution)/shard_map/pallas_call | solution.py:673
  715.4 14.3 %shard_map.305 = (f32[64,6144]{1,0:T(8,128)}, f32[64,6144]{1,0:T(8,128)}, f32[64,6144]{1,0:T(8,128)}) custom-call(bf16[8,64,768]{2,1,0:T(8,128)(2,1)} %get-tuple-element.74.grad, f32[64,6144]{1,0:T(8,128)} %refs_0_.6, f32[64,6144]{1,0:T(8,128)} %refs_1_.6, f32[64,6144]{1,0:T(8,128)} %refs_2_.4), custom_call_target="tpu_custom_call" | custom-call | bytes 10223616 | tf_op jit(solution)/shard_map/pallas_call | solution.py:673
  729.7 5.1 shard_map.306
  (80 shorter events, 15.1 us)
Async XLA Ops:
  7.2 138.6 %all-gather.5.cloned.1.call-start = ((), (), s32[]{:S(2)}) async-start(), calls=%async_computation.4 | async-start | bytes 3932160 | tf_op jit(solution)/shard_map/all_gather | solution.py:644
  12.4 33.2 %copy-start = (bf16[1,128,2048]{2,1,0:T(8,128)(2,1)S(1)}, bf16[1,128,2048]{2,1,0:T(8,128)(2,1)}, u32[]{:S(2)}) copy-start(bf16[1,128,2048]{2,1,0:T(8,128)(2,1)} %param.18) | copy-start | bytes 1572868
  12.4 33.4 %copy-start.13 = (f32[2048]{0:T(1024)S(1)}, f32[2048]{0:T(1024)}, u32[]{:S(2)}) copy-start(f32[2048]{0:T(1024)} %param.22) | copy-start | bytes 24580
  44.8 148.9 %all-gather.7.cloned.1.call-start = ((), (), s32[]{:S(2)}) async-start(), calls=%async_computation.5 | async-start | bytes 1310720 | tf_op jit(solution)/shard_map/all_gather | solution.py:644
  45.5 196.1 %all-gather.9.cloned.1.call-start = ((), (), s32[]{:S(2)}) async-start(), calls=%async_computation.6 | async-start | bytes 10485760 | tf_op jit(solution)/shard_map/all_gather | solution.py:644
  52.8 82.8 %copy-start.14 = (s32[1,16]{1,0:T(1,128)S(1)}, s32[1,16]{1,0:T(1,128)}, u32[]{:S(2)}) copy-start(s32[1,16]{1,0:T(1,128)} %param.21) | copy-start | bytes 196
  135.6 200.4 %all-gather.11.cloned.1.call-start = ((), (), s32[]{:S(2)}) async-start(), calls=%async_computation.7 | async-start | bytes 5242880 | tf_op jit(solution)/shard_map/all_gather | solution.py:644
  145.7 16.7 %copy-start.4 = (f32[1024,32]{1,0:T(8,128)}, f32[1024,32]{1,0:T(8,128)S(1)}, u32[]{:S(2)}) copy-start(f32[1024,32]{1,0:T(8,128)S(1)} %get-tuple-element.116) | copy-start | bytes 393220
  145.7 16.7 %copy-start.6 = (f32[1024,32]{1,0:T(8,128)}, f32[1024,32]{1,0:T(8,128)S(1)}, u32[]{:S(2)}) copy-start(f32[1024,32]{1,0:T(8,128)S(1)} %get-tuple-element.117) | copy-start | bytes 393220
  191.0 288.1 %reduce-scatter.5.cloned.1.call-start = ((), (), s32[]{:S(2)}) async-start(), calls=%async_computation.8 | async-start | bytes 5242880 | tf_op jit(solution)/shard_map/reduce_scatter | solution.py:649
  192.6 1.0 copy-start.9
  193.6 45.5 %copy-start.1 = (bf16[1,128,2048]{2,1,0:T(8,128)(2,1)S(1)}, bf16[1,128,2048]{2,1,0:T(8,128)(2,1)}, u32[]{:S(2)}) copy-start(bf16[1,128,2048]{2,1,0:T(8,128)(2,1)} %param.18) | copy-start | bytes 1572868
  239.2 1.5 copy-start.12
  336.0 14.2 %copy-start.8 = (bf16[1024,2048]{1,0:T(8,128)(2,1)S(1)}, bf16[1024,2048]{1,0:T(8,128)(2,1)}, u32[]{:S(2)}) copy-start(bf16[1024,2048]{1,0:T(8,128)(2,1)} %shard_map.298) | copy-start | bytes 12582916
  348.9 1.3 copy-start.15
  356.4 179.3 %reduce-scatter.7.cloned.1.call-start = ((), (), s32[]{:S(2)}) async-start(), calls=%async_computation.9 | async-start | bytes 10485760 | tf_op jit(solution)/shard_map/reduce_scatter | solution.py:649
  370.5 264.1 %reduce-scatter.9.cloned.1.call-start = ((), (), s32[]{:S(2)}) async-start(), calls=%async_computation.10 | async-start | bytes 1310720 | tf_op jit(solution)/shard_map/reduce_scatter | solution.py:649
  421.4 1.7 copy-start.2
  421.4 1.7 copy-start.3
  478.9 155.7 %reduce-scatter.11.cloned.1.call-start = ((), (), s32[]{:S(2)}) async-start(), calls=%async_computation.11 | async-start | bytes 3932160 | tf_op jit(solution)/shard_map/reduce_scatter | solution.py:649
  502.7 2.2 copy-start.11
  504.9 1.0 copy-start.5
  504.9 1.2 copy-start.7
  508.2 1.6 copy-start.10
Sparse Core Ops, SparseCore 0:
  44.9 45.7 all-gather.4
  92.5 26.6 all-gather.6
  135.7 87.6 all-gather.8
  225.1 52.6 all-gather.10
  356.5 52.7 reduce-scatter.4
  412.5 86.4 reduce-scatter.6
  501.9 27.7 reduce-scatter.8
  533.5 43.9 reduce-scatter.10

commit v3 on v2

v3 whole, which is shorter than its diff:
```python
import functools
import math

import jax
import jax.numpy as jnp
from jax import lax
from jax.experimental import pallas as pl
from jax.experimental.pallas import tpu as pltpu
from jax.sharding import PartitionSpec as P

HEADS = 32
HEAD_DIM = 64
MESH = pl.DeviceIdType.MESH
MIB = 1 << 20

theta_base = 130000.0
norm_eps = 1e-05
neg_large = -1e30
beta_one = 0.9
beta_two = 0.95
learn_rate = 0.01
decay_rate = 0.1
adam_eps = 1e-08
step_count = 10


def line_place():
    b = lax.axis_index("blk")
    return lax.axis_index("rows"), b // 2, b % 2


def greet(chips, swaps):
    r, z, c = line_place()
    barrier = pltpu.get_barrier_semaphore()

    def signal(b):
        pl.semaphore_signal(barrier, inc=1, device_id=(r, b), device_id_type=MESH)

    if swaps:
        b, nb = 2 * z + c, 2 * chips
        for k in range(1, nb):
            signal(lax.rem(b + k, nb))
        pl.semaphore_wait(barrier, nb - 1)
        return
    signal(2 * z + 1 - c)
    pl.when(z < chips - 1)(lambda: signal(2 * (z + 1) + c))
    pl.when(z > 0)(lambda: signal(2 * (z - 1) + c))
    pl.semaphore_wait(barrier, 1 + (z < chips - 1).astype(jnp.int32) + (z > 0).astype(jnp.int32))


def swap_copies(src, dst, local, send, recv):
    r, b = lax.axis_index("rows"), lax.axis_index("blk")
    nb = src.shape[0]
    others = [lax.rem(b + k, nb) for k in range(1, nb)]

    def remote(other, slot):
        return pltpu.make_async_remote_copy(
            src_ref=src.at[other], dst_ref=dst.at[slot], send_sem=send.at[other],
            recv_sem=recv.at[slot], device_id=(r, other), device_id_type=MESH,
        )

    def start():
        for other in others:
            remote(other, b).start()
        pltpu.make_async_copy(src.at[b], dst.at[b], local).start()

    def wait():
        for other in others:
            remote(other, other).wait_recv()
        for other in others:
            remote(other, b).wait_send()
        pltpu.make_async_copy(src.at[b], dst.at[b], local).wait()

    return start, wait


def swap_sems(swaps):
    sems = []
    for pieces in swaps:
        sems += [pltpu.SemaphoreType.DMA] + [pltpu.SemaphoreType.DMA((pieces.shape[0],))] * 2
    return sems


def swap_list(srcs, dsts, sems):
    made = [swap_copies(s, d, *sems[3 * i : 3 * i + 3]) for i, (s, d) in enumerate(zip(srcs, dsts))]
    return [one[0] for one in made], [one[1] for one in made]


def like(value):
    return jax.ShapeDtypeStruct(value.shape, value.dtype)


ANY = pl.BlockSpec(memory_space=pl.ANY)
VMEM = pl.BlockSpec(memory_space=pltpu.VMEM)


def params(cid):
    return pltpu.CompilerParams(
        collective_id=cid, has_side_effects=True, vmem_limit_bytes=60 * MIB
    )


def cost(flops):
    return pl.CostEstimate(flops=flops, bytes_accessed=150_000_000, transcendentals=0)


def gather_task(chips, cuts, x_ref, o_ref, sems):
    copy_sem, send_up, send_down, send_side, recv = sems
    r, z, c = line_place()
    t = x_ref.shape[0]
    h = t // cuts
    up, down, side = (r, 2 * (z + 1) + c), (r, 2 * (z - 1) + c), (r, 2 * z + 1 - c)
    has_up, has_down = z < chips - 1, z > 0
    mine = 2 * z + c

    def piece(j, q):
        return o_ref.at[pl.ds(pl.multiple_of(j * t + q * h, h), h)]

    def remote(src, j, q, sem, dev):
        return pltpu.make_async_remote_copy(
            src_ref=src, dst_ref=piece(j, q), send_sem=sem.at[j, q], recv_sem=recv.at[j, q],
            device_id=dev, device_id_type=MESH,
        )

    def local():
        whole = o_ref.at[pl.ds(pl.multiple_of(mine * t, t), t)]
        return pltpu.make_async_copy(x_ref, whole, copy_sem)

    def start():
        for q in range(cuts):
            from_here = x_ref.at[pl.ds(q * h, h)]
            pl.when(has_up)(lambda: remote(from_here, mine, q, send_up, up).start())
            pl.when(has_down)(lambda: remote(from_here, mine, q, send_down, down).start())
            remote(from_here, mine, q, send_side, side).start()
        local().start()

    def hop(k):
        for q in range(cuts):
            @pl.when(z - k >= 0)
            def _():
                j = 2 * (z - k) + c
                remote(piece(j, q), j, q, send_up, up).wait_recv()
                pl.when(has_up)(lambda: remote(piece(j, q), j, q, send_up, up).start())
                remote(piece(j, q), j, q, send_side, side).start()

            @pl.when(z + k < chips)
            def _():
                j = 2 * (z + k) + c
                remote(piece(j, q), j, q, send_down, down).wait_recv()
                pl.when(has_down)(lambda: remote(piece(j, q), j, q, send_down, down).start())
                remote(piece(j, q), j, q, send_side, side).start()

    def from_side(y):
        for q in range(cuts):
            j = 2 * y + 1 - c
            remote(piece(j, q), j, q, send_side, side).wait_recv()

    def finish():
        for y in range(chips):
            j = 2 * y + c
            for q in range(cuts):
                pl.when(has_up & (z >= y))(
                    lambda: remote(piece(j, q), j, q, send_up, up).wait_send()
                )
                pl.when(has_down & (z <= y))(
                    lambda: remote(piece(j, q), j, q, send_down, down).wait_send()
                )
                remote(piece(j, q), j, q, send_side, side).wait_send()

    return start, hop, from_side, local, finish


def gather_sems(nb, cuts):
    return [pltpu.SemaphoreType.DMA] + [pltpu.SemaphoreType.DMA((nb, cuts))] * 4


def gather_kernel(chips, cuts, tile, n, ff, n_prod, *refs):
    refs = list(refs)
    x_ref = refs.pop(0)
    w_ref = refs.pop(0) if n_prod else None
    srcs = [refs.pop(0) for _ in range(n)]
    o_ref = refs.pop(0)
    prods = [refs.pop(0) for _ in range(n_prod)]
    dsts = [refs.pop(0) for _ in range(n)]
    begin, hop, from_side, local, finish = gather_task(chips, cuts, x_ref, o_ref, refs[:5])
    starts, waits = swap_list(srcs, dsts, refs[5:])
    r, z, c = line_place()
    t = x_ref.shape[0]
    f32 = jnp.float32
    greet(chips, n > 0)

    def dot(y):
        if not n_prod:
            return
        rows = pl.ds(pl.multiple_of(y * 2 * t, 2 * t), 2 * t)
        units = prods[0].shape[1]

        def product(at):
            cols = pl.ds(pl.multiple_of(at, tile), tile)
            return jnp.dot(o_ref[rows, :], w_ref[:, cols], preferred_element_type=f32)

        def one(i, _):
            cols = pl.ds(pl.multiple_of(i * tile, tile), tile)
            got = product(i * tile)
            if ff:
                up = product(units + i * tile)
                sigmoid = jax.nn.sigmoid(got)
                silu = got * sigmoid
                values = (silu * up, up * (sigmoid * (1.0 + got * (1.0 - sigmoid))), silu)
            else:
                values = (got,)
            for ref, value in zip(prods, values):
                ref[rows, cols] = value.astype(ref.dtype)
            return 0

        lax.fori_loop(0, units // tile, one, 0)

    begin()
    for start in starts:
        start()
    from_side(z)
    local().wait()
    dot(z)
    for k in range(1, chips):
        hop(k)

        @pl.when(z - k >= 0)
        def _():
            from_side(z - k)
            dot(z - k)

        @pl.when(z + k < chips)
        def _():
            from_side(z + k)
            dot(z + k)

    finish()
    for wait in waits:
        wait()


def line_gather(cid, x, w=None, swaps=(), ff=False, cuts=2, tile=512):
    nb = lax.axis_size("blk")
    all_rows = nb * x.shape[0]
    with_dot = w is not None
    place = VMEM if with_dot else ANY
    outs = [jax.ShapeDtypeStruct((all_rows, x.shape[1]), x.dtype)]
    flops, n_prod = 0, 0
    if with_dot:
        n_prod = 3 if ff else 1
        units = w.shape[1] // 2 if ff else w.shape[1]
        outs += [jax.ShapeDtypeStruct((all_rows, units), jnp.bfloat16)] * n_prod
        flops = 2 * all_rows * w.shape[0] * w.shape[1]
        tile = min(tile, units)
    return pl.pallas_call(
        functools.partial(gather_kernel, nb // 2, cuts, tile, len(swaps), ff, n_prod),
        out_shape=outs + [like(value) for value in swaps],
        in_specs=[place] * (1 + with_dot) + [ANY] * len(swaps),
        out_specs=[place] * (1 + n_prod) + [ANY] * len(swaps),
        scratch_shapes=gather_sems(nb, cuts) + swap_sems(swaps),
        compiler_params=params(cid),
        cost_estimate=cost(flops),
    )(*([x, w] if with_dot else [x]), *swaps)


def need_order(chips):
    table = []
    for z in range(chips):
        need = {
            y: (chips - 1 + z - y) if y > z else (chips - 1 - z + y)
            for y in range(chips) if y != z
        }
        table.append(sorted(need, key=lambda y: need[y]) + [z])
    return table


def pick(table, z, k):
    out = 0
    for at, row in enumerate(table):
        for step, block in enumerate(row):
            out = out + jnp.where((z == at) & (k == step), block, 0)
    return out


def scatter_task(chips, cuts, tile, o_ref, bufs, sems):
    mine, away, side_buf, line_buf = bufs
    send_side, recv_side, send_up, recv_up, send_down, recv_down = sems
    r, z, c = line_place()
    t, width = o_ref.shape
    low, f32 = away.dtype, jnp.float32
    up, down, side = (r, 2 * (z + 1) + c), (r, 2 * (z - 1) + c), (r, 2 * z + 1 - c)
    has_up, has_down = z < chips - 1, z > 0
    h = t // cuts
    table = need_order(chips)

    def remote(src, dst, y, q, send, recv, dev):
        return pltpu.make_async_remote_copy(
            src_ref=src.at[y, pl.ds(q * h, h)], dst_ref=dst.at[y, pl.ds(q * h, h)],
            send_sem=send.at[y, q], recv_sem=recv.at[y, q], device_id=dev, device_id_type=MESH,
        )

    def to_side(y, q):
        return remote(away, side_buf, y, q, send_side, recv_side, side)

    def along(y, slot, q, send, recv, dev):
        return pltpu.make_async_remote_copy(
            src_ref=mine.at[y, pl.ds(q * h, h)], dst_ref=line_buf.at[slot, pl.ds(q * h, h)],
            send_sem=send.at[y, q], recv_sem=recv.at[y, q], device_id=dev, device_id_type=MESH,
        )

    def to_up(y, q):
        return along(y, y, q, send_up, recv_up, up)

    def to_down(y, q):
        return along(y, jnp.where(y == z - 1, chips, y), q, send_down, recv_down, down)

    def from_up(y, q):
        return along(y, jnp.where(y == z, chips, y), q, send_down, recv_down, down)

    def rows(q):
        return pl.ds(q * h, h)

    def total(y, q):
        to_side(y, q).wait_recv()
        return mine[y, rows(q)].astype(f32) + side_buf[y, rows(q)].astype(f32)

    def put(s, rows_of, w_ref):
        y = pick(table, z, s)
        a = rows_of(pl.ds(pl.multiple_of(2 * y * t, 2 * t), 2 * t))

        def one(i, _):
            cols = pl.ds(pl.multiple_of(i * tile, tile), tile)
            got = lax.dot_general(
                a[...], w_ref[cols], (((1,), (1,)), ((), ())), preferred_element_type=f32
            ).astype(low)

            @pl.when(c == 0)
            def _():
                mine[y, :, cols] = got[:t]
                away[y, :, cols] = got[t:]

            @pl.when(c == 1)
            def _():
                mine[y, :, cols] = got[t:]
                away[y, :, cols] = got[:t]

            return 0

        lax.fori_loop(0, width // tile, one, 0)
        for q in range(cuts):
            to_side(y, q).start()

    def hop(s):
        y = chips - 1 + z - s
        w = s - (chips - 1) + z
        for q in range(cuts):
            @pl.when(y <= chips - 1)
            def _():
                now = total(y, q)

                @pl.when(has_down)
                def _():
                    to_up(y, q).wait_recv()
                    mine[y, rows(q)] = (now + line_buf[y, rows(q)].astype(f32)).astype(low)

                @pl.when(z == 0)
                def _():
                    mine[y, rows(q)] = now.astype(low)

                to_up(y, q).start()

            @pl.when(w >= 0)
            def _():
                now = total(w, q)

                @pl.when(has_up)
                def _():
                    from_up(w, q).wait_recv()
                    mine[w, rows(q)] = (now + line_buf[w, rows(q)].astype(f32)).astype(low)

                @pl.when(z == chips - 1)
                def _():
                    mine[w, rows(q)] = now.astype(low)

                to_down(w, q).start()

    def finish():
        for q in range(cuts):
            o_ref[rows(q)] = total(z, q)
        for q in range(cuts):
            @pl.when(has_down)
            def _():
                to_up(z, q).wait_recv()
                o_ref[rows(q)] += line_buf[z, rows(q)].astype(f32)

            @pl.when(has_up)
            def _():
                from_up(z, q).wait_recv()
                o_ref[rows(q)] += line_buf[chips, rows(q)].astype(f32)

        for y in range(chips):
            for q in range(cuts):
                to_side(y, q).wait_send()
                pl.when(y > z)(lambda: to_up(y, q).wait_send())
                pl.when(y < z)(lambda: to_down(y, q).wait_send())

    return put, hop, finish


def scatter_scratch(chips, cuts, t, width):
    return (
        [pltpu.VMEM((chips, t, width), jnp.bfloat16)] * 3
        + [pltpu.VMEM((chips + 1, t, width), jnp.bfloat16)]
        + [pltpu.SemaphoreType.DMA((chips, cuts))] * 6
    )


def scatter_kernel(chips, cuts, tile, n, *refs):
    a_ref, w_ref, srcs, o_ref = refs[0], refs[1], refs[2 : 2 + n], refs[2 + n]
    dsts, refs = refs[3 + n : 3 + 2 * n], refs[3 + 2 * n :]
    put, hop, finish = scatter_task(chips, cuts, tile, o_ref, refs[:4], refs[4:10])
    starts, waits = swap_list(srcs, dsts, refs[10:])
    greet(chips, n > 0)
    for s in range(chips):
        put(s, lambda rows: a_ref.at[rows], w_ref)
        if s < chips - 1:
            hop(s)
        if s == 0:
            for start in starts:
                start()
    finish()
    for wait in waits:
        wait()


def ff_back_kernel(
    chips, cuts, tile, g_ref, one_ref, two_ref, red_ref, w_ref, h2_ref, o_ref, dw_ref, grad_ref, *refs
):
    put, hop, finish = scatter_task(chips, cuts, tile, o_ref, refs[:4], refs[4:10])
    f32 = jnp.float32
    units = red_ref.shape[1]
    span = min(512, units)
    greet(chips, False)

    def rows_of(rows):
        def one(i, _):
            cols = pl.ds(pl.multiple_of(i * span, span), span)
            more = pl.ds(pl.multiple_of(units + i * span, span), span)
            grad = jnp.dot(g_ref[rows], red_ref[:, cols], preferred_element_type=f32)
            grad_ref[rows, cols] = (grad * one_ref[rows, cols].astype(f32)).astype(grad_ref.dtype)
            grad_ref[rows, more] = (grad * two_ref[rows, cols].astype(f32)).astype(grad_ref.dtype)
            return 0

        lax.fori_loop(0, units // span, one, 0)
        return grad_ref.at[rows]

    for s in range(chips):
        put(s, rows_of, w_ref)
        if s < chips - 1:
            hop(s)

    def one(i, _):
        cols = pl.ds(pl.multiple_of(i * 256, 256), 256)
        dw_ref[cols] = lax.dot_general(
            h2_ref[:, cols], grad_ref[...], (((0,), (0,)), ((), ())), preferred_element_type=f32
        ).astype(dw_ref.dtype)
        return 0

    lax.fori_loop(0, dw_ref.shape[0] // 256, one, 0)
    finish()


def ff_back(cid, g_all, slope_gate, slope_up, w_red, w_gu, h2_all, cuts=2, tile=1024):
    nb = lax.axis_size("blk")
    seq, width = g_all.shape
    both = w_gu.shape[1]
    t = seq // nb
    return pl.pallas_call(
        functools.partial(ff_back_kernel, nb // 2, cuts, tile),
        out_shape=[
            jax.ShapeDtypeStruct((t, width), jnp.float32),
            jax.ShapeDtypeStruct((width, both), jnp.bfloat16),
        ],
        in_specs=[VMEM] * 6,
        out_specs=[VMEM] * 2,
        scratch_shapes=[pltpu.VMEM((seq, both), jnp.bfloat16)]
        + scatter_scratch(nb // 2, cuts, t, width),
        compiler_params=params(cid),
        cost_estimate=cost(5 * seq * width * both),
    )(g_all, slope_gate, slope_up, w_red, w_gu, h2_all)


def dot_scatter(cid, a, w, swaps=(), cuts=2, tile=1024):
    nb = lax.axis_size("blk")
    t, width = a.shape[0] // nb, w.shape[0]
    n = len(swaps)
    return pl.pallas_call(
        functools.partial(scatter_kernel, nb // 2, cuts, tile, n),
        out_shape=[jax.ShapeDtypeStruct((t, width), jnp.float32)] + [like(s) for s in swaps],
        in_specs=[VMEM, VMEM] + [ANY] * n,
        out_specs=[VMEM] + [ANY] * n,
        scratch_shapes=scatter_scratch(nb // 2, cuts, t, width) + swap_sems(swaps),
        compiler_params=params(cid),
        cost_estimate=cost(2 * a.shape[0] * width * w.shape[1]),
    )(a, w, *swaps)


def pair_tables(positions):
    half = HEAD_DIM // 2
    frequency = jnp.exp(
        -jnp.arange(half, dtype=jnp.float32) * (2.0 / HEAD_DIM) * math.log(theta_base)
    )
    angles = positions.astype(jnp.float32)[:, None] * frequency[None, :]
    cosine, sine = jnp.cos(angles), jnp.sin(angles)
    return (
        jnp.concatenate([cosine] * 4, axis=1),
        jnp.concatenate([-sine, sine] * 2, axis=1),
    )


def norm_forward(values, gain_vector):
    inverse = lax.rsqrt(jnp.mean(values * values, axis=-1, keepdims=True) + norm_eps)
    unit_values = values * inverse
    return (unit_values, inverse, (unit_values * gain_vector).astype(jnp.bfloat16))


def norm_backward(grad_normed, unit_values, inverse, gain_vector):
    grad_unit = grad_normed * gain_vector
    grad_values = inverse * (
        grad_unit - unit_values * jnp.mean(grad_unit * unit_values, axis=-1, keepdims=True)
    )
    return (grad_values, jnp.sum(grad_normed * unit_values, axis=0))


def contract_last(left, right):
    return lax.dot_general(
        left, right, (((1,), (1,)), ((), ())), preferred_element_type=jnp.float32
    )


def adam_step(master, moment_one, moment_two, gradient):
    moment_one = beta_one * moment_one + (1.0 - beta_one) * gradient
    moment_two = beta_two * moment_two + (1.0 - beta_two) * gradient * gradient
    update = (
        moment_one
        / (1.0 - beta_one**step_count)
        / (jnp.sqrt(moment_two / (1.0 - beta_two**step_count)) + adam_eps)
    )
    return (master - learn_rate * (update + decay_rate * master), moment_one, moment_two)


def moment_step(moment_one, moment_two, gradient):
    moment_one = beta_one * moment_one + (1.0 - beta_one) * gradient
    moment_two = beta_two * moment_two + (1.0 - beta_two) * gradient * gradient
    return (moment_one, moment_two)


def once(*shape):
    return pl.BlockSpec(shape, lambda i: (0,) * len(shape), pipeline_mode=pl.Buffered(1))


def partner(values):
    width = values.shape[1]
    half = HEAD_DIM // 2
    feature = lax.broadcasted_iota(jnp.int32, values.shape, 1) % HEAD_DIM
    return jnp.where(
        feature < half, pltpu.roll(values, width - half, 1), pltpu.roll(values, half, 1)
    )


def spread_table(table, width):
    return jnp.concatenate([table] * (width // table.shape[1]), axis=1)


def head_lanes(shape):
    return lax.broadcasted_iota(jnp.int32, shape, 1) // HEAD_DIM


def attend_kernel(chips, cuts, n, h1_ref, w_ref, cos_ref, sin_ref, q_place, k_place, length_ref, g_ref, *refs):
    srcs, refs = refs[:n], refs[n:]
    o_ref, q_ref, k_ref, v_ref, p_ref, g_all = refs[:6]
    dsts, sems = refs[6 : 6 + n], refs[6 + n :]
    begin, hop, from_side, local, finish = gather_task(chips, cuts, g_ref, g_all, sems[:5])
    starts, waits = swap_list(srcs, dsts, sems[5:])
    step, steps = pl.program_id(0), pl.num_programs(0)
    tile, width = o_ref.shape
    f32, bf16 = jnp.float32, jnp.bfloat16

    @pl.when(step == 0)
    def _():
        greet(chips, True)
        for start in starts:
            start()
        begin()

        def one(i, _):
            rows = pl.ds(pl.multiple_of(i * tile, tile), tile)
            mixed = jnp.dot(h1_ref[rows], w_ref[...], preferred_element_type=f32)
            cosine, sine = spread_table(cos_ref[rows], width), spread_table(sin_ref[rows], width)
            for at, ref in enumerate((q_ref, k_ref)):
                got = mixed[:, at * width : (at + 1) * width]
                ref[rows] = (got * cosine + partner(got) * sine).astype(bf16)
            v_ref[rows] = mixed[:, 2 * width :].astype(bf16)
            return 0

        lax.fori_loop(0, steps, one, 0)

    @pl.when((step > 0) & (step < chips))
    def _():
        hop(step)

    rows = pl.ds(pl.multiple_of(step * tile, tile), tile)
    queries = q_ref[rows] * jnp.asarray(1.0 / math.sqrt(HEAD_DIM), bf16)
    lanes = head_lanes((tile, width))
    place = q_place[...]
    allowed = k_place[...] <= place
    out = jnp.zeros((tile, width), f32)
    for head in range(width // HEAD_DIM):
        here = lanes == head
        one_head = jnp.where(here, queries, jnp.zeros((), bf16))
        scores = lax.dot_general(
            one_head, k_ref[...], (((1,), (1,)), ((), ())), preferred_element_type=f32
        )
        scores = jnp.where(allowed, scores, neg_large)
        weights = jnp.exp(scores - jnp.max(scores, axis=-1, keepdims=True))
        weights = weights * (1.0 / jnp.sum(weights, axis=-1, keepdims=True))
        low = weights.astype(bf16)
        p_ref[head] = low
        out = jnp.where(here, jnp.dot(low, v_ref[...], preferred_element_type=f32), out)
    o_ref[...] = jnp.where(place < length_ref[0], out, 0.0).astype(bf16)

    @pl.when(step == steps - 1)
    def _():
        local().wait()
        for y in range(chips):
            from_side(y)
        finish()
        for wait in waits:
            wait()


def attend(cid, h1_all, w_in, cosine, sine, place, live_place, length, g, swaps=(), cuts=2):
    seq, wide = h1_all.shape
    width = w_in.shape[1] // 3
    heads = width // HEAD_DIM
    nb = lax.axis_size("blk")
    tile = seq // (nb // 2)
    n = len(swaps)
    part = pl.BlockSpec((tile, width), lambda i: (i, 0))

    full = jax.ShapeDtypeStruct((seq, width), jnp.bfloat16)
    return pl.pallas_call(
        functools.partial(attend_kernel, nb // 2, cuts, n),
        grid=(seq // tile,),
        in_specs=[
            once(seq, wide), once(wide, 3 * width), once(seq, 2 * HEAD_DIM), once(seq, 2 * HEAD_DIM),
            pl.BlockSpec((tile, 1), lambda i: (i, 0)),
            once(1, seq),
            pl.BlockSpec(memory_space=pltpu.SMEM),
            ANY,
        ]
        + [ANY] * n,
        out_specs=[part] + [once(seq, width)] * 3
        + [pl.BlockSpec((heads, tile, seq), lambda i: (0, i, 0)), ANY] + [ANY] * n,
        out_shape=[full] * 4
        + [
            jax.ShapeDtypeStruct((heads, seq, seq), jnp.bfloat16),
            jax.ShapeDtypeStruct((seq, g.shape[1]), g.dtype),
        ]
        + [like(value) for value in swaps],
        scratch_shapes=gather_sems(nb, cuts) + swap_sems(swaps),
        compiler_params=params(cid),
        cost_estimate=cost(4 * seq * seq * width + 6 * seq * wide * width),
    )(h1_all, w_in, cosine, sine, place[:, None], live_place[None, :], length.reshape(1), g, *swaps)


def attend_back_kernel(
    chips, cuts, tile_y, q_ref, k_ref, v_ref, o_ref, g_ref, p_ref, cos_ref, sin_ref, q_place, length_ref,
    hidden_ref, red_ref, mixed_ref, y_ref, ds_ref, qm_ref, gm_ref, dk_acc, dv_acc, *refs
):
    put, hop, finish = scatter_task(chips, cuts, tile_y, y_ref, refs[:4], refs[4:10])
    step, steps = pl.program_id(0), pl.num_programs(0)
    tile, width = o_ref.shape
    f32, bf16 = jnp.float32, jnp.bfloat16
    factor = 1.0 / math.sqrt(HEAD_DIM)

    @pl.when(step == 0)
    def _():
        greet(chips, False)
        dk_acc[...] = jnp.zeros_like(dk_acc)
        dv_acc[...] = jnp.zeros_like(dv_acc)

    put(step, lambda rows: hidden_ref.at[rows], red_ref)
    pl.when(step == 0)(lambda: hop(step))
    over_rows = (((0,), (0,)), ((), ()))
    rows = pl.ds(pl.multiple_of(step * tile, tile), tile)
    lanes = head_lanes((tile, width))
    nothing = jnp.zeros((), bf16)
    grad = jnp.where(q_place[...] < length_ref[0], g_ref[...], nothing)
    both = grad.astype(f32) * o_ref[...].astype(f32)
    queries = q_ref[rows]
    grad_q = jnp.zeros((tile, width), f32)
    for head in range(width // HEAD_DIM):
        here = lanes == head
        block = pl.ds(head * tile, tile)
        delta = jnp.sum(jnp.where(here, both, 0.0), axis=-1, keepdims=True)
        one_grad = jnp.where(here, grad, nothing)
        gm_ref[block] = one_grad
        qm_ref[block] = jnp.where(here, queries, nothing)
        grad_p = lax.dot_general(
            one_grad, v_ref[...], (((1,), (1,)), ((), ())), preferred_element_type=f32
        )
        grad_s = (p_ref[head].astype(f32) * (grad_p - delta)).astype(bf16)
        ds_ref[block] = grad_s
        grad_q = jnp.where(here, jnp.dot(grad_s, k_ref[...], preferred_element_type=f32), grad_q)
    heads = width // HEAD_DIM
    dv_acc[...] += lax.dot_general(
        p_ref[...].reshape(heads * tile, p_ref.shape[2]), gm_ref[...], over_rows,
        preferred_element_type=f32,
    )
    dk_acc[...] += lax.dot_general(ds_ref[...], qm_ref[...], over_rows, preferred_element_type=f32)

    def back(value, cosine, sine):
        value = (value * factor).astype(bf16).astype(f32)
        cosine, sine = spread_table(cosine, width), spread_table(sine, width)
        return (value * cosine - partner(value) * sine).astype(bf16)

    mixed_ref[rows, :width] = back(grad_q, cos_ref[rows], sin_ref[rows])
    pl.when((step > 0) & (step < steps - 1))(lambda: hop(step))

    @pl.when(step == steps - 1)
    def _():
        mixed_ref[:, width : 2 * width] = back(dk_acc[...], cos_ref[...], sin_ref[...])
        mixed_ref[:, 2 * width :] = dv_acc[...].astype(bf16)
        finish()


def attend_back(cid, q, k, v, o, g, p, cosine, sine, place, length, hidden, w_red, cuts=2):
    seq, width = q.shape
    heads = width // HEAD_DIM
    nb = lax.axis_size("blk")
    tile = seq // (nb // 2)
    wide, units = w_red.shape
    part = pl.BlockSpec((tile, width), lambda i: (i, 0))

    full = once(seq, width)
    return pl.pallas_call(
        functools.partial(attend_back_kernel, nb // 2, cuts, 1024),
        grid=(seq // tile,),
        in_specs=[
            full, full, full, part, part,
            pl.BlockSpec((heads, tile, seq), lambda i: (0, i, 0)),
            once(seq, 2 * HEAD_DIM), once(seq, 2 * HEAD_DIM),
            pl.BlockSpec((tile, 1), lambda i: (i, 0)),
            pl.BlockSpec(memory_space=pltpu.SMEM),
            once(seq, units),
            once(wide, units),
        ],
        out_specs=[once(seq, 3 * width), once(seq // nb, wide)],
        out_shape=[
            jax.ShapeDtypeStruct((seq, 3 * width), jnp.bfloat16),
            jax.ShapeDtypeStruct((seq // nb, wide), jnp.float32),
        ],
        scratch_shapes=[
            pltpu.VMEM((heads * tile, seq), jnp.bfloat16),
            pltpu.VMEM((heads * tile, width), jnp.bfloat16),
            pltpu.VMEM((heads * tile, width), jnp.bfloat16),
            pltpu.VMEM((seq, width), jnp.float32),
            pltpu.VMEM((seq, width), jnp.float32),
        ]
        + scatter_scratch(nb // 2, cuts, seq // nb, wide),
        compiler_params=params(cid),
        cost_estimate=cost(10 * seq * seq * width),
    )(q, k, v, o, g, p, cosine, sine, place[:, None], length.reshape(1), hidden, w_red)


def arrange(weight, out, parts):
    nb, _, wide = out.shape
    span = wide // parts
    for j in range(nb):
        for part in range(parts):
            at = (part * nb + j) * span
            out[j, :, part * span : (part + 1) * span] = weight[:, at : at + span].astype(out.dtype)


def first_swap_kernel(parts, *refs):
    n = len(parts)
    weights, dsts, later, held, sems = (
        refs[:n], refs[n : n + 2], refs[n + 2 : 2 * n], refs[2 * n : 2 * n + 2], refs[2 * n + 2 :],
    )
    starts, waits = swap_list(held, dsts, sems)
    greet(held[0].shape[0] // 2, True)
    for weight, out, part, start in zip(weights, held, parts, starts):
        arrange(weight, out, part)
        start()
    for weight, out, part in zip(weights[2:], later, parts[2:]):
        arrange(weight, out, part)
    for wait in waits:
        wait()


def first_swap(cid, weights, parts):
    nb = lax.axis_size("blk")
    shapes = [(nb, value.shape[0], value.shape[1] // nb) for value in weights]
    n = len(weights)
    return pl.pallas_call(
        functools.partial(first_swap_kernel, parts),
        out_shape=[jax.ShapeDtypeStruct(shape, jnp.bfloat16) for shape in shapes],
        in_specs=[VMEM] * n,
        out_specs=[ANY] * 2 + [VMEM] * (n - 2),
        scratch_shapes=[pltpu.VMEM(shape, jnp.bfloat16) for shape in shapes[:2]]
        + [pltpu.SemaphoreType.DMA, pltpu.SemaphoreType.DMA((nb,)), pltpu.SemaphoreType.DMA((nb,))] * 2,
        compiler_params=params(cid),
        cost_estimate=cost(0),
    )(*weights)


def over_rows(pieces):
    nb, rows, wide = pieces.shape
    return lax.all_gather(pieces.reshape(nb * rows, wide), "rows", axis=0, tiled=True)


def sum_rows(gradient):
    nb = lax.axis_size("blk")
    mine = lax.psum_scatter(
        gradient.astype(jnp.bfloat16), "rows", scatter_dimension=0, tiled=True
    )
    return mine.reshape(nb, mine.shape[0] // nb, mine.shape[1])


def total_task(nr, nb, x_ref, o_ref, held, rows_held, send_one, recv_one, send_two, recv_two):
    r, b = lax.axis_index("rows"), lax.axis_index("blk")
    across = [lax.rem(b + k, nb) for k in range(1, nb)]
    along = [lax.rem(r + k, nr) for k in range(1, nr)]

    def first(other, slot):
        return pltpu.make_async_remote_copy(
            src_ref=held.at[b], dst_ref=held.at[slot], send_sem=send_one.at[other],
            recv_sem=recv_one.at[slot], device_id=(r, other), device_id_type=MESH,
        )

    def second(other, slot):
        return pltpu.make_async_remote_copy(
            src_ref=rows_held.at[r], dst_ref=rows_held.at[slot], send_sem=send_two.at[other],
            recv_sem=recv_two.at[slot], device_id=(other, b), device_id_type=MESH,
        )

    def greet_all():
        barrier = pltpu.get_barrier_semaphore()
        for other in across:
            pl.semaphore_signal(barrier, inc=1, device_id=(r, other), device_id_type=MESH)
        for other in along:
            pl.semaphore_signal(barrier, inc=1, device_id=(other, b), device_id_type=MESH)
        pl.semaphore_wait(barrier, nb + nr - 2)

    def start():
        held[b] = x_ref[...]
        for other in across:
            first(other, b).start()

    def middle():
        for other in across:
            first(other, other).wait_recv()
        rows_held[r] = jnp.sum(held[...], axis=0)
        for other in along:
            second(other, r).start()

    def finish():
        for other in along:
            second(other, other).wait_recv()
        o_ref[...] = jnp.sum(rows_held[...], axis=0)
        for other in across:
            first(other, b).wait_send()
        for other in along:
            second(other, r).wait_send()

    return greet_all, start, middle, finish


def last_scatter_kernel(chips, nr, cuts, tile, n, a_ref, w_ref, x_ref, inverse_ref, gain_ref, resid_ref, gain_two_ref, *refs):
    srcs, refs = refs[:n], refs[n:]
    o_ref, total_ref, dsts, refs = refs[0], refs[1], refs[2 : 2 + n], refs[2 + n :]
    sum_ref, part_ref, refs = refs[0], refs[1], refs[2:]
    put, hop, finish = scatter_task(chips, cuts, tile, sum_ref, refs[:4], refs[4:10])
    greet_all, start_total, middle, finish_total = total_task(
        nr, 2 * chips, part_ref, total_ref, *refs[10:16]
    )
    starts, waits = swap_list(srcs, dsts, refs[16:])
    greet_all()
    for s in range(chips):
        put(s, lambda rows: a_ref.at[rows], w_ref)
        if s < chips - 1:
            hop(s)
        if s == 0:
            starts[0]()
    finish()
    inverse = inverse_ref[...]
    unit = x_ref[...].astype(jnp.float32) * inverse
    grad, gain = norm_backward(sum_ref[...], unit, inverse, gain_ref[...])
    part_ref[0:1] = gain[None]
    part_ref[1:2] = gain_two_ref[...]
    start_total()
    for start in starts[1:]:
        start()
    o_ref[...] = resid_ref[...] + grad
    middle()
    finish_total()
    for wait in waits:
        wait()


def last_scatter(cid, a, w, x, inverse, gain, resid, gain_two, swaps, cuts=2, tile=1024):
    nr, nb = lax.axis_size("rows"), lax.axis_size("blk")
    t, width = x.shape
    n = len(swaps)
    pair = (2, width)
    dma, f32 = pltpu.SemaphoreType.DMA, jnp.float32
    return pl.pallas_call(
        functools.partial(last_scatter_kernel, nb // 2, nr, cuts, tile, n),
        out_shape=[jax.ShapeDtypeStruct((t, width), f32), jax.ShapeDtypeStruct(pair, f32)]
        + [like(value) for value in swaps],
        in_specs=[VMEM] * 7 + [ANY] * n,
        out_specs=[VMEM] * 2 + [ANY] * n,
        scratch_shapes=[pltpu.VMEM((t, width), f32), pltpu.VMEM(pair, f32)]
        + scatter_scratch(nb // 2, cuts, t, width)
        + [pltpu.VMEM((nb,) + pair, f32), pltpu.VMEM((nr,) + pair, f32)]
        + [dma((nb,))] * 2 + [dma((nr,))] * 2
        + swap_sems(swaps),
        compiler_params=params(cid),
        cost_estimate=cost(2 * a.shape[0] * width * w.shape[1]),
    )(a, w, x, inverse, gain[None], resid, gain_two[None], *swaps)


def step_kernel(grad, *refs):
    outs = len(refs) // 2
    wide = grad.shape[2]
    for j in range(grad.shape[0]):
        cols = slice(j * wide, (j + 1) * wide)
        gradient = grad[j].astype(jnp.float32)
        rule = adam_step if outs == 3 else moment_step
        for ref, value in zip(refs[outs:], rule(*[ref[:, cols] for ref in refs[:outs]], gradient)):
            ref[:, cols] = value


def step(pieces, parts, states):
    nb = pieces.shape[0]
    rows, columns = states[0].shape
    span = columns // parts
    tile = max(16, min(rows, (1 << 17) // span))
    at = pl.BlockSpec((tile, span), lambda part, i: (i, part))
    outs = len(states)
    return pl.pallas_call(
        step_kernel,
        grid=(parts, rows // tile),
        in_specs=[pl.BlockSpec((nb, tile, span // nb), lambda part, i: (0, i, part))] + [at] * outs,
        out_specs=[at] * outs,
        out_shape=[jax.ShapeDtypeStruct((rows, columns), jnp.float32)] * outs,
        compiler_params=pltpu.CompilerParams(vmem_limit_bytes=60 * MIB),
        cost_estimate=pl.CostEstimate(
            flops=0, bytes_accessed=(8 * outs + 2) * rows * columns, transcendentals=0
        ),
    )(pieces, *states)


def after(value, *others):
    return lax.optimization_barrier((value,) + others)[0]


def over_tokens(left, right):
    return lax.dot_general(
        left, right, (((0,), (0,)), ((), ())), preferred_element_type=jnp.float32
    )


def shards(
    tokens, cotangent, lengths, block_map, gain_attend, gain_expand,
    attend_in, attend_out, expand_in, reduce_out,
    attend_in_first, attend_out_first, expand_in_first, reduce_out_first,
    attend_in_second, attend_out_second, expand_in_second, reduce_out_second,
):
    f32, bf16 = jnp.float32, jnp.bfloat16
    nb = lax.axis_size("blk")
    near = tokens.shape[1]
    seq = near * nb
    heads = HEADS // nb
    block_rows = near // 2
    length = lengths[0]
    offsets = jnp.arange(block_rows, dtype=jnp.int32)
    place = (block_map[0][:, None] * block_rows + offsets[None, :]).reshape(-1)
    live_place = jnp.where(place < length, place, jnp.int32(1 << 30))
    cosine, sine = pair_tables(place)

    x = tokens[0].astype(f32)
    unit_one, inverse_one, h1 = norm_forward(x, gain_attend)
    swap_in, swap_out, pieces_gu, pieces_red = first_swap(
        2, (attend_in, attend_out.T, expand_in, reduce_out.T), (3, 1, 2, 1)
    )
    w_in = over_rows(swap_in)
    w_out = over_rows(swap_out)
    h1_all, swap_gu = line_gather(3, after(h1, swap_in), swaps=[pieces_gu])
    w_gu = over_rows(swap_gu)

    attended, q, k, v, p, g_all, swap_red = attend(
        4, h1_all, w_in, cosine, sine, place, live_place, length, cotangent[0],
        swaps=[pieces_red],
    )
    w_red = over_rows(swap_red)
    x1 = x + dot_scatter(5, attended, w_out)[0]
    unit_two, inverse_two, h2 = norm_forward(x1, gain_expand)
    h2_all, hidden, slope_gate, slope_up = line_gather(6, h2, w_gu, ff=True)
    part_reduce = over_tokens(g_all, hidden).astype(bf16)
    grad_h2, part_expand = ff_back(
        8, after(g_all, part_reduce), slope_gate, slope_up, w_red, w_gu, h2_all
    )
    rows_reduce = sum_rows(part_reduce)
    rows_expand = sum_rows(part_expand)
    middle, gain_two = norm_backward(grad_h2, unit_two, inverse_two, gain_expand)
    grad_x1 = cotangent[0].astype(f32) + middle
    branch_all, grad_o = line_gather(9, grad_x1.astype(bf16), w_out)
    part_out = over_tokens(branch_all, attended).astype(bf16)
    rows_out = sum_rows(part_out)
    grad_mixed, y = attend_back(
        10, q, k, v, attended, after(grad_o, part_out), p, cosine, sine, place, length, hidden, w_red
    )
    y = x1 + y
    part_in = over_tokens(h1_all, grad_mixed).astype(bf16)
    grad_input, gains, own_expand, own_reduce = last_scatter(
        11, after(grad_mixed, part_in), w_in, tokens[0], inverse_one, gain_attend, grad_x1, gain_two,
        [rows_expand, rows_reduce],
    )
    rows_in = sum_rows(part_in)
    rows_in, rows_out = after((rows_in, rows_out), own_expand)
    both = lax.all_to_all(
        jnp.concatenate([rows_in, rows_out], axis=2), "blk", 0, 0, tiled=True
    )
    set_three = step(own_expand, 2, (expand_in, expand_in_first, expand_in_second))
    set_four = step(own_reduce, 1, (reduce_out.T, reduce_out_first.T, reduce_out_second.T))
    both = after(both, set_three[2], set_four[2])
    width_in = rows_in.shape[2]
    set_one = step(both[:, :, :width_in], 3, (attend_in, attend_in_first, attend_in_second))
    set_two = step(both[:, :, width_in:], 1, (attend_out_first.T, attend_out_second.T))
    return (
        y.astype(bf16).reshape(tokens.shape),
        grad_input.reshape(tokens.shape),
        gains[0],
        gains[1],
        *set_one,
        *[value.T for value in set_two],
        *set_three,
        *[value.T for value in set_four],
    )


def solution(mesh):
    placed = (
        P("rows", "blk", None),
        P("rows", "blk", None),
        P("rows"),
        P("rows", None),
        P(),
        P(),
        P(("rows", "blk"), None),
        P(None, ("rows", "blk")),
        P(("rows", "blk"), None),
        P(None, ("rows", "blk")),
        P(("rows", "blk"), None),
        P(None, ("rows", "blk")),
        P(("rows", "blk"), None),
        P(None, ("rows", "blk")),
        P(("rows", "blk"), None),
        P(None, ("rows", "blk")),
        P(("rows", "blk"), None),
        P(None, ("rows", "blk")),
    )
    return jax.shard_map(
        shards,
        mesh=mesh,
        in_specs=placed,
        out_specs=(
            P("rows", "blk", None),
            P("rows", "blk", None),
            P(),
            P(),
            P(("rows", "blk"), None),
            P(("rows", "blk"), None),
            P(("rows", "blk"), None),
            P(None, ("rows", "blk")),
            P(None, ("rows", "blk")),
            P(("rows", "blk"), None),
            P(("rows", "blk"), None),
            P(("rows", "blk"), None),
            P(None, ("rows", "blk")),
            P(None, ("rows", "blk")),
            P(None, ("rows", "blk")),
        ),
        check_vma=False,
    )
```

time: 755 us -> 629 us (0.83)
  Pallas kernels: 607 us -> 543 us
  matrix products: 52.8 us -> 22.1 us
  local copies, waits for them, and re-layouts: 30.2 us -> 6.6 us
  other arithmetic: 34.8 us -> 13.7 us
  starting transfers between devices: 0.97 us -> 11.7 us
    pallas_call x4 -> x1, Pallas kernels: 235 us -> 39.3 us  [dot_scatter(): pl.pallas_call(functools.partial(scatter_kernel, nb // 2, cuts, tile, n),...]
    pallas_call x16 -> x12, Pallas kernels: 372 us -> 504 us  [the longest x3 179 us: line_gather(): pl.pallas_call(functools.partial(gather_kernel, nb // 2, cuts, tile, len(...]
    dot_general x2 -> x0, matrix products: 19.9 us -> none  [the longest x1 12.9 us: shards(): grad_hidden = jnp.dot(g_all, w_red, preferred_element_type=f32)]
    all_to_all x0 -> x1, starting transfers between devices: none -> 11.2 us  [shards(): lax.all_to_all(jnp.concatenate([rows_in, rows_out], axis=2), 'blk', 0, 0,...]
    dot_general x4 -> x3, matrix products: 32.9 us -> 22.1 us  [over_tokens(): lax.dot_general(left, right, (((0,), (0,)), ((), ())), preferred_element_...]
    another operation x7 -> x0, other arithmetic: 9.42 us -> none
    unnamed x35 -> x21, local copies, waits for them, and re-layouts: 11.1 us -> 2.15 us
  transfers between devices with their start and end apart: 8 -> 9, of which waited for: 0 -> 1; matrix products, arithmetic and copies ran while one was open for 12% -> 6% of each run, Pallas kernels for 64% -> 81%
where the time goes in v3:
time: 629 us; the launch traced here: 619 us
  Pallas kernels  543 us (86%)
  matrix products  22.1 us (4%)
  between operations  15.5 us (2%)
  other arithmetic  13.7 us (2%)
  starting transfers between devices  11.7 us (2%)
  waiting for transfers between devices  6.64 us (1%)
  local copies, waits for them, and re-layouts  6.6 us (1%)
    pallas_call x3, Pallas kernels, line_gather(): pl.pallas_call(functools.partial(gather_kernel, nb // 2, cuts, tile, len(...  179 us
    pallas_call x1, Pallas kernels, last_scatter(): pl.pallas_call(functools.partial(last_scatter_kernel, nb // 2, nr, cuts,...  98.8 us
    pallas_call x1, Pallas kernels, attend(): pl.pallas_call(functools.partial(attend_kernel, nb // 2, cuts, n), grid=(...  66 us
    pallas_call x1, Pallas kernels, ff_back(): pl.pallas_call(functools.partial(ff_back_kernel, nb // 2, cuts, tile), ou...  54.4 us
    pallas_call x1, Pallas kernels, attend_back(): pl.pallas_call(functools.partial(attend_back_kernel, nb // 2, cuts, 1024)...  44.8 us
    pallas_call x1, Pallas kernels, dot_scatter(): pl.pallas_call(functools.partial(scatter_kernel, nb // 2, cuts, tile, n),...  39.3 us
    pallas_call x1, Pallas kernels, first_swap(): pl.pallas_call(functools.partial(first_swap_kernel, parts), out_shape=[ja...  32.8 us
    pallas_call x4, Pallas kernels, step(): pl.pallas_call(step_kernel, grid=(parts, rows // tile), in_specs=[pl.Bloc...  27.8 us
  transfers between devices with their start and end apart: 9, of which 1 were waited for; matrix products, arithmetic and copies ran while one was open for 6% of the time, Pallas kernels for 81%

profile of v3, /device:TPU:0, one launch (start us, length us, event | category | flops | bytes accessed | tf_op | source)
XLA Modules:
  0.0 619.4 jit_solution(9934473800251001795)
XLA Ops:
  7.2 0.0 all-gather.5.cloned.1.call-start
  7.2 32.8 %shard_map.289 = (bf16[8,64,768]{2,1,0:T(8,128)(2,1)}, bf16[8,64,256]{2,1,0:T(8,128)(2,1)}, bf16[8,64,2048]{2,1,0:T(8,128)(2,1)}, bf16[8,64,1024]{2,1,0:T(8,128)(2,1)}) custom-call(f32[64,6144]{1,0:T(8,128)} %refs_0_.5, f32[64,2048]{1,0:T(8,128)} %bitcast.56, f32[64,16384]{1,0:T(8,128)} %refs_0_.4, f32[64,8192]{1,0:T(8,128)} %bitcast.46), custom_call_target="tpu_custom_call" | custom-call | bytes 150000000 | tf_op jit(solution)/shard_map/pallas_call | solution.py:806
  40.0 0.0 all-gather.7.cloned.1.call-start
  40.1 0.7 all-gather.7.cloned.1.call-update
  40.8 0.0 all-gather.9.cloned.1.call-start
  40.9 0.2 fusion
  41.1 1.0 fusion.2.refs_0_
  42.1 82.7 %shard_map.290 = (bf16[1024,2048]{1,0:T(8,128)(2,1)}, bf16[8,64,2048]{2,1,0:T(8,128)(2,1)}) custom-call(bf16[128,2048]{1,0:T(8,128)(2,1)} %fusion.2.refs_0_, bf16[8,64,2048]{2,1,0:T(8,128)(2,1)} %get-tuple-element.62.refs_1_), custom_call_target="tpu_custom_call" | custom-call | bytes 150000000 | tf_op jit(solution)/shard_map/pallas_call | solution.py:255
  124.8 0.0 all-gather.11.cloned.1.call-start
  124.9 0.1 iota_add_fusion
  124.9 0.1 add.81
  125.0 1.3 add.86.q_place
  126.3 0.1 convert_element_type.40
  127.0 1.9 fusion.4
  128.9 1.8 pad_maximum_fusion.1
  130.8 0.6 compare_select_fusion.k_place
  131.4 66.0 %shard_map.291 = (bf16[1024,256]{1,0:T(8,128)(2,1)}, bf16[1024,256]{1,0:T(8,128)(2,1)}, bf16[1024,256]{1,0:T(8,128)(2,1)}, bf16[1024,256]{1,0:T(8,128)(2,1)}, bf...) custom-call(bf16[1024,2048]{1,0:T(8,128)(2,1)} %get-tuple-element.63.h1_ref, ...), custom_call_target="tpu_custom_call" | custom-call | flops 4294967296 | bytes 150000000 | tf_op jit(solution)/shard_map/pallas_call | solution.py:652
  197.4 0.0 reduce-scatter.7.cloned.1.call-start
  197.5 39.3 %shard_map.292 = f32[128,2048]{1,0:T(8,128)} custom-call(bf16[1024,256]{1,0:T(8,128)(2,1)} %get-tuple-element.65.refs_0_.o_ref, bf16[2048,256]{1,0:T(8,128)(2,1)} %all-gather.7.cloned.1.call-done.refs_1_), custom_call_target="tpu_custom_call" | custom-call | flops 1073741824 | bytes 150000000 | tf_op jit(solution)/shard_map/pallas_call | solution.py:497
  236.8 1.5 multiply_reduce_fusion.2
  238.3 1.0 multiply_convert_fusion.refs_0_
  239.3 49.4 %shard_map.293 = (bf16[1024,2048]{1,0:T(8,128)(2,1)}, bf16[1024,1024]{1,0:T(8,128)(2,1)}, bf16[1024,1024]{1,0:T(8,128)(2,1)}, bf16[1024,1024]{1,0:T(8,128)(2,1)}) custom-call(bf16[128,2048]{1,0:T(8,128)(2,1)} %multiply_convert_fusion.refs_0_, bf16[2048,2048]{1,0:T(8,128)(2,1)} %all-gather.9.cloned.1.call-done.refs_1_.w_ref), custom_call_target="tpu_custom_call" | custom-call | flops 8589934592 | bytes 150000000 | tf_op jit(solution)/shard_map/pallas_call | solution.py:255
  288.7 9.5 %convolution_convert_fusion = bf16[2048,1024]{1,0:T(8,128)(2,1)} fusion(bf16[1024,2048]{1,0:T(8,128)(2,1)} %get-tuple-element.73.g_ref, bf16[1024,1024]{1,0:T(8,128)(2,1)} %get-tuple-element.72.hidden_ref), kind=kOutput, calls=%fused_computation | convolution fusion | flops 4297064448 | bytes 10485760 | tf_op jit(solution)/shard_map/dot_general | solution.py:970
  298.2 0.0 reduce-scatter.5.cloned.1.call-start
  298.2 54.4 %shard_map.294 = (f32[128,2048]{1,0:T(8,128)}, bf16[2048,2048]{1,0:T(8,128)(2,1)}) custom-call(bf16[1024,2048]{1,0:T(8,128)(2,1)} %get-tuple-element.73.g_ref, bf16[1024,1024]{1,0:T(8,128)(2,1)} %get-tuple-element.74.one_ref, bf16[1024,1024]{1,0:T(8,128)(2,1)} %get-tuple-element.75.two_ref, bf16[2048,1024]{1,0:T(8,128)(2,1)} %all-gather.11.cloned.1.call-done.red_ref, ...), custom_call_target="tpu_custom_call" | custom-call | flops 21474836480 | bytes 150000000 | tf_op jit(solution)/shard_map/pallas_call | solution.py:478
  352.8 0.0 reduce-scatter.11.cloned.1.call-start
  352.8 1.1 copy-done.1
  353.9 0.9 multiply_reduce_fusion
  354.8 1.5 fusion.7
  356.3 47.1 %shard_map.295 = (bf16[1024,2048]{1,0:T(8,128)(2,1)}, bf16[1024,256]{1,0:T(8,128)(2,1)}) custom-call(bf16[128,2048]{1,0:T(8,128)(2,1)} %get-tuple-element.107.refs_0_, bf16[2048,256]{1,0:T(8,128)(2,1)} %all-gather.7.cloned.1.call-done.refs_1_), custom_call_target="tpu_custom_call" | custom-call | flops 1073741824 | bytes 150000000 | tf_op jit(solution)/shard_map/pallas_call | solution.py:255
  403.4 4.6 convolution_convert_fusion.2
  408.1 0.3 reduce-scatter.9.cloned.1.call-start
  408.3 44.8 %shard_map.296 = (bf16[1024,768]{1,0:T(8,128)(2,1)}, f32[128,2048]{1,0:T(8,128)}) custom-call(bf16[1024,256]{1,0:T(8,128)(2,1)} %get-tuple-element.67.q_ref, bf16[1024,256]{1,0:T(8,128)(2,1)} %get-tuple-element.68.k_ref, bf16[1024,256]{1,0:T(8,128)(2,1)} %get-tuple-element.69.v_ref, bf16[1024,256]{1,0:T(8,128)(2,1)} %get-tuple-element.65.refs_0_.o_ref, ...), custom_call_target="tpu_custom_call" | custom-call | flops 2684354560 | bytes 150000000 | tf_op jit(solution)/shard_map/pallas_call | solution.py:747
  453.1 8.0 %convolution_convert_fusion.1 = bf16[2048,768]{1,0:T(8,128)(2,1)} fusion(bf16[1024,2048]{1,0:T(8,128)(2,1)} %get-tuple-element.63.h1_ref, bf16[1024,768]{1,0:T(8,128)(2,1)} %get-tuple-element.85.a_ref), kind=kOutput, calls=%fused_computation.1 | convolution fusion | flops 3222798336 | bytes 8912896 | tf_op jit(solution)/shard_map/dot_general | solution.py:970
  461.2 0.7 copy.40.inverse_ref
  461.9 98.8 %shard_map.297 = (f32[128,2048]{1,0:T(8,128)}, f32[2,2048]{1,0:T(2,128)}, bf16[8,64,2048]{2,1,0:T(8,128)(2,1)}, bf16[8,64,1024]{2,1,0:T(8,128)(2,1)}) custom-call(bf16[1024,768]{1,0:T(8,128)(2,1)} %get-tuple-element.85.a_ref, bf16[2048,768]{1,0:T(8,128)(2,1)} %all-gather.5.cloned.1.call-done.w_ref, bf16[128,2048]{1,0:T(8,128)(2,1)} %bitcast.48, ...), custom_call_target="tpu_custom_call" | custom-call | flops 3221225472 | bytes 150000000 | tf_op jit(solution)/shard_map/pallas_call | solution.py:918
  560.8 2.4 pad_maximum_fusion
  563.2 11.2 %all-to-all-start = ((bf16[8,64,1024]{2,1,0:T(8,128)(2,1)}), bf16[8,64,1024]{2,1,0:T(8,128)(2,1)S(1)}, u32[]{:S(2)}, u32[]{:S(2)}) async-start(bf16[8,64,1024]{2,1,0:T(8,128)(2,1)} %pad_maximum_fusion), calls=%async_computation.4 | async-start | bytes 2097152 | tf_op jit(solution)/shard_map/all_to_all | solution.py:1033
  574.4 0.9 fusion.3
  575.3 12.7 %shard_map.298 = (f32[64,16384]{1,0:T(8,128)}, f32[64,16384]{1,0:T(8,128)}, f32[64,16384]{1,0:T(8,128)}) custom-call(bf16[8,64,2048]{2,1,0:T(8,128)(2,1)} %get-tuple-element.89.grad, f32[64,16384]{1,0:T(8,128)} %refs_0_.4, f32[64,16384]{1,0:T(8,128)} %refs_1_.2, f32[64,16384]{1,0:T(8,128)} %refs_2_.4), custom_call_target="tpu_custom_call" | custom-call | bytes 27262976 | tf_op jit(solution)/shard_map/pallas_call | solution.py:952
  587.9 6.7 %shard_map.299 = (f32[64,8192]{1,0:T(8,128)}, f32[64,8192]{1,0:T(8,128)}, f32[64,8192]{1,0:T(8,128)}) custom-call(bf16[8,64,1024]{2,1,0:T(8,128)(2,1)} %get-tuple-element.93.grad, f32[64,8192]{1,0:T(8,128)} %bitcast.47, f32[64,8192]{1,0:T(8,128)} %bitcast.49, f32[64,8192]{1,0:T(8,128)} %bitcast.50), custom_call_target="tpu_custom_call" | custom-call | bytes 13631488 | tf_op jit(solution)/shard_map/pallas_call | solution.py:952
  594.6 0.6 fusion.8
  595.2 5.7 all-to-all-done
  601.0 1.0 slice.14.grad
  601.9 0.7 slice.15.grad
  602.7 6.1 shard_map.300
  608.8 2.4 shard_map.301
  611.1 1.0 copy.43
  (39 shorter events, 0.3 us)
Async XLA Ops:
  7.2 124.2 %all-gather.5.cloned.1.call-start = ((), (), s32[]{:S(2)}) async-start(), calls=%async_computation.5 | async-start | bytes 3932160 | tf_op jit(solution)/shard_map/all_gather | solution.py:820
  7.2 33.6 %copy-start = (bf16[1,128,2048]{2,1,0:T(8,128)(2,1)S(1)}, bf16[1,128,2048]{2,1,0:T(8,128)(2,1)}, u32[]{:S(2)}) copy-start(bf16[1,128,2048]{2,1,0:T(8,128)(2,1)} %param.18) | copy-start | bytes 1572868
  7.2 33.8 %copy-start.8 = (f32[2048]{0:T(1024)S(1)}, f32[2048]{0:T(1024)}, u32[]{:S(2)}) copy-start(f32[2048]{0:T(1024)} %param.22) | copy-start | bytes 24580
  40.0 157.4 %all-gather.7.cloned.1.call-start = ((), (), s32[]{:S(2)}) async-start(), calls=%async_computation.6 | async-start | bytes 1310720 | tf_op jit(solution)/shard_map/all_gather | solution.py:820
  40.8 84.1 %copy-start.9 = (s32[1,16]{1,0:T(1,128)S(1)}, s32[1,16]{1,0:T(1,128)}, u32[]{:S(2)}) copy-start(s32[1,16]{1,0:T(1,128)} %param.21) | copy-start | bytes 196
  40.8 198.5 %all-gather.9.cloned.1.call-start = ((), (), s32[]{:S(2)}) async-start(), calls=%async_computation.7 | async-start | bytes 10485760 | tf_op jit(solution)/shard_map/all_gather | solution.py:820
  124.8 173.4 %all-gather.11.cloned.1.call-start = ((), (), s32[]{:S(2)}) async-start(), calls=%async_computation.8 | async-start | bytes 5242880 | tf_op jit(solution)/shard_map/all_gather | solution.py:820
  197.4 264.5 %reduce-scatter.7.cloned.1.call-start = ((), (), s32[]{:S(2)}) async-start(), calls=%async_computation.10 | async-start | bytes 5242880 | tf_op jit(solution)/shard_map/reduce_scatter | solution.py:825
  197.5 40.8 %copy-start.6 = (f32[2048]{0:T(1024)S(1)}, f32[2048]{0:T(1024)}, u32[]{:S(2)}) copy-start(f32[2048]{0:T(1024)} %param.23) | copy-start | bytes 24580
  298.2 163.7 %reduce-scatter.5.cloned.1.call-start = ((), (), s32[]{:S(2)}) async-start(), calls=%async_computation.9 | async-start | bytes 10485760 | tf_op jit(solution)/shard_map/reduce_scatter | solution.py:825
  352.7 1.2 copy-start.1
  352.7 2.1 copy-start.4
  352.8 208.0 %reduce-scatter.11.cloned.1.call-start = ((), (), s32[]{:S(2)}) async-start(), calls=%async_computation.12 | async-start | bytes 1310720 | tf_op jit(solution)/shard_map/reduce_scatter | solution.py:825
  354.8 48.6 %copy-start.5 = (bf16[1024,256]{1,0:T(8,128)(2,1)S(1)}, bf16[1024,256]{1,0:T(8,128)(2,1)}, u32[]{:S(2)}) copy-start(bf16[1024,256]{1,0:T(8,128)(2,1)} %get-tuple-element.65.refs_0_.o_ref) | copy-start | bytes 1572868
  408.1 152.7 %reduce-scatter.9.cloned.1.call-start = ((), (), s32[]{:S(2)}) async-start(), calls=%async_computation.11 | async-start | bytes 3932160 | tf_op jit(solution)/shard_map/reduce_scatter | solution.py:825
  560.7 13.7 %copy-start.2 = (f32[128,2048]{1,0:T(8,128)S(1)}, f32[128,2048]{1,0:T(8,128)}, u32[]{:S(2)}) copy-start(f32[128,2048]{1,0:T(8,128)} %get-tuple-element.83) | copy-start | bytes 3145732
  563.2 37.8 %all-to-all-start = ((bf16[8,64,1024]{2,1,0:T(8,128)(2,1)}), bf16[8,64,1024]{2,1,0:T(8,128)(2,1)S(1)}, u32[]{:S(2)}, u32[]{:S(2)}) async-start(bf16[8,64,1024]{2,1,0:T(8,128)(2,1)} %pad_maximum_fusion), calls=%async_computation.4 | async-start | bytes 2097152 | tf_op jit(solution)/shard_map/all_to_all | solution.py:1033
  587.9 6.7 %copy-start.7 = (f32[2,2048]{1,0:T(2,128)S(1)}, f32[2,2048]{1,0:T(2,128)}, u32[]{:S(2)}) copy-start(f32[2,2048]{1,0:T(2,128)} %get-tuple-element.88) | copy-start | bytes 49156
  602.7 8.5 %copy-start.3 = (f32[128,2048]{1,0:T(8,128)S(1)}, f32[128,2048]{1,0:T(8,128)}, u32[]{:S(2)}) copy-start(f32[128,2048]{1,0:T(8,128)} %get-tuple-element.87) | copy-start | bytes 3145732
Sparse Core Ops, SparseCore 0:
  40.2 45.7 all-gather.4
  87.8 26.6 all-gather.6
  124.9 87.5 all-gather.8
  214.3 52.6 all-gather.10
  298.3 53.7 reduce-scatter.6
  355.3 88.7 reduce-scatter.4
  447.6 27.7 reduce-scatter.10
  479.2 43.9 reduce-scatter.8

commit v4 on v3

--- a/solution.py
+++ b/solution.py
@@ -102,6 +102,20 @@
 
 def cost(flops):
     return pl.CostEstimate(flops=flops, bytes_accessed=150_000_000, transcendentals=0)
+
+
+def mover(pairs, sem):
+    copies = [pltpu.make_async_copy(a, b, sem.at[i]) for i, (a, b) in enumerate(pairs)]
+
+    def start(*which):
+        for i in which or range(len(copies)):
+            copies[i].start()
+
+    def wait(*which):
+        for i in which or range(len(copies)):
+            copies[i].wait()
+
+    return start, wait
 
 
 def gather_task(chips, cuts, x_ref, o_ref, sems):
@@ -174,24 +188,63 @@
     return [pltpu.SemaphoreType.DMA] + [pltpu.SemaphoreType.DMA((nb, cuts))] * 4
 
 
-def gather_kernel(chips, cuts, tile, n, ff, n_prod, *refs):
-    refs = list(refs)
-    x_ref = refs.pop(0)
-    w_ref = refs.pop(0) if n_prod else None
-    srcs = [refs.pop(0) for _ in range(n)]
-    o_ref = refs.pop(0)
-    prods = [refs.pop(0) for _ in range(n_prod)]
-    dsts = [refs.pop(0) for _ in range(n)]
+def gather_kernel(chips, cuts, n, x_ref, *refs):
+    srcs, o_ref, dsts, refs = refs[:n], refs[n], refs[n + 1 : 2 * n + 1], refs[2 * n + 1 :]
     begin, hop, from_side, local, finish = gather_task(chips, cuts, x_ref, o_ref, refs[:5])
     starts, waits = swap_list(srcs, dsts, refs[5:])
+    greet(chips, n > 0)
+    begin()
+    for k in range(1, chips):
+        if k == min(3, chips - 1):
+            for start in starts:
+                start()
+        hop(k)
+    local().wait()
+    for y in range(chips):
+        from_side(y)
+    finish()
+    for wait in waits:
+        wait()
+
+
+def line_gather(cid, x, swaps=(), cuts=4):
+    nb, n = lax.axis_size("blk"), len(swaps)
+    return pl.pallas_call(
+        functools.partial(gather_kernel, nb // 2, cuts, n),
+        out_shape=[jax.ShapeDtypeStruct((nb * x.shape[0], x.shape[1]), x.dtype)]
+        + [like(value) for value in swaps],
+        in_specs=[ANY] * (1 + n),
+        out_specs=[ANY] * (1 + n),
+        scratch_shapes=gather_sems(nb, cuts) + swap_sems(swaps),
+        compiler_params=params(cid),
+        cost_estimate=cost(0),
+    )(x, *swaps)
+
+
+def gather_dot_kernel(chips, cuts, tile, ff, n_prod, x_ref, w_hbm, *refs):
+    refs = list(refs)
+    g_hbm = refs.pop(0) if ff else None
+    outs = [refs.pop(0) for _ in range(1 + n_prod)]
+    dw_out = refs.pop(0) if ff else None
+    held = [refs.pop(0) for _ in range(1 + n_prod)]
+    w_ref, load_sem, save_sem = [refs.pop(0) for _ in range(3)]
+    if ff:
+        g_ref, acc_ref, dw_ref, dw_sem = [refs.pop(0) for _ in range(4)]
+    o_ref, prods = held[0], held[1:]
+    begin, hop, from_side, local, finish = gather_task(chips, cuts, x_ref, o_ref, refs)
+    load, loaded = mover([(w_hbm, w_ref)] + ([(g_hbm, g_ref)] if ff else []), load_sem)
     r, z, c = line_place()
     t = x_ref.shape[0]
     f32 = jnp.float32
-    greet(chips, n > 0)
+    load()
+    greet(chips, False)
+    begin()
+
+    def saves(y):
+        rows = pl.ds(pl.multiple_of(y * 2 * t, 2 * t), 2 * t)
+        return mover([(a.at[rows], b.at[rows]) for a, b in zip(held, outs)], save_sem.at[y])
 
     def dot(y):
-        if not n_prod:
-            return
         rows = pl.ds(pl.multiple_of(y * 2 * t, 2 * t), 2 * t)
         units = prods[0].shape[1]
 
@@ -214,13 +267,41 @@
             return 0
 
         lax.fori_loop(0, units // tile, one, 0)
-
-    begin()
-    for start in starts:
-        start()
+        saves(y)[0]()
+
+    deep = 256
+
+    def more(y, first=False, last=False):
+        if not ff:
+            return
+        rows = pl.ds(pl.multiple_of(y * 2 * t, 2 * t), 2 * t)
+
+        def one(i, _):
+            at = pl.ds(pl.multiple_of(i * deep, deep), deep)
+            got = lax.dot_general(
+                g_ref[rows, at], prods[0][rows, :], (((0,), (0,)), ((), ())),
+                preferred_element_type=f32,
+            )
+            if not first:
+                got = got + acc_ref[at]
+            if last:
+                dw_ref[at] = got.astype(dw_ref.dtype)
+                save_dw(i).start()
+            else:
+                acc_ref[at] = got
+            return 0
+
+        lax.fori_loop(0, g_ref.shape[1] // deep, one, 0)
+
+    def save_dw(i):
+        at = pl.ds(pl.multiple_of(i * deep, deep), deep)
+        return pltpu.make_async_copy(dw_ref.at[at], dw_out.at[at], dw_sem.at[i])
+
     from_side(z)
     local().wait()
+    loaded()
     dot(z)
+    more(z, first=True)
     for k in range(1, chips):
         hop(k)
 
@@ -234,33 +315,54 @@
             from_side(z + k)
             dot(z + k)
 
+        if k < chips - 1:
+            more(pick(arrival_order(chips), z, k))
+    more(pick(arrival_order(chips), z, chips - 1), last=True)
     finish()
-    for wait in waits:
-        wait()
-
-
-def line_gather(cid, x, w=None, swaps=(), ff=False, cuts=2, tile=512):
+    for y in range(chips):
+        saves(y)[1]()
+    if ff:
+        for i in range(g_ref.shape[1] // deep):
+            save_dw(i).wait()
+
+
+def arrival_order(chips):
+    table = []
+    for z in range(chips):
+        row = [z]
+        for k in range(1, chips):
+            row += [y for y in (z - k, z + k) if 0 <= y < chips]
+        table.append(row)
+    return table
+
+
+def gather_dot(cid, x, w, g_all=None, cuts=2, tile=512):
     nb = lax.axis_size("blk")
+    ff = g_all is not None
     all_rows = nb * x.shape[0]
-    with_dot = w is not None
-    place = VMEM if with_dot else ANY
-    outs = [jax.ShapeDtypeStruct((all_rows, x.shape[1]), x.dtype)]
-    flops, n_prod = 0, 0
-    if with_dot:
-        n_prod = 3 if ff else 1
-        units = w.shape[1] // 2 if ff else w.shape[1]
-        outs += [jax.ShapeDtypeStruct((all_rows, units), jnp.bfloat16)] * n_prod
-        flops = 2 * all_rows * w.shape[0] * w.shape[1]
-        tile = min(tile, units)
+    n_prod = 3 if ff else 1
+    units = w.shape[1] // 2 if ff else w.shape[1]
+    tile = min(tile, units)
+    dma, bf16 = pltpu.SemaphoreType.DMA, jnp.bfloat16
+    shapes = [(all_rows, x.shape[1])] + [(all_rows, units)] * n_prod
+    weight = (x.shape[1], units)
+    scratch = [pltpu.VMEM(shape, bf16) for shape in shapes]
+    scratch += [pltpu.VMEM(w.shape, w.dtype), dma((2,)), dma((nb // 2, len(shapes)))]
+    if ff:
+        scratch += [
+            pltpu.VMEM(g_all.shape, g_all.dtype), pltpu.VMEM(weight, jnp.float32),
+            pltpu.VMEM(weight, bf16), dma((x.shape[1] // 256,)),
+        ]
+    outs = shapes + ([weight] if ff else [])
     return pl.pallas_call(
-        functools.partial(gather_kernel, nb // 2, cuts, tile, len(swaps), ff, n_prod),
-        out_shape=outs + [like(value) for value in swaps],
-        in_specs=[place] * (1 + with_dot) + [ANY] * len(swaps),
-        out_specs=[place] * (1 + n_prod) + [ANY] * len(swaps),
-        scratch_shapes=gather_sems(nb, cuts) + swap_sems(swaps),
+        functools.partial(gather_dot_kernel, nb // 2, cuts, tile, ff, n_prod),
+        out_shape=[jax.ShapeDtypeStruct(shape, bf16) for shape in outs],
+        in_specs=[VMEM, ANY] + [ANY] * ff,
+        out_specs=[ANY] * len(outs),
+        scratch_shapes=scratch + gather_sems(nb, cuts),
         compiler_params=params(cid),
-        cost_estimate=cost(flops),
-    )(*([x, w] if with_dot else [x]), *swaps)
+        cost_estimate=cost(2 * all_rows * w.shape[0] * w.shape[1]),
+    )(x, w, *([g_all] if ff else []))
 
 
 def need_order(chips):
@@ -324,15 +426,19 @@
         to_side(y, q).wait_recv()
         return mine[y, rows(q)].astype(f32) + side_buf[y, rows(q)].astype(f32)
 
-    def put(s, rows_of, w_ref):
+    def put(s, rows_of, w_ref, seen=None):
         y = pick(table, z, s)
-        a = rows_of(pl.ds(pl.multiple_of(2 * y * t, 2 * t), 2 * t))
+        block = pl.ds(pl.multiple_of(2 * y * t, 2 * t), 2 * t)
+        a = rows_of(block)
 
         def one(i, _):
             cols = pl.ds(pl.multiple_of(i * tile, tile), tile)
             got = lax.dot_general(
                 a[...], w_ref[cols], (((1,), (1,)), ((), ())), preferred_element_type=f32
-            ).astype(low)
+            )
+            if seen is not None:
+                seen(block, cols, got)
+            got = got.astype(low)
 
             @pl.when(c == 0)
             def _():
@@ -433,14 +539,18 @@
         wait()
 
 
-def ff_back_kernel(
-    chips, cuts, tile, g_ref, one_ref, two_ref, red_ref, w_ref, h2_ref, o_ref, dw_ref, grad_ref, *refs
-):
-    put, hop, finish = scatter_task(chips, cuts, tile, o_ref, refs[:4], refs[4:10])
+def ff_back_kernel(chips, cuts, tile, *refs):
+    sources, (o_ref, dw_out), held, refs = refs[:6], refs[6:8], refs[8:14], refs[14:]
+    grad_ref, dw_ref, load_sem, save_sem = refs[:4]
+    g_ref, one_ref, two_ref, red_ref, w_ref, h2_ref = held
+    put, hop, finish = scatter_task(chips, cuts, tile, o_ref, refs[4:8], refs[8:14])
+    load, loaded = mover(list(zip(sources, held)), load_sem)
     f32 = jnp.float32
     units = red_ref.shape[1]
     span = min(512, units)
+    load(3, 0, 1, 2, 4, 5)
     greet(chips, False)
+    loaded(0, 1, 2, 3)
 
     def rows_of(rows):
         def one(i, _):
@@ -455,39 +565,56 @@
         return grad_ref.at[rows]
 
     for s in range(chips):
-        put(s, rows_of, w_ref)
+        if s == 0:
+            put(s, lambda rows: (rows_of(rows), loaded(4))[0], w_ref)
+        else:
+            put(s, rows_of, w_ref)
         if s < chips - 1:
             hop(s)
+    loaded(5)
+    deep = 256
+    turns = dw_ref.shape[0] // deep
+
+    def save(i):
+        cols = pl.ds(pl.multiple_of(i * deep, deep), deep)
+        return pltpu.make_async_copy(dw_ref.at[cols], dw_out.at[cols], save_sem.at[i])
 
     def one(i, _):
-        cols = pl.ds(pl.multiple_of(i * 256, 256), 256)
+        cols = pl.ds(pl.multiple_of(i * deep, deep), deep)
         dw_ref[cols] = lax.dot_general(
             h2_ref[:, cols], grad_ref[...], (((0,), (0,)), ((), ())), preferred_element_type=f32
         ).astype(dw_ref.dtype)
+        save(i).start()
         return 0
 
-    lax.fori_loop(0, dw_ref.shape[0] // 256, one, 0)
+    lax.fori_loop(0, turns, one, 0)
     finish()
-
-
-def ff_back(cid, g_all, slope_gate, slope_up, w_red, w_gu, h2_all, cuts=2, tile=1024):
+    for i in range(turns):
+        save(i).wait()
+
+
+def ff_back(cid, *operands, cuts=2, tile=1024):
     nb = lax.axis_size("blk")
+    g_all, w_gu = operands[0], operands[4]
     seq, width = g_all.shape
     both = w_gu.shape[1]
     t = seq // nb
+    dma = pltpu.SemaphoreType.DMA
     return pl.pallas_call(
         functools.partial(ff_back_kernel, nb // 2, cuts, tile),
         out_shape=[
             jax.ShapeDtypeStruct((t, width), jnp.float32),
             jax.ShapeDtypeStruct((width, both), jnp.bfloat16),
         ],
-        in_specs=[VMEM] * 6,
-        out_specs=[VMEM] * 2,
-        scratch_shapes=[pltpu.VMEM((seq, both), jnp.bfloat16)]
+        in_specs=[ANY] * 6,
+        out_specs=[VMEM, ANY],
+        scratch_shapes=[pltpu.VMEM(value.shape, value.dtype) for value in operands]
+        + [pltpu.VMEM((seq, both), jnp.bfloat16), pltpu.VMEM((width, both), jnp.bfloat16)]
+        + [dma((6,)), dma((width // 256,))]
         + scatter_scratch(nb // 2, cuts, t, width),
         compiler_params=params(cid),
         cost_estimate=cost(5 * seq * width * both),
-    )(g_all, slope_gate, slope_up, w_red, w_gu, h2_all)
+    )(*operands)
 
 
 def dot_scatter(cid, a, w, swaps=(), cuts=2, tile=1024):
@@ -576,10 +703,11 @@
     return lax.broadcasted_iota(jnp.int32, shape, 1) // HEAD_DIM
 
 
-def attend_kernel(chips, cuts, n, h1_ref, w_ref, cos_ref, sin_ref, q_place, k_place, length_ref, g_ref, *refs):
+def attend_kernel(chips, cuts, n, h1_hbm, w_hbm, cos_ref, sin_ref, q_place, k_place, length_ref, g_ref, *refs):
     srcs, refs = refs[:n], refs[n:]
     o_ref, q_ref, k_ref, v_ref, p_ref, g_all = refs[:6]
-    dsts, sems = refs[6 : 6 + n], refs[6 + n :]
+    dsts, (h1_ref, w_ref, load_sem), sems = refs[6 : 6 + n], refs[6 + n : 9 + n], refs[9 + n :]
+    load, loaded = mover([(w_hbm, w_ref), (h1_hbm, h1_ref)], load_sem)
     begin, hop, from_side, local, finish = gather_task(chips, cuts, g_ref, g_all, sems[:5])
     starts, waits = swap_list(srcs, dsts, sems[5:])
     step, steps = pl.program_id(0), pl.num_programs(0)
@@ -588,10 +716,12 @@
 
     @pl.when(step == 0)
     def _():
+        load()
         greet(chips, True)
+        begin()
         for start in starts:
             start()
-        begin()
+        loaded()
 
         def one(i, _):
             rows = pl.ds(pl.multiple_of(i * tile, tile), tile)
@@ -653,7 +783,7 @@
         functools.partial(attend_kernel, nb // 2, cuts, n),
         grid=(seq // tile,),
         in_specs=[
-            once(seq, wide), once(wide, 3 * width), once(seq, 2 * HEAD_DIM), once(seq, 2 * HEAD_DIM),
+            ANY, ANY, once(seq, 2 * HEAD_DIM), once(seq, 2 * HEAD_DIM),
             pl.BlockSpec((tile, 1), lambda i: (i, 0)),
             once(1, seq),
             pl.BlockSpec(memory_space=pltpu.SMEM),
@@ -668,36 +798,57 @@
             jax.ShapeDtypeStruct((seq, g.shape[1]), g.dtype),
         ]
         + [like(value) for value in swaps],
-        scratch_shapes=gather_sems(nb, cuts) + swap_sems(swaps),
+        scratch_shapes=[
+            pltpu.VMEM(h1_all.shape, h1_all.dtype),
+            pltpu.VMEM(w_in.shape, w_in.dtype),
+            pltpu.SemaphoreType.DMA((2,)),
+        ]
+        + gather_sems(nb, cuts)
+        + swap_sems(swaps),
         compiler_params=params(cid),
         cost_estimate=cost(4 * seq * seq * width + 6 * seq * wide * width),
     )(h1_all, w_in, cosine, sine, place[:, None], live_place[None, :], length.reshape(1), g, *swaps)
 
 
 def attend_back_kernel(
-    chips, cuts, tile_y, q_ref, k_ref, v_ref, o_ref, g_ref, p_ref, cos_ref, sin_ref, q_place, length_ref,
-    hidden_ref, red_ref, mixed_ref, y_ref, ds_ref, qm_ref, gm_ref, dk_acc, dv_acc, *refs
+    chips, cuts, tile_y, n, q_ref, k_ref, v_ref, o_all, g_ref, p_ref, cos_ref, sin_ref, q_place, length_ref,
+    hidden_hbm, red_hbm, branch_hbm, h1_hbm, *refs
 ):
+    srcs, (mixed_ref, y_ref, dw_out, dw_in), dsts = refs[:n], refs[n : n + 4], refs[n + 4 : 2 * n + 4]
+    refs = refs[2 * n + 4 :]
+    (ds_ref, qm_ref, gm_ref, dk_acc, dv_acc, hidden_ref, red_ref, branch_ref, h1_ref, load_sem), refs = (
+        refs[:10], refs[10:],
+    )
     put, hop, finish = scatter_task(chips, cuts, tile_y, y_ref, refs[:4], refs[4:10])
+    starts, waits = swap_list(srcs, dsts, refs[10:])
+    load, loaded = mover(
+        [(red_hbm, red_ref), (hidden_hbm, hidden_ref), (branch_hbm, branch_ref), (h1_hbm, h1_ref)], load_sem
+    )
     step, steps = pl.program_id(0), pl.num_programs(0)
-    tile, width = o_ref.shape
+    tile, width = g_ref.shape
     f32, bf16 = jnp.float32, jnp.bfloat16
     factor = 1.0 / math.sqrt(HEAD_DIM)
 
     @pl.when(step == 0)
     def _():
-        greet(chips, False)
+        load()
+        greet(chips, n > 0)
+        for start in starts:
+            start()
         dk_acc[...] = jnp.zeros_like(dk_acc)
         dv_acc[...] = jnp.zeros_like(dv_acc)
 
+        loaded(0, 1)
+
     put(step, lambda rows: hidden_ref.at[rows], red_ref)
+
     pl.when(step == 0)(lambda: hop(step))
     over_rows = (((0,), (0,)), ((), ()))
     rows = pl.ds(pl.multiple_of(step * tile, tile), tile)
     lanes = head_lanes((tile, width))
     nothing = jnp.zeros((), bf16)
     grad = jnp.where(q_place[...] < length_ref[0], g_ref[...], nothing)
-    both = grad.astype(f32) * o_ref[...].astype(f32)
+    both = grad.astype(f32) * o_all[rows].astype(f32)
     queries = q_ref[rows]
     grad_q = jnp.zeros((tile, width), f32)
     for head in range(width // HEAD_DIM):
@@ -726,52 +877,83 @@
         return (value * cosine - partner(value) * sine).astype(bf16)
 
     mixed_ref[rows, :width] = back(grad_q, cos_ref[rows], sin_ref[rows])
+    pl.when(step == 0)(lambda: loaded(2))
+    share = dw_out.shape[0] // chips
+    cols = pl.ds(pl.multiple_of(step * share, share), share)
+    dw_out[cols] = lax.dot_general(
+        branch_ref[:, cols], o_all[...], over_rows, preferred_element_type=f32
+    ).astype(bf16)
     pl.when((step > 0) & (step < steps - 1))(lambda: hop(step))
 
     @pl.when(step == steps - 1)
     def _():
         mixed_ref[:, width : 2 * width] = back(dk_acc[...], cos_ref[...], sin_ref[...])
         mixed_ref[:, 2 * width :] = dv_acc[...].astype(bf16)
+        loaded(3)
+        deep = 256
+
+        def one(i, _):
+            at = pl.ds(pl.multiple_of(i * deep, deep), deep)
+            dw_in[at] = lax.dot_general(
+                h1_ref[:, at], mixed_ref[...], over_rows, preferred_element_type=f32
+            ).astype(bf16)
+            return 0
+
+        lax.fori_loop(0, dw_in.shape[0] // deep, one, 0)
         finish()
-
-
-def attend_back(cid, q, k, v, o, g, p, cosine, sine, place, length, hidden, w_red, cuts=2):
+        for wait in waits:
+            wait()
+
+
+def attend_back(
+    cid, q, k, v, o, g, p, cosine, sine, place, length, hidden, w_red, branch_all, h1_all, swaps, cuts=2
+):
     seq, width = q.shape
     heads = width // HEAD_DIM
     nb = lax.axis_size("blk")
     tile = seq // (nb // 2)
     wide, units = w_red.shape
-    part = pl.BlockSpec((tile, width), lambda i: (i, 0))
-
+    n = len(swaps)
     full = once(seq, width)
+    f32, bf16 = jnp.float32, jnp.bfloat16
+    loads = (hidden, w_red, branch_all, h1_all)
     return pl.pallas_call(
-        functools.partial(attend_back_kernel, nb // 2, cuts, 1024),
+        functools.partial(attend_back_kernel, nb // 2, cuts, 1024, n),
         grid=(seq // tile,),
         in_specs=[
-            full, full, full, part, part,
+            full, full, full, full,
+            pl.BlockSpec((tile, width), lambda i: (i, 0)),
             pl.BlockSpec((heads, tile, seq), lambda i: (0, i, 0)),
             once(seq, 2 * HEAD_DIM), once(seq, 2 * HEAD_DIM),
             pl.BlockSpec((tile, 1), lambda i: (i, 0)),
             pl.BlockSpec(memory_space=pltpu.SMEM),
-            once(seq, units),
-            once(wide, units),
-        ],
-        out_specs=[once(seq, 3 * width), once(seq // nb, wide)],
+        ]
+        + [ANY] * (4 + n),
+        out_specs=[
+            once(seq, 3 * width), once(seq // nb, wide), once(wide, width), once(wide, 3 * width)
+        ]
+        + [ANY] * n,
         out_shape=[
-            jax.ShapeDtypeStruct((seq, 3 * width), jnp.bfloat16),
-            jax.ShapeDtypeStruct((seq // nb, wide), jnp.float32),
-        ],
+            jax.ShapeDtypeStruct((seq, 3 * width), bf16),
+            jax.ShapeDtypeStruct((seq // nb, wide), f32),
+            jax.ShapeDtypeStruct((wide, width), bf16),
+            jax.ShapeDtypeStruct((wide, 3 * width), bf16),
+        ]
+        + [like(value) for value in swaps],
         scratch_shapes=[
-            pltpu.VMEM((heads * tile, seq), jnp.bfloat16),
-            pltpu.VMEM((heads * tile, width), jnp.bfloat16),
-            pltpu.VMEM((heads * tile, width), jnp.bfloat16),
-            pltpu.VMEM((seq, width), jnp.float32),
-            pltpu.VMEM((seq, width), jnp.float32),
+            pltpu.VMEM((heads * tile, seq), bf16),
+            pltpu.VMEM((heads * tile, width), bf16),
+            pltpu.VMEM((heads * tile, width), bf16),
+            pltpu.VMEM((seq, width), f32),
+            pltpu.VMEM((seq, width), f32),
         ]
-        + scatter_scratch(nb // 2, cuts, seq // nb, wide),
+        + [pltpu.VMEM(value.shape, value.dtype) for value in loads]
+        + [pltpu.SemaphoreType.DMA((4,))]
+        + scatter_scratch(nb // 2, cuts, seq // nb, wide)
+        + swap_sems(swaps),
         compiler_params=params(cid),
         cost_estimate=cost(10 * seq * seq * width),
-    )(q, k, v, o, g, p, cosine, sine, place[:, None], length.reshape(1), hidden, w_red)
+    )(q, k, v, o, g, p, cosine, sine, place[:, None], length.reshape(1), *loads, *swaps)
 
 
 def arrange(weight, out, parts):
@@ -785,16 +967,17 @@
 
 def first_swap_kernel(parts, *refs):
     n = len(parts)
-    weights, dsts, later, held, sems = (
-        refs[:n], refs[n : n + 2], refs[n + 2 : 2 * n], refs[2 * n : 2 * n + 2], refs[2 * n + 2 :],
-    )
+    sources, dsts, later, refs = refs[:n], refs[n : n + 2], refs[n + 2 : 2 * n], refs[2 * n :]
+    weights, held, load_sem, sems = refs[:n], refs[n : n + 2], refs[n + 2], refs[n + 3 :]
     starts, waits = swap_list(held, dsts, sems)
+    load, loaded = mover(list(zip(sources, weights)), load_sem)
+    load()
     greet(held[0].shape[0] // 2, True)
-    for weight, out, part, start in zip(weights, held, parts, starts):
-        arrange(weight, out, part)
-        start()
-    for weight, out, part in zip(weights[2:], later, parts[2:]):
-        arrange(weight, out, part)
+    for i in range(n):
+        loaded(i)
+        arrange(weights[i], held[i] if i < 2 else later[i - 2], parts[i])
+        if i < 2:
+            starts[i]()
     for wait in waits:
         wait()
 
@@ -803,13 +986,15 @@
     nb = lax.axis_size("blk")
     shapes = [(nb, value.shape[0], value.shape[1] // nb) for value in weights]
     n = len(weights)
+    dma = pltpu.SemaphoreType.DMA
     return pl.pallas_call(
         functools.partial(first_swap_kernel, parts),
         out_shape=[jax.ShapeDtypeStruct(shape, jnp.bfloat16) for shape in shapes],
-        in_specs=[VMEM] * n,
+        in_specs=[ANY] * n,
         out_specs=[ANY] * 2 + [VMEM] * (n - 2),
-        scratch_shapes=[pltpu.VMEM(shape, jnp.bfloat16) for shape in shapes[:2]]
-        + [pltpu.SemaphoreType.DMA, pltpu.SemaphoreType.DMA((nb,)), pltpu.SemaphoreType.DMA((nb,))] * 2,
+        scratch_shapes=[pltpu.VMEM(value.shape, value.dtype) for value in weights]
+        + [pltpu.VMEM(shape, jnp.bfloat16) for shape in shapes[:2]]
+        + [dma((n,))] + [dma, dma((nb,)), dma((nb,))] * 2,
         compiler_params=params(cid),
         cost_estimate=cost(0),
     )(*weights)
@@ -835,14 +1020,14 @@
 
     def first(other, slot):
         return pltpu.make_async_remote_copy(
+            src_ref=rows_held.at[r], dst_ref=rows_held.at[slot], send_sem=send_two.at[other],
+            recv_sem=recv_two.at[slot], device_id=(other, b), device_id_type=MESH,
+        )
+
+    def second(other, slot):
+        return pltpu.make_async_remote_copy(
             src_ref=held.at[b], dst_ref=held.at[slot], send_sem=send_one.at[other],
             recv_sem=recv_one.at[slot], device_id=(r, other), device_id_type=MESH,
-        )
-
-    def second(other, slot):
-        return pltpu.make_async_remote_copy(
-            src_ref=rows_held.at[r], dst_ref=rows_held.at[slot], send_sem=send_two.at[other],
-            recv_sem=recv_two.at[slot], device_id=(other, b), device_id_type=MESH,
         )
 
     def greet_all():
@@ -854,62 +1039,69 @@
         pl.semaphore_wait(barrier, nb + nr - 2)
 
     def start():
-        held[b] = x_ref[...]
+        rows_held[r] = x_ref[...]
+        for other in along:
+            first(other, r).start()
+
+    def middle():
+        for other in along:
+            first(other, other).wait_recv()
+        held[b] = jnp.sum(rows_held[...], axis=0)
         for other in across:
-            first(other, b).start()
-
-    def middle():
+            second(other, b).start()
+
+    def finish():
         for other in across:
-            first(other, other).wait_recv()
-        rows_held[r] = jnp.sum(held[...], axis=0)
+            second(other, other).wait_recv()
+        o_ref[...] = jnp.sum(held[...], axis=0)
         for other in along:
-            second(other, r).start()
-
-    def finish():
-        for other in along:
-            second(other, other).wait_recv()
-        o_ref[...] = jnp.sum(rows_held[...], axis=0)
+            first(other, r).wait_send()
         for other in across:
-            first(other, b).wait_send()
-        for other in along:
-            second(other, r).wait_send()
+            second(other, b).wait_send()
 
     return greet_all, start, middle, finish
 
 
-def last_scatter_kernel(chips, nr, cuts, tile, n, a_ref, w_ref, x_ref, inverse_ref, gain_ref, resid_ref, gain_two_ref, *refs):
+def last_scatter_kernel(
+    chips, nr, cuts, tile, n, a_ref, w_ref, x_ref, inverse_ref, gain_ref, resid_ref, gain_two_ref, h1_hbm, *refs
+):
     srcs, refs = refs[:n], refs[n:]
     o_ref, total_ref, dsts, refs = refs[0], refs[1], refs[2 : 2 + n], refs[2 + n :]
-    sum_ref, part_ref, refs = refs[0], refs[1], refs[2:]
+    sum_ref, part_ref, h1_ref, load_sem, refs = refs[0], refs[1], refs[2], refs[3], refs[4:]
     put, hop, finish = scatter_task(chips, cuts, tile, sum_ref, refs[:4], refs[4:10])
     greet_all, start_total, middle, finish_total = total_task(
         nr, 2 * chips, part_ref, total_ref, *refs[10:16]
     )
     starts, waits = swap_list(srcs, dsts, refs[16:])
+    load, loaded = mover([(h1_hbm, h1_ref)], load_sem)
+    load()
     greet_all()
+    for start in starts:
+        start()
+    part_ref[0:1] = jnp.zeros_like(part_ref[0:1])
+    part_ref[1:2] = gain_two_ref[...]
+    loaded()
+
+    def seen(rows, cols, got):
+        part_ref[0:1, cols] += jnp.sum(got * h1_ref[rows, cols].astype(jnp.float32), axis=0)[None]
+
     for s in range(chips):
-        put(s, lambda rows: a_ref.at[rows], w_ref)
+        put(s, lambda rows: a_ref.at[rows], w_ref, seen)
         if s < chips - 1:
             hop(s)
-        if s == 0:
-            starts[0]()
+    part_ref[0:1] = part_ref[0:1] / gain_ref[...]
+    start_total()
+    middle()
     finish()
     inverse = inverse_ref[...]
     unit = x_ref[...].astype(jnp.float32) * inverse
-    grad, gain = norm_backward(sum_ref[...], unit, inverse, gain_ref[...])
-    part_ref[0:1] = gain[None]
-    part_ref[1:2] = gain_two_ref[...]
-    start_total()
-    for start in starts[1:]:
-        start()
-    o_ref[...] = resid_ref[...] + grad
-    middle()
+    o_ref[...] = resid_ref[...] + norm_backward(sum_ref[...], unit, inverse, gain_ref[...])[0]
     finish_total()
     for wait in waits:
         wait()
 
 
-def last_scatter(cid, a, w, x, inverse, gain, resid, gain_two, swaps, cuts=2, tile=1024):
+def last_scatter(cid, a, w, x, inverse, gain, resid, gain_two, h1_all, swaps, cuts=2, tile=1024):
     nr, nb = lax.axis_size("rows"), lax.axis_size("blk")
     t, width = x.shape
     n = len(swaps)
@@ -919,16 +1111,21 @@
         functools.partial(last_scatter_kernel, nb // 2, nr, cuts, tile, n),
         out_shape=[jax.ShapeDtypeStruct((t, width), f32), jax.ShapeDtypeStruct(pair, f32)]
         + [like(value) for value in swaps],
-        in_specs=[VMEM] * 7 + [ANY] * n,
+        in_specs=[VMEM] * 7 + [ANY] * (1 + n),
         out_specs=[VMEM] * 2 + [ANY] * n,
-        scratch_shapes=[pltpu.VMEM((t, width), f32), pltpu.VMEM(pair, f32)]
+        scratch_shapes=[
+            pltpu.VMEM((t, width), f32),
+            pltpu.VMEM(pair, f32),
+            pltpu.VMEM(h1_all.shape, h1_all.dtype),
+            dma((1,)),
+        ]
         + scatter_scratch(nb // 2, cuts, t, width)
         + [pltpu.VMEM((nb,) + pair, f32), pltpu.VMEM((nr,) + pair, f32)]
         + [dma((nb,))] * 2 + [dma((nr,))] * 2
         + swap_sems(swaps),
         compiler_params=params(cid),
         cost_estimate=cost(2 * a.shape[0] * width * w.shape[1]),
-    )(a, w, x, inverse, gain[None], resid, gain_two[None], *swaps)
+    )(a, w, x, inverse, gain[None], resid, gain_two[None], h1_all, *swaps)
 
 
 def step_kernel(grad, *refs):
@@ -945,8 +1142,8 @@
 def step(pieces, parts, states):
     nb = pieces.shape[0]
     rows, columns = states[0].shape
+    tile = min(rows, 64 if parts > 1 else 32)
     span = columns // parts
-    tile = max(16, min(rows, (1 << 17) // span))
     at = pl.BlockSpec((tile, span), lambda part, i: (i, part))
     outs = len(states)
     return pl.pallas_call(
@@ -1007,27 +1204,24 @@
     w_red = over_rows(swap_red)
     x1 = x + dot_scatter(5, attended, w_out)[0]
     unit_two, inverse_two, h2 = norm_forward(x1, gain_expand)
-    h2_all, hidden, slope_gate, slope_up = line_gather(6, h2, w_gu, ff=True)
-    part_reduce = over_tokens(g_all, hidden).astype(bf16)
-    grad_h2, part_expand = ff_back(
-        8, after(g_all, part_reduce), slope_gate, slope_up, w_red, w_gu, h2_all
-    )
+    h2_all, hidden, slope_gate, slope_up, part_reduce = gather_dot(6, h2, w_gu, g_all)
+    grad_h2, part_expand = ff_back(8, g_all, slope_gate, slope_up, w_red, w_gu, h2_all)
     rows_reduce = sum_rows(part_reduce)
     rows_expand = sum_rows(part_expand)
     middle, gain_two = norm_backward(grad_h2, unit_two, inverse_two, gain_expand)
     grad_x1 = cotangent[0].astype(f32) + middle
-    branch_all, grad_o = line_gather(9, grad_x1.astype(bf16), w_out)
-    part_out = over_tokens(branch_all, attended).astype(bf16)
+    branch_all, grad_o = gather_dot(9, grad_x1.astype(bf16), w_out)
+    grad_mixed, y, part_out, part_in, own_reduce = attend_back(
+        10, q, k, v, attended, grad_o, p, cosine, sine, place, length,
+        hidden, w_red, branch_all, h1_all, [rows_reduce],
+    )
     rows_out = sum_rows(part_out)
-    grad_mixed, y = attend_back(
-        10, q, k, v, attended, after(grad_o, part_out), p, cosine, sine, place, length, hidden, w_red
-    )
     y = x1 + y
-    part_in = over_tokens(h1_all, grad_mixed).astype(bf16)
-    grad_input, gains, own_expand, own_reduce = last_scatter(
-        11, after(grad_mixed, part_in), w_in, tokens[0], inverse_one, gain_attend, grad_x1, gain_two,
-        [rows_expand, rows_reduce],
-    )
+    grad_input, gain_one_two, own_expand = last_scatter(
+        11, grad_mixed, w_in, tokens[0], inverse_one, gain_attend, grad_x1, gain_two,
+        h1_all, [rows_expand],
+    )
+    gains = gain_one_two
     rows_in = sum_rows(part_in)
     rows_in, rows_out = after((rows_in, rows_out), own_expand)
     both = lax.all_to_all(

time: 629 us -> 571 us (0.908)
  Pallas kernels: 543 us -> 512 us
  matrix products: 22.1 us -> 0 us
  starting transfers between devices: 11.7 us -> 4.37 us
    dot_general x3 -> x0, matrix products: 22.1 us -> none  [over_tokens(): lax.dot_general(left, right, (((0,), (0,)), ((), ())), preferred_element_...]
    pallas_call x1, Pallas kernels: 98.8 us -> 80.8 us  [last_scatter(): pl.pallas_call(functools.partial(last_scatter_kernel, nb // 2, nr, cuts,...]
    pallas_call x1, Pallas kernels: 54.4 us -> 47.2 us  [ff_back(): pl.pallas_call(functools.partial(ff_back_kernel, nb // 2, cuts, tile), ou...]
    all_to_all x1, starting transfers between devices: 11.2 us -> 4.04 us  [shards(): lax.all_to_all(jnp.concatenate([rows_in, rows_out], axis=2), 'blk', 0, 0,...]
  transfers between devices with their start and end apart: 9 -> 9, of which waited for: 1 -> 1; matrix products, arithmetic and copies ran while one was open for 6% -> 2% of each run, Pallas kernels for 81% -> 84%
where the time goes in v4:
time: 571 us; the launch traced here: 563 us
  Pallas kernels  512 us (90%)
  between operations  15.5 us (3%)
  other arithmetic  13.6 us (2%)
  waiting for transfers between devices  11.1 us (2%)
  local copies, waits for them, and re-layouts  6.65 us (1%)
    pallas_call x2, Pallas kernels, gather_dot(): pl.pallas_call(functools.partial(gather_dot_kernel, nb // 2, cuts, tile,...  93.6 us
    pallas_call x1, Pallas kernels, last_scatter(): pl.pallas_call(functools.partial(last_scatter_kernel, nb // 2, nr, cuts,...  80.8 us
    pallas_call x1, Pallas kernels, line_gather(): pl.pallas_call(functools.partial(gather_kernel, nb // 2, cuts, n), out_sh...  69 us
    pallas_call x1, Pallas kernels, attend(): pl.pallas_call(functools.partial(attend_kernel, nb // 2, cuts, n), grid=(...  68.7 us
    pallas_call x1, Pallas kernels, attend_back(): pl.pallas_call(functools.partial(attend_back_kernel, nb // 2, cuts, 1024,...  59.2 us
    pallas_call x1, Pallas kernels, ff_back(): pl.pallas_call(functools.partial(ff_back_kernel, nb // 2, cuts, tile), ou...  47.2 us
    pallas_call x1, Pallas kernels, dot_scatter(): pl.pallas_call(functools.partial(scatter_kernel, nb // 2, cuts, tile, n),...  39.4 us
    pallas_call x1, Pallas kernels, first_swap(): pl.pallas_call(functools.partial(first_swap_kernel, parts), out_shape=[ja...  29.9 us
  transfers between devices with their start and end apart: 9, of which 1 were waited for; matrix products, arithmetic and copies ran while one was open for 2% of the time, Pallas kernels for 84%

profile of v4, /device:TPU:0, one launch (start us, length us, event | category | flops | bytes accessed | tf_op | source)
XLA Modules:
  0.0 562.8 jit_solution(17360479806482674418)
XLA Ops:
  7.2 0.0 all-gather.5.cloned.1.call-start
  7.2 29.9 %shard_map.289 = (bf16[8,64,768]{2,1,0:T(8,128)(2,1)}, bf16[8,64,256]{2,1,0:T(8,128)(2,1)}, bf16[8,64,2048]{2,1,0:T(8,128)(2,1)}, bf16[8,64,1024]{2,1,0:T(8,128)(2,1)}) custom-call(f32[64,6144]{1,0:T(8,128)} %refs_0_.5, f32[64,2048]{1,0:T(8,128)} %bitcast.52, f32[64,16384]{1,0:T(8,128)} %refs_0_.4, f32[64,8192]{1,0:T(8,128)} %bitcast.40), custom_call_target="tpu_custom_call" | custom-call | bytes 150000000 | tf_op jit(solution)/shard_map/pallas_call | solution.py:990
  37.2 0.0 all-gather.7.cloned.1.call-start
  37.2 0.7 all-gather.7.cloned.1.call-update
  37.9 0.0 all-gather.9.cloned.1.call-start
  38.0 0.2 fusion
  38.2 1.0 fusion.2.x_ref
  39.2 69.0 %shard_map.290 = (bf16[1024,2048]{1,0:T(8,128)(2,1)}, bf16[8,64,2048]{2,1,0:T(8,128)(2,1)}) custom-call(bf16[128,2048]{1,0:T(8,128)(2,1)} %fusion.2.x_ref, bf16[8,64,2048]{2,1,0:T(8,128)(2,1)} %get-tuple-element.62.refs_0_), custom_call_target="tpu_custom_call" | custom-call | bytes 150000000 | tf_op jit(solution)/shard_map/pallas_call | solution.py:212
  108.2 0.0 all-gather.11.cloned.1.call-start
  108.3 0.1 iota_add_fusion
  108.4 0.1 add.81
  108.4 1.3 add.86.q_place
  109.7 0.1 convert_element_type.31
  110.5 1.9 fusion.4
  112.4 1.8 pad_maximum_fusion.1
  114.2 0.6 compare_select_fusion.k_place
  114.8 68.7 %shard_map.291 = (bf16[1024,256]{1,0:T(8,128)(2,1)}, bf16[1024,256]{1,0:T(8,128)(2,1)}, bf16[1024,256]{1,0:T(8,128)(2,1)}, bf16[1024,256]{1,0:T(8,128)(2,1)}, bf...) custom-call(bf16[1024,2048]{1,0:T(8,128)(2,1)} %get-tuple-element.63.h1_hbm, ...), custom_call_target="tpu_custom_call" | custom-call | flops 4294967296 | bytes 150000000 | tf_op jit(solution)/shard_map/pallas_call | solution.py:782
  183.6 0.0 reduce-scatter.5.cloned.1.call-start
  183.7 39.4 %shard_map.292 = f32[128,2048]{1,0:T(8,128)} custom-call(bf16[1024,256]{1,0:T(8,128)(2,1)} %get-tuple-element.65.refs_0_.o_all, bf16[2048,256]{1,0:T(8,128)(2,1)} %all-gather.7.cloned.1.call-done.refs_1_.w_hbm), custom_call_target="tpu_custom_call" | custom-call | flops 1073741824 | bytes 150000000 | tf_op jit(solution)/shard_map/pallas_call | solution.py:624
  223.0 1.5 multiply_reduce_fusion.2
  224.5 1.0 multiply_convert_fusion.x_ref
  225.5 46.4 %shard_map.293 = (bf16[1024,2048]{1,0:T(8,128)(2,1)}, bf16[1024,1024]{1,0:T(8,128)(2,1)}, bf16[1024,1024]{1,0:T(8,128)(2,1)}, bf16[1024,1024]{1,0:T(8,128)(2,1)}, bf16[2048,1024]{1,0:T(8,128)(2,1)}) custom-call(bf16[128,2048]{1,0:T(8,128)(2,1)} %multiply_convert_fusion.x_ref, bf16[2048,2048]{1,0:T(8,128)(2,1)} %all-gather.9.cloned.1.call-done.w_hbm.refs_4_, ...), custom_call_target="tpu_custom_call" | custom-call | flops 8589934592 | bytes 150000000 | tf_op jit(solution)/shard_map/pallas_call | solution.py:357
  271.9 0.0 reduce-scatter.7.cloned.1.call-start
  272.0 47.2 %shard_map.294 = (f32[128,2048]{1,0:T(8,128)}, bf16[2048,2048]{1,0:T(8,128)(2,1)}) custom-call(bf16[1024,2048]{1,0:T(8,128)(2,1)} %get-tuple-element.70.refs_0_, bf16[1024,1024]{1,0:T(8,128)(2,1)} %get-tuple-element.72.refs_1_, bf16[1024,1024]{1,0:T(8,128)(2,1)} %get-tuple-element.73.refs_2_, ...), custom_call_target="tpu_custom_call" | custom-call | flops 21474836480 | bytes 150000000 | tf_op jit(solution)/shard_map/pallas_call | solution.py:603
  319.2 0.0 reduce-scatter.11.cloned.1.call-start
  319.3 1.2 copy-done.1
  320.4 0.9 multiply_reduce_fusion
  321.3 1.5 fusion.7
  322.8 47.2 %shard_map.295 = (bf16[1024,2048]{1,0:T(8,128)(2,1)}, bf16[1024,256]{1,0:T(8,128)(2,1)}) custom-call(bf16[128,2048]{1,0:T(8,128)(2,1)} %get-tuple-element.107.x_ref, bf16[2048,256]{1,0:T(8,128)(2,1)} %all-gather.7.cloned.1.call-done.refs_1_.w_hbm), custom_call_target="tpu_custom_call" | custom-call | flops 1073741824 | bytes 150000000 | tf_op jit(solution)/shard_map/pallas_call | solution.py:357
  370.0 0.0 reduce-scatter.5.cloned.1.call-done
  370.0 59.2 %shard_map.296 = (bf16[1024,768]{1,0:T(8,128)(2,1)}, f32[128,2048]{1,0:T(8,128)}, bf16[2048,256]{1,0:T(8,128)(2,1)}, bf16[2048,768]{1,0:T(8,128)(2,1)}, bf16[8,64,1024]{2,1,0:T(8,128)(2,1)}) custom-call(bf16[1024,256]{1,0:T(8,128)(2,1)} %get-tuple-element.67.q_ref, bf16[1024,256]{1,0:T(8,128)(2,1)} %get-tuple-element.68.k_ref, ...), custom_call_target="tpu_custom_call" | custom-call | flops 2684354560 | bytes 150000000 | tf_op jit(solution)/shard_map/pallas_call | solution.py:920
  429.2 0.0 reduce-scatter.9.cloned.1.call-start
  429.2 0.7 reduce-scatter.9.cloned.1.call-update
  429.9 0.7 copy.40.inverse_ref
  430.7 80.8 %shard_map.297 = (f32[128,2048]{1,0:T(8,128)}, f32[2,2048]{1,0:T(2,128)}, bf16[8,64,2048]{2,1,0:T(8,128)(2,1)}) custom-call(bf16[1024,768]{1,0:T(8,128)(2,1)} %get-tuple-element.83.a_ref, bf16[2048,768]{1,0:T(8,128)(2,1)} %all-gather.5.cloned.1.call-done.w_hbm.w_ref, bf16[128,2048]{1,0:T(8,128)(2,1)} %bitcast.42, f32[128,1]{1,0:T(8,128)} %copy.40.inverse_ref, ...), custom_call_target="tpu_custom_call" | custom-call | flops 3221225472 | bytes 150000000 | tf_op jit(solution)/shard_map/pallas_call | solution.py:1110
  511.5 0.0 reduce-scatter.11.cloned.1.call-done
  511.6 2.3 pad_maximum_fusion
  513.9 4.0 all-to-all-start
  518.0 5.8 %shard_map.299 = (f32[64,8192]{1,0:T(8,128)}, f32[64,8192]{1,0:T(8,128)}, f32[64,8192]{1,0:T(8,128)}) custom-call(bf16[8,64,1024]{2,1,0:T(8,128)(2,1)} %get-tuple-element.93.grad, f32[64,8192]{1,0:T(8,128)} %bitcast.41, f32[64,8192]{1,0:T(8,128)} %bitcast.43, f32[64,8192]{1,0:T(8,128)} %bitcast.44), custom_call_target="tpu_custom_call" | custom-call | bytes 13631488 | tf_op jit(solution)/shard_map/pallas_call | solution.py:1149
  523.8 0.9 fusion.3
  524.7 9.8 %shard_map.298 = (f32[64,16384]{1,0:T(8,128)}, f32[64,16384]{1,0:T(8,128)}, f32[64,16384]{1,0:T(8,128)}) custom-call(bf16[8,64,2048]{2,1,0:T(8,128)(2,1)} %get-tuple-element.89.grad, f32[64,16384]{1,0:T(8,128)} %refs_0_.4, f32[64,16384]{1,0:T(8,128)} %refs_1_.2, f32[64,16384]{1,0:T(8,128)} %refs_2_.4), custom_call_target="tpu_custom_call" | custom-call | bytes 27262976 | tf_op jit(solution)/shard_map/pallas_call | solution.py:1149
  534.5 0.6 fusion.8
  535.1 9.5 %all-to-all-done = bf16[8,64,1024]{2,1,0:T(8,128)(2,1)S(1)} async-done(((bf16[8,64,1024]{2,1,0:T(8,128)(2,1)}), bf16[8,64,1024]{2,1,0:T(8,128)(2,1)S(1)}, u32[]{:S(2)}, u32[]{:S(2)}) %all-to-all-start) | async-done | bytes 1048608 | tf_op jit(solution)/shard_map/all_to_all | solution.py:1227
  544.5 1.0 slice.14.grad
  545.5 0.7 slice.15.grad
  546.2 6.1 %shard_map.300 = (f32[64,6144]{1,0:T(8,128)}, f32[64,6144]{1,0:T(8,128)}, f32[64,6144]{1,0:T(8,128)}) custom-call(bf16[8,64,768]{2,1,0:T(8,128)(2,1)} %slice.14.grad, f32[64,6144]{1,0:T(8,128)} %refs_0_.5, f32[64,6144]{1,0:T(8,128)} %refs_1_.3, f32[64,6144]{1,0:T(8,128)} %refs_2_.5), custom_call_target="tpu_custom_call" | custom-call | bytes 10223616 | tf_op jit(solution)/shard_map/pallas_call | solution.py:1149
  552.3 2.2 shard_map.301
  554.5 1.0 copy.43
  (34 shorter events, 0.2 us)
Async XLA Ops:
  7.2 107.6 %all-gather.5.cloned.1.call-start = ((), (), s32[]{:S(2)}) async-start(), calls=%async_computation.5 | async-start | bytes 3932160 | tf_op jit(solution)/shard_map/all_gather | solution.py:1005
  7.2 30.7 %copy-start = (bf16[1,128,2048]{2,1,0:T(8,128)(2,1)S(1)}, bf16[1,128,2048]{2,1,0:T(8,128)(2,1)}, u32[]{:S(2)}) copy-start(bf16[1,128,2048]{2,1,0:T(8,128)(2,1)} %param.18) | copy-start | bytes 1572868
  7.2 30.9 %copy-start.6 = (f32[2048]{0:T(1024)S(1)}, f32[2048]{0:T(1024)}, u32[]{:S(2)}) copy-start(f32[2048]{0:T(1024)} %param.22) | copy-start | bytes 24580
  37.2 146.5 %all-gather.7.cloned.1.call-start = ((), (), s32[]{:S(2)}) async-start(), calls=%async_computation.6 | async-start | bytes 1310720 | tf_op jit(solution)/shard_map/all_gather | solution.py:1005
  37.9 187.5 %all-gather.9.cloned.1.call-start = ((), (), s32[]{:S(2)}) async-start(), calls=%async_computation.7 | async-start | bytes 10485760 | tf_op jit(solution)/shard_map/all_gather | solution.py:1005
  39.2 69.1 %copy-start.8 = (s32[1,16]{1,0:T(1,128)S(1)}, s32[1,16]{1,0:T(1,128)}, u32[]{:S(2)}) copy-start(s32[1,16]{1,0:T(1,128)} %param.21) | copy-start | bytes 196
  108.2 163.8 %all-gather.11.cloned.1.call-start = ((), (), s32[]{:S(2)}) async-start(), calls=%async_computation.8 | async-start | bytes 5242880 | tf_op jit(solution)/shard_map/all_gather | solution.py:1005
  183.6 186.4 %reduce-scatter.5.cloned.1.call-start = ((), (), s32[]{:S(2)}) async-start(), calls=%async_computation.9 | async-start | bytes 5242880 | tf_op jit(solution)/shard_map/reduce_scatter | solution.py:1010
  223.0 1.5 copy-start.5
  271.9 158.8 %reduce-scatter.7.cloned.1.call-start = ((), (), s32[]{:S(2)}) async-start(), calls=%async_computation.10 | async-start | bytes 10485760 | tf_op jit(solution)/shard_map/reduce_scatter | solution.py:1010
  319.2 1.3 copy-start.1
  319.2 2.1 copy-start.4
  319.2 192.3 %reduce-scatter.11.cloned.1.call-start = ((), (), s32[]{:S(2)}) async-start(), calls=%async_computation.12 | async-start | bytes 1310720 | tf_op jit(solution)/shard_map/reduce_scatter | solution.py:1010
  429.2 82.4 %reduce-scatter.9.cloned.1.call-start = ((), (), s32[]{:S(2)}) async-start(), calls=%async_computation.11 | async-start | bytes 3932160 | tf_op jit(solution)/shard_map/reduce_scatter | solution.py:1010
  513.9 30.6 %all-to-all-start = ((bf16[8,64,1024]{2,1,0:T(8,128)(2,1)}), bf16[8,64,1024]{2,1,0:T(8,128)(2,1)S(1)}, u32[]{:S(2)}, u32[]{:S(2)}) async-start(bf16[8,64,1024]{2,1,0:T(8,128)(2,1)} %pad_maximum_fusion), calls=%async_computation.4 | async-start | bytes 2097152 | tf_op jit(solution)/shard_map/all_to_all | solution.py:1227
  517.9 5.8 %copy-start.2 = (f32[128,2048]{1,0:T(8,128)S(1)}, f32[128,2048]{1,0:T(8,128)}, u32[]{:S(2)}) copy-start(f32[128,2048]{1,0:T(8,128)} %get-tuple-element.82) | copy-start | bytes 3145732
  524.7 9.8 %copy-start.7 = (f32[2,2048]{1,0:T(2,128)S(1)}, f32[2,2048]{1,0:T(2,128)}, u32[]{:S(2)}) copy-start(f32[2,2048]{1,0:T(2,128)} %get-tuple-element.86) | copy-start | bytes 49156
  546.2 8.3 %copy-start.3 = (f32[128,2048]{1,0:T(8,128)S(1)}, f32[128,2048]{1,0:T(8,128)}, u32[]{:S(2)}) copy-start(f32[128,2048]{1,0:T(8,128)} %get-tuple-element.85) | copy-start | bytes 3145732
Sparse Core Ops, SparseCore 0:
  37.3 45.1 all-gather.4
  84.3 26.6 all-gather.6
  112.8 89.1 all-gather.8
  203.7 52.6 all-gather.10
  272.0 53.1 reduce-scatter.4
  328.4 86.3 reduce-scatter.6
  429.3 29.5 reduce-scatter.10
  462.2 43.9 reduce-scatter.8

commit v5 on v4

v5 whole, which is shorter than its diff:
```python
import functools
import math

import jax
import jax.numpy as jnp
from jax import lax
from jax.experimental import pallas as pl
from jax.experimental.pallas import tpu as pltpu
from jax.sharding import PartitionSpec as P

HEADS = 32
HEAD_DIM = 64
MESH = pl.DeviceIdType.MESH
MIB = 1 << 20

theta_base = 130000.0
norm_eps = 1e-05
neg_large = -1e30
beta_one = 0.9
beta_two = 0.95
learn_rate = 0.01
decay_rate = 0.1
adam_eps = 1e-08
step_count = 10


def line_place():
    b = lax.axis_index("blk")
    return lax.axis_index("rows"), b // 2, b % 2


def greet(chips, swaps=False, rows=False):
    r, z, c = line_place()
    barrier = pltpu.get_barrier_semaphore()
    count = 0

    def signal(row, b):
        pl.semaphore_signal(barrier, inc=1, device_id=(row, b), device_id_type=MESH)

    b, nb, nr = 2 * z + c, 2 * chips, lax.axis_size("rows")
    if rows:
        for k in range(1, nr):
            signal(lax.rem(r + k, nr), b)
        count = nr - 1
    if swaps:
        for k in range(1, nb):
            signal(r, lax.rem(b + k, nb))
        count = count + nb - 1
    else:
        signal(r, b + 1 - 2 * c)
        pl.when(z < chips - 1)(lambda: signal(r, b + 2))
        pl.when(z > 0)(lambda: signal(r, b - 2))
        count = count + 1 + (z < chips - 1).astype(jnp.int32) + (z > 0).astype(jnp.int32)
    pl.semaphore_wait(barrier, count)


def swap_task(src, dst, local, send, recv):
    r, b = lax.axis_index("rows"), lax.axis_index("blk")
    nb = src.shape[0]
    others = [lax.rem(b + k, nb) for k in range(1, nb)]

    def remote(other, slot):
        return pltpu.make_async_remote_copy(
            src_ref=src.at[other], dst_ref=dst.at[slot], send_sem=send.at[other],
            recv_sem=recv.at[slot], device_id=(r, other), device_id_type=MESH,
        )

    def start():
        for other in others:
            remote(other, b).start()
        pltpu.make_async_copy(src.at[b], dst.at[b], local).start()

    def wait():
        for other in others:
            remote(other, other).wait_recv()
        for other in others:
            remote(other, b).wait_send()
        pltpu.make_async_copy(src.at[b], dst.at[b], local).wait()

    return start, wait


def rows_copy(src, dst, send, recv, device):
    return pltpu.make_async_remote_copy(
        src_ref=src, dst_ref=dst, send_sem=send, recv_sem=recv,
        device_id=(device, lax.axis_index("blk")), device_id_type=MESH,
    )


def through(src, stage, dst, local):
    first = pltpu.make_async_copy(src, stage, local)
    second = pltpu.make_async_copy(stage, dst, local)

    def store():
        first.wait()
        second.start()

    return first.start, store, second.wait


def direct_gather(src, dst, stage, local, send, recv):
    r, nr = lax.axis_index("rows"), dst.shape[0]
    others = [lax.rem(r + k, nr) for k in range(1, nr)]
    load, store, stored = through(src, stage, dst.at[r], local)

    def start():
        for other in others:
            rows_copy(src, dst.at[r], send.at[other], recv.at[r], other).start()
        load()

    def wait():
        for other in others:
            rows_copy(src, dst.at[other], send.at[other], recv.at[other], other).wait()
        stored()

    return start, store, wait


def square_gather(src, dst, stage, local, send, recv):
    r = lax.axis_index("rows")
    half = src.shape[0] // 2
    load, store, stored = through(src, stage, dst.at[r], local)

    def near(sem, origin, device):
        return rows_copy(src, dst.at[origin], send.at[sem], recv.at[sem], device)

    def onward(sem, origin, device):
        part = dst.at[origin, pl.ds((sem - 2) * half, half)]
        return rows_copy(part, part, send.at[sem], recv.at[sem], device)

    def start():
        near(0, r, r ^ 1).start()
        near(1, r, r ^ 2).start()
        load()

    def middle():
        store()
        near(0, r ^ 1, r ^ 1).wait_recv()
        onward(2, r ^ 1, r ^ 2).start()
        near(1, r ^ 2, r ^ 2).wait_recv()
        onward(3, r ^ 2, r ^ 1).start()

    def wait():
        onward(2, r ^ 3, r ^ 2).wait_recv()
        onward(3, r ^ 3, r ^ 1).wait_recv()
        near(0, r, r ^ 1).wait_send()
        near(1, r, r ^ 2).wait_send()
        onward(2, r ^ 1, r ^ 2).wait_send()
        onward(3, r ^ 2, r ^ 1).wait_send()
        stored()

    return start, middle, wait


def direct_sum(src, dst, held, local, send, recv):
    r, nr = lax.axis_index("rows"), src.shape[0]
    others = [lax.rem(r + k, nr) for k in range(1, nr)]

    def start():
        for other in others:
            rows_copy(src.at[other], held.at[r], send.at[other], recv.at[r], other).start()
        pltpu.make_async_copy(src.at[r], held.at[r], local).start()

    def wait():
        for other in others:
            rows_copy(src.at[other], held.at[other], send.at[other], recv.at[other], other).wait()
        pltpu.make_async_copy(src.at[r], held.at[r], local).wait()

        def one(j, _):
            total = held[0, j].astype(jnp.float32)
            for slot in range(1, nr):
                total = total + held[slot, j].astype(jnp.float32)
            held[0, j] = total.astype(held.dtype)
            return 0

        lax.fori_loop(0, held.shape[1], one, 0)
        done = pltpu.make_async_copy(held.at[0], dst, local)
        done.start()
        done.wait()

    return start, lambda: None, wait


def square_sum(src, dst, held, local, send, recv):
    r = lax.axis_index("rows")
    half = src.shape[1] // 2
    parts = [(pl.ds(0, half), r ^ 1, r ^ 2), (pl.ds(half, half), r ^ 2, r ^ 1)]

    def out(i, k):
        at, one, two = parts[i]
        return rows_copy(
            src.at[one if k == 0 else r ^ 3, at], held.at[k, at], send.at[2 * i + k],
            recv.at[2 * i + k], one,
        )

    def own(i, k):
        at, one, two = parts[i]
        return pltpu.make_async_copy(
            src.at[r if k == 0 else two, at], held.at[2 + k, at], local.at[2 * i + k]
        )

    def onward(i):
        at, one, two = parts[i]
        return rows_copy(held.at[3, at], held.at[4, at], send.at[4 + i], recv.at[4 + i], two)

    def add(i, into, *slots):
        def one(j, _):
            j = i * half + j
            total = held[into, j].astype(jnp.float32)
            for slot in slots:
                total = total + held[slot, j].astype(jnp.float32)
            held[into, j] = total.astype(held.dtype)
            return 0

        lax.fori_loop(0, half, one, 0)

    def start():
        for i in range(2):
            for k in (1, 0):
                out(i, k).start()
                own(i, k).start()

    def start_as(make):
        for i, k in ((0, 1), (1, 1), (0, 0), (1, 0)):
            make((parts[i][1] if k == 0 else r ^ 3), i)
            out(i, k).start()
        for i, k in ((0, 1), (1, 1), (0, 0), (1, 0)):
            make((r if k == 0 else parts[i][2]), i)
            own(i, k).start()

    start.as_made = start_as

    def middle():
        for i in range(2):
            out(i, 1).wait_recv()
            own(i, 1).wait()
            add(i, 3, 1)
            onward(i).start()

    def wait():
        for i in range(2):
            out(i, 0).wait_recv()
            own(i, 0).wait()
            onward(i).wait_recv()
            add(i, 2, 0, 4)
        done = pltpu.make_async_copy(held.at[2], dst, local.at[0])
        done.start()
        done.wait()
        for i in range(2):
            out(i, 0).wait_send()
            out(i, 1).wait_send()
            onward(i).wait_send()

    return start, middle, wait


class Extras:
    def __init__(self, swaps=(), gathers=(), scatters=()):
        nr, nb = lax.axis_size("rows"), lax.axis_size("blk")
        dma = pltpu.SemaphoreType.DMA
        self.swaps, self.gathers, self.scatters = len(swaps), [g[1:] for g in gathers], len(scatters)
        self.operands = [*swaps, *[g[0] for g in gathers], *scatters]
        self.n = len(self.operands)
        self.rows = bool(gathers) or bool(scatters)
        self.specs = [ANY] * self.n
        self.shapes = [like(value) for value in swaps]
        self.scratch = [dma, dma((nb,)), dma((nb,))] * len(swaps)
        self.square = nr == 4
        sems = 6 if self.square else nr
        for value, _, count in gathers:
            self.shapes.append(jax.ShapeDtypeStruct((nr, count, value.shape[1]), value.dtype))
            self.scratch += [pltpu.VMEM((count, value.shape[1]), value.dtype)]
            self.scratch += [dma, dma((sems,)), dma((sems,))]
        for value in scatters:
            self.shapes.append(jax.ShapeDtypeStruct(value.shape[1:], value.dtype))
            slots = 5 if self.square else nr
            local = dma((4,)) if self.square else dma
            self.scratch += [pltpu.VMEM((slots,) + value.shape[1:], value.dtype)]
            self.scratch += [local, dma((sems,)), dma((sems,))]

    def tasks(self, srcs, dsts, scratch):
        scratch = list(scratch)
        swaps, rows = [], []
        for i, (src, dst) in enumerate(zip(srcs, dsts)):
            if i < self.swaps:
                swaps.append(swap_task(src, dst, *scratch[:3]))
                scratch = scratch[3:]
            elif i < self.swaps + len(self.gathers):
                first, count = self.gathers[i - self.swaps]
                task = square_gather if self.square else direct_gather
                rows.append(task(src.at[pl.ds(first, count)], dst, *scratch[:4]))
                scratch = scratch[4:]
            else:
                task = square_sum if self.square else direct_sum
                rows.append(task(src, dst, *scratch[:4]))
                scratch = scratch[4:]

        def start_swaps():
            for start, _ in swaps:
                start()

        def start_rows():
            for start, _, _ in rows:
                start()

        def middle():
            for _, one, _ in rows:
                one()

        def wait_rows():
            for _, _, one in rows:
                one()

        def wait_swaps():
            for _, one in swaps:
                one()

        return start_swaps, start_rows, middle, wait_rows, wait_swaps


def like(value):
    return jax.ShapeDtypeStruct(value.shape, value.dtype)


ANY = pl.BlockSpec(memory_space=pl.ANY)
VMEM = pl.BlockSpec(memory_space=pltpu.VMEM)


def params(cid):
    return pltpu.CompilerParams(
        collective_id=cid, has_side_effects=True, vmem_limit_bytes=60 * MIB
    )


def cost(flops):
    return pl.CostEstimate(flops=flops, bytes_accessed=150_000_000, transcendentals=0)


def mover(pairs, sem):
    copies = [pltpu.make_async_copy(a, b, sem.at[i]) for i, (a, b) in enumerate(pairs)]

    def start(*which):
        for i in which or range(len(copies)):
            copies[i].start()

    def wait(*which):
        for i in which or range(len(copies)):
            copies[i].wait()

    return start, wait


def gather_task(chips, cuts, x_ref, o_ref, sems):
    copy_sem, send_up, send_down, send_side, recv = sems
    r, z, c = line_place()
    t = x_ref.shape[0]
    h = t // cuts
    up, down, side = (r, 2 * (z + 1) + c), (r, 2 * (z - 1) + c), (r, 2 * z + 1 - c)
    has_up, has_down = z < chips - 1, z > 0
    mine = 2 * z + c

    def piece(j, q):
        return o_ref.at[pl.ds(pl.multiple_of(j * t + q * h, h), h)]

    def remote(src, j, q, sem, dev):
        return pltpu.make_async_remote_copy(
            src_ref=src, dst_ref=piece(j, q), send_sem=sem.at[j, q], recv_sem=recv.at[j, q],
            device_id=dev, device_id_type=MESH,
        )

    def local():
        whole = o_ref.at[pl.ds(pl.multiple_of(mine * t, t), t)]
        return pltpu.make_async_copy(x_ref, whole, copy_sem)

    def start():
        for q in range(cuts):
            from_here = x_ref.at[pl.ds(q * h, h)]
            pl.when(has_up)(lambda: remote(from_here, mine, q, send_up, up).start())
            pl.when(has_down)(lambda: remote(from_here, mine, q, send_down, down).start())
            remote(from_here, mine, q, send_side, side).start()
        local().start()

    def hop(k):
        for q in range(cuts):
            @pl.when(z - k >= 0)
            def _():
                j = 2 * (z - k) + c
                remote(piece(j, q), j, q, send_up, up).wait_recv()
                pl.when(has_up)(lambda: remote(piece(j, q), j, q, send_up, up).start())
                remote(piece(j, q), j, q, send_side, side).start()

            @pl.when(z + k < chips)
            def _():
                j = 2 * (z + k) + c
                remote(piece(j, q), j, q, send_down, down).wait_recv()
                pl.when(has_down)(lambda: remote(piece(j, q), j, q, send_down, down).start())
                remote(piece(j, q), j, q, send_side, side).start()

    def from_side(y):
        for q in range(cuts):
            j = 2 * y + 1 - c
            remote(piece(j, q), j, q, send_side, side).wait_recv()

    def finish():
        for y in range(chips):
            j = 2 * y + c
            for q in range(cuts):
                pl.when(has_up & (z >= y))(
                    lambda: remote(piece(j, q), j, q, send_up, up).wait_send()
                )
                pl.when(has_down & (z <= y))(
                    lambda: remote(piece(j, q), j, q, send_down, down).wait_send()
                )
                remote(piece(j, q), j, q, send_side, side).wait_send()

    return start, hop, from_side, local, finish


def gather_sems(nb, cuts):
    return [pltpu.SemaphoreType.DMA] + [pltpu.SemaphoreType.DMA((nb, cuts))] * 4


def gather_kernel(chips, cuts, extras, x_ref, *refs):
    n = extras.n
    srcs, o_ref, dsts, refs = refs[:n], refs[n], refs[n + 1 : 2 * n + 1], refs[2 * n + 1 :]
    begin, hop, from_side, local, finish = gather_task(chips, cuts, x_ref, o_ref, refs[:5])
    start_swaps, start_rows, middle, wait_rows, wait_swaps = extras.tasks(srcs, dsts, refs[5:])
    greet(chips, True, extras.rows)
    begin()
    start_rows()
    for k in range(1, chips):
        if k == min(3, chips - 1):
            start_swaps()
        hop(k)
    middle()
    local().wait()
    for y in range(chips):
        from_side(y)
    finish()
    wait_rows()
    wait_swaps()


def line_gather(cid, x, extras, cuts=4):
    nb = lax.axis_size("blk")
    return pl.pallas_call(
        functools.partial(gather_kernel, nb // 2, cuts, extras),
        out_shape=[jax.ShapeDtypeStruct((nb * x.shape[0], x.shape[1]), x.dtype)] + extras.shapes,
        in_specs=[VMEM] + extras.specs,
        out_specs=[ANY] + extras.specs,
        scratch_shapes=gather_sems(nb, cuts) + extras.scratch,
        compiler_params=params(cid),
        cost_estimate=cost(0),
    )(x, *extras.operands)


def gather_dot_kernel(chips, cuts, extras, x_ref, w_ref, *refs):
    n = extras.n
    srcs, outs, dsts, refs = refs[:n], refs[n : n + 2], refs[n + 2 : 2 * n + 2], refs[2 * n + 2 :]
    held, save_sem, refs = refs[:2], refs[2], refs[3:]
    o_ref, prod_ref = held
    begin, hop, from_side, local, finish = gather_task(chips, cuts, x_ref, o_ref, refs[:5])
    start_swaps, start_rows, middle, wait_rows, wait_swaps = extras.tasks(srcs, dsts, refs[5:])
    r, z, c = line_place()
    t = x_ref.shape[0]
    greet(chips, False, extras.rows)
    begin()
    start_rows()

    def rows_of(y):
        return pl.ds(pl.multiple_of(y * 2 * t, 2 * t), 2 * t)

    def saves(y):
        return mover([(a.at[rows_of(y)], b.at[rows_of(y)]) for a, b in zip(held, outs)], save_sem.at[y])

    def dot(y):
        rows = rows_of(y)
        prod_ref[rows] = jnp.dot(
            o_ref[rows], w_ref[...], preferred_element_type=jnp.float32
        ).astype(prod_ref.dtype)
        saves(y)[0]()

    from_side(z)
    local().wait()
    dot(z)
    for k in range(1, chips):
        hop(k)

        @pl.when(z - k >= 0)
        def _():
            from_side(z - k)
            dot(z - k)

        @pl.when(z + k < chips)
        def _():
            from_side(z + k)
            dot(z + k)

        if k == max(1, chips - 2):
            middle()
    finish()
    for y in range(chips):
        saves(y)[1]()
    wait_rows()


def gather_dot(cid, x, w, extras, cuts=2):
    nb = lax.axis_size("blk")
    all_rows = nb * x.shape[0]
    dma, bf16 = pltpu.SemaphoreType.DMA, jnp.bfloat16
    shapes = [(all_rows, x.shape[1]), (all_rows, w.shape[1])]
    return pl.pallas_call(
        functools.partial(gather_dot_kernel, nb // 2, cuts, extras),
        out_shape=[jax.ShapeDtypeStruct(shape, bf16) for shape in shapes] + extras.shapes,
        in_specs=[VMEM, VMEM] + extras.specs,
        out_specs=[ANY] * 2 + extras.specs,
        scratch_shapes=[pltpu.VMEM(shape, bf16) for shape in shapes]
        + [dma((nb // 2, 2))]
        + gather_sems(nb, cuts)
        + extras.scratch,
        compiler_params=params(cid),
        cost_estimate=cost(2 * all_rows * w.shape[0] * w.shape[1]),
    )(x, w, *extras.operands)


def need_order(chips):
    table = []
    for z in range(chips):
        need = {
            y: (chips - 1 + z - y) if y > z else (chips - 1 - z + y)
            for y in range(chips) if y != z
        }
        table.append(sorted(need, key=lambda y: need[y]) + [z])
    return table


def pick(table, z, k):
    out = 0
    for at, row in enumerate(table):
        for step, block in enumerate(row):
            out = out + jnp.where((z == at) & (k == step), block, 0)
    return out


def scatter_task(chips, cuts, tile, o_ref, bufs, sems):
    mine, away, side_buf, line_buf = bufs
    send_side, recv_side, send_up, recv_up, send_down, recv_down = sems
    r, z, c = line_place()
    t, width = o_ref.shape
    low, f32 = away.dtype, jnp.float32
    up, down, side = (r, 2 * (z + 1) + c), (r, 2 * (z - 1) + c), (r, 2 * z + 1 - c)
    has_up, has_down = z < chips - 1, z > 0
    h = t // cuts
    table = need_order(chips)

    def remote(src, dst, y, q, send, recv, dev):
        return pltpu.make_async_remote_copy(
            src_ref=src.at[y, pl.ds(q * h, h)], dst_ref=dst.at[y, pl.ds(q * h, h)],
            send_sem=send.at[y, q], recv_sem=recv.at[y, q], device_id=dev, device_id_type=MESH,
        )

    def to_side(y, q):
        return remote(away, side_buf, y, q, send_side, recv_side, side)

    def along(y, slot, q, send, recv, dev):
        return pltpu.make_async_remote_copy(
            src_ref=mine.at[y, pl.ds(q * h, h)], dst_ref=line_buf.at[slot, pl.ds(q * h, h)],
            send_sem=send.at[y, q], recv_sem=recv.at[y, q], device_id=dev, device_id_type=MESH,
        )

    def to_up(y, q):
        return along(y, y, q, send_up, recv_up, up)

    def to_down(y, q):
        return along(y, jnp.where(y == z - 1, chips, y), q, send_down, recv_down, down)

    def from_up(y, q):
        return along(y, jnp.where(y == z, chips, y), q, send_down, recv_down, down)

    def rows(q):
        return pl.ds(q * h, h)

    def total(y, q):
        to_side(y, q).wait_recv()
        return mine[y, rows(q)].astype(f32) + side_buf[y, rows(q)].astype(f32)

    def put(s, rows_of, w_ref, seen=None):
        put_at(pick(table, z, s), rows_of, w_ref, seen)

    def put_at(y, rows_of, w_ref, seen=None):
        block = pl.ds(pl.multiple_of(2 * y * t, 2 * t), 2 * t)
        a = rows_of(block)

        def one(i, _):
            cols = pl.ds(pl.multiple_of(i * tile, tile), tile)
            got = lax.dot_general(
                a[...], w_ref[cols], (((1,), (1,)), ((), ())), preferred_element_type=f32
            )
            if seen is not None:
                seen(block, cols, got)
            got = got.astype(low)

            @pl.when(c == 0)
            def _():
                mine[y, :, cols] = got[:t]
                away[y, :, cols] = got[t:]

            @pl.when(c == 1)
            def _():
                mine[y, :, cols] = got[t:]
                away[y, :, cols] = got[:t]

            return 0

        lax.fori_loop(0, width // tile, one, 0)
        for q in range(cuts):
            to_side(y, q).start()

    def hop(s):
        hop_up(chips - 1 + z - s)
        hop_down(s - (chips - 1) + z)

    def hop_up(y):
        for q in range(cuts):
            @pl.when((y > z) & (y <= chips - 1))
            def _():
                now = total(y, q)

                @pl.when(has_down)
                def _():
                    to_up(y, q).wait_recv()
                    mine[y, rows(q)] = (now + line_buf[y, rows(q)].astype(f32)).astype(low)

                @pl.when(z == 0)
                def _():
                    mine[y, rows(q)] = now.astype(low)

                to_up(y, q).start()

    def hop_down(w):
        for q in range(cuts):
            @pl.when((w >= 0) & (w < z))
            def _():
                now = total(w, q)

                @pl.when(has_up)
                def _():
                    from_up(w, q).wait_recv()
                    mine[w, rows(q)] = (now + line_buf[w, rows(q)].astype(f32)).astype(low)

                @pl.when(z == chips - 1)
                def _():
                    mine[w, rows(q)] = now.astype(low)

                to_down(w, q).start()

    def finish():
        for q in range(cuts):
            o_ref[rows(q)] = total(z, q)
        for q in range(cuts):
            @pl.when(has_down)
            def _():
                to_up(z, q).wait_recv()
                o_ref[rows(q)] += line_buf[z, rows(q)].astype(f32)

            @pl.when(has_up)
            def _():
                from_up(z, q).wait_recv()
                o_ref[rows(q)] += line_buf[chips, rows(q)].astype(f32)

        for y in range(chips):
            for q in range(cuts):
                to_side(y, q).wait_send()
                pl.when(y > z)(lambda: to_up(y, q).wait_send())
                pl.when(y < z)(lambda: to_down(y, q).wait_send())

    return put, (put_at, hop_up, hop_down), hop, finish


def scatter_scratch(chips, cuts, t, width):
    return (
        [pltpu.VMEM((chips, t, width), jnp.bfloat16)] * 3
        + [pltpu.VMEM((chips + 1, t, width), jnp.bfloat16)]
        + [pltpu.SemaphoreType.DMA((chips, cuts))] * 6
    )


def attend_out_kernel(chips, cuts, tile, extras, a_ref, w_ref, x_ref, gain_ref, *refs):
    n = extras.n
    srcs, (x1_ref, inverse_ref, h2_ref), dsts, refs = (
        refs[:n], refs[n : n + 3], refs[3 + n : 3 + 2 * n], refs[3 + 2 * n :],
    )
    put, _, hop, finish = scatter_task(chips, cuts, tile, x1_ref, refs[:4], refs[4:10])
    start_swaps, start_rows, middle, wait_rows, wait_swaps = extras.tasks(srcs, dsts, refs[10:])
    greet(chips, False, extras.rows)
    start_rows()
    for s in range(chips):
        put(s, lambda rows: a_ref.at[rows], w_ref)
        if s < chips - 1:
            hop(s)
    middle()
    finish()
    x1 = x_ref[...].astype(jnp.float32) + x1_ref[...]
    x1_ref[...] = x1
    _, inverse_ref[...], h2_ref[...] = norm_forward(x1, gain_ref[...])
    wait_rows()


def feed_forward_kernel(
    chips, cuts, tile, h2_here, x1_ref, inverse_ref, gain_ref, cotangent_ref, early_hbm, late_hbm, red_hbm, g_hbm,
    grad_out, low_out, gain_out, hidden_out, gate_out, up_out, reduce_out,
    h2_ref, hidden_ref, grad_ref, w_ref, red_ref, g_ref, dw_red, dw_ref, red_held,
    load_sem, save_sem, dw_sem, red_local, red_send, red_recv, *refs
):
    begin, pass_on, from_side, local, sent = gather_task(chips, cuts, h2_here, h2_ref, refs[:5])
    _, (put_at, hop_up, hop_down), _, finish = scatter_task(chips, cuts, tile, grad_out, refs[5:9], refs[9:])
    task = square_sum if dw_red.shape[0] == 4 else direct_sum
    start_red, middle_red, wait_red = task(
        dw_red, reduce_out, red_held, red_local, red_send, red_recv
    )
    nr, early, late = early_hbm.shape[0], early_hbm.shape[1], late_hbm.shape[1]
    pairs = [(g_hbm, g_ref), (red_hbm, red_ref)]
    for q in range(nr):
        first = q * (early + late)
        pairs += [
            (early_hbm.at[q], w_ref.at[pl.ds(first, early)]),
            (late_hbm.at[q], w_ref.at[pl.ds(first + early, late)]),
        ]
    load, loaded = mover(pairs, load_sem)
    w_loads = range(2, len(pairs))
    r, z, c = line_place()
    t, width = h2_here.shape
    units = hidden_ref.shape[1]
    span = min(512, units)
    f32, low = jnp.float32, jnp.bfloat16
    over_rows = (((0,), (0,)), ((), ()))
    load(*w_loads, 0, 1)
    greet(chips, False, True)
    begin()

    def rows_of(y):
        return pl.ds(pl.multiple_of(y * 2 * t, 2 * t), 2 * t)

    def save(y):
        return pltpu.make_async_copy(
            hidden_ref.at[rows_of(y)], hidden_out.at[rows_of(y)], save_sem.at[y]
        )

    def columns(i):
        at, more = i * span, units + i * span
        return pl.ds(pl.multiple_of(at, span), span), pl.ds(pl.multiple_of(more, span), span)

    def forward(y):
        rows = rows_of(y)

        def one(i, _):
            cols, more = columns(i)
            gate = jnp.dot(h2_ref[rows], w_ref[:, cols], preferred_element_type=f32)
            up = jnp.dot(h2_ref[rows], w_ref[:, more], preferred_element_type=f32)
            sigmoid = jax.nn.sigmoid(gate)
            silu = gate * sigmoid
            hidden_ref[rows, cols] = (silu * up).astype(low)
            grad_ref[rows, cols] = (up * (sigmoid * (1.0 + gate * (1.0 - sigmoid)))).astype(low)
            grad_ref[rows, more] = silu.astype(low)
            return 0

        lax.fori_loop(0, units // span, one, 0)
        save(y).start()

    def backward(rows):
        def one(i, _):
            cols, more = columns(i)
            grad = jnp.dot(g_ref[rows], red_ref[:, cols], preferred_element_type=f32)
            grad_ref[rows, cols] = (grad * grad_ref[rows, cols].astype(f32)).astype(low)
            grad_ref[rows, more] = (grad * grad_ref[rows, more].astype(f32)).astype(low)
            return 0

        lax.fori_loop(0, units // span, one, 0)
        return grad_ref.at[rows]

    from_side(z)
    local().wait()
    loaded(*w_loads)
    forward(z)
    loaded(0, 1)
    put_at(z, backward, w_ref)
    deep = 256
    turns = width // deep
    piece = dw_red.shape[2]
    run = dw_red.shape[1] * piece

    def reduce_grad(i, _):
        at = pl.ds(pl.multiple_of(i * deep, deep), deep)
        got = lax.dot_general(g_ref[:, at], hidden_ref[...], over_rows, preferred_element_type=f32)
        first = i * deep
        dw_red[first // run, pl.ds(lax.rem(first, run) // piece, deep // piece)] = (
            got.astype(low).reshape(deep // piece, piece, units)
        )
        return 0

    def make_reduce_grad():
        if dw_red.shape[0] == 4:
            tiles = turns // 8

            def make(slot, half):
                first = (slot * 2 + half) * tiles
                lax.fori_loop(first, first + tiles, reduce_grad, 0)

            start_red.as_made(make)
        else:
            lax.fori_loop(0, turns, reduce_grad, 0)
            start_red()

    def save_dw(i, half):
        at = pl.ds(pl.multiple_of(i * deep, deep), deep)
        return pltpu.make_async_copy(
            dw_ref.at[lax.rem(i, 2), half], (gate_out, up_out)[half].at[at], dw_sem.at[lax.rem(i, 2), half]
        )

    def expand_grad(i, _):
        at = pl.ds(pl.multiple_of(i * deep, deep), deep)
        for half in range(2):
            pl.when(i >= 2)(lambda: save_dw(i - 2, half).wait())
            dw_ref[lax.rem(i, 2), half] = lax.dot_general(
                h2_ref[:, at], grad_ref[:, half * units : (half + 1) * units], over_rows,
                preferred_element_type=f32,
            ).astype(low)
            save_dw(i, half).start()
        return 0

    last = 2 * chips - 3
    done = 0
    for turn in range(1, last + 1):
        if turn < chips:
            pass_on(turn)

            @pl.when(z - turn >= 0)
            def _():
                from_side(z - turn)
                forward(z - turn)
                put_at(z - turn, backward, w_ref)

            @pl.when(z + turn < chips)
            def _():
                from_side(z + turn)
                forward(z + turn)
                put_at(z + turn, backward, w_ref)

        hop_up(turn - z)
        hop_down(2 * (chips - 1) - z - turn)
        if turn == chips - 1:
            make_reduce_grad()
        elif turn >= chips:
            until = turns * (turn - chips + 1) // (last - chips + 1)
            lax.fori_loop(done, until, expand_grad, 0)
            done = until
    middle_red()
    finish()
    inverse = inverse_ref[...]
    middle_grad, gain = norm_backward(grad_out[...], x1_ref[...] * inverse, inverse, gain_ref[...])
    grad_x1 = cotangent_ref[...].astype(f32) + middle_grad
    grad_out[...] = grad_x1
    low_out[...] = grad_x1.astype(low)
    gain_out[...] = gain[None]
    wait_red()
    sent()
    for y in range(chips):
        save(y).wait()
    for i in range(max(0, turns - 2), turns):
        for half in range(2):
            save_dw(i, half).wait()


def feed_forward(
    cid, h2, x1, inverse, gain, cotangent, gu_early, gu_late, w_red, g_all, cuts=2, tile=1024
):
    nr, nb = lax.axis_size("rows"), lax.axis_size("blk")
    seq, width = g_all.shape
    both = gu_early.shape[2]
    units = both // 2
    t = seq // nb
    piece = width // (nr * nb)
    dma, f32, bf16 = pltpu.SemaphoreType.DMA, jnp.float32, jnp.bfloat16
    half = jax.ShapeDtypeStruct((width, units), bf16)
    slots, sems = (5, 6) if nr == 4 else (nr, nr)
    return pl.pallas_call(
        functools.partial(feed_forward_kernel, nb // 2, cuts, tile),
        out_shape=[
            jax.ShapeDtypeStruct((t, width), f32),
            jax.ShapeDtypeStruct((t, width), bf16),
            jax.ShapeDtypeStruct((1, width), f32),
            jax.ShapeDtypeStruct((seq, units), bf16),
            half,
            half,
            jax.ShapeDtypeStruct((nb, piece, units), bf16),
        ],
        in_specs=[VMEM] * 5 + [ANY] * 4,
        out_specs=[VMEM] * 3 + [ANY] * 4,
        scratch_shapes=[
            pltpu.VMEM((seq, width), bf16),
            pltpu.VMEM((seq, units), bf16),
            pltpu.VMEM((seq, both), bf16),
            pltpu.VMEM((width, both), bf16),
            pltpu.VMEM((width, units), bf16),
            pltpu.VMEM((seq, width), bf16),
            pltpu.VMEM((nr, nb, piece, units), bf16),
            pltpu.VMEM((2, 2, 256, units), bf16),
            pltpu.VMEM((slots, nb, piece, units), bf16),
            dma((2 + 2 * nr,)),
            dma((nb // 2,)),
            dma((2, 2)),
            dma((4,)) if nr == 4 else dma,
            dma((sems,)),
            dma((sems,)),
        ]
        + gather_sems(nb, cuts)
        + scatter_scratch(nb // 2, cuts, t, width),
        compiler_params=params(cid),
        cost_estimate=cost(9 * seq * width * both),
    )(h2, x1, inverse, gain[None], cotangent, gu_early, gu_late, w_red, g_all)


def attend_out_kernel(chips, cuts, tile, extras, a_ref, w_ref, x_ref, gain_ref, *refs):
    n = extras.n
    srcs, (x1_ref, inverse_ref, h2_ref), dsts, refs = (
        refs[:n], refs[n : n + 3], refs[3 + n : 3 + 2 * n], refs[3 + 2 * n :],
    )
    put, _, hop, finish = scatter_task(chips, cuts, tile, x1_ref, refs[:4], refs[4:10])
    start_swaps, start_rows, middle, wait_rows, wait_swaps = extras.tasks(srcs, dsts, refs[10:])
    greet(chips, False, extras.rows)
    start_rows()
    for s in range(chips):
        put(s, lambda rows: a_ref.at[rows], w_ref)
        if s < chips - 1:
            hop(s)
    middle()
    finish()
    x1 = x_ref[...].astype(jnp.float32) + x1_ref[...]
    x1_ref[...] = x1
    _, inverse_ref[...], h2_ref[...] = norm_forward(x1, gain_ref[...])
    wait_rows()


def attend_out_sum(cid, a, w, x, gain, extras, cuts=2, tile=1024):
    nb = lax.axis_size("blk")
    t, width = x.shape
    f32 = jnp.float32
    return pl.pallas_call(
        functools.partial(attend_out_kernel, nb // 2, cuts, tile, extras),
        out_shape=[
            jax.ShapeDtypeStruct((t, width), f32),
            jax.ShapeDtypeStruct((t, 1), f32),
            jax.ShapeDtypeStruct((t, width), jnp.bfloat16),
        ]
        + extras.shapes,
        in_specs=[VMEM] * 4 + extras.specs,
        out_specs=[VMEM] * 3 + extras.specs,
        scratch_shapes=scatter_scratch(nb // 2, cuts, t, width) + extras.scratch,
        compiler_params=params(cid),
        cost_estimate=cost(2 * a.shape[0] * width * w.shape[1]),
    )(a, w, x, gain[None], *extras.operands)


def norm_forward(values, gain_vector):
    inverse = lax.rsqrt(jnp.mean(values * values, axis=-1, keepdims=True) + norm_eps)
    unit_values = values * inverse
    return (unit_values, inverse, (unit_values * gain_vector).astype(jnp.bfloat16))


def norm_backward(grad_normed, unit_values, inverse, gain_vector):
    grad_unit = grad_normed * gain_vector
    grad_values = inverse * (
        grad_unit - unit_values * jnp.mean(grad_unit * unit_values, axis=-1, keepdims=True)
    )
    return (grad_values, jnp.sum(grad_normed * unit_values, axis=0))


def contract_last(left, right):
    return lax.dot_general(
        left, right, (((1,), (1,)), ((), ())), preferred_element_type=jnp.float32
    )


def adam_step(master, moment_one, moment_two, gradient):
    moment_one = beta_one * moment_one + (1.0 - beta_one) * gradient
    moment_two = beta_two * moment_two + (1.0 - beta_two) * gradient * gradient
    update = (
        moment_one
        / (1.0 - beta_one**step_count)
        / (jnp.sqrt(moment_two / (1.0 - beta_two**step_count)) + adam_eps)
    )
    return (master - learn_rate * (update + decay_rate * master), moment_one, moment_two)


def moment_step(moment_one, moment_two, gradient):
    moment_one = beta_one * moment_one + (1.0 - beta_one) * gradient
    moment_two = beta_two * moment_two + (1.0 - beta_two) * gradient * gradient
    return (moment_one, moment_two)


def once(*shape):
    return pl.BlockSpec(shape, lambda i: (0,) * len(shape), pipeline_mode=pl.Buffered(1))


def partner(values):
    width = values.shape[1]
    half = HEAD_DIM // 2
    feature = lax.broadcasted_iota(jnp.int32, values.shape, 1) % HEAD_DIM
    return jnp.where(
        feature < half, pltpu.roll(values, width - half, 1), pltpu.roll(values, half, 1)
    )


def spread_table(table, width):
    return jnp.concatenate([table] * (width // table.shape[1]), axis=1)


def head_lanes(shape):
    return lax.broadcasted_iota(jnp.int32, shape, 1) // HEAD_DIM


def attend_kernel(
    chips, cuts, extras, h1_hbm, w_hbm, cos_ref, sin_ref, q_place, k_place, length_ref, g_ref, *refs
):
    n = extras.n
    srcs, refs = refs[:n], refs[n:]
    o_ref, q_ref, k_ref, v_ref, p_ref, g_all = refs[:6]
    dsts, (h1_ref, w_ref, load_sem), sems = refs[6 : 6 + n], refs[6 + n : 9 + n], refs[9 + n :]
    load, loaded = mover([(w_hbm, w_ref), (h1_hbm, h1_ref)], load_sem)
    begin, hop, from_side, local, finish = gather_task(chips, cuts, g_ref, g_all, sems[:5])
    start_swaps, start_rows, middle, wait_rows, wait_swaps = extras.tasks(srcs, dsts, sems[5:])
    step, steps = pl.program_id(0), pl.num_programs(0)
    tile, width = o_ref.shape
    f32, bf16 = jnp.float32, jnp.bfloat16

    @pl.when(step == 0)
    def _():
        load()
        greet(chips, extras.swaps > 0, extras.rows)
        begin()
        start_rows()
        start_swaps()
        loaded()

        def one(i, _):
            rows = pl.ds(pl.multiple_of(i * tile, tile), tile)
            mixed = jnp.dot(h1_ref[rows], w_ref[...], preferred_element_type=f32)
            cosine, sine = spread_table(cos_ref[rows], width), spread_table(sin_ref[rows], width)
            for at, ref in enumerate((q_ref, k_ref)):
                got = mixed[:, at * width : (at + 1) * width]
                ref[rows] = (got * cosine + partner(got) * sine).astype(bf16)
            v_ref[rows] = mixed[:, 2 * width :].astype(bf16)
            return 0

        lax.fori_loop(0, steps, one, 0)

    @pl.when((step > 0) & (step < chips))
    def _():
        hop(step)


    rows = pl.ds(pl.multiple_of(step * tile, tile), tile)
    queries = q_ref[rows] * jnp.asarray(1.0 / math.sqrt(HEAD_DIM), bf16)
    lanes = head_lanes((tile, width))
    place = q_place[...]
    allowed = k_place[...] <= place
    out = jnp.zeros((tile, width), f32)
    for head in range(width // HEAD_DIM):
        here = lanes == head
        one_head = jnp.where(here, queries, jnp.zeros((), bf16))
        scores = lax.dot_general(
            one_head, k_ref[...], (((1,), (1,)), ((), ())), preferred_element_type=f32
        )
        scores = jnp.where(allowed, scores, neg_large)
        weights = jnp.exp(scores - jnp.max(scores, axis=-1, keepdims=True))
        weights = weights * (1.0 / jnp.sum(weights, axis=-1, keepdims=True))
        low = weights.astype(bf16)
        p_ref[head] = low
        out = jnp.where(here, jnp.dot(low, v_ref[...], preferred_element_type=f32), out)
    o_ref[...] = jnp.where(place < length_ref[0], out, 0.0).astype(bf16)
    pl.when(step == max(0, chips - 2))(middle)

    @pl.when(step == steps - 1)
    def _():
        local().wait()
        for y in range(chips):
            from_side(y)
        finish()
        wait_rows()
        wait_swaps()


def attend(cid, h1_all, w_in, cosine, sine, place, live_place, length, g, extras, cuts=2):
    seq, wide = h1_all.shape
    width = w_in.shape[1] // 3
    heads = width // HEAD_DIM
    nb = lax.axis_size("blk")
    tile = seq // (nb // 2)
    part = pl.BlockSpec((tile, width), lambda i: (i, 0))

    full = jax.ShapeDtypeStruct((seq, width), jnp.bfloat16)
    return pl.pallas_call(
        functools.partial(attend_kernel, nb // 2, cuts, extras),
        grid=(seq // tile,),
        in_specs=[
            ANY, ANY, once(seq, 2 * HEAD_DIM), once(seq, 2 * HEAD_DIM),
            pl.BlockSpec((tile, 1), lambda i: (i, 0)),
            once(1, seq),
            pl.BlockSpec(memory_space=pltpu.SMEM),
            once(*g.shape),
        ]
        + extras.specs,
        out_specs=[part] + [once(seq, width)] * 3
        + [pl.BlockSpec((heads, tile, seq), lambda i: (0, i, 0)), ANY]
        + extras.specs,
        out_shape=[full] * 4
        + [
            jax.ShapeDtypeStruct((heads, seq, seq), jnp.bfloat16),
            jax.ShapeDtypeStruct((seq, g.shape[1]), g.dtype),
        ]
        + extras.shapes,
        scratch_shapes=[
            pltpu.VMEM(h1_all.shape, h1_all.dtype),
            pltpu.VMEM(w_in.shape, w_in.dtype),
            pltpu.SemaphoreType.DMA((2,)),
        ]
        + gather_sems(nb, cuts)
        + extras.scratch,
        compiler_params=params(cid),
        cost_estimate=cost(4 * seq * seq * width + 6 * seq * wide * width),
    )(h1_all, w_in, cosine, sine, place, live_place, length.reshape(1), g, *extras.operands)


def attend_back_kernel(
    chips, cuts, tile_y, extras, q_ref, k_ref, v_ref, o_all, g_ref, p_ref, cos_ref, sin_ref, q_place, length_ref,
    hidden_hbm, red_hbm, branch_hbm, h1_hbm, *refs
):
    n = extras.n
    srcs, (mixed_ref, y_ref, dw_ref), dsts = refs[:n], refs[n : n + 3], refs[n + 3 : 2 * n + 3]
    refs = refs[2 * n + 3 :]
    (ds_ref, qm_ref, gm_ref, dk_acc, dv_acc, hidden_ref, red_ref, branch_ref, h1_ref, load_sem), refs = (
        refs[:10], refs[10:],
    )
    put, _, hop, finish = scatter_task(chips, cuts, tile_y, y_ref, refs[:4], refs[4:10])
    start_swaps, start_rows, middle, wait_rows, wait_swaps = extras.tasks(srcs, dsts, refs[10:])
    load, loaded = mover(
        [(red_hbm, red_ref), (hidden_hbm, hidden_ref), (branch_hbm, branch_ref), (h1_hbm, h1_ref)], load_sem
    )
    step, steps = pl.program_id(0), pl.num_programs(0)
    tile, width = g_ref.shape
    f32, bf16 = jnp.float32, jnp.bfloat16
    factor = 1.0 / math.sqrt(HEAD_DIM)

    @pl.when(step == 0)
    def _():
        load()
        greet(chips, True, extras.rows)
        start_swaps()
        start_rows()
        dk_acc[...] = jnp.zeros_like(dk_acc)
        dv_acc[...] = jnp.zeros_like(dv_acc)

        loaded(0, 1)

    pl.when(step == steps // 2)(middle)
    put(step, lambda rows: hidden_ref.at[rows], red_ref)

    pl.when(step == 0)(lambda: hop(step))
    over_rows = (((0,), (0,)), ((), ()))
    rows = pl.ds(pl.multiple_of(step * tile, tile), tile)
    lanes = head_lanes((tile, width))
    nothing = jnp.zeros((), bf16)
    grad = jnp.where(q_place[...] < length_ref[0], g_ref[...], nothing)
    both = grad.astype(f32) * o_all[rows].astype(f32)
    queries = q_ref[rows]
    grad_q = jnp.zeros((tile, width), f32)
    for head in range(width // HEAD_DIM):
        here = lanes == head
        block = pl.ds(head * tile, tile)
        delta = jnp.sum(jnp.where(here, both, 0.0), axis=-1, keepdims=True)
        one_grad = jnp.where(here, grad, nothing)
        gm_ref[block] = one_grad
        qm_ref[block] = jnp.where(here, queries, nothing)
        grad_p = lax.dot_general(
            one_grad, v_ref[...], (((1,), (1,)), ((), ())), preferred_element_type=f32
        )
        grad_s = (p_ref[head].astype(f32) * (grad_p - delta)).astype(bf16)
        ds_ref[block] = grad_s
        grad_q = jnp.where(here, jnp.dot(grad_s, k_ref[...], preferred_element_type=f32), grad_q)
    heads = width // HEAD_DIM
    dv_acc[...] += lax.dot_general(
        p_ref[...].reshape(heads * tile, p_ref.shape[2]), gm_ref[...], over_rows,
        preferred_element_type=f32,
    )
    dk_acc[...] += lax.dot_general(ds_ref[...], qm_ref[...], over_rows, preferred_element_type=f32)

    def back(value, cosine, sine):
        value = (value * factor).astype(bf16).astype(f32)
        cosine, sine = spread_table(cosine, width), spread_table(sine, width)
        return (value * cosine - partner(value) * sine).astype(bf16)

    mixed_ref[rows, :width] = back(grad_q, cos_ref[rows], sin_ref[rows])
    pl.when(step == 0)(lambda: loaded(2))
    share = dw_ref.shape[0] // chips
    cols = pl.ds(pl.multiple_of(step * share, share), share)
    dw_ref[cols, 3 * width :] = lax.dot_general(
        branch_ref[:, cols], o_all[...], over_rows, preferred_element_type=f32
    ).astype(bf16)
    pl.when((step > 0) & (step < steps - 1))(lambda: hop(step))

    @pl.when(step == steps - 1)
    def _():
        mixed_ref[:, width : 2 * width] = back(dk_acc[...], cos_ref[...], sin_ref[...])
        mixed_ref[:, 2 * width :] = dv_acc[...].astype(bf16)
        loaded(3)
        deep = 256

        def one(i, _):
            at = pl.ds(pl.multiple_of(i * deep, deep), deep)
            dw_ref[at, : 3 * width] = lax.dot_general(
                h1_ref[:, at], mixed_ref[...], over_rows, preferred_element_type=f32
            ).astype(bf16)
            return 0

        lax.fori_loop(0, dw_ref.shape[0] // deep, one, 0)
        wait_rows()
        finish()
        wait_swaps()


def attend_back(
    cid, q, k, v, o, g, p, cosine, sine, place, length, hidden, w_red, branch_all, h1_all, extras, cuts=2
):
    seq, width = q.shape
    heads = width // HEAD_DIM
    nb = lax.axis_size("blk")
    tile = seq // (nb // 2)
    wide, units = w_red.shape
    full = once(seq, width)
    f32, bf16 = jnp.float32, jnp.bfloat16
    loads = (hidden, w_red, branch_all, h1_all)
    return pl.pallas_call(
        functools.partial(attend_back_kernel, nb // 2, cuts, 1024, extras),
        grid=(seq // tile,),
        in_specs=[
            full, full, full, full,
            pl.BlockSpec((tile, width), lambda i: (i, 0)),
            pl.BlockSpec((heads, tile, seq), lambda i: (0, i, 0)),
            once(seq, 2 * HEAD_DIM), once(seq, 2 * HEAD_DIM),
            pl.BlockSpec((tile, 1), lambda i: (i, 0)),
            pl.BlockSpec(memory_space=pltpu.SMEM),
        ]
        + [ANY] * 4
        + extras.specs,
        out_specs=[
            once(seq, 3 * width), once(seq // nb, wide), once(wide, 4 * width)
        ]
        + extras.specs,
        out_shape=[
            jax.ShapeDtypeStruct((seq, 3 * width), bf16),
            jax.ShapeDtypeStruct((seq // nb, wide), f32),
            jax.ShapeDtypeStruct((wide, 4 * width), bf16),
        ]
        + extras.shapes,
        scratch_shapes=[
            pltpu.VMEM((heads * tile, seq), bf16),
            pltpu.VMEM((heads * tile, width), bf16),
            pltpu.VMEM((heads * tile, width), bf16),
            pltpu.VMEM((seq, width), f32),
            pltpu.VMEM((seq, width), f32),
        ]
        + [pltpu.VMEM(value.shape, value.dtype) for value in loads]
        + [pltpu.SemaphoreType.DMA((4,))]
        + scatter_scratch(nb // 2, cuts, seq // nb, wide)
        + extras.scratch,
        compiler_params=params(cid),
        cost_estimate=cost(10 * seq * seq * width),
    )(q, k, v, o, g, p, cosine, sine, place, length.reshape(1), *loads, *extras.operands)


def arrange(weight, out, parts):
    nb, _, wide = out.shape
    span = wide // parts
    for j in range(nb):
        for part in range(parts):
            at = (part * nb + j) * span
            out[j, :, part * span : (part + 1) * span] = weight[:, at : at + span].astype(out.dtype)


def first_kernel(parts, m, map_ref, tokens_ref, gain_ref, frequency_ref, *refs):
    n = len(parts)
    sources, dsts, later, refs = refs[:n], refs[n : n + m], refs[n + m : 2 * n], refs[2 * n :]
    (h1_ref, inverse_ref, place_ref, cos_ref, sin_ref), refs = refs[:5], refs[5:]
    weights, held, load_sem, sems = refs[:n], refs[n : n + m], refs[n + m], refs[n + m + 1 :]
    swaps = [swap_task(a, b, *sems[3 * i : 3 * i + 3]) for i, (a, b) in enumerate(zip(held, dsts))]
    load, loaded = mover(list(zip(sources, weights)), load_sem)
    load()
    greet(held[0].shape[0] // 2, True)
    for i in range(m):
        loaded(i)
        arrange(weights[i], held[i], parts[i])
        swaps[i][0]()
    _, inverse_ref[...], h1_ref[...] = norm_forward(
        tokens_ref[...].astype(jnp.float32), gain_ref[...]
    )
    for i in range(m, n):
        loaded(i)
        arrange(weights[i], later[i - m], parts[i])
    blocks = map_ref.shape[1]
    block = place_ref.shape[0] // blocks
    lanes = cos_ref.shape[1]
    front = lax.broadcasted_iota(jnp.int32, (block, lanes), 1) % HEAD_DIM < HEAD_DIM // 2
    for j in range(blocks):
        rows = slice(j * block, (j + 1) * block)
        place = map_ref[0, j] * block + lax.broadcasted_iota(jnp.int32, (block, lanes), 0)
        place_ref[rows] = place[:, :1]
        angle = place.astype(jnp.float32) * frequency_ref[...]
        cos_ref[rows] = jnp.cos(angle)
        sine = jnp.sin(angle)
        sin_ref[rows] = jnp.where(front, -sine, sine)
    for _, wait in swaps:
        wait()


def first(cid, block_map, tokens, gain, weights, parts, m):
    nb = lax.axis_size("blk")
    shapes = [(nb, value.shape[0], value.shape[1] // nb) for value in weights]
    n = len(weights)
    t, width = tokens.shape
    half = HEAD_DIM // 2
    frequency = jnp.exp(
        -jnp.arange(half, dtype=jnp.float32) * (2.0 / HEAD_DIM) * math.log(theta_base)
    )
    dma, f32 = pltpu.SemaphoreType.DMA, jnp.float32
    table = jax.ShapeDtypeStruct((nb * t, 2 * HEAD_DIM), f32)
    return pl.pallas_call(
        functools.partial(first_kernel, parts, m),
        out_shape=[jax.ShapeDtypeStruct(shape, jnp.bfloat16) for shape in shapes]
        + [
            jax.ShapeDtypeStruct((t, width), jnp.bfloat16),
            jax.ShapeDtypeStruct((t, 1), f32),
            jax.ShapeDtypeStruct((nb * t, 1), jnp.int32),
            table,
            table,
        ],
        in_specs=[pl.BlockSpec(memory_space=pltpu.SMEM)] + [VMEM] * 3 + [ANY] * n,
        out_specs=[ANY] * m + [VMEM] * (n - m + 5),
        scratch_shapes=[pltpu.VMEM(value.shape, value.dtype) for value in weights]
        + [pltpu.VMEM(shape, jnp.bfloat16) for shape in shapes[:m]]
        + [dma((n,))] + [dma, dma((nb,)), dma((nb,))] * m,
        compiler_params=params(cid),
        cost_estimate=cost(0),
    )(block_map, tokens, gain[None], jnp.tile(frequency, 4)[None], *weights)


def total_task(nr, nb, x_ref, o_ref, held, rows_held, send_one, recv_one, send_two, recv_two):
    r, b = lax.axis_index("rows"), lax.axis_index("blk")
    across = [lax.rem(b + k, nb) for k in range(1, nb)]
    along = [lax.rem(r + k, nr) for k in range(1, nr)]

    def first(other, slot):
        return pltpu.make_async_remote_copy(
            src_ref=rows_held.at[r], dst_ref=rows_held.at[slot], send_sem=send_two.at[other],
            recv_sem=recv_two.at[slot], device_id=(other, b), device_id_type=MESH,
        )

    def second(other, slot):
        return pltpu.make_async_remote_copy(
            src_ref=held.at[b], dst_ref=held.at[slot], send_sem=send_one.at[other],
            recv_sem=recv_one.at[slot], device_id=(r, other), device_id_type=MESH,
        )

    def start():
        rows_held[r] = x_ref[...]
        for other in along:
            first(other, r).start()

    def middle():
        for other in along:
            first(other, other).wait_recv()
        held[b] = jnp.sum(rows_held[...], axis=0)
        for other in across:
            second(other, b).start()

    def finish():
        for other in across:
            second(other, other).wait_recv()
        o_ref[...] = jnp.sum(held[...], axis=0)
        for other in along:
            first(other, r).wait_send()
        for other in across:
            second(other, b).wait_send()

    return start, middle, finish


def last_scatter_kernel(
    chips, nr, cuts, tile, extras, a_ref, w_ref, x_ref, inverse_ref, gain_ref, resid_ref, gain_two_ref, h1_hbm, *refs
):
    n = extras.n
    srcs, refs = refs[:n], refs[n:]
    o_ref, total_ref, dsts, refs = refs[0], refs[1], refs[2 : 2 + n], refs[2 + n :]
    sum_ref, part_ref, h1_ref, load_sem, refs = refs[0], refs[1], refs[2], refs[3], refs[4:]
    put, _, hop, finish = scatter_task(chips, cuts, tile, sum_ref, refs[:4], refs[4:10])
    start_total, middle_total, finish_total = total_task(
        nr, 2 * chips, part_ref, total_ref, *refs[10:16]
    )
    start_swaps, start_rows, middle, wait_rows, wait_swaps = extras.tasks(srcs, dsts, refs[16:])
    load, loaded = mover([(h1_hbm, h1_ref)], load_sem)
    load()
    greet(chips, True, True)
    start_swaps()
    start_rows()
    part_ref[0:1] = jnp.zeros_like(part_ref[0:1])
    part_ref[1:2] = gain_two_ref[...]
    loaded()

    def seen(rows, cols, got):
        part_ref[0:1, cols] += jnp.sum(got * h1_ref[rows, cols].astype(jnp.float32), axis=0)[None]

    for s in range(chips):
        put(s, lambda rows: a_ref.at[rows], w_ref, seen)
        if s < chips - 1:
            hop(s)
    part_ref[0:1] = part_ref[0:1] / gain_ref[...]
    start_total()
    middle()
    middle_total()
    wait_rows()
    finish()
    inverse = inverse_ref[...]
    unit = x_ref[...].astype(jnp.float32) * inverse
    o_ref[...] = resid_ref[...] + norm_backward(sum_ref[...], unit, inverse, gain_ref[...])[0]
    finish_total()
    wait_swaps()


def last_scatter(cid, a, w, x, inverse, gain, resid, gain_two, h1_all, extras, cuts=2, tile=1024):
    nr, nb = lax.axis_size("rows"), lax.axis_size("blk")
    t, width = x.shape
    pair = (2, width)
    dma, f32 = pltpu.SemaphoreType.DMA, jnp.float32
    return pl.pallas_call(
        functools.partial(last_scatter_kernel, nb // 2, nr, cuts, tile, extras),
        out_shape=[jax.ShapeDtypeStruct((t, width), f32), jax.ShapeDtypeStruct(pair, f32)]
        + extras.shapes,
        in_specs=[VMEM] * 7 + [ANY] + extras.specs,
        out_specs=[VMEM] * 2 + extras.specs,
        scratch_shapes=[
            pltpu.VMEM((t, width), f32),
            pltpu.VMEM(pair, f32),
            pltpu.VMEM(h1_all.shape, h1_all.dtype),
            dma((1,)),
        ]
        + scatter_scratch(nb // 2, cuts, t, width)
        + [pltpu.VMEM((nb,) + pair, f32), pltpu.VMEM((nr,) + pair, f32)]
        + [dma((nb,))] * 2 + [dma((nr,))] * 2
        + extras.scratch,
        compiler_params=params(cid),
        cost_estimate=cost(2 * a.shape[0] * width * w.shape[1]),
    )(a, w, x, inverse, gain[None], resid, gain_two, h1_all, *extras.operands)


def step_kernel(parts, one_array, *refs):
    count = 1 if one_array else parts
    grads, refs = refs[:count], refs[count:]
    outs = len(refs) // 2
    rule = adam_step if outs == 3 else moment_step

    def go(grad):
        wide = grad.shape[2]
        for j in range(grad.shape[0]):
            cols = slice(j * wide, (j + 1) * wide)
            gradient = grad[j].astype(jnp.float32)
            for ref, value in zip(
                refs[outs:], rule(*[ref[:, cols] for ref in refs[:outs]], gradient)
            ):
                ref[:, cols] = value

    if one_array:
        go(grads[0])
        return
    for part, grad in enumerate(grads):
        pl.when(pl.program_id(0) == part)(functools.partial(go, grad))


def step(pieces, parts, states, first=0):
    one_array = not isinstance(pieces, list)
    pieces = [pieces] if one_array else pieces
    nb = pieces[0].shape[0]
    rows, columns = states[0].shape
    tile = min(rows, 64 if parts > 1 else 32)
    span = columns // parts
    at = pl.BlockSpec((tile, span), lambda part, i: (i, part))
    block = (nb, tile, span // nb)
    if one_array:
        grads = [pl.BlockSpec(block, lambda part, i: (0, i, first + part))]
    else:
        grads = [pl.BlockSpec(block, lambda part, i: (0, i, 0))] * parts
    outs = len(states)
    return pl.pallas_call(
        functools.partial(step_kernel, parts, one_array),
        grid=(parts, rows // tile),
        in_specs=grads + [at] * outs,
        out_specs=[at] * outs,
        out_shape=[jax.ShapeDtypeStruct((rows, columns), jnp.float32)] * outs,
        compiler_params=pltpu.CompilerParams(vmem_limit_bytes=60 * MIB),
        cost_estimate=pl.CostEstimate(
            flops=0, bytes_accessed=(8 * outs + 2) * rows * columns, transcendentals=0
        ),
    )(*pieces, *states)


def after(value, *others):
    return lax.optimization_barrier((value,) + others)[0]


def over_tokens(left, right):
    return lax.dot_general(
        left, right, (((0,), (0,)), ((), ())), preferred_element_type=jnp.float32
    )


def shards(
    tokens, cotangent, lengths, block_map, gain_attend, gain_expand,
    attend_in, attend_out, expand_in, reduce_out,
    attend_in_first, attend_out_first, expand_in_first, reduce_out_first,
    attend_in_second, attend_out_second, expand_in_second, reduce_out_second,
):
    nb = lax.axis_size("blk")
    length = lengths[0]
    swap_in, swap_out, swap_red, pieces_gu, h1, inverse_one, place, cosine, sine = first(
        2, block_map, tokens[0], gain_attend,
        (attend_in, attend_out.T, reduce_out.T, expand_in), (3, 1, 1, 2), 3,
    )
    block_rows = tokens.shape[1] // 2
    row_place = (block_map[0][:, None] * block_rows + jnp.arange(block_rows)[None, :]).reshape(1, -1)
    live_place = jnp.where(row_place < length, row_place, jnp.int32(1 << 30))
    nr = lax.axis_size("rows")
    deep = nb * attend_in.shape[0]
    wide = tokens.shape[2]

    def flat(pieces):
        return pieces.reshape(deep, pieces.shape[2])

    h1_all, swap_gu, w_in, w_out, w_red = line_gather(
        3, h1,
        Extras([pieces_gu], [(flat(value), 0, deep) for value in (swap_in, swap_out, swap_red)]),
    )
    w_in, w_out, w_red = [value.reshape(wide, -1) for value in (w_in, w_out, w_red)]
    early = deep * 5 // 8
    attended, q, k, v, p, g_all, gu_early = attend(
        4, h1_all, w_in, cosine, sine, place, live_place, length, cotangent[0],
        Extras([], [(flat(swap_gu), 0, early)]),
    )
    x1, inverse_two, h2, gu_late = attend_out_sum(
        5, attended, w_out, tokens[0], gain_expand,
        Extras([], [(flat(swap_gu), early, deep - early)]),
    )

    def by_rows(gradient):
        return gradient.reshape(nr, nb, deep // nb, gradient.shape[1])

    grad_x1, branch, gain_two, hidden, part_gate, part_up, rows_reduce = feed_forward(
        6, h2, x1, inverse_two, gain_expand, cotangent[0], gu_early, gu_late, w_red, g_all
    )
    branch_all, grad_o, rows_gate = gather_dot(
        9, branch, w_out, Extras([], [], [by_rows(part_gate)])
    )
    grad_mixed, y, part_both, own_reduce, rows_up = attend_back(
        10, q, k, v, attended, grad_o, p, cosine, sine, place, length,
        hidden, w_red, branch_all, h1_all, Extras([rows_reduce], [], [by_rows(part_up)]),
    )
    y = x1 + y
    grad_input, gains, own_gate, own_up, rows_both = last_scatter(
        11, grad_mixed, w_in, tokens[0], inverse_one, gain_attend, grad_x1, gain_two, h1_all,
        Extras([rows_gate, rows_up], [], [by_rows(part_both)]),
    )
    both = lax.all_to_all(rows_both, "blk", 0, 0, tiled=True)
    set_four = step(own_reduce, 1, (reduce_out.T, reduce_out_first.T, reduce_out_second.T))
    set_three = step([own_gate, own_up], 2, (expand_in, expand_in_first, expand_in_second))
    both = after(both, set_three[2], set_four[2])
    set_one = step(both, 3, (attend_in, attend_in_first, attend_in_second))
    set_two = step(both, 1, (attend_out_first.T, attend_out_second.T), 3)
    return (
        y.astype(jnp.bfloat16).reshape(tokens.shape),
        grad_input.reshape(tokens.shape),
        gains[0],
        gains[1],
        *set_one,
        *[value.T for value in set_two],
        *set_three,
        *[value.T for value in set_four],
    )


def solution(mesh):
    placed = (
        P("rows", "blk", None),
        P("rows", "blk", None),
        P("rows"),
        P("rows", None),
        P(),
        P(),
        P(("rows", "blk"), None),
        P(None, ("rows", "blk")),
        P(("rows", "blk"), None),
        P(None, ("rows", "blk")),
        P(("rows", "blk"), None),
        P(None, ("rows", "blk")),
        P(("rows", "blk"), None),
        P(None, ("rows", "blk")),
        P(("rows", "blk"), None),
        P(None, ("rows", "blk")),
        P(("rows", "blk"), None),
        P(None, ("rows", "blk")),
    )
    return jax.shard_map(
        shards,
        mesh=mesh,
        in_specs=placed,
        out_specs=(
            P("rows", "blk", None),
            P("rows", "blk", None),
            P(),
            P(),
            P(("rows", "blk"), None),
            P(("rows", "blk"), None),
            P(("rows", "blk"), None),
            P(None, ("rows", "blk")),
            P(None, ("rows", "blk")),
            P(("rows", "blk"), None),
            P(("rows", "blk"), None),
            P(("rows", "blk"), None),
            P(None, ("rows", "blk")),
            P(None, ("rows", "blk")),
            P(None, ("rows", "blk")),
        ),
        check_vma=False,
    )
```

time: 571 us -> 565 us (0.989)
  Pallas kernels: 512 us -> 535 us
  between operations: 15.5 us -> 1.84 us
  other arithmetic: 13.6 us -> 2.25 us
    pallas_call x11 -> x10, Pallas kernels: 372 us -> 392 us  [the longest x1 95.8 us: feed_forward(): pl.pallas_call(functools.partial(feed_forward_kernel, nb // 2, cuts, tile...]
  transfers between devices with their start and end apart: 9 -> 1, of which waited for: 1 -> 1; matrix products, arithmetic and copies ran while one was open for 2% -> 0% of each run, Pallas kernels for 84% -> 3%
where the time goes in v5:
time: 565 us; the launch traced here: 556 us
  Pallas kernels  535 us (95%)
  waiting for transfers between devices  8.9 us (2%)
    pallas_call x1, Pallas kernels, feed_forward(): pl.pallas_call(functools.partial(feed_forward_kernel, nb // 2, cuts, tile...  95.8 us
    pallas_call x1, Pallas kernels, line_gather(): pl.pallas_call(functools.partial(gather_kernel, nb // 2, cuts, extras), o...  83.9 us
    pallas_call x1, Pallas kernels, last_scatter(): pl.pallas_call(functools.partial(last_scatter_kernel, nb // 2, nr, cuts,...  80.5 us
    pallas_call x1, Pallas kernels, attend_back(): pl.pallas_call(functools.partial(attend_back_kernel, nb // 2, cuts, 1024,...  63 us
    pallas_call x1, Pallas kernels, attend(): pl.pallas_call(functools.partial(attend_kernel, nb // 2, cuts, extras), g...  50.6 us
    pallas_call x1, Pallas kernels, first(): pl.pallas_call(functools.partial(first_kernel, parts, m), out_shape=[jax....  47.6 us
    pallas_call x1, Pallas kernels, gather_dot(): pl.pallas_call(functools.partial(gather_dot_kernel, nb // 2, cuts, extras...  45 us
    pallas_call x1, Pallas kernels, attend_out_sum(): pl.pallas_call(functools.partial(attend_out_kernel, nb // 2, cuts, tile,...  44.3 us
  transfers between devices with their start and end apart: 1, of which 1 were waited for; matrix products, arithmetic and copies ran while one was open for 0% of the time, Pallas kernels for 3%

profile of v5, /device:TPU:0, one launch (start us, length us, event | category | flops | bytes accessed | tf_op | source)
XLA Modules:
  0.0 556.2 jit_solution(711102016897338123)
XLA Ops:
  1.3 0.7 multiply_bitcast_fusion
  2.0 0.6 broadcast_in_dim_tile.3.frequency_ref
  2.6 0.1 iota_add_fusion
  2.6 0.1 add.32
  2.7 0.6 compare_select_fusion.k_place
  3.3 47.6 %shard_map.289 = (bf16[8,64,768]{2,1,0:T(8,128)(2,1)}, bf16[8,64,256]{2,1,0:T(8,128)(2,1)}, bf16[8,64,1024]{2,1,0:T(8,128)(2,1)}, bf16[8,64,2048]{2,1,0:T(8,128)...) custom-call(s32[1,16]{1,0:T(1,128)} %map_ref.1, ...), custom_call_target="tpu_custom_call" | custom-call | bytes 150000000 | tf_op jit(solution)/shard_map/pallas_call | solution.py:1336
  50.9 83.9 %shard_map.290 = (bf16[1024,2048]{1,0:T(8,128)(2,1)}, bf16[8,64,2048]{2,1,0:T(8,128)(2,1)}, bf16[4,512,768]{2,1,0:T(8,128)(2,1)}, bf16[4,512,256]{2,1,0:T(8,128)(2,1)}, bf16[4,512,1024]{2,1,0:T(8,128)(2,1)}) custom-call(bf16[128,2048]{1,0:T(8,128)(2,1)} %get-tuple-element.72.x_ref, bf16[8,64,2048]{2,1,0:T(8,128)(2,1)} %get-tuple-element.73.refs_0_, ...), custom_call_target="tpu_custom_call" | custom-call | bytes 150000000 | tf_op jit(solution)/shard_map/pallas_call | solution.py:446
  134.9 50.6 %shard_map.291 = (bf16[1024,256]{1,0:T(8,128)(2,1)}, bf16[1024,256]{1,0:T(8,128)(2,1)}, bf16[1024,256]{1,0:T(8,128)(2,1)}, bf16[1024,256]{1,0:T(8,128)(2,1)}, bf...) custom-call(bf16[1024,2048]{1,0:T(8,128)(2,1)} %get-tuple-element.77.h1_hbm, ...), custom_call_target="tpu_custom_call" | custom-call | flops 4294967296 | bytes 150000000 | tf_op jit(solution)/shard_map/pallas_call | solution.py:1102
  185.5 44.3 %shard_map.292 = (f32[128,2048]{1,0:T(8,128)}, f32[128,1]{1,0:T(8,128)}, bf16[128,2048]{1,0:T(8,128)(2,1)}, bf16[4,192,2048]{2,1,0:T(8,128)(2,1)}) custom-call(bf16[1024,256]{1,0:T(8,128)(2,1)} %get-tuple-element.83.a_ref.o_all, bf16[2048,256]{1,0:T(8,128)(2,1)} %bitcast.44, bf16[128,2048]{1,0:T(8,128)(2,1)} %bitcast.37, f32[1,2048]{1,0:T(1,128)} %bitcast.61, ...), custom_call_target="tpu_custom_call" | custom-call | flops 1073741824 | bytes 150000000 | tf_op jit(solution)/shard_map/pallas_call | solution.py:948
  229.8 95.8 %shard_map.293 = (f32[128,2048]{1,0:T(8,128)}, bf16[128,2048]{1,0:T(8,128)(2,1)}, f32[1,2048]{1,0:T(1,128)}, bf16[1024,1024]{1,0:T(8,128)(2,1)}, bf16[2048,1024]...) custom-call(bf16[128,2048]{1,0:T(8,128)(2,1)} %get-tuple-element.89.h2_here, ...), custom_call_target="tpu_custom_call" | custom-call | flops 38654705664 | bytes 150000000 | tf_op jit(solution)/shard_map/pallas_call | solution.py:886
  325.6 45.0 %shard_map.294 = (bf16[1024,2048]{1,0:T(8,128)(2,1)}, bf16[1024,256]{1,0:T(8,128)(2,1)}, bf16[8,64,1024]{2,1,0:T(8,128)(2,1)}) custom-call(bf16[128,2048]{1,0:T(8,128)(2,1)} %get-tuple-element.95.x_ref, bf16[2048,256]{1,0:T(8,128)(2,1)} %bitcast.45, bf16[4,8,64,1024]{3,2,1,0:T(8,128)(2,1)} %bitcast.43), custom_call_target="tpu_custom_call" | custom-call | flops 1073741824 | bytes 150000000 | tf_op jit(solution)/shard_map/pallas_call | solution.py:512
  370.7 63.0 %shard_map.295 = (bf16[1024,768]{1,0:T(8,128)(2,1)}, f32[128,2048]{1,0:T(8,128)}, bf16[2048,1024]{1,0:T(8,128)(2,1)}, bf16[8,64,1024]{2,1,0:T(8,128)(2,1)}, bf16[8,64,1024]{2,1,0:T(8,128)(2,1)}) custom-call(bf16[1024,256]{1,0:T(8,128)(2,1)} %get-tuple-element.86.q_ref, bf16[1024,256]{1,0:T(8,128)(2,1)} %get-tuple-element.87.k_ref, ...), custom_call_target="tpu_custom_call" | custom-call | flops 2684354560 | bytes 150000000 | tf_op jit(solution)/shard_map/pallas_call | solution.py:1242
  433.7 80.5 %shard_map.296 = (f32[128,2048]{1,0:T(8,128)}, f32[2,2048]{1,0:T(2,128)}, bf16[8,64,1024]{2,1,0:T(8,128)(2,1)}, bf16[8,64,1024]{2,1,0:T(8,128)(2,1)}, bf16[8,64,1024]{2,1,0:T(8,128)(2,1)}) custom-call(bf16[1024,768]{1,0:T(8,128)(2,1)} %get-tuple-element.104.a_ref, bf16[2048,768]{1,0:T(8,128)(2,1)} %bitcast.47, bf16[128,2048]{1,0:T(8,128)(2,1)} %bitcast.38, ...), custom_call_target="tpu_custom_call" | custom-call | flops 3221225472 | bytes 150000000 | tf_op jit(solution)/shard_map/pallas_call | solution.py:1443
  514.2 4.8 all-to-all-start
  518.9 5.7 %shard_map.298 = (f32[64,8192]{1,0:T(8,128)}, f32[64,8192]{1,0:T(8,128)}, f32[64,8192]{1,0:T(8,128)}) custom-call(bf16[8,64,1024]{2,1,0:T(8,128)(2,1)} %get-tuple-element.117.refs_0_, f32[64,8192]{1,0:T(8,128)} %bitcast.35, f32[64,8192]{1,0:T(8,128)} %bitcast.48, f32[64,8192]{1,0:T(8,128)} %bitcast.49), custom_call_target="tpu_custom_call" | custom-call | bytes 13631488 | tf_op jit(solution)/shard_map/pallas_call | solution.py:1501
  524.7 0.0 copy-start.4
  524.7 0.0 copy-start.1
  524.7 0.0 copy-start.2
  524.7 10.4 %shard_map.297 = (f32[64,16384]{1,0:T(8,128)}, f32[64,16384]{1,0:T(8,128)}, f32[64,16384]{1,0:T(8,128)}) custom-call(bf16[8,64,1024]{2,1,0:T(8,128)(2,1)} %get-tuple-element.114.refs_0_, bf16[8,64,1024]{2,1,0:T(8,128)(2,1)} %get-tuple-element.115.refs_1_, f32[64,16384]{1,0:T(8,128)} %refs_2_.2, f32[64,16384]{1,0:T(8,128)} %refs_3_.4, f32[64,16384]{1,0:T(8,128)} %refs_4_.1), custom_call_target="tpu_custom_call" | custom-call | bytes 27262976 | tf_op jit(solution)/shard_map/pallas_call | solution.py:1501
  535.1 0.0 copy-done.4
  535.1 0.6 fusion.1
  535.7 0.0 copy-done.1
  535.7 0.0 copy-done.2
  535.7 0.9 fusion
  536.6 8.9 %all-to-all-done.refs_0_ = bf16[8,64,1024]{2,1,0:T(8,128)(2,1)S(1)} async-done(((bf16[8,64,1024]{2,1,0:T(8,128)(2,1)}), bf16[8,64,1024]{2,1,0:T(8,128)(2,1)S(1)}, u32[]{:S(2)}, u32[]{:S(2)}) %all-to-all-start) | async-done | bytes 1048608 | tf_op jit(solution)/shard_map/all_to_all | solution.py:1579
  545.5 0.0 copy-start
  545.5 1.0 copy-done
  546.5 2.2 shard_map.300
  548.7 0.0 copy-start.3
  548.7 6.1 %shard_map.299 = (f32[64,6144]{1,0:T(8,128)}, f32[64,6144]{1,0:T(8,128)}, f32[64,6144]{1,0:T(8,128)}) custom-call(bf16[8,64,1024]{2,1,0:T(8,128)(2,1)} %copy-done, f32[64,6144]{1,0:T(8,128)} %refs_1_.1, f32[64,6144]{1,0:T(8,128)} %refs_2_.3, f32[64,6144]{1,0:T(8,128)} %refs_3_.5), custom_call_target="tpu_custom_call" | custom-call | bytes 10223616 | tf_op jit(solution)/shard_map/pallas_call | solution.py:1501
  554.8 0.0 copy-done.3
  554.8 1.0 copy.35
  (2 shorter events, 0.0 us)
Async XLA Ops:
  514.2 31.4 %all-to-all-start = ((bf16[8,64,1024]{2,1,0:T(8,128)(2,1)}), bf16[8,64,1024]{2,1,0:T(8,128)(2,1)S(1)}, u32[]{:S(2)}, u32[]{:S(2)}) async-start(bf16[8,64,1024]{2,1,0:T(8,128)(2,1)} %get-tuple-element.113), calls=%async_computation | async-start | bytes 2097152 | tf_op jit(solution)/shard_map/all_to_all | solution.py:1579
  524.7 10.4 %copy-start.4 = (f32[2,2048]{1,0:T(2,128)S(1)}, f32[2,2048]{1,0:T(2,128)}, u32[]{:S(2)}) copy-start(f32[2,2048]{1,0:T(2,128)} %get-tuple-element.112) | copy-start | bytes 49156
  524.7 11.0 %copy-start.1 = (f32[128,2048]{1,0:T(8,128)S(1)}, f32[128,2048]{1,0:T(8,128)}, u32[]{:S(2)}) copy-start(f32[128,2048]{1,0:T(8,128)} %get-tuple-element.85.x1_ref) | copy-start | bytes 3145732
  524.7 11.0 %copy-start.2 = (f32[128,2048]{1,0:T(8,128)S(1)}, f32[128,2048]{1,0:T(8,128)}, u32[]{:S(2)}) copy-start(f32[128,2048]{1,0:T(8,128)} %get-tuple-element.103) | copy-start | bytes 3145732
  545.5 1.0 copy-start
  548.7 6.1 %copy-start.3 = (f32[128,2048]{1,0:T(8,128)S(1)}, f32[128,2048]{1,0:T(8,128)}, u32[]{:S(2)}) copy-start(f32[128,2048]{1,0:T(8,128)} %get-tuple-element.111) | copy-start | bytes 3145732

commit v6 on v5

--- a/solution.py
+++ b/solution.py
@@ -454,73 +454,14 @@
     )(x, *extras.operands)
 
 
-def gather_dot_kernel(chips, cuts, extras, x_ref, w_ref, *refs):
-    n = extras.n
-    srcs, outs, dsts, refs = refs[:n], refs[n : n + 2], refs[n + 2 : 2 * n + 2], refs[2 * n + 2 :]
-    held, save_sem, refs = refs[:2], refs[2], refs[3:]
-    o_ref, prod_ref = held
-    begin, hop, from_side, local, finish = gather_task(chips, cuts, x_ref, o_ref, refs[:5])
-    start_swaps, start_rows, middle, wait_rows, wait_swaps = extras.tasks(srcs, dsts, refs[5:])
-    r, z, c = line_place()
-    t = x_ref.shape[0]
-    greet(chips, False, extras.rows)
-    begin()
-    start_rows()
-
-    def rows_of(y):
-        return pl.ds(pl.multiple_of(y * 2 * t, 2 * t), 2 * t)
-
-    def saves(y):
-        return mover([(a.at[rows_of(y)], b.at[rows_of(y)]) for a, b in zip(held, outs)], save_sem.at[y])
-
-    def dot(y):
-        rows = rows_of(y)
-        prod_ref[rows] = jnp.dot(
-            o_ref[rows], w_ref[...], preferred_element_type=jnp.float32
-        ).astype(prod_ref.dtype)
-        saves(y)[0]()
-
-    from_side(z)
-    local().wait()
-    dot(z)
-    for k in range(1, chips):
-        hop(k)
-
-        @pl.when(z - k >= 0)
-        def _():
-            from_side(z - k)
-            dot(z - k)
-
-        @pl.when(z + k < chips)
-        def _():
-            from_side(z + k)
-            dot(z + k)
-
-        if k == max(1, chips - 2):
-            middle()
-    finish()
-    for y in range(chips):
-        saves(y)[1]()
-    wait_rows()
-
-
-def gather_dot(cid, x, w, extras, cuts=2):
-    nb = lax.axis_size("blk")
-    all_rows = nb * x.shape[0]
-    dma, bf16 = pltpu.SemaphoreType.DMA, jnp.bfloat16
-    shapes = [(all_rows, x.shape[1]), (all_rows, w.shape[1])]
-    return pl.pallas_call(
-        functools.partial(gather_dot_kernel, nb // 2, cuts, extras),
-        out_shape=[jax.ShapeDtypeStruct(shape, bf16) for shape in shapes] + extras.shapes,
-        in_specs=[VMEM, VMEM] + extras.specs,
-        out_specs=[ANY] * 2 + extras.specs,
-        scratch_shapes=[pltpu.VMEM(shape, bf16) for shape in shapes]
-        + [dma((nb // 2, 2))]
-        + gather_sems(nb, cuts)
-        + extras.scratch,
-        compiler_params=params(cid),
-        cost_estimate=cost(2 * all_rows * w.shape[0] * w.shape[1]),
-    )(x, w, *extras.operands)
+def arrival_order(chips):
+    table = []
+    for z in range(chips):
+        row = [z]
+        for k in range(1, chips):
+            row += [y for y in (z - k, z + k) if 0 <= y < chips]
+        table.append(row)
+    return table
 
 
 def need_order(chips):
@@ -685,29 +626,8 @@
     )
 
 
-def attend_out_kernel(chips, cuts, tile, extras, a_ref, w_ref, x_ref, gain_ref, *refs):
-    n = extras.n
-    srcs, (x1_ref, inverse_ref, h2_ref), dsts, refs = (
-        refs[:n], refs[n : n + 3], refs[3 + n : 3 + 2 * n], refs[3 + 2 * n :],
-    )
-    put, _, hop, finish = scatter_task(chips, cuts, tile, x1_ref, refs[:4], refs[4:10])
-    start_swaps, start_rows, middle, wait_rows, wait_swaps = extras.tasks(srcs, dsts, refs[10:])
-    greet(chips, False, extras.rows)
-    start_rows()
-    for s in range(chips):
-        put(s, lambda rows: a_ref.at[rows], w_ref)
-        if s < chips - 1:
-            hop(s)
-    middle()
-    finish()
-    x1 = x_ref[...].astype(jnp.float32) + x1_ref[...]
-    x1_ref[...] = x1
-    _, inverse_ref[...], h2_ref[...] = norm_forward(x1, gain_ref[...])
-    wait_rows()
-
-
 def feed_forward_kernel(
-    chips, cuts, tile, h2_here, x1_ref, inverse_ref, gain_ref, cotangent_ref, early_hbm, late_hbm, red_hbm, g_hbm,
+    chips, cuts, tile, h2_here, x1_ref, inverse_ref, gain_ref, cotangent_ref, w_hbm, red_hbm, g_hbm,
     grad_out, low_out, gain_out, hidden_out, gate_out, up_out, reduce_out,
     h2_ref, hidden_ref, grad_ref, w_ref, red_ref, g_ref, dw_red, dw_ref, red_held,
     load_sem, save_sem, dw_sem, red_local, red_send, red_recv, *refs
@@ -718,23 +638,14 @@
     start_red, middle_red, wait_red = task(
         dw_red, reduce_out, red_held, red_local, red_send, red_recv
     )
-    nr, early, late = early_hbm.shape[0], early_hbm.shape[1], late_hbm.shape[1]
-    pairs = [(g_hbm, g_ref), (red_hbm, red_ref)]
-    for q in range(nr):
-        first = q * (early + late)
-        pairs += [
-            (early_hbm.at[q], w_ref.at[pl.ds(first, early)]),
-            (late_hbm.at[q], w_ref.at[pl.ds(first + early, late)]),
-        ]
-    load, loaded = mover(pairs, load_sem)
-    w_loads = range(2, len(pairs))
+    load, loaded = mover([(w_hbm, w_ref), (g_hbm, g_ref), (red_hbm, red_ref)], load_sem)
     r, z, c = line_place()
     t, width = h2_here.shape
     units = hidden_ref.shape[1]
     span = min(512, units)
     f32, low = jnp.float32, jnp.bfloat16
     over_rows = (((0,), (0,)), ((), ()))
-    load(*w_loads, 0, 1)
+    load()
     greet(chips, False, True)
     begin()
 
@@ -780,9 +691,9 @@
 
     from_side(z)
     local().wait()
-    loaded(*w_loads)
+    loaded(0)
     forward(z)
-    loaded(0, 1)
+    loaded(1, 2)
     put_at(z, backward, w_ref)
     deep = 256
     turns = width // deep
@@ -872,11 +783,11 @@
 
 
 def feed_forward(
-    cid, h2, x1, inverse, gain, cotangent, gu_early, gu_late, w_red, g_all, cuts=2, tile=1024
+    cid, h2, x1, inverse, gain, cotangent, w_gu, w_red, g_all, cuts=2, tile=1024
 ):
     nr, nb = lax.axis_size("rows"), lax.axis_size("blk")
     seq, width = g_all.shape
-    both = gu_early.shape[2]
+    both = w_gu.shape[1]
     units = both // 2
     t = seq // nb
     piece = width // (nr * nb)
@@ -894,7 +805,7 @@
             half,
             jax.ShapeDtypeStruct((nb, piece, units), bf16),
         ],
-        in_specs=[VMEM] * 5 + [ANY] * 4,
+        in_specs=[VMEM] * 5 + [ANY] * 3,
         out_specs=[VMEM] * 3 + [ANY] * 4,
         scratch_shapes=[
             pltpu.VMEM((seq, width), bf16),
@@ -906,7 +817,7 @@
             pltpu.VMEM((nr, nb, piece, units), bf16),
             pltpu.VMEM((2, 2, 256, units), bf16),
             pltpu.VMEM((slots, nb, piece, units), bf16),
-            dma((2 + 2 * nr,)),
+            dma((3,)),
             dma((nb // 2,)),
             dma((2, 2)),
             dma((4,)) if nr == 4 else dma,
@@ -917,7 +828,7 @@
         + scatter_scratch(nb // 2, cuts, t, width),
         compiler_params=params(cid),
         cost_estimate=cost(9 * seq * width * both),
-    )(h2, x1, inverse, gain[None], cotangent, gu_early, gu_late, w_red, g_all)
+    )(h2, x1, inverse, gain[None], cotangent, w_gu, w_red, g_all)
 
 
 def attend_out_kernel(chips, cuts, tile, extras, a_ref, w_ref, x_ref, gain_ref, *refs):
@@ -941,26 +852,6 @@
     wait_rows()
 
 
-def attend_out_sum(cid, a, w, x, gain, extras, cuts=2, tile=1024):
-    nb = lax.axis_size("blk")
-    t, width = x.shape
-    f32 = jnp.float32
-    return pl.pallas_call(
-        functools.partial(attend_out_kernel, nb // 2, cuts, tile, extras),
-        out_shape=[
-            jax.ShapeDtypeStruct((t, width), f32),
-            jax.ShapeDtypeStruct((t, 1), f32),
-            jax.ShapeDtypeStruct((t, width), jnp.bfloat16),
-        ]
-        + extras.shapes,
-        in_specs=[VMEM] * 4 + extras.specs,
-        out_specs=[VMEM] * 3 + extras.specs,
-        scratch_shapes=scatter_scratch(nb // 2, cuts, t, width) + extras.scratch,
-        compiler_params=params(cid),
-        cost_estimate=cost(2 * a.shape[0] * width * w.shape[1]),
-    )(a, w, x, gain[None], *extras.operands)
-
-
 def norm_forward(values, gain_vector):
     inverse = lax.rsqrt(jnp.mean(values * values, axis=-1, keepdims=True) + norm_eps)
     unit_values = values * inverse
@@ -1020,26 +911,30 @@
 
 
 def attend_kernel(
-    chips, cuts, extras, h1_hbm, w_hbm, cos_ref, sin_ref, q_place, k_place, length_ref, g_ref, *refs
+    chips, cuts, tile_o, extras, h1_hbm, w_hbm, cos_ref, sin_ref, q_place, k_place, length_ref, g_ref,
+    x_ref, gain_ref, w_out_ref, *refs
 ):
     n = extras.n
     srcs, refs = refs[:n], refs[n:]
-    o_ref, q_ref, k_ref, v_ref, p_ref, g_all = refs[:6]
-    dsts, (h1_ref, w_ref, load_sem), sems = refs[6 : 6 + n], refs[6 + n : 9 + n], refs[9 + n :]
+    (o_ref, q_ref, k_ref, v_ref, p_out, g_all, x1_ref, inverse_ref, h2_ref), refs = refs[:9], refs[9:]
+    dsts, (h1_ref, w_ref, p_ref, load_sem, p_sem), refs = refs[:n], refs[n : n + 5], refs[n + 5 :]
     load, loaded = mover([(w_hbm, w_ref), (h1_hbm, h1_ref)], load_sem)
-    begin, hop, from_side, local, finish = gather_task(chips, cuts, g_ref, g_all, sems[:5])
-    start_swaps, start_rows, middle, wait_rows, wait_swaps = extras.tasks(srcs, dsts, sems[5:])
+    begin, pass_on, from_side, local, sent = gather_task(chips, cuts, g_ref, g_all, refs[:5])
+    put, _, hop, finish = scatter_task(chips, cuts, tile_o, x1_ref, refs[5:9], refs[9:15])
+    start_swaps, start_rows, middle, wait_rows, wait_swaps = extras.tasks(srcs, dsts, refs[15:])
     step, steps = pl.program_id(0), pl.num_programs(0)
-    tile, width = o_ref.shape
+    seq, width = o_ref.shape
+    tile = seq // chips
     f32, bf16 = jnp.float32, jnp.bfloat16
+    table = need_order(chips)
+    _, z, _ = line_place()
 
     @pl.when(step == 0)
     def _():
         load()
-        greet(chips, extras.swaps > 0, extras.rows)
+        greet(chips, False, extras.rows)
         begin()
         start_rows()
-        start_swaps()
         loaded()
 
         def one(i, _):
@@ -1054,15 +949,24 @@
 
         lax.fori_loop(0, steps, one, 0)
 
-    @pl.when((step > 0) & (step < chips))
+    pl.when(step == steps - 1)(middle)
+
+    @pl.when(step > 0)
     def _():
-        hop(step)
-
-
-    rows = pl.ds(pl.multiple_of(step * tile, tile), tile)
+        pass_on(step)
+
+    def rows_at(s):
+        return pl.ds(pl.multiple_of(pick(table, z, s) * tile, tile), tile)
+
+    def save(s):
+        slot = lax.rem(s, 2)
+        return pltpu.make_async_copy(p_ref.at[slot], p_out.at[:, rows_at(s)], p_sem.at[slot])
+
+    pl.when(step >= 2)(lambda: save(step - 2).wait())
+    rows = rows_at(step)
     queries = q_ref[rows] * jnp.asarray(1.0 / math.sqrt(HEAD_DIM), bf16)
     lanes = head_lanes((tile, width))
-    place = q_place[...]
+    place = q_place[rows]
     allowed = k_place[...] <= place
     out = jnp.zeros((tile, width), f32)
     for head in range(width // HEAD_DIM):
@@ -1075,106 +979,147 @@
         weights = jnp.exp(scores - jnp.max(scores, axis=-1, keepdims=True))
         weights = weights * (1.0 / jnp.sum(weights, axis=-1, keepdims=True))
         low = weights.astype(bf16)
-        p_ref[head] = low
+        p_ref[lax.rem(step, 2), head] = low
         out = jnp.where(here, jnp.dot(low, v_ref[...], preferred_element_type=f32), out)
-    o_ref[...] = jnp.where(place < length_ref[0], out, 0.0).astype(bf16)
-    pl.when(step == max(0, chips - 2))(middle)
+    save(step).start()
+    o_ref[rows] = jnp.where(place < length_ref[0], out, 0.0).astype(bf16)
+    put(step, lambda rows: o_ref.at[rows], w_out_ref)
+    pl.when(step < steps - 1)(lambda: hop(step))
 
     @pl.when(step == steps - 1)
     def _():
+        finish()
+        x1 = x_ref[...].astype(f32) + x1_ref[...]
+        x1_ref[...] = x1
+        _, inverse_ref[...], h2_ref[...] = norm_forward(x1, gain_ref[...])
+        for s in range(max(0, chips - 2), chips):
+            save(s).wait()
         local().wait()
         for y in range(chips):
             from_side(y)
-        finish()
+        sent()
         wait_rows()
-        wait_swaps()
-
-
-def attend(cid, h1_all, w_in, cosine, sine, place, live_place, length, g, extras, cuts=2):
+
+
+def attend(
+    cid, h1_all, w_in, cosine, sine, place, live_place, length, g, x, gain, w_out, extras, cuts=2, tile_o=1024
+):
     seq, wide = h1_all.shape
     width = w_in.shape[1] // 3
     heads = width // HEAD_DIM
     nb = lax.axis_size("blk")
-    tile = seq // (nb // 2)
-    part = pl.BlockSpec((tile, width), lambda i: (i, 0))
-
+    chips = nb // 2
+    tile = seq // chips
+    t = x.shape[0]
     full = jax.ShapeDtypeStruct((seq, width), jnp.bfloat16)
     return pl.pallas_call(
-        functools.partial(attend_kernel, nb // 2, cuts, extras),
-        grid=(seq // tile,),
+        functools.partial(attend_kernel, chips, cuts, tile_o, extras),
+        grid=(chips,),
         in_specs=[
-            ANY, ANY, once(seq, 2 * HEAD_DIM), once(seq, 2 * HEAD_DIM),
-            pl.BlockSpec((tile, 1), lambda i: (i, 0)),
-            once(1, seq),
+            ANY, ANY, once(seq, 2 * HEAD_DIM), once(seq, 2 * HEAD_DIM), once(seq, 1), once(1, seq),
             pl.BlockSpec(memory_space=pltpu.SMEM),
-            once(*g.shape),
+            once(*g.shape), once(t, wide), once(1, wide), once(wide, width),
         ]
         + extras.specs,
-        out_specs=[part] + [once(seq, width)] * 3
-        + [pl.BlockSpec((heads, tile, seq), lambda i: (0, i, 0)), ANY]
+        out_specs=[once(seq, width)] * 4
+        + [ANY, ANY, once(t, wide), once(t, 1), once(t, wide)]
         + extras.specs,
         out_shape=[full] * 4
         + [
             jax.ShapeDtypeStruct((heads, seq, seq), jnp.bfloat16),
             jax.ShapeDtypeStruct((seq, g.shape[1]), g.dtype),
+            jax.ShapeDtypeStruct((t, wide), jnp.float32),
+            jax.ShapeDtypeStruct((t, 1), jnp.float32),
+            jax.ShapeDtypeStruct((t, wide), jnp.bfloat16),
         ]
         + extras.shapes,
         scratch_shapes=[
             pltpu.VMEM(h1_all.shape, h1_all.dtype),
             pltpu.VMEM(w_in.shape, w_in.dtype),
+            pltpu.VMEM((2, heads, tile, seq), jnp.bfloat16),
+            pltpu.SemaphoreType.DMA((2,)),
             pltpu.SemaphoreType.DMA((2,)),
         ]
         + gather_sems(nb, cuts)
+        + scatter_scratch(chips, cuts, t, wide)
         + extras.scratch,
         compiler_params=params(cid),
         cost_estimate=cost(4 * seq * seq * width + 6 * seq * wide * width),
-    )(h1_all, w_in, cosine, sine, place, live_place, length.reshape(1), g, *extras.operands)
+    )(
+        h1_all, w_in, cosine, sine, place, live_place, length.reshape(1), g, x, gain[None], w_out,
+        *extras.operands,
+    )
 
 
 def attend_back_kernel(
-    chips, cuts, tile_y, extras, q_ref, k_ref, v_ref, o_all, g_ref, p_ref, cos_ref, sin_ref, q_place, length_ref,
-    hidden_hbm, red_hbm, branch_hbm, h1_hbm, *refs
+    chips, cuts, tile_y, extras, q_ref, k_ref, v_ref, o_all, cos_ref, sin_ref, q_place, length_ref, x_ref,
+    w_out_ref, p_hbm, hidden_hbm, red_hbm, h1_hbm, *refs
 ):
     n = extras.n
     srcs, (mixed_ref, y_ref, dw_ref), dsts = refs[:n], refs[n : n + 3], refs[n + 3 : 2 * n + 3]
     refs = refs[2 * n + 3 :]
-    (ds_ref, qm_ref, gm_ref, dk_acc, dv_acc, hidden_ref, red_ref, branch_ref, h1_ref, load_sem), refs = (
-        refs[:10], refs[10:],
-    )
-    put, _, hop, finish = scatter_task(chips, cuts, tile_y, y_ref, refs[:4], refs[4:10])
-    start_swaps, start_rows, middle, wait_rows, wait_swaps = extras.tasks(srcs, dsts, refs[10:])
-    load, loaded = mover(
-        [(red_hbm, red_ref), (hidden_hbm, hidden_ref), (branch_hbm, branch_ref), (h1_hbm, h1_ref)], load_sem
-    )
+    (
+        branch_ref, p_ref, ds_ref, qm_ref, gm_ref, dk_acc, dv_acc, hidden_ref, red_ref, h1_ref, load_sem, p_sem,
+    ), refs = refs[:12], refs[12:]
+    begin, pass_on, from_side, local, sent = gather_task(chips, cuts, x_ref, branch_ref, refs[:5])
+    put, _, hop, finish = scatter_task(chips, cuts, tile_y, y_ref, refs[5:9], refs[9:15])
+    start_swaps, start_rows, middle, wait_rows, wait_swaps = extras.tasks(srcs, dsts, refs[15:])
+    one_buffer = h1_ref.shape != branch_ref.shape
+    h1_ref = branch_ref if one_buffer else h1_ref
+    load, loaded = mover([(red_hbm, red_ref), (hidden_hbm, hidden_ref), (h1_hbm, h1_ref)], load_sem)
     step, steps = pl.program_id(0), pl.num_programs(0)
-    tile, width = g_ref.shape
+    seq, width = q_ref.shape
+    tile = seq // chips
     f32, bf16 = jnp.float32, jnp.bfloat16
     factor = 1.0 / math.sqrt(HEAD_DIM)
+    over_rows = (((0,), (0,)), ((), ()))
+    table = arrival_order(chips)
+    _, z, _ = line_place()
+
+    def rows_at(s):
+        return pl.ds(pl.multiple_of(pick(table, z, s) * tile, tile), tile)
+
+    def p_load(s):
+        slot = lax.rem(s, 2)
+        return pltpu.make_async_copy(p_hbm.at[:, rows_at(s)], p_ref.at[slot], p_sem.at[slot])
 
     @pl.when(step == 0)
     def _():
-        load()
+        p_load(step).start()
+        load(0, 1)
+        if not one_buffer:
+            load(2)
         greet(chips, True, extras.rows)
+        begin()
+        start_rows()
         start_swaps()
-        start_rows()
         dk_acc[...] = jnp.zeros_like(dk_acc)
         dv_acc[...] = jnp.zeros_like(dv_acc)
-
         loaded(0, 1)
-
-    pl.when(step == steps // 2)(middle)
+        local().wait()
+
+    pl.when(step < steps - 1)(lambda: p_load(step + 1).start())
     put(step, lambda rows: hidden_ref.at[rows], red_ref)
-
     pl.when(step == 0)(lambda: hop(step))
-    over_rows = (((0,), (0,)), ((), ()))
-    rows = pl.ds(pl.multiple_of(step * tile, tile), tile)
+
+    @pl.when(step > 0)
+    def _():
+        pass_on(step)
+
+    pl.when(step == steps - 1)(middle)
+    from_side(pick(table, z, step))
+    rows = rows_at(step)
     lanes = head_lanes((tile, width))
     nothing = jnp.zeros((), bf16)
-    grad = jnp.where(q_place[...] < length_ref[0], g_ref[...], nothing)
+    grad = jnp.dot(branch_ref[rows], w_out_ref[...], preferred_element_type=f32).astype(bf16)
+    grad = jnp.where(q_place[rows] < length_ref[0], grad, nothing)
     both = grad.astype(f32) * o_all[rows].astype(f32)
     queries = q_ref[rows]
     grad_q = jnp.zeros((tile, width), f32)
-    for head in range(width // HEAD_DIM):
+    p_load(step).wait()
+    low = p_ref.at[lax.rem(step, 2)]
+    heads = width // HEAD_DIM
+    for head in range(heads):
         here = lanes == head
         block = pl.ds(head * tile, tile)
         delta = jnp.sum(jnp.where(here, both, 0.0), axis=-1, keepdims=True)
@@ -1184,13 +1129,11 @@
         grad_p = lax.dot_general(
             one_grad, v_ref[...], (((1,), (1,)), ((), ())), preferred_element_type=f32
         )
-        grad_s = (p_ref[head].astype(f32) * (grad_p - delta)).astype(bf16)
+        grad_s = (low[head].astype(f32) * (grad_p - delta)).astype(bf16)
         ds_ref[block] = grad_s
         grad_q = jnp.where(here, jnp.dot(grad_s, k_ref[...], preferred_element_type=f32), grad_q)
-    heads = width // HEAD_DIM
     dv_acc[...] += lax.dot_general(
-        p_ref[...].reshape(heads * tile, p_ref.shape[2]), gm_ref[...], over_rows,
-        preferred_element_type=f32,
+        low[...].reshape(heads * tile, seq), gm_ref[...], over_rows, preferred_element_type=f32
     )
     dk_acc[...] += lax.dot_general(ds_ref[...], qm_ref[...], over_rows, preferred_element_type=f32)
 
@@ -1200,82 +1143,90 @@
         return (value * cosine - partner(value) * sine).astype(bf16)
 
     mixed_ref[rows, :width] = back(grad_q, cos_ref[rows], sin_ref[rows])
-    pl.when(step == 0)(lambda: loaded(2))
-    share = dw_ref.shape[0] // chips
-    cols = pl.ds(pl.multiple_of(step * share, share), share)
-    dw_ref[cols, 3 * width :] = lax.dot_general(
-        branch_ref[:, cols], o_all[...], over_rows, preferred_element_type=f32
-    ).astype(bf16)
     pl.when((step > 0) & (step < steps - 1))(lambda: hop(step))
 
     @pl.when(step == steps - 1)
     def _():
         mixed_ref[:, width : 2 * width] = back(dk_acc[...], cos_ref[...], sin_ref[...])
         mixed_ref[:, 2 * width :] = dv_acc[...].astype(bf16)
-        loaded(3)
         deep = 256
 
-        def one(i, _):
+        def out_grad(i, _):
+            at = pl.ds(pl.multiple_of(i * deep, deep), deep)
+            dw_ref[at, 3 * width :] = lax.dot_general(
+                branch_ref[:, at], o_all[...], over_rows, preferred_element_type=f32
+            ).astype(bf16)
+            return 0
+
+        def in_grad(i, _):
             at = pl.ds(pl.multiple_of(i * deep, deep), deep)
             dw_ref[at, : 3 * width] = lax.dot_general(
                 h1_ref[:, at], mixed_ref[...], over_rows, preferred_element_type=f32
             ).astype(bf16)
             return 0
 
-        lax.fori_loop(0, dw_ref.shape[0] // deep, one, 0)
+        turns = dw_ref.shape[0] // deep
+        lax.fori_loop(0, turns, out_grad, 0)
+        if one_buffer:
+            sent()
+            load(2)
+        loaded(2)
+        lax.fori_loop(0, turns, in_grad, 0)
         wait_rows()
         finish()
+        if not one_buffer:
+            sent()
         wait_swaps()
 
 
 def attend_back(
-    cid, q, k, v, o, g, p, cosine, sine, place, length, hidden, w_red, branch_all, h1_all, extras, cuts=2
+    cid, q, k, v, o, p, cosine, sine, place, length, branch, w_out, hidden, w_red, h1_all, extras, cuts=2
 ):
     seq, width = q.shape
     heads = width // HEAD_DIM
     nb = lax.axis_size("blk")
-    tile = seq // (nb // 2)
+    chips = nb // 2
+    tile = seq // chips
     wide, units = w_red.shape
+    t = seq // nb
     full = once(seq, width)
     f32, bf16 = jnp.float32, jnp.bfloat16
-    loads = (hidden, w_red, branch_all, h1_all)
+    loads = (hidden, w_red, h1_all)
+    dma = pltpu.SemaphoreType.DMA
     return pl.pallas_call(
-        functools.partial(attend_back_kernel, nb // 2, cuts, 1024, extras),
-        grid=(seq // tile,),
+        functools.partial(attend_back_kernel, chips, cuts, 1024, extras),
+        grid=(chips,),
         in_specs=[
-            full, full, full, full,
-            pl.BlockSpec((tile, width), lambda i: (i, 0)),
-            pl.BlockSpec((heads, tile, seq), lambda i: (0, i, 0)),
-            once(seq, 2 * HEAD_DIM), once(seq, 2 * HEAD_DIM),
-            pl.BlockSpec((tile, 1), lambda i: (i, 0)),
-            pl.BlockSpec(memory_space=pltpu.SMEM),
+            full, full, full, full, once(seq, 2 * HEAD_DIM), once(seq, 2 * HEAD_DIM), once(seq, 1),
+            pl.BlockSpec(memory_space=pltpu.SMEM), once(t, wide), once(wide, width),
         ]
         + [ANY] * 4
         + extras.specs,
-        out_specs=[
-            once(seq, 3 * width), once(seq // nb, wide), once(wide, 4 * width)
-        ]
-        + extras.specs,
+        out_specs=[once(seq, 3 * width), once(t, wide), once(wide, 4 * width)] + extras.specs,
         out_shape=[
             jax.ShapeDtypeStruct((seq, 3 * width), bf16),
-            jax.ShapeDtypeStruct((seq // nb, wide), f32),
+            jax.ShapeDtypeStruct((t, wide), f32),
             jax.ShapeDtypeStruct((wide, 4 * width), bf16),
         ]
         + extras.shapes,
         scratch_shapes=[
+            pltpu.VMEM((seq, wide), bf16),
+            pltpu.VMEM((2, heads, tile, seq), bf16),
             pltpu.VMEM((heads * tile, seq), bf16),
             pltpu.VMEM((heads * tile, width), bf16),
             pltpu.VMEM((heads * tile, width), bf16),
             pltpu.VMEM((seq, width), f32),
             pltpu.VMEM((seq, width), f32),
         ]
-        + [pltpu.VMEM(value.shape, value.dtype) for value in loads]
-        + [pltpu.SemaphoreType.DMA((4,))]
-        + scatter_scratch(nb // 2, cuts, seq // nb, wide)
+        + [pltpu.VMEM(value.shape, value.dtype) for value in loads[:2]]
+        + [pltpu.VMEM(h1_all.shape if seq <= 1024 else (16, 128), bf16)]
+        + [dma((3,)), dma((2,))]
+        + gather_sems(nb, cuts)
+        + scatter_scratch(chips, cuts, t, wide)
         + extras.scratch,
         compiler_params=params(cid),
         cost_estimate=cost(10 * seq * seq * width),
-    )(q, k, v, o, g, p, cosine, sine, place, length.reshape(1), *loads, *extras.operands)
+    )(q, k, v, o, cosine, sine, place, length.reshape(1), branch, w_out, p, *loads, *extras.operands)
 
 
 def arrange(weight, out, parts):
@@ -1548,28 +1499,21 @@
         Extras([pieces_gu], [(flat(value), 0, deep) for value in (swap_in, swap_out, swap_red)]),
     )
     w_in, w_out, w_red = [value.reshape(wide, -1) for value in (w_in, w_out, w_red)]
-    early = deep * 5 // 8
-    attended, q, k, v, p, g_all, gu_early = attend(
+    attended, q, k, v, p, g_all, x1, inverse_two, h2, w_gu = attend(
         4, h1_all, w_in, cosine, sine, place, live_place, length, cotangent[0],
-        Extras([], [(flat(swap_gu), 0, early)]),
-    )
-    x1, inverse_two, h2, gu_late = attend_out_sum(
-        5, attended, w_out, tokens[0], gain_expand,
-        Extras([], [(flat(swap_gu), early, deep - early)]),
-    )
+        tokens[0], gain_expand, w_out, Extras([], [(flat(swap_gu), 0, deep)]),
+    )
+    w_gu = w_gu.reshape(wide, -1)
 
     def by_rows(gradient):
         return gradient.reshape(nr, nb, deep // nb, gradient.shape[1])
 
     grad_x1, branch, gain_two, hidden, part_gate, part_up, rows_reduce = feed_forward(
-        6, h2, x1, inverse_two, gain_expand, cotangent[0], gu_early, gu_late, w_red, g_all
-    )
-    branch_all, grad_o, rows_gate = gather_dot(
-        9, branch, w_out, Extras([], [], [by_rows(part_gate)])
-    )
-    grad_mixed, y, part_both, own_reduce, rows_up = attend_back(
-        10, q, k, v, attended, grad_o, p, cosine, sine, place, length,
-        hidden, w_red, branch_all, h1_all, Extras([rows_reduce], [], [by_rows(part_up)]),
+        6, h2, x1, inverse_two, gain_expand, cotangent[0], w_gu, w_red, g_all
+    )
+    grad_mixed, y, part_both, own_reduce, rows_gate, rows_up = attend_back(
+        10, q, k, v, attended, p, cosine, sine, place, length, branch, w_out, hidden, w_red, h1_all,
+        Extras([rows_reduce], [], [by_rows(part_gate), by_rows(part_up)]),
     )
     y = x1 + y
     grad_input, gains, own_gate, own_up, rows_both = last_scatter(

time: 565 us -> 533 us (0.943)
  Pallas kernels: 535 us -> 505 us
    pallas_call x4 -> x2, Pallas kernels: 203 us -> 171 us  [the longest x1 93.7 us: attend_back(): pl.pallas_call(functools.partial(attend_back_kernel, chips, cuts, 1024, e...]
where the time goes in v6:
time: 533 us; the launch traced here: 526 us
  Pallas kernels  505 us (95%)
  waiting for transfers between devices  8.9 us (2%)
    pallas_call x1, Pallas kernels, attend_back(): pl.pallas_call(functools.partial(attend_back_kernel, chips, cuts, 1024, e...  93.7 us
    pallas_call x1, Pallas kernels, feed_forward(): pl.pallas_call(functools.partial(feed_forward_kernel, nb // 2, cuts, tile...  93.3 us
    pallas_call x1, Pallas kernels, last_scatter(): pl.pallas_call(functools.partial(last_scatter_kernel, nb // 2, nr, cuts,...  85.1 us
    pallas_call x1, Pallas kernels, line_gather(): pl.pallas_call(functools.partial(gather_kernel, nb // 2, cuts, extras), o...  83.9 us
    pallas_call x1, Pallas kernels, attend(): pl.pallas_call(functools.partial(attend_kernel, chips, cuts, tile_o, extr...  77 us
    pallas_call x1, Pallas kernels, first(): pl.pallas_call(functools.partial(first_kernel, parts, m), out_shape=[jax....  47.5 us
    pallas_call x4, Pallas kernels, step(): pl.pallas_call(functools.partial(step_kernel, parts, one_array), grid=(pa...  24.4 us
  transfers between devices with their start and end apart: 1, of which 1 were waited for; matrix products, arithmetic and copies ran while one was open for 0% of the time, Pallas kernels for 3%

profile of v6, /device:TPU:0, one launch (start us, length us, event | category | flops | bytes accessed | tf_op | source)
XLA Modules:
  0.0 525.7 jit_solution(475010113558550396)
XLA Ops:
  1.3 0.7 multiply_bitcast_fusion
  2.0 0.6 broadcast_in_dim_tile.3.frequency_ref
  2.6 0.1 iota_add_fusion
  2.6 0.1 add.32
  2.7 0.6 compare_select_fusion.k_place
  3.3 47.5 %shard_map.289 = (bf16[8,64,768]{2,1,0:T(8,128)(2,1)}, bf16[8,64,256]{2,1,0:T(8,128)(2,1)}, bf16[8,64,1024]{2,1,0:T(8,128)(2,1)}, bf16[8,64,2048]{2,1,0:T(8,128)...) custom-call(s32[1,16]{1,0:T(1,128)} %map_ref.1, ...), custom_call_target="tpu_custom_call" | custom-call | bytes 150000000 | tf_op jit(solution)/shard_map/pallas_call | solution.py:1287
  50.9 83.9 %shard_map.290 = (bf16[1024,2048]{1,0:T(8,128)(2,1)}, bf16[8,64,2048]{2,1,0:T(8,128)(2,1)}, bf16[4,512,768]{2,1,0:T(8,128)(2,1)}, bf16[4,512,256]{2,1,0:T(8,128)(2,1)}, bf16[4,512,1024]{2,1,0:T(8,128)(2,1)}) custom-call(bf16[128,2048]{1,0:T(8,128)(2,1)} %get-tuple-element.69.x_ref, bf16[8,64,2048]{2,1,0:T(8,128)(2,1)} %get-tuple-element.70.refs_0_, ...), custom_call_target="tpu_custom_call" | custom-call | bytes 150000000 | tf_op jit(solution)/shard_map/pallas_call | solution.py:446
  134.8 77.0 %shard_map.291 = (bf16[1024,256]{1,0:T(8,128)(2,1)}, bf16[1024,256]{1,0:T(8,128)(2,1)}, bf16[1024,256]{1,0:T(8,128)(2,1)}, bf16[1024,256]{1,0:T(8,128)(2,1)}, bf...) custom-call(bf16[1024,2048]{1,0:T(8,128)(2,1)} %get-tuple-element.74, ...), custom_call_target="tpu_custom_call" | custom-call | flops 4294967296 | bytes 150000000 | tf_op jit(solution)/shard_map/pallas_call | solution.py:1015
  211.8 93.3 %shard_map.292 = (f32[128,2048]{1,0:T(8,128)}, bf16[128,2048]{1,0:T(8,128)(2,1)}, f32[1,2048]{1,0:T(1,128)}, bf16[1024,1024]{1,0:T(8,128)(2,1)}, bf16[2048,1024]...) custom-call(bf16[128,2048]{1,0:T(8,128)(2,1)} %get-tuple-element.86.h2_here, ...), custom_call_target="tpu_custom_call" | custom-call | flops 38654705664 | bytes 150000000 | tf_op jit(solution)/shard_map/pallas_call | solution.py:797
  305.1 93.7 %shard_map.293 = (bf16[1024,768]{1,0:T(8,128)(2,1)}, f32[128,2048]{1,0:T(8,128)}, bf16[2048,1024]{1,0:T(8,128)(2,1)}, bf16[8,64,1024]{2,1,0:T(8,128)(2,1)}, bf16...) custom-call(bf16[1024,256]{1,0:T(8,128)(2,1)} %get-tuple-element.82.q_ref, ...), custom_call_target="tpu_custom_call" | custom-call | flops 2684354560 | bytes 150000000 | tf_op jit(solution)/shard_map/pallas_call | solution.py:1196
  398.8 85.1 %shard_map.294 = (f32[128,2048]{1,0:T(8,128)}, f32[2,2048]{1,0:T(2,128)}, bf16[8,64,1024]{2,1,0:T(8,128)(2,1)}, bf16[8,64,1024]{2,1,0:T(8,128)(2,1)}, bf16[8,64,1024]{2,1,0:T(8,128)(2,1)}) custom-call(bf16[1024,768]{1,0:T(8,128)(2,1)} %get-tuple-element.98.a_ref, bf16[2048,768]{1,0:T(8,128)(2,1)} %bitcast.43, bf16[128,2048]{1,0:T(8,128)(2,1)} %bitcast.48, ...), custom_call_target="tpu_custom_call" | custom-call | flops 3221225472 | bytes 150000000 | tf_op jit(solution)/shard_map/pallas_call | solution.py:1394
  483.9 4.6 all-to-all-start
  488.5 5.7 %shard_map.296 = (f32[64,8192]{1,0:T(8,128)}, f32[64,8192]{1,0:T(8,128)}, f32[64,8192]{1,0:T(8,128)}) custom-call(bf16[8,64,1024]{2,1,0:T(8,128)(2,1)} %get-tuple-element.111.refs_0_, f32[64,8192]{1,0:T(8,128)} %bitcast.36, f32[64,8192]{1,0:T(8,128)} %bitcast.44, f32[64,8192]{1,0:T(8,128)} %bitcast.45), custom_call_target="tpu_custom_call" | custom-call | bytes 13631488 | tf_op jit(solution)/shard_map/pallas_call | solution.py:1452
  494.2 0.0 copy-start.4
  494.2 0.0 copy-start.1
  494.2 0.0 copy-start.2
  494.2 10.4 %shard_map.295 = (f32[64,16384]{1,0:T(8,128)}, f32[64,16384]{1,0:T(8,128)}, f32[64,16384]{1,0:T(8,128)}) custom-call(bf16[8,64,1024]{2,1,0:T(8,128)(2,1)} %get-tuple-element.108.refs_0_, bf16[8,64,1024]{2,1,0:T(8,128)(2,1)} %get-tuple-element.109.refs_1_, f32[64,16384]{1,0:T(8,128)} %refs_2_.2, f32[64,16384]{1,0:T(8,128)} %refs_3_.4, f32[64,16384]{1,0:T(8,128)} %refs_4_.1), custom_call_target="tpu_custom_call" | custom-call | bytes 27262976 | tf_op jit(solution)/shard_map/pallas_call | solution.py:1452
  504.6 0.0 copy-done.4
  504.6 0.6 fusion.1
  505.3 0.0 copy-done.1
  505.3 0.0 copy-done.2
  505.3 0.9 fusion
  506.2 8.9 %all-to-all-done.refs_0_ = bf16[8,64,1024]{2,1,0:T(8,128)(2,1)S(1)} async-done(((bf16[8,64,1024]{2,1,0:T(8,128)(2,1)}), bf16[8,64,1024]{2,1,0:T(8,128)(2,1)S(1)}, u32[]{:S(2)}, u32[]{:S(2)}) %all-to-all-start) | async-done | bytes 1048608 | tf_op jit(solution)/shard_map/all_to_all | solution.py:1523
  515.1 0.0 copy-start
  515.1 1.0 copy-done
  516.0 2.2 shard_map.298
  518.2 0.0 copy-start.3
  518.2 6.1 %shard_map.297 = (f32[64,6144]{1,0:T(8,128)}, f32[64,6144]{1,0:T(8,128)}, f32[64,6144]{1,0:T(8,128)}) custom-call(bf16[8,64,1024]{2,1,0:T(8,128)(2,1)} %copy-done, f32[64,6144]{1,0:T(8,128)} %refs_1_.1, f32[64,6144]{1,0:T(8,128)} %refs_2_.3, f32[64,6144]{1,0:T(8,128)} %refs_3_.5), custom_call_target="tpu_custom_call" | custom-call | bytes 10223616 | tf_op jit(solution)/shard_map/pallas_call | solution.py:1452
  524.3 0.0 copy-done.3
  524.3 1.0 copy.35
  (2 shorter events, 0.0 us)
Async XLA Ops:
  483.9 31.1 %all-to-all-start = ((bf16[8,64,1024]{2,1,0:T(8,128)(2,1)}), bf16[8,64,1024]{2,1,0:T(8,128)(2,1)S(1)}, u32[]{:S(2)}, u32[]{:S(2)}) async-start(bf16[8,64,1024]{2,1,0:T(8,128)(2,1)} %get-tuple-element.107), calls=%async_computation | async-start | bytes 2097152 | tf_op jit(solution)/shard_map/all_to_all | solution.py:1523
  494.2 10.4 %copy-start.4 = (f32[2,2048]{1,0:T(2,128)S(1)}, f32[2,2048]{1,0:T(2,128)}, u32[]{:S(2)}) copy-start(f32[2,2048]{1,0:T(2,128)} %get-tuple-element.106) | copy-start | bytes 49156
  494.2 11.0 %copy-start.1 = (f32[128,2048]{1,0:T(8,128)S(1)}, f32[128,2048]{1,0:T(8,128)}, u32[]{:S(2)}) copy-start(f32[128,2048]{1,0:T(8,128)} %get-tuple-element.81.x1_ref) | copy-start | bytes 3145732
  494.2 11.0 %copy-start.2 = (f32[128,2048]{1,0:T(8,128)S(1)}, f32[128,2048]{1,0:T(8,128)}, u32[]{:S(2)}) copy-start(f32[128,2048]{1,0:T(8,128)} %get-tuple-element.97) | copy-start | bytes 3145732
  515.1 1.0 copy-start
  518.2 6.1 %copy-start.3 = (f32[128,2048]{1,0:T(8,128)S(1)}, f32[128,2048]{1,0:T(8,128)}, u32[]{:S(2)}) copy-start(f32[128,2048]{1,0:T(8,128)} %get-tuple-element.105) | copy-start | bytes 3145732

commit v7 on v6

--- a/solution.py
+++ b/solution.py
@@ -418,40 +418,6 @@
 
 def gather_sems(nb, cuts):
     return [pltpu.SemaphoreType.DMA] + [pltpu.SemaphoreType.DMA((nb, cuts))] * 4
-
-
-def gather_kernel(chips, cuts, extras, x_ref, *refs):
-    n = extras.n
-    srcs, o_ref, dsts, refs = refs[:n], refs[n], refs[n + 1 : 2 * n + 1], refs[2 * n + 1 :]
-    begin, hop, from_side, local, finish = gather_task(chips, cuts, x_ref, o_ref, refs[:5])
-    start_swaps, start_rows, middle, wait_rows, wait_swaps = extras.tasks(srcs, dsts, refs[5:])
-    greet(chips, True, extras.rows)
-    begin()
-    start_rows()
-    for k in range(1, chips):
-        if k == min(3, chips - 1):
-            start_swaps()
-        hop(k)
-    middle()
-    local().wait()
-    for y in range(chips):
-        from_side(y)
-    finish()
-    wait_rows()
-    wait_swaps()
-
-
-def line_gather(cid, x, extras, cuts=4):
-    nb = lax.axis_size("blk")
-    return pl.pallas_call(
-        functools.partial(gather_kernel, nb // 2, cuts, extras),
-        out_shape=[jax.ShapeDtypeStruct((nb * x.shape[0], x.shape[1]), x.dtype)] + extras.shapes,
-        in_specs=[VMEM] + extras.specs,
-        out_specs=[ANY] + extras.specs,
-        scratch_shapes=gather_sems(nb, cuts) + extras.scratch,
-        compiler_params=params(cid),
-        cost_estimate=cost(0),
-    )(x, *extras.operands)
 
 
 def arrival_order(chips):
@@ -1238,43 +1204,67 @@
             out[j, :, part * span : (part + 1) * span] = weight[:, at : at + span].astype(out.dtype)
 
 
-def first_kernel(parts, m, map_ref, tokens_ref, gain_ref, frequency_ref, *refs):
+def first_kernel(chips, cuts, parts, map_ref, tokens_ref, gain_ref, frequency_ref, *refs):
     n = len(parts)
-    sources, dsts, later, refs = refs[:n], refs[n : n + m], refs[n + m : 2 * n], refs[2 * n :]
-    (h1_ref, inverse_ref, place_ref, cos_ref, sin_ref), refs = refs[:5], refs[5:]
-    weights, held, load_sem, sems = refs[:n], refs[n : n + m], refs[n + m], refs[n + m + 1 :]
-    swaps = [swap_task(a, b, *sems[3 * i : 3 * i + 3]) for i, (a, b) in enumerate(zip(held, dsts))]
+    refs = list(refs)
+
+    def take(count):
+        return [refs.pop(0) for _ in range(count)]
+
+    sources, h1_all, swapped, gathered = take(n), take(1)[0], take(n), take(n - 1)
+    inverse_ref, place_ref, cos_ref, sin_ref = take(4)
+    weights, held, (h1_ref, load_sem) = take(n), take(n), take(2)
+    swaps = [swap_task(a, b, *take(3)) for a, b in zip(held, swapped)]
+    task = square_gather if gathered[0].shape[0] == 4 else direct_gather
+    rows = [task(a, b, *take(4)) for a, b in zip(swapped, gathered)]
+    begin, pass_on, from_side, local, sent = gather_task(chips, cuts, h1_ref, h1_all, refs)
     load, loaded = mover(list(zip(sources, weights)), load_sem)
     load()
-    greet(held[0].shape[0] // 2, True)
-    for i in range(m):
+    greet(chips, True, True)
+    for i in range(n - 1):
         loaded(i)
         arrange(weights[i], held[i], parts[i])
         swaps[i][0]()
     _, inverse_ref[...], h1_ref[...] = norm_forward(
         tokens_ref[...].astype(jnp.float32), gain_ref[...]
     )
-    for i in range(m, n):
-        loaded(i)
-        arrange(weights[i], later[i - m], parts[i])
+    loaded(n - 1)
+    arrange(weights[n - 1], held[n - 1], parts[n - 1])
     blocks = map_ref.shape[1]
     block = place_ref.shape[0] // blocks
     lanes = cos_ref.shape[1]
     front = lax.broadcasted_iota(jnp.int32, (block, lanes), 1) % HEAD_DIM < HEAD_DIM // 2
     for j in range(blocks):
-        rows = slice(j * block, (j + 1) * block)
+        at = slice(j * block, (j + 1) * block)
         place = map_ref[0, j] * block + lax.broadcasted_iota(jnp.int32, (block, lanes), 0)
-        place_ref[rows] = place[:, :1]
+        place_ref[at] = place[:, :1]
         angle = place.astype(jnp.float32) * frequency_ref[...]
-        cos_ref[rows] = jnp.cos(angle)
+        cos_ref[at] = jnp.cos(angle)
         sine = jnp.sin(angle)
-        sin_ref[rows] = jnp.where(front, -sine, sine)
-    for _, wait in swaps:
+        sin_ref[at] = jnp.where(front, -sine, sine)
+    for i in range(n - 2):
+        swaps[i][1]()
+        rows[i][0]()
+    swaps[n - 2][1]()
+    rows[n - 2][0]()
+    begin()
+    for k in range(1, chips):
+        if k == min(3, chips - 1):
+            swaps[n - 1][0]()
+        pass_on(k)
+    for _, middle, _ in rows:
+        middle()
+    local().wait()
+    for y in range(chips):
+        from_side(y)
+    sent()
+    for _, _, wait in rows:
         wait()
-
-
-def first(cid, block_map, tokens, gain, weights, parts, m):
-    nb = lax.axis_size("blk")
+    swaps[n - 1][1]()
+
+
+def first(cid, block_map, tokens, gain, weights, parts, cuts=4):
+    nr, nb = lax.axis_size("rows"), lax.axis_size("blk")
     shapes = [(nb, value.shape[0], value.shape[1] // nb) for value in weights]
     n = len(weights)
     t, width = tokens.shape
@@ -1282,23 +1272,29 @@
     frequency = jnp.exp(
         -jnp.arange(half, dtype=jnp.float32) * (2.0 / HEAD_DIM) * math.log(theta_base)
     )
-    dma, f32 = pltpu.SemaphoreType.DMA, jnp.float32
+    dma, f32, bf16 = pltpu.SemaphoreType.DMA, jnp.float32, jnp.bfloat16
     table = jax.ShapeDtypeStruct((nb * t, 2 * HEAD_DIM), f32)
+    sems = 6 if nr == 4 else nr
+    scratch = [pltpu.VMEM(value.shape, value.dtype) for value in weights]
+    scratch += [pltpu.VMEM(shape, bf16) for shape in shapes]
+    scratch += [pltpu.VMEM((t, width), bf16), dma((n,))]
+    scratch += [dma, dma((nb,)), dma((nb,))] * n
+    for shape in shapes[:-1]:
+        scratch += [pltpu.VMEM(shape, bf16), dma, dma((sems,)), dma((sems,))]
     return pl.pallas_call(
-        functools.partial(first_kernel, parts, m),
-        out_shape=[jax.ShapeDtypeStruct(shape, jnp.bfloat16) for shape in shapes]
+        functools.partial(first_kernel, nb // 2, cuts, parts),
+        out_shape=[jax.ShapeDtypeStruct((nb * t, width), bf16)]
+        + [jax.ShapeDtypeStruct(shape, bf16) for shape in shapes]
+        + [jax.ShapeDtypeStruct((nr,) + shape, bf16) for shape in shapes[:-1]]
         + [
-            jax.ShapeDtypeStruct((t, width), jnp.bfloat16),
             jax.ShapeDtypeStruct((t, 1), f32),
             jax.ShapeDtypeStruct((nb * t, 1), jnp.int32),
             table,
             table,
         ],
         in_specs=[pl.BlockSpec(memory_space=pltpu.SMEM)] + [VMEM] * 3 + [ANY] * n,
-        out_specs=[ANY] * m + [VMEM] * (n - m + 5),
-        scratch_shapes=[pltpu.VMEM(value.shape, value.dtype) for value in weights]
-        + [pltpu.VMEM(shape, jnp.bfloat16) for shape in shapes[:m]]
-        + [dma((n,))] + [dma, dma((nb,)), dma((nb,))] * m,
+        out_specs=[ANY] * (2 * n) + [VMEM] * 4,
+        scratch_shapes=scratch + gather_sems(nb, cuts),
         compiler_params=params(cid),
         cost_estimate=cost(0),
     )(block_map, tokens, gain[None], jnp.tile(frequency, 4)[None], *weights)
@@ -1480,9 +1476,9 @@
 ):
     nb = lax.axis_size("blk")
     length = lengths[0]
-    swap_in, swap_out, swap_red, pieces_gu, h1, inverse_one, place, cosine, sine = first(
+    h1_all, _, _, _, swap_gu, w_in, w_out, w_red, inverse_one, place, cosine, sine = first(
         2, block_map, tokens[0], gain_attend,
-        (attend_in, attend_out.T, reduce_out.T, expand_in), (3, 1, 1, 2), 3,
+        (attend_in, attend_out.T, reduce_out.T, expand_in), (3, 1, 1, 2),
     )
     block_rows = tokens.shape[1] // 2
     row_place = (block_map[0][:, None] * block_rows + jnp.arange(block_rows)[None, :]).reshape(1, -1)
@@ -1494,11 +1490,7 @@
     def flat(pieces):
         return pieces.reshape(deep, pieces.shape[2])
 
-    h1_all, swap_gu, w_in, w_out, w_red = line_gather(
-        3, h1,
-        Extras([pieces_gu], [(flat(value), 0, deep) for value in (swap_in, swap_out, swap_red)]),
-    )
-    w_in, w_out, w_red = [value.reshape(wide, -1) for value in (w_in, w_out, w_red)]
+    w_in, w_out, w_red = [value.reshape(wide, value.shape[3]) for value in (w_in, w_out, w_red)]
     attended, q, k, v, p, g_all, x1, inverse_two, h2, w_gu = attend(
         4, h1_all, w_in, cosine, sine, place, live_place, length, cotangent[0],
         tokens[0], gain_expand, w_out, Extras([], [(flat(swap_gu), 0, deep)]),

time: 533 us -> 529 us (level)
    pallas_call x2 -> x1, Pallas kernels: 131 us -> 127 us  [first(): pl.pallas_call(functools.partial(first_kernel, nb // 2, cuts, parts), out...]
where the time goes in v7:
time: 529 us; the launch traced here: 522 us
  Pallas kernels  501 us (95%)
  waiting for transfers between devices  8.9 us (2%)
    pallas_call x1, Pallas kernels, first(): pl.pallas_call(functools.partial(first_kernel, nb // 2, cuts, parts), out...  127 us
    pallas_call x1, Pallas kernels, feed_forward(): pl.pallas_call(functools.partial(feed_forward_kernel, nb // 2, cuts, tile...  94.5 us
    pallas_call x1, Pallas kernels, attend_back(): pl.pallas_call(functools.partial(attend_back_kernel, chips, cuts, 1024, e...  91.1 us
    pallas_call x1, Pallas kernels, last_scatter(): pl.pallas_call(functools.partial(last_scatter_kernel, nb // 2, nr, cuts,...  85.1 us
    pallas_call x1, Pallas kernels, attend(): pl.pallas_call(functools.partial(attend_kernel, chips, cuts, tile_o, extr...  78.4 us
    pallas_call x4, Pallas kernels, step(): pl.pallas_call(functools.partial(step_kernel, parts, one_array), grid=(pa...  24.4 us
  transfers between devices with their start and end apart: 1, of which 1 were waited for; matrix products, arithmetic and copies ran while one was open for 0% of the time, Pallas kernels for 3%

profile of v7, /device:TPU:0, one launch (start us, length us, event | category | flops | bytes accessed | tf_op | source)
XLA Modules:
  0.0 521.8 jit_solution(11438612032663885473)
XLA Ops:
  1.3 0.7 multiply_bitcast_fusion
  2.0 0.6 broadcast_in_dim_tile.3.frequency_ref
  2.6 0.1 iota_add_fusion
  2.6 0.1 add.32
  2.7 0.6 compare_select_fusion.k_place
  3.3 127.1 %shard_map.289 = (bf16[1024,2048]{1,0:T(8,128)(2,1)}, bf16[8,64,768]{2,1,0:T(8,128)(2,1)}, bf16[8,64,256]{2,1,0:T(8,128)(2,1)}, bf16[8,64,1024]{2,1,0:T(8,128)(2...) custom-call(s32[1,16]{1,0:T(1,128)} %map_ref.1, ...), custom_call_target="tpu_custom_call" | custom-call | bytes 150000000 | tf_op jit(solution)/shard_map/pallas_call | solution.py:1284
  130.4 78.4 %shard_map.290 = (bf16[1024,256]{1,0:T(8,128)(2,1)}, bf16[1024,256]{1,0:T(8,128)(2,1)}, bf16[1024,256]{1,0:T(8,128)(2,1)}, bf16[1024,256]{1,0:T(8,128)(2,1)}, bf...) custom-call(bf16[1024,2048]{1,0:T(8,128)(2,1)} %get-tuple-element.64, ...), custom_call_target="tpu_custom_call" | custom-call | flops 4294967296 | bytes 150000000 | tf_op jit(solution)/shard_map/pallas_call | solution.py:981
  208.8 94.5 %shard_map.291 = (f32[128,2048]{1,0:T(8,128)}, bf16[128,2048]{1,0:T(8,128)(2,1)}, f32[1,2048]{1,0:T(1,128)}, bf16[1024,1024]{1,0:T(8,128)(2,1)}, bf16[2048,1024]...) custom-call(bf16[128,2048]{1,0:T(8,128)(2,1)} %get-tuple-element.76.h2_here, ...), custom_call_target="tpu_custom_call" | custom-call | flops 38654705664 | bytes 150000000 | tf_op jit(solution)/shard_map/pallas_call | solution.py:763
  303.3 91.1 %shard_map.292 = (bf16[1024,768]{1,0:T(8,128)(2,1)}, f32[128,2048]{1,0:T(8,128)}, bf16[2048,1024]{1,0:T(8,128)(2,1)}, bf16[8,64,1024]{2,1,0:T(8,128)(2,1)}, bf16...) custom-call(bf16[1024,256]{1,0:T(8,128)(2,1)} %get-tuple-element.72.q_ref, ...), custom_call_target="tpu_custom_call" | custom-call | flops 2684354560 | bytes 150000000 | tf_op jit(solution)/shard_map/pallas_call | solution.py:1162
  394.5 85.1 %shard_map.293 = (f32[128,2048]{1,0:T(8,128)}, f32[2,2048]{1,0:T(2,128)}, bf16[8,64,1024]{2,1,0:T(8,128)(2,1)}, bf16[8,64,1024]{2,1,0:T(8,128)(2,1)}, bf16[8,64,1024]{2,1,0:T(8,128)(2,1)}) custom-call(bf16[1024,768]{1,0:T(8,128)(2,1)} %get-tuple-element.88.a_ref, bf16[2048,768]{1,0:T(8,128)(2,1)} %bitcast.40, bf16[128,2048]{1,0:T(8,128)(2,1)} %bitcast.45, ...), custom_call_target="tpu_custom_call" | custom-call | flops 3221225472 | bytes 150000000 | tf_op jit(solution)/shard_map/pallas_call | solution.py:1390
  479.6 4.9 all-to-all-start
  484.5 5.7 %shard_map.295 = (f32[64,8192]{1,0:T(8,128)}, f32[64,8192]{1,0:T(8,128)}, f32[64,8192]{1,0:T(8,128)}) custom-call(bf16[8,64,1024]{2,1,0:T(8,128)(2,1)} %get-tuple-element.101.refs_0_, f32[64,8192]{1,0:T(8,128)} %bitcast.33, f32[64,8192]{1,0:T(8,128)} %bitcast.41, f32[64,8192]{1,0:T(8,128)} %bitcast.42), custom_call_target="tpu_custom_call" | custom-call | bytes 13631488 | tf_op jit(solution)/shard_map/pallas_call | solution.py:1448
  490.2 0.0 copy-start.4
  490.2 0.0 copy-start.1
  490.2 0.0 copy-start.2
  490.3 10.4 %shard_map.294 = (f32[64,16384]{1,0:T(8,128)}, f32[64,16384]{1,0:T(8,128)}, f32[64,16384]{1,0:T(8,128)}) custom-call(bf16[8,64,1024]{2,1,0:T(8,128)(2,1)} %get-tuple-element.98.refs_0_, bf16[8,64,1024]{2,1,0:T(8,128)(2,1)} %get-tuple-element.99.refs_1_, f32[64,16384]{1,0:T(8,128)} %refs_2_.2, f32[64,16384]{1,0:T(8,128)} %refs_3_.4, f32[64,16384]{1,0:T(8,128)} %refs_4_.1), custom_call_target="tpu_custom_call" | custom-call | bytes 27262976 | tf_op jit(solution)/shard_map/pallas_call | solution.py:1448
  500.7 0.0 copy-done.4
  500.7 0.6 fusion.1
  501.3 0.0 copy-done.1
  501.3 0.0 copy-done.2
  501.3 0.9 fusion
  502.2 8.9 %all-to-all-done.refs_0_ = bf16[8,64,1024]{2,1,0:T(8,128)(2,1)S(1)} async-done(((bf16[8,64,1024]{2,1,0:T(8,128)(2,1)}), bf16[8,64,1024]{2,1,0:T(8,128)(2,1)S(1)}, u32[]{:S(2)}, u32[]{:S(2)}) %all-to-all-start) | async-done | bytes 1048608 | tf_op jit(solution)/shard_map/all_to_all | solution.py:1515
  511.1 0.0 copy-start
  511.1 1.0 copy-done
  512.1 2.2 shard_map.297
  514.2 0.0 copy-start.3
  514.2 6.1 %shard_map.296 = (f32[64,6144]{1,0:T(8,128)}, f32[64,6144]{1,0:T(8,128)}, f32[64,6144]{1,0:T(8,128)}) custom-call(bf16[8,64,1024]{2,1,0:T(8,128)(2,1)} %copy-done, f32[64,6144]{1,0:T(8,128)} %refs_1_.1, f32[64,6144]{1,0:T(8,128)} %refs_2_.3, f32[64,6144]{1,0:T(8,128)} %refs_3_.5), custom_call_target="tpu_custom_call" | custom-call | bytes 10223616 | tf_op jit(solution)/shard_map/pallas_call | solution.py:1448
  520.3 0.0 copy-done.3
  520.3 1.0 copy.35
  (2 shorter events, 0.0 us)
Async XLA Ops:
  479.6 31.5 %all-to-all-start = ((bf16[8,64,1024]{2,1,0:T(8,128)(2,1)}), bf16[8,64,1024]{2,1,0:T(8,128)(2,1)S(1)}, u32[]{:S(2)}, u32[]{:S(2)}) async-start(bf16[8,64,1024]{2,1,0:T(8,128)(2,1)} %get-tuple-element.97), calls=%async_computation | async-start | bytes 2097152 | tf_op jit(solution)/shard_map/all_to_all | solution.py:1515
  490.2 10.4 %copy-start.4 = (f32[2,2048]{1,0:T(2,128)S(1)}, f32[2,2048]{1,0:T(2,128)}, u32[]{:S(2)}) copy-start(f32[2,2048]{1,0:T(2,128)} %get-tuple-element.96) | copy-start | bytes 49156
  490.2 11.0 %copy-start.1 = (f32[128,2048]{1,0:T(8,128)S(1)}, f32[128,2048]{1,0:T(8,128)}, u32[]{:S(2)}) copy-start(f32[128,2048]{1,0:T(8,128)} %get-tuple-element.71.x1_ref) | copy-start | bytes 3145732
  490.2 11.0 %copy-start.2 = (f32[128,2048]{1,0:T(8,128)S(1)}, f32[128,2048]{1,0:T(8,128)}, u32[]{:S(2)}) copy-start(f32[128,2048]{1,0:T(8,128)} %get-tuple-element.87) | copy-start | bytes 3145732
  511.1 1.0 copy-start
  514.2 6.1 %copy-start.3 = (f32[128,2048]{1,0:T(8,128)S(1)}, f32[128,2048]{1,0:T(8,128)}, u32[]{:S(2)}) copy-start(f32[128,2048]{1,0:T(8,128)} %get-tuple-element.95) | copy-start | bytes 3145732

commit v8 on v7

--- a/solution.py
+++ b/solution.py
@@ -1058,7 +1058,6 @@
         greet(chips, True, extras.rows)
         begin()
         start_rows()
-        start_swaps()
         dk_acc[...] = jnp.zeros_like(dk_acc)
         dv_acc[...] = jnp.zeros_like(dv_acc)
         loaded(0, 1)
@@ -1072,6 +1071,7 @@
     def _():
         pass_on(step)
 
+    pl.when(step == steps // 2)(start_swaps)
     pl.when(step == steps - 1)(middle)
     from_side(pick(table, z, step))
     rows = rows_at(step)

time: 529 us -> 515 us (0.974)
  Pallas kernels: 501 us -> 487 us
    pallas_call x1, Pallas kernels: 91.1 us -> 81.8 us  [attend_back(): pl.pallas_call(functools.partial(attend_back_kernel, chips, cuts, 1024, e...]
where the time goes in v8:
time: 515 us; the launch traced here: 508 us
  Pallas kernels  487 us (95%)
  waiting for transfers between devices  8.9 us (2%)
    pallas_call x1, Pallas kernels, first(): pl.pallas_call(functools.partial(first_kernel, nb // 2, cuts, parts), out...  127 us
    pallas_call x1, Pallas kernels, feed_forward(): pl.pallas_call(functools.partial(feed_forward_kernel, nb // 2, cuts, tile...  94.5 us
    pallas_call x1, Pallas kernels, attend_back(): pl.pallas_call(functools.partial(attend_back_kernel, chips, cuts, 1024, e...  81.8 us
    pallas_call x1, Pallas kernels, last_scatter(): pl.pallas_call(functools.partial(last_scatter_kernel, nb // 2, nr, cuts,...  81 us
    pallas_call x1, Pallas kernels, attend(): pl.pallas_call(functools.partial(attend_kernel, chips, cuts, tile_o, extr...  78.4 us
    pallas_call x4, Pallas kernels, step(): pl.pallas_call(functools.partial(step_kernel, parts, one_array), grid=(pa...  24.4 us
  transfers between devices with their start and end apart: 1, of which 1 were waited for; matrix products, arithmetic and copies ran while one was open for 0% of the time, Pallas kernels for 3%

profile of v8, /device:TPU:0, one launch (start us, length us, event | category | flops | bytes accessed | tf_op | source)
XLA Modules:
  0.0 507.8 jit_solution(10994649058674967567)
XLA Ops:
  1.3 0.7 multiply_bitcast_fusion
  2.0 0.6 broadcast_in_dim_tile.3.frequency_ref
  2.6 0.1 iota_add_fusion
  2.6 0.1 add.32
  2.7 0.6 compare_select_fusion.k_place
  3.3 127.1 %shard_map.289 = (bf16[1024,2048]{1,0:T(8,128)(2,1)}, bf16[8,64,768]{2,1,0:T(8,128)(2,1)}, bf16[8,64,256]{2,1,0:T(8,128)(2,1)}, bf16[8,64,1024]{2,1,0:T(8,128)(2...) custom-call(s32[1,16]{1,0:T(1,128)} %map_ref.1, ...), custom_call_target="tpu_custom_call" | custom-call | bytes 150000000 | tf_op jit(solution)/shard_map/pallas_call | solution.py:1284
  130.4 78.4 %shard_map.290 = (bf16[1024,256]{1,0:T(8,128)(2,1)}, bf16[1024,256]{1,0:T(8,128)(2,1)}, bf16[1024,256]{1,0:T(8,128)(2,1)}, bf16[1024,256]{1,0:T(8,128)(2,1)}, bf...) custom-call(bf16[1024,2048]{1,0:T(8,128)(2,1)} %get-tuple-element.64, ...), custom_call_target="tpu_custom_call" | custom-call | flops 4294967296 | bytes 150000000 | tf_op jit(solution)/shard_map/pallas_call | solution.py:981
  208.8 94.5 %shard_map.291 = (f32[128,2048]{1,0:T(8,128)}, bf16[128,2048]{1,0:T(8,128)(2,1)}, f32[1,2048]{1,0:T(1,128)}, bf16[1024,1024]{1,0:T(8,128)(2,1)}, bf16[2048,1024]...) custom-call(bf16[128,2048]{1,0:T(8,128)(2,1)} %get-tuple-element.76.h2_here, ...), custom_call_target="tpu_custom_call" | custom-call | flops 38654705664 | bytes 150000000 | tf_op jit(solution)/shard_map/pallas_call | solution.py:763
  303.3 81.8 %shard_map.292 = (bf16[1024,768]{1,0:T(8,128)(2,1)}, f32[128,2048]{1,0:T(8,128)}, bf16[2048,1024]{1,0:T(8,128)(2,1)}, bf16[8,64,1024]{2,1,0:T(8,128)(2,1)}, bf16...) custom-call(bf16[1024,256]{1,0:T(8,128)(2,1)} %get-tuple-element.72.q_ref, ...), custom_call_target="tpu_custom_call" | custom-call | flops 2684354560 | bytes 150000000 | tf_op jit(solution)/shard_map/pallas_call | solution.py:1162
  385.2 81.0 %shard_map.293 = (f32[128,2048]{1,0:T(8,128)}, f32[2,2048]{1,0:T(2,128)}, bf16[8,64,1024]{2,1,0:T(8,128)(2,1)}, bf16[8,64,1024]{2,1,0:T(8,128)(2,1)}, bf16[8,64,1024]{2,1,0:T(8,128)(2,1)}) custom-call(bf16[1024,768]{1,0:T(8,128)(2,1)} %get-tuple-element.88.a_ref, bf16[2048,768]{1,0:T(8,128)(2,1)} %bitcast.40, bf16[128,2048]{1,0:T(8,128)(2,1)} %bitcast.45, ...), custom_call_target="tpu_custom_call" | custom-call | flops 3221225472 | bytes 150000000 | tf_op jit(solution)/shard_map/pallas_call | solution.py:1390
  466.2 4.4 all-to-all-start
  470.6 5.7 %shard_map.295 = (f32[64,8192]{1,0:T(8,128)}, f32[64,8192]{1,0:T(8,128)}, f32[64,8192]{1,0:T(8,128)}) custom-call(bf16[8,64,1024]{2,1,0:T(8,128)(2,1)} %get-tuple-element.101.refs_0_, f32[64,8192]{1,0:T(8,128)} %bitcast.33, f32[64,8192]{1,0:T(8,128)} %bitcast.41, f32[64,8192]{1,0:T(8,128)} %bitcast.42), custom_call_target="tpu_custom_call" | custom-call | bytes 13631488 | tf_op jit(solution)/shard_map/pallas_call | solution.py:1448
  476.3 0.0 copy-start.4
  476.3 0.0 copy-start.1
  476.3 0.0 copy-start.2
  476.3 10.4 %shard_map.294 = (f32[64,16384]{1,0:T(8,128)}, f32[64,16384]{1,0:T(8,128)}, f32[64,16384]{1,0:T(8,128)}) custom-call(bf16[8,64,1024]{2,1,0:T(8,128)(2,1)} %get-tuple-element.98.refs_0_, bf16[8,64,1024]{2,1,0:T(8,128)(2,1)} %get-tuple-element.99.refs_1_, f32[64,16384]{1,0:T(8,128)} %refs_2_.2, f32[64,16384]{1,0:T(8,128)} %refs_3_.4, f32[64,16384]{1,0:T(8,128)} %refs_4_.1), custom_call_target="tpu_custom_call" | custom-call | bytes 27262976 | tf_op jit(solution)/shard_map/pallas_call | solution.py:1448
  486.7 0.0 copy-done.4
  486.7 0.6 fusion.1
  487.4 0.0 copy-done.1
  487.4 0.0 copy-done.2
  487.4 0.9 fusion
  488.3 8.9 %all-to-all-done.refs_0_ = bf16[8,64,1024]{2,1,0:T(8,128)(2,1)S(1)} async-done(((bf16[8,64,1024]{2,1,0:T(8,128)(2,1)}), bf16[8,64,1024]{2,1,0:T(8,128)(2,1)S(1)}, u32[]{:S(2)}, u32[]{:S(2)}) %all-to-all-start) | async-done | bytes 1048608 | tf_op jit(solution)/shard_map/all_to_all | solution.py:1515
  497.2 0.0 copy-start
  497.2 1.0 copy-done
  498.1 2.2 shard_map.297
  500.3 0.0 copy-start.3
  500.3 6.1 %shard_map.296 = (f32[64,6144]{1,0:T(8,128)}, f32[64,6144]{1,0:T(8,128)}, f32[64,6144]{1,0:T(8,128)}) custom-call(bf16[8,64,1024]{2,1,0:T(8,128)(2,1)} %copy-done, f32[64,6144]{1,0:T(8,128)} %refs_1_.1, f32[64,6144]{1,0:T(8,128)} %refs_2_.3, f32[64,6144]{1,0:T(8,128)} %refs_3_.5), custom_call_target="tpu_custom_call" | custom-call | bytes 10223616 | tf_op jit(solution)/shard_map/pallas_call | solution.py:1448
  506.4 0.0 copy-done.3
  506.4 1.0 copy.35
  (2 shorter events, 0.0 us)
Async XLA Ops:
  466.2 31.0 %all-to-all-start = ((bf16[8,64,1024]{2,1,0:T(8,128)(2,1)}), bf16[8,64,1024]{2,1,0:T(8,128)(2,1)S(1)}, u32[]{:S(2)}, u32[]{:S(2)}) async-start(bf16[8,64,1024]{2,1,0:T(8,128)(2,1)} %get-tuple-element.97), calls=%async_computation | async-start | bytes 2097152 | tf_op jit(solution)/shard_map/all_to_all | solution.py:1515
  476.3 10.4 %copy-start.4 = (f32[2,2048]{1,0:T(2,128)S(1)}, f32[2,2048]{1,0:T(2,128)}, u32[]{:S(2)}) copy-start(f32[2,2048]{1,0:T(2,128)} %get-tuple-element.96) | copy-start | bytes 49156
  476.3 11.0 %copy-start.1 = (f32[128,2048]{1,0:T(8,128)S(1)}, f32[128,2048]{1,0:T(8,128)}, u32[]{:S(2)}) copy-start(f32[128,2048]{1,0:T(8,128)} %get-tuple-element.71.x1_ref) | copy-start | bytes 3145732
  476.3 11.0 %copy-start.2 = (f32[128,2048]{1,0:T(8,128)S(1)}, f32[128,2048]{1,0:T(8,128)}, u32[]{:S(2)}) copy-start(f32[128,2048]{1,0:T(8,128)} %get-tuple-element.87) | copy-start | bytes 3145732
  497.2 1.0 copy-start
  500.3 6.1 %copy-start.3 = (f32[128,2048]{1,0:T(8,128)S(1)}, f32[128,2048]{1,0:T(8,128)}, u32[]{:S(2)}) copy-start(f32[128,2048]{1,0:T(8,128)} %get-tuple-element.95) | copy-start | bytes 3145732

commit v9 on v8

--- a/solution.py
+++ b/solution.py
@@ -1065,7 +1065,6 @@
 
     pl.when(step < steps - 1)(lambda: p_load(step + 1).start())
     put(step, lambda rows: hidden_ref.at[rows], red_ref)
-    pl.when(step == 0)(lambda: hop(step))
 
     @pl.when(step > 0)
     def _():
@@ -1109,7 +1108,7 @@
         return (value * cosine - partner(value) * sine).astype(bf16)
 
     mixed_ref[rows, :width] = back(grad_q, cos_ref[rows], sin_ref[rows])
-    pl.when((step > 0) & (step < steps - 1))(lambda: hop(step))
+    pl.when(step < steps - 1)(lambda: hop(step))
 
     @pl.when(step == steps - 1)
     def _():

time: 515 us -> 516 us (level)
  no operation moved by 1% of the time
where the time goes in v9:
time: 516 us; the launch traced here: 508 us
  Pallas kernels  487 us (94%)
  waiting for transfers between devices  8.9 us (2%)
    pallas_call x1, Pallas kernels, first(): pl.pallas_call(functools.partial(first_kernel, nb // 2, cuts, parts), out...  127 us
    pallas_call x1, Pallas kernels, feed_forward(): pl.pallas_call(functools.partial(feed_forward_kernel, nb // 2, cuts, tile...  94.5 us
    pallas_call x1, Pallas kernels, attend_back(): pl.pallas_call(functools.partial(attend_back_kernel, chips, cuts, 1024, e...  81.8 us
    pallas_call x1, Pallas kernels, last_scatter(): pl.pallas_call(functools.partial(last_scatter_kernel, nb // 2, nr, cuts,...  81.3 us
    pallas_call x1, Pallas kernels, attend(): pl.pallas_call(functools.partial(attend_kernel, chips, cuts, tile_o, extr...  78.4 us
    pallas_call x4, Pallas kernels, step(): pl.pallas_call(functools.partial(step_kernel, parts, one_array), grid=(pa...  24.4 us
  transfers between devices with their start and end apart: 1, of which 1 were waited for; matrix products, arithmetic and copies ran while one was open for 0% of the time, Pallas kernels for 3%

profile of v9, /device:TPU:0, one launch (start us, length us, event | category | flops | bytes accessed | tf_op | source)
XLA Modules:
  0.0 508.1 jit_solution(12273934436958914132)
XLA Ops:
  1.3 0.7 multiply_bitcast_fusion
  2.0 0.6 broadcast_in_dim_tile.3.frequency_ref
  2.6 0.1 iota_add_fusion
  2.6 0.1 add.32
  2.7 0.6 compare_select_fusion.k_place
  3.3 127.1 %shard_map.289 = (bf16[1024,2048]{1,0:T(8,128)(2,1)}, bf16[8,64,768]{2,1,0:T(8,128)(2,1)}, bf16[8,64,256]{2,1,0:T(8,128)(2,1)}, bf16[8,64,1024]{2,1,0:T(8,128)(2...) custom-call(s32[1,16]{1,0:T(1,128)} %map_ref.1, ...), custom_call_target="tpu_custom_call" | custom-call | bytes 150000000 | tf_op jit(solution)/shard_map/pallas_call | solution.py:1283
  130.4 78.4 %shard_map.290 = (bf16[1024,256]{1,0:T(8,128)(2,1)}, bf16[1024,256]{1,0:T(8,128)(2,1)}, bf16[1024,256]{1,0:T(8,128)(2,1)}, bf16[1024,256]{1,0:T(8,128)(2,1)}, bf...) custom-call(bf16[1024,2048]{1,0:T(8,128)(2,1)} %get-tuple-element.64, ...), custom_call_target="tpu_custom_call" | custom-call | flops 4294967296 | bytes 150000000 | tf_op jit(solution)/shard_map/pallas_call | solution.py:981
  208.8 94.5 %shard_map.291 = (f32[128,2048]{1,0:T(8,128)}, bf16[128,2048]{1,0:T(8,128)(2,1)}, f32[1,2048]{1,0:T(1,128)}, bf16[1024,1024]{1,0:T(8,128)(2,1)}, bf16[2048,1024]...) custom-call(bf16[128,2048]{1,0:T(8,128)(2,1)} %get-tuple-element.76.h2_here, ...), custom_call_target="tpu_custom_call" | custom-call | flops 38654705664 | bytes 150000000 | tf_op jit(solution)/shard_map/pallas_call | solution.py:763
  303.3 81.8 %shard_map.292 = (bf16[1024,768]{1,0:T(8,128)(2,1)}, f32[128,2048]{1,0:T(8,128)}, bf16[2048,1024]{1,0:T(8,128)(2,1)}, bf16[8,64,1024]{2,1,0:T(8,128)(2,1)}, bf16...) custom-call(bf16[1024,256]{1,0:T(8,128)(2,1)} %get-tuple-element.72.q_ref, ...), custom_call_target="tpu_custom_call" | custom-call | flops 2684354560 | bytes 150000000 | tf_op jit(solution)/shard_map/pallas_call | solution.py:1161
  385.2 81.3 %shard_map.293 = (f32[128,2048]{1,0:T(8,128)}, f32[2,2048]{1,0:T(2,128)}, bf16[8,64,1024]{2,1,0:T(8,128)(2,1)}, bf16[8,64,1024]{2,1,0:T(8,128)(2,1)}, bf16[8,64,1024]{2,1,0:T(8,128)(2,1)}) custom-call(bf16[1024,768]{1,0:T(8,128)(2,1)} %get-tuple-element.88.a_ref, bf16[2048,768]{1,0:T(8,128)(2,1)} %bitcast.40, bf16[128,2048]{1,0:T(8,128)(2,1)} %bitcast.45, ...), custom_call_target="tpu_custom_call" | custom-call | flops 3221225472 | bytes 150000000 | tf_op jit(solution)/shard_map/pallas_call | solution.py:1389
  466.4 4.4 all-to-all-start
  470.8 5.7 %shard_map.295 = (f32[64,8192]{1,0:T(8,128)}, f32[64,8192]{1,0:T(8,128)}, f32[64,8192]{1,0:T(8,128)}) custom-call(bf16[8,64,1024]{2,1,0:T(8,128)(2,1)} %get-tuple-element.101.refs_0_, f32[64,8192]{1,0:T(8,128)} %bitcast.33, f32[64,8192]{1,0:T(8,128)} %bitcast.41, f32[64,8192]{1,0:T(8,128)} %bitcast.42), custom_call_target="tpu_custom_call" | custom-call | bytes 13631488 | tf_op jit(solution)/shard_map/pallas_call | solution.py:1447
  476.6 0.0 copy-start.4
  476.6 0.0 copy-start.1
  476.6 0.0 copy-start.2
  476.6 10.4 %shard_map.294 = (f32[64,16384]{1,0:T(8,128)}, f32[64,16384]{1,0:T(8,128)}, f32[64,16384]{1,0:T(8,128)}) custom-call(bf16[8,64,1024]{2,1,0:T(8,128)(2,1)} %get-tuple-element.98.refs_0_, bf16[8,64,1024]{2,1,0:T(8,128)(2,1)} %get-tuple-element.99.refs_1_, f32[64,16384]{1,0:T(8,128)} %refs_2_.2, f32[64,16384]{1,0:T(8,128)} %refs_3_.4, f32[64,16384]{1,0:T(8,128)} %refs_4_.1), custom_call_target="tpu_custom_call" | custom-call | bytes 27262976 | tf_op jit(solution)/shard_map/pallas_call | solution.py:1447
  487.0 0.0 copy-done.4
  487.0 0.6 fusion.1
  487.6 0.0 copy-done.1
  487.6 0.0 copy-done.2
  487.6 0.9 fusion
  488.5 8.9 %all-to-all-done.refs_0_ = bf16[8,64,1024]{2,1,0:T(8,128)(2,1)S(1)} async-done(((bf16[8,64,1024]{2,1,0:T(8,128)(2,1)}), bf16[8,64,1024]{2,1,0:T(8,128)(2,1)S(1)}, u32[]{:S(2)}, u32[]{:S(2)}) %all-to-all-start) | async-done | bytes 1048608 | tf_op jit(solution)/shard_map/all_to_all | solution.py:1514
  497.4 0.0 copy-start
  497.4 1.0 copy-done
  498.4 2.2 shard_map.297
  500.6 0.0 copy-start.3
  500.6 6.1 %shard_map.296 = (f32[64,6144]{1,0:T(8,128)}, f32[64,6144]{1,0:T(8,128)}, f32[64,6144]{1,0:T(8,128)}) custom-call(bf16[8,64,1024]{2,1,0:T(8,128)(2,1)} %copy-done, f32[64,6144]{1,0:T(8,128)} %refs_1_.1, f32[64,6144]{1,0:T(8,128)} %refs_2_.3, f32[64,6144]{1,0:T(8,128)} %refs_3_.5), custom_call_target="tpu_custom_call" | custom-call | bytes 10223616 | tf_op jit(solution)/shard_map/pallas_call | solution.py:1447
  506.7 0.0 copy-done.3
  506.7 1.0 copy.35
  (2 shorter events, 0.0 us)
Async XLA Ops:
  466.4 31.0 %all-to-all-start = ((bf16[8,64,1024]{2,1,0:T(8,128)(2,1)}), bf16[8,64,1024]{2,1,0:T(8,128)(2,1)S(1)}, u32[]{:S(2)}, u32[]{:S(2)}) async-start(bf16[8,64,1024]{2,1,0:T(8,128)(2,1)} %get-tuple-element.97), calls=%async_computation | async-start | bytes 2097152 | tf_op jit(solution)/shard_map/all_to_all | solution.py:1514
  476.6 10.4 %copy-start.4 = (f32[2,2048]{1,0:T(2,128)S(1)}, f32[2,2048]{1,0:T(2,128)}, u32[]{:S(2)}) copy-start(f32[2,2048]{1,0:T(2,128)} %get-tuple-element.96) | copy-start | bytes 49156
  476.6 11.0 %copy-start.1 = (f32[128,2048]{1,0:T(8,128)S(1)}, f32[128,2048]{1,0:T(8,128)}, u32[]{:S(2)}) copy-start(f32[128,2048]{1,0:T(8,128)} %get-tuple-element.71.x1_ref) | copy-start | bytes 3145732
  476.6 11.0 %copy-start.2 = (f32[128,2048]{1,0:T(8,128)S(1)}, f32[128,2048]{1,0:T(8,128)}, u32[]{:S(2)}) copy-start(f32[128,2048]{1,0:T(8,128)} %get-tuple-element.87) | copy-start | bytes 3145732
  497.4 1.0 copy-start
  500.6 6.1 %copy-start.3 = (f32[128,2048]{1,0:T(8,128)S(1)}, f32[128,2048]{1,0:T(8,128)}, u32[]{:S(2)}) copy-start(f32[128,2048]{1,0:T(8,128)} %get-tuple-element.95) | copy-start | bytes 3145732
